TPU v7x, 32 devices: a whole 2x2x4 slice. The times are simulated.
32 devices in a mesh: cuts: 8 (over z, core), rank: 4 (over y, x).
Axes of the slice: x: 2, y: 2, z: 4, core: 2. Of those that a mesh axis runs over, the one named last changes fastest.
Arguments:
- core_one: float32 [512, 320, 512], P('rank', 'cuts'), may hold values from -6 to 6
- core_two: float32 [512, 320, 512], P('rank', 'cuts'), may hold values from -0.25 to 0.25
- right_sketch: float32 [512, 128], replicated, may hold values from -0.25 to 0.25
- sketch_core: float32 [128, 320, 128], P(None, 'cuts'), may hold values from -0.03125 to 0.03125
Outputs:
- left_core: float32 [512, 320, 128], P('rank', 'cuts')
- middle_core: float32 [128, 320, 128], P('rank', 'cuts')
- carry: float32 [128, 512], replicated
All inputs are finite; a program needn't handle non-finite values.
Results may differ from a plain program's by a relative error of at most 0.00015.
Values sent between devices are 32-bit elements; how exact they have to be, the bound alone decides.
No kernel may reach another device: no remote copies, remote signals or barrier semaphores. Data moves between devices by JAX's collectives and lax.ppermute only.
A program may use at most 128 MiB of HBM per device.

v0:
```python
import jax
import jax.numpy as jnp
from jax import lax
from jax.sharding import PartitionSpec as P

R = 512
NM = 320
L = 128


def orthonormalize(all_rows, own_rows, carry_of):
    highest = lax.Precision.HIGHEST
    local_gram = jnp.dot(
        own_rows.T, own_rows, precision=highest, preferred_element_type=jnp.float32
    )
    gram, raw = lax.psum((local_gram, carry_of(all_rows)), ("cuts", "rank"))
    factor = jnp.linalg.cholesky(gram)
    ortho = lax.linalg.triangular_solve(
        factor, all_rows, left_side=False, lower=True, transpose_a=True
    )
    carried = lax.linalg.triangular_solve(factor, raw, left_side=True, lower=True)
    return (ortho, carried)


def on_device(core_one, core_two, right_sketch, sketch_core):
    highest = lax.Precision.HIGHEST
    local_rows, slices, width = core_one.shape
    sketch_width = right_sketch.shape[1]
    band = sketch_width // lax.axis_size("rank")
    sketched = jnp.einsum("anj,jc->anc", core_two, right_sketch, precision=highest)
    part_bridge = jnp.einsum("anc,bnc->ab", sketched, sketch_core, precision=highest)
    bridge_rows = lax.psum(part_bridge, "cuts")
    flat_one = core_one.reshape(local_rows * slices, width)
    first_rows = jnp.dot(
        flat_one,
        lax.all_gather(bridge_rows, "rank", axis=0, tiled=True),
        precision=highest,
        preferred_element_type=jnp.float32,
    )

    def first_carry_of(matrix):
        return jnp.dot(matrix.T, flat_one, precision=highest, preferred_element_type=jnp.float32)

    first_q, first_carry = orthonormalize(first_rows, first_rows, first_carry_of)
    left_core = (jnp.sqrt(jnp.float32(R * NM)) * first_q).reshape(local_rows, slices, sketch_width)
    offset = lax.axis_index("rank") * local_rows
    local_carry = lax.dynamic_slice_in_dim(first_carry, offset, local_rows, 1)
    projected = lax.psum_scatter(
        jnp.einsum("ba,ank->bnk", local_carry, core_two, precision=highest),
        "rank",
        scatter_dimension=0,
        tiled=True,
    )
    flat_two = projected.reshape(band * slices, width)
    second_rows = jnp.dot(
        flat_two, right_sketch, precision=highest, preferred_element_type=jnp.float32
    )

    def second_carry_of(matrix):
        return jnp.dot(matrix.T, flat_two, precision=highest, preferred_element_type=jnp.float32)

    second_flat, carry = orthonormalize(second_rows, second_rows, second_carry_of)
    second_q = second_flat.reshape(band, slices, sketch_width)
    middle_core = jnp.sqrt(jnp.float32(L * NM)) * second_q
    return (left_core, middle_core, carry)


def solution(mesh):
    placed = (P("rank", "cuts", None), P("rank", "cuts", None), P(), P(None, "cuts", None))
    return jax.shard_map(
        on_device,
        mesh=mesh,
        in_specs=placed,
        out_specs=(P("rank", "cuts", None), P("rank", "cuts", None), P()),
        check_vma=False,
    )
```

profile of v0, /device:TPU:0, one launch (start us, length us, event | category | flops | bytes accessed | tf_op | source)
XLA Modules:
  0.0 558.5 jit_solution(13520730866586099310)
XLA Ops:
  7.2 0.0 copy-start
  7.2 0.0 all-reduce.6.cloned.1.call-start
  7.2 11.3 %fusion.10 = f32[128,40,128]{2,1,0:T(8,128)S(1)} fusion(f32[128,40,512]{2,1,0:T(8,128)} %param.8, f32[512,128]{1,0:T(8,128)} %param.9), kind=kOutput, calls=%fused_computation.8 | convolution fusion | flops 4026531840 | bytes 13369344 | tf_op jit(solution)/shard_map/anj,jc->anc/dot_general | solution.py:30
  18.5 0.0 copy-done
  18.5 3.4 fusion.5
  21.9 0.0 all-reduce.6.cloned.1.call-update
  21.9 0.0 all-reduce.10.cloned.1.call-start
  22.0 56.4 %all-reduce.6.cloned.1.call-done = f32[128,128]{1,0:T(8,128)} async-done(((f32[128,128]{1,0:T(8,128)}), f32[128,128]{1,0:T(8,128)}) %all-reduce.6.cloned.1.call-update) | async-done | bytes 65552 | tf_op jit(solution)/shard_map/psum | solution.py:32
  78.4 9.6 %all_gather.3 = f32[512,128]{1,0:T(8,128)S(1)} all-gather(f32[128,128]{1,0:T(8,128)} %all-reduce.6.cloned.1.call-done), channel_id=1, replica_groups=mesh['cuts'=8,'rank'=4] {'rank'}, dimensions={0}, use_global_device_ids=true | all-gather | bytes 327680 | tf_op jit(solution)/shard_map/all_gather | solution.py:36
  88.0 13.9 %fusion.25 = f32[128,5120]{1,0:T(8,128)S(1)} fusion(f32[512,128]{1,0:T(8,128)S(1)} %all_gather.3, f32[5120,512]{1,0:T(8,128)} %bitcast.57), kind=kOutput, calls=%fused_computation.33 | convolution fusion | flops 4026531840 | bytes 13369344 | tf_op jit(solution)/shard_map/dot_general | solution.py:34
  102.0 0.0 copy-start.1
  102.0 2.8 fusion.26
  104.8 0.0 copy-done.1
  104.8 9.3 %fusion.27 = f32[128,512]{1,0:T(8,128)} fusion(f32[128,5120]{1,0:T(8,128)S(1)} %fusion.25, f32[5120,512]{1,0:T(8,128)} %bitcast.58), kind=kOutput, calls=%fused_computation.35 | convolution fusion | flops 4026531840 | bytes 13369344 | tf_op jit(solution)/shard_map/dot_general | solution.py:42
  114.1 0.0 all-reduce.10.cloned.1.call-update
  114.1 0.4 reduce-scatter.2.cloned.1.call-start
  114.6 123.5 %all-reduce.10.cloned.1.call-done = (f32[128,128]{0,1:T(8,128)}, f32[128,512]{1,0:T(8,128)}) async-done(((f32[128,128]{0,1:T(8,128)}, f32[128,512]{1,0:T(8,128)}), (f32[128,128]{0,1:T(8,128)}, f32[128,512]{1,0:T(8,128)})) %all-reduce.10.cloned.1.call-update) | async-done | bytes 327696 | tf_op jit(solution)/shard_map/psum | solution.py:16
  238.1 0.9 copy.14
  239.1 0.9 fusion.22
  239.9 11.7 %cholesky.44 = f32[128,128]{1,0:T(8,128)S(1)} custom-call(f32[128,128]{1,0:T(8,128)S(1)} %fusion.22), custom_call_target="Cholesky" | custom-call | tf_op jit(solution)/shard_map/jit(cholesky)/cholesky | solution.py:17
  251.7 0.6 compare_reduce_fusion.1
  252.3 0.7 fusion.12
  253.0 9.8 %custom-call.11 = f32[1,128,128]{1,2,0:T(8,128)S(1)} custom-call(f32[1,128,128]{2,1,0:T(8,128)S(1)} %fusion.12), custom_call_target="InvertDiagBlocksLowerTriangular" | custom-call | tf_op jit(solution)/shard_map/triangular_solve | solution.py:18
  262.8 0.0 copy-start.3
  262.8 1.4 fusion.19
  264.2 18.5 %fusion = f32[128,40,512]{2,0,1:T(8,128)} fusion(f32[128,40,512]{2,1,0:T(8,128)} %param.8, f32[128,512]{1,0:T(8,128)S(1)} %fusion.19, s32[]{:T(128)S(6)} %select_n.6), kind=kOutput, calls=%fused_computation | convolution fusion | flops 4026531840 | bytes 21037060 | tf_op jit(solution)/shard_map/ba,ank->bnk/dot_general | solution.py:49
  282.7 0.0 copy-done.3
  282.7 0.0 reduce-scatter.2.cloned.1.call-update
  282.7 0.0 copy-start.2
  282.8 0.2 all-reduce.8.cloned.1.call-start
  283.0 104.4 %reduce-scatter.2.cloned.1.call-done = f32[32,40,512]{2,0,1:T(8,128)} async-done(((f32[128,40,512]{2,0,1:T(8,128)}), f32[32,40,512]{2,0,1:T(8,128)}) %reduce-scatter.2.cloned.1.call-update) | async-done | bytes 2621456 | tf_op jit(solution)/shard_map/reduce_scatter | solution.py:48
  387.4 3.3 copy.16
  390.7 0.0 copy-done.2
  390.7 2.2 fusion.28
  392.9 0.0 copy-start.4
  392.9 2.4 fusion.30
  395.3 1.8 fusion.29
  397.2 0.0 all-reduce.8.cloned.1.call-update
  397.2 0.0 copy-done.4
  397.2 7.5 %convolution_multiply_fusion = f32[5120,128]{1,0:T(8,128)} fusion(f32[128,5120]{1,0:T(8,128)} %copy-done.1, f32[1,128,128]{1,2,0:T(8,128)S(1)} %copy-done.4), kind=kOutput, calls=%fused_computation.2 | convolution fusion | flops 1007288320 | bytes 5308416 | tf_op jit(solution)/shard_map/triangular_solve | solution.py:18
  404.7 118.6 %all-reduce.8.cloned.1.call-done = (f32[128,128]{0,1:T(8,128)}, f32[128,512]{1,0:T(8,128)}) async-done(((f32[128,128]{0,1:T(8,128)}, f32[128,512]{1,0:T(8,128)}), (f32[128,128]{0,1:T(8,128)}, f32[128,512]{1,0:T(8,128)})) %all-reduce.8.cloned.1.call-update) | async-done | bytes 327696 | tf_op jit(solution)/shard_map/psum | solution.py:16
  523.3 0.9 copy.18
  524.2 0.9 fusion.17
  525.1 11.9 %cholesky.55 = f32[128,128]{1,0:T(8,128)S(1)} custom-call(f32[128,128]{1,0:T(8,128)S(1)} %fusion.17), custom_call_target="Cholesky" | custom-call | tf_op jit(solution)/shard_map/jit(cholesky)/cholesky | solution.py:17
  537.0 0.6 compare_reduce_fusion
  537.6 0.7 fusion.13
  538.3 9.8 %custom-call.12 = f32[1,128,128]{1,2,0:T(8,128)S(1)} custom-call(f32[1,128,128]{2,1,0:T(8,128)S(1)} %fusion.13), custom_call_target="InvertDiagBlocksLowerTriangular" | custom-call | tf_op jit(solution)/shard_map/triangular_solve | solution.py:18
  548.1 1.5 convolution_multiply_fusion.1
  549.6 2.1 fusion.15
  (2 shorter events, 0.1 us)
Async XLA Ops:
  7.2 11.3 %copy-start = (f32[128,40,128]{2,1,0:T(8,128)S(1)}, f32[128,40,128]{2,1,0:T(8,128)}, u32[]{:S(2)}) copy-start(f32[128,40,128]{2,1,0:T(8,128)} %param.10) | copy-start | bytes 7864324
  7.2 71.2 %all-reduce.6.cloned.1.call-start = ((), (), s32[]{:S(2)}) async-start(), calls=%async_computation.1 | async-start | bytes 131072 | tf_op jit(solution)/shard_map/psum | solution.py:32
  21.9 216.2 %all-reduce.10.cloned.1.call-start = ((), (), s32[]{:S(2)}) async-start(), calls=%async_computation.4 | async-start | bytes 655360 | tf_op jit(solution)/shard_map/psum | solution.py:16
  102.0 2.9 copy-start.1
  114.1 273.3 %reduce-scatter.2.cloned.1.call-start = ((), (), s32[]{:S(2)}) async-start(), calls=%async_computation.2 | async-start | bytes 13107200 | tf_op jit(solution)/shard_map/reduce_scatter | solution.py:48
  262.8 19.9 %copy-start.3 = (f32[1,128,128]{1,2,0:T(8,128)}, f32[1,128,128]{1,2,0:T(8,128)S(1)}, u32[]{:S(2)}) copy-start(f32[1,128,128]{1,2,0:T(8,128)S(1)} %custom-call.11) | copy-start | bytes 196612
  282.7 107.9 %copy-start.2 = (f32[512,128]{1,0:T(8,128)S(1)}, f32[512,128]{1,0:T(8,128)}, u32[]{:S(2)}) copy-start(f32[512,128]{1,0:T(8,128)} %param.9) | copy-start | bytes 786436
  282.8 240.5 %all-reduce.8.cloned.1.call-start = ((), (), s32[]{:S(2)}) async-start(), calls=%async_computation.3 | async-start | bytes 655360 | tf_op jit(solution)/shard_map/psum | solution.py:16
  392.9 4.3 copy-start.4
Sparse Core Ops, SparseCore 0:
  22.1 56.3 all-reduce.5
  114.3 123.8 all-reduce.9
  282.9 104.5 reduce-scatter.1
  397.3 125.8 all-reduce.7
where the time goes:
time: 565 us; the launch traced here: 558 us
  waiting for transfers between devices  403 us (71%)
  matrix products  78.1 us (14%)
  other arithmetic  47.6 us (8%)
  between operations  14.1 us (2%)
  blocking collectives  9.62 us (2%)
    psum x2, waiting for transfers between devices, orthonormalize(): gram, raw = lax.psum((local_gram, carry_of(all_rows)), ('cuts', 'rank'))  242 us
    reduce_scatter x1, waiting for transfers between devices, on_device(): lax.psum_scatter(jnp.einsum('ba,ank->bnk', local_carry, core_two, precisi...  104 us
    psum x1, waiting for transfers between devices, on_device(): bridge_rows = lax.psum(part_bridge, 'cuts')  56.4 us
    another operation x6, other arithmetic, orthonormalize(): factor = jnp.linalg.cholesky(gram)  25 us
    another operation x4, other arithmetic, orthonormalize(): lax.linalg.triangular_solve(factor, all_rows, left_side=False, lower=True...  20.9 us
    dot_general x1, matrix products, on_device(): jnp.einsum('ba,ank->bnk', local_carry, core_two, precision=highest)  18.5 us
    dot_general x1, matrix products, on_device(): jnp.dot(flat_one, lax.all_gather(bridge_rows, 'rank', axis=0, tiled=True)...  13.9 us
  transfers between devices with their start and end apart: 4, of which 4 were waited for; matrix products, arithmetic and copies ran while one was open for 1% of the time, Pallas kernels for 0%

commit v1 on v0

v1 whole, which is shorter than its diff:
```python
import functools
import math

import jax
import jax.numpy as jnp
from jax import lax
from jax.experimental import pallas as pl
from jax.experimental.pallas import tpu as pltpu
from jax.sharding import PartitionSpec as P

NT = (((1,), (1,)), ((), ()))
NN = (((1,), (0,)), ((), ()))
TN = (((0,), (0,)), ((), ()))
VMEM_LIMIT = 56 * 1024 * 1024
BLOCK = 8


def call(kernel, flops, size, **more):
    return pl.pallas_call(
        kernel,
        compiler_params=pltpu.CompilerParams(vmem_limit_bytes=VMEM_LIMIT),
        cost_estimate=pl.CostEstimate(flops=flops, bytes_accessed=size, transcendentals=0),
        **more,
    )


def shape(*extent):
    return jax.ShapeDtypeStruct(extent, jnp.float32)


def split(value):
    high = value.astype(jnp.bfloat16)
    return high, (value - high.astype(jnp.float32)).astype(jnp.bfloat16)


def mxu(a, b, form):
    return lax.dot_general(a, b, form, preferred_element_type=jnp.float32)


def exact(a, b, form):
    return lax.dot_general(a, b, form, precision=lax.Precision.HIGHEST, preferred_element_type=jnp.float32)


def both_parts(value, axis):
    return jnp.concatenate(split(value), axis=axis)


def fold(value, axis):
    half = value.shape[axis] // 2
    return lax.slice_in_dim(value, 0, half, axis=axis) + lax.slice_in_dim(value, half, 2 * half, axis=axis)


def rows_of(ref):
    return ref.reshape(ref.shape[0] * ref.shape[1], ref.shape[2])


def sketch_kernel(core_ref, right_ref, left_ref, sketched_ref, part_ref, rows_ref):
    local_rows, block, _ = core_ref.shape
    columns = right_ref.shape[1]
    right = both_parts(right_ref[...], 1)
    product = mxu(both_parts(rows_of(core_ref)[...], 0), right, NN)
    rows_ref[...] = fold(fold(product, 0), 1)
    left_rows = rows_of(left_ref)

    @pl.when(pl.program_id(0) == 0)
    def _():
        part_ref[...] = jnp.zeros_like(part_ref)

    total = jnp.zeros(part_ref.shape, jnp.float32)
    for pair in range(0, block, 2):
        sides, lefts = [], []
        for n in (pair, pair + 1):
            rows = rows_ref[pl.ds(n, local_rows, stride=block), :]
            sketched_ref[n] = rows
            sides.append(rows)
            lefts.append(left_rows[pl.ds(n, columns, stride=block), :])
        side = both_parts(jnp.concatenate(sides, axis=1), 0)
        left = both_parts(jnp.concatenate(lefts, axis=1), 0)
        total = total + fold(fold(mxu(side, left, NT), 0), 1)
    part_ref[...] += total


def sketch(core_two, right_sketch, sketch_core):
    local_rows, slices, width = core_two.shape
    columns = right_sketch.shape[1]
    return call(
        sketch_kernel,
        2 * core_two.size * columns * 4,
        4 * (core_two.size + 2 * sketch_core.size),
        grid=(slices // BLOCK,),
        in_specs=[
            pl.BlockSpec((local_rows, BLOCK, width), lambda i: (0, i, 0)),
            pl.BlockSpec((width, columns), lambda i: (0, 0)),
            pl.BlockSpec((columns, BLOCK, columns), lambda i: (0, i, 0)),
        ],
        out_specs=[
            pl.BlockSpec((BLOCK, local_rows, columns), lambda i: (i, 0, 0)),
            pl.BlockSpec((local_rows, columns), lambda i: (0, 0)),
        ],
        out_shape=[shape(slices, local_rows, columns), shape(local_rows, columns)],
        scratch_shapes=[pltpu.VMEM((local_rows * BLOCK, columns), jnp.float32)],
    )(core_two, right_sketch, sketch_core)


def block_of(rows):
    block = 1024
    while rows % block:
        block //= 2
    return block


def square_kernel(core_ref, core_index_ref, keep_ref, give_ref, sum_ref):
    step = pl.program_id(0)
    width = core_ref.shape[1]
    high, low = split(core_ref[...])

    @pl.when(step == 0)
    def _():
        sum_ref[...] = jnp.zeros_like(sum_ref)

    sum_ref[...] += mxu(high, jnp.concatenate([high, low], axis=1), TN)

    @pl.when(step == pl.num_programs(0) - 1)
    def _():
        cross = sum_ref[:, width:]
        sum_ref[:, :width] = sum_ref[:, :width] + cross + cross.T
        half = width // 2
        own = core_index_ref[0]
        keep_ref[...] = sum_ref[pl.ds(pl.multiple_of(own * half, half), half), :width]
        give_ref[...] = sum_ref[pl.ds(pl.multiple_of((1 - own) * half, half), half), :width]


def square_of(flat_one, core_index):
    rows, width = flat_one.shape
    block = block_of(rows)
    half = pl.BlockSpec((width // 2, width), lambda i: (0, 0))
    return call(
        square_kernel,
        4 * rows * width * width,
        4 * flat_one.size,
        grid=(rows // block,),
        in_specs=[
            pl.BlockSpec((block, width), lambda i: (i, 0)),
            pl.BlockSpec(memory_space=pltpu.SMEM),
        ],
        out_specs=[half, half],
        out_shape=[shape(width // 2, width)] * 2,
        scratch_shapes=[pltpu.VMEM((width, 2 * width), jnp.float32)],
    )(flat_one, core_index)


def loose_kernel(halves, rank_ref, raw_ref, *refs):
    piece_refs, out_refs = refs[:-len(halves)], refs[-len(halves):]
    ranks = len(piece_refs) // len(halves)
    local_rows = piece_refs[0].shape[1]
    rows = []
    for offset in range(ranks):
        start = pl.multiple_of((rank_ref[0] ^ offset) * local_rows, local_rows)
        rows.append(raw_ref[pl.ds(start, local_rows), :])
    raw = both_parts(jnp.concatenate(rows, axis=0), 1).T
    for half, count in enumerate(halves):
        refs = piece_refs[half * ranks:(half + 1) * ranks]
        for n in range(count):
            value = jnp.concatenate([ref[n] for ref in refs], axis=0)
            product = mxu(raw, jnp.concatenate(split(value), axis=1), NN)
            out_refs[half][n] = fold(fold(product, 0), 1)


def loosen(rank_index, raw, pieces, halves):
    columns = raw.shape[1]
    size = sum(piece.size for piece in pieces)
    whole = pl.BlockSpec(memory_space=pltpu.VMEM)
    return call(
        functools.partial(loose_kernel, halves),
        8 * size * columns,
        4 * raw.size + 4 * size,
        in_specs=[pl.BlockSpec(memory_space=pltpu.SMEM)] + [whole] * (len(pieces) + 1),
        out_specs=[whole] * len(halves),
        out_shape=[shape(count, columns, columns) for count in halves],
    )(rank_index, raw, *pieces)


def carry_kernel(halves, share, rank_ref, weight_ref, core_ref, *refs):
    piece_refs = refs[:-4]
    joined_ref, middle_ref, rows_ref, sum_ref = refs[-4:]
    step = pl.program_id(0)
    block, width = core_ref.shape
    columns = weight_ref.shape[1]
    ranks = len(piece_refs) // len(halves)
    room = share * ranks
    local_rows = rows_ref.shape[0] // room
    band = middle_ref.shape[0] // room

    @pl.when(step == 0)
    def _():
        sum_ref[...] = jnp.zeros_like(sum_ref)
        weight_high, weight_low = split(weight_ref[...])
        weight = jnp.concatenate([weight_high, weight_low], axis=0)
        for half, count in enumerate(halves):
            for offset in range(ranks):
                ref = piece_refs[half * ranks + offset]
                first = (rank_ref[0] ^ offset) * share + sum(halves[:half])
                high, low = split(jnp.concatenate([ref[n] for n in range(count)], axis=1))
                spread = fold(mxu(weight, high, NN), 0) + mxu(weight_high, low, NN)
                for n in range(count):
                    piece = lax.slice_in_dim(spread, n * columns, (n + 1) * columns, axis=1)
                    rows_ref[pl.ds(first + n, local_rows, stride=room), :] = piece[:local_rows]
                    middle_ref[pl.ds(first + n, band, stride=room), :] = piece[local_rows:]

    rows = both_parts(rows_ref[pl.ds(pl.multiple_of(step * block, block), block), :], 1)
    product = mxu(rows, both_parts(core_ref[...], 1), TN)
    product = fold(fold(product, 0), 1)
    sum_ref[...] += product

    @pl.when(step == pl.num_programs(0) - 1)
    def _():
        joined_ref[:width, :] = sum_ref[...].T
        middle = both_parts(middle_ref[...], 1)
        joined_ref[width:, :] = fold(fold(mxu(middle, middle, TN), 0), 1)


def carry_rows(rank_index, weight, flat_two, pieces, halves, share, band):
    rows, width = flat_two.shape
    columns = weight.shape[1]
    block = block_of(rows)
    ranks = len(pieces) // len(halves)
    whole = pl.BlockSpec(memory_space=pltpu.VMEM)
    return call(
        functools.partial(carry_kernel, halves, share),
        8 * flat_two.size * columns,
        4 * flat_two.size + 4 * sum(piece.size for piece in pieces),
        grid=(rows // block,),
        in_specs=[
            pl.BlockSpec(memory_space=pltpu.SMEM),
            pl.BlockSpec((weight.shape[0], columns), lambda i: (0, 0)),
            pl.BlockSpec((block, width), lambda i: (i, 0)),
        ]
        + [pl.BlockSpec(piece.shape, lambda i: (0, 0, 0)) for piece in pieces],
        out_specs=[
            pl.BlockSpec((width + columns, columns), lambda i: (0, 0)),
            pl.BlockSpec((band * share * ranks, columns), lambda i: (0, 0)),
        ],
        out_shape=[shape(width + columns, columns), shape(band * share * ranks, columns)],
        scratch_shapes=[pltpu.VMEM((rows, columns), jnp.float32), pltpu.VMEM((columns, width), jnp.float32)],
    )(rank_index, weight, flat_two, *pieces)


def apply_kernel(rows_ref, weight_ref, out_ref):
    weight = both_parts(weight_ref[...], 1)
    product = mxu(both_parts(rows_ref[...], 0), weight, NN)
    out_ref[...] = fold(fold(product, 0), 1)


def apply_to(rows, weight):
    count, width = rows.shape
    columns = weight.shape[1]
    block = block_of(count)
    return call(
        apply_kernel,
        8 * rows.size * columns,
        4 * (rows.size + count * columns),
        grid=(count // block,),
        in_specs=[
            pl.BlockSpec((block, width), lambda i: (i, 0)),
            pl.BlockSpec((width, columns), lambda i: (0, 0)),
        ],
        out_specs=pl.BlockSpec((block, columns), lambda i: (i, 0)),
        out_shape=shape(count, columns),
    )(rows, weight)


def small_inverse(entry):
    size = len(entry)
    entry = [list(row) for row in entry]
    inverse = [[None] * size for _ in range(size)]
    for k in range(size):
        pivot = entry[k][k]
        root = lax.rsqrt(pivot)
        root = root * (1.5 - 0.5 * pivot * root * root)
        inverse[k][k] = root
        for i in range(k + 1, size):
            entry[i][k] = entry[i][k] * root
        for i in range(k + 1, size):
            for m in range(k + 1, i + 1):
                entry[i][m] = entry[i][m] - entry[i][k] * entry[m][k]
    for k in range(size):
        for i in range(k + 1, size):
            total = entry[i][k] * inverse[k][k]
            for m in range(k + 1, i):
                total = total + entry[i][m] * inverse[m][k]
            inverse[i][k] = -total * inverse[i][i]
    return inverse


def factor(gram, inverse_ref):
    size, tile = gram.shape[0], BLOCK
    count = size // tile
    left = [gram[i * tile:(i + 1) * tile, :] for i in range(count)]
    lane = lax.broadcasted_iota(jnp.int32, (tile, size), 1)
    sublane = lax.broadcasted_iota(jnp.int32, (tile, size), 0)
    right = [jnp.where(lane == sublane + i * tile, 1.0, 0.0) for i in range(count)]

    def spread(value, row, column):
        return jnp.broadcast_to(value[row:row + 1, column:column + 1], (tile, size))

    for j in range(count):
        corner = [[spread(left[j], i, j * tile + k) for k in range(i + 1)] for i in range(tile)]
        small = small_inverse(corner)
        columns = []
        for k in range(tile):
            column = jnp.where(sublane == k, small[k][k], 0.0)
            for i in range(k + 1, tile):
                column = jnp.where(sublane == i, small[i][k], column)
            columns.append(column)
        done_left = sum(columns[k] * left[j][k:k + 1, :] for k in range(tile))
        done_right = sum(columns[k] * right[j][k:k + 1, :] for k in range(tile))
        inverse_ref[pl.ds(j * tile, tile), :] = done_right
        if j + 1 < count:
            turned = done_left.T
            for i in range(j + 1, count):
                for k in range(tile):
                    factor = jnp.broadcast_to(turned[i * tile:(i + 1) * tile, k:k + 1], (tile, size))
                    left[i] = left[i] - factor * done_left[k:k + 1, :]
                    right[i] = right[i] - factor * done_right[k:k + 1, :]


def first_kernel(scale, band, rank_ref, bridge_ref, raw_ref, weight_ref, solve_ref, inverse_ref):
    local_rows = weight_ref.shape[0] - band
    factor(exact(bridge_ref[...], raw_ref[...], TN), inverse_ref)
    inverse = inverse_ref[...]
    start = pl.multiple_of(rank_ref[0] * local_rows, local_rows)
    own = exact(raw_ref[pl.ds(start, local_rows), :], inverse, NT)
    weight_ref[:local_rows, :] = exact(own, inverse, NN)
    weight_ref[local_rows:, :] = inverse_ref[pl.ds(pl.multiple_of(rank_ref[0] * band, band), band), :]
    solve_ref[...] = scale * exact(bridge_ref[...], inverse, NT)


def first_factor(rank_index, bridge, raw, scale, local_rows, band):
    columns = raw.shape[1]
    whole = pl.BlockSpec(memory_space=pltpu.VMEM)
    return call(
        functools.partial(first_kernel, scale, band),
        8 * raw.size * columns,
        16 * raw.size,
        in_specs=[pl.BlockSpec(memory_space=pltpu.SMEM), whole, whole],
        out_specs=[whole, whole],
        out_shape=[shape(local_rows + band, columns), shape(*raw.shape)],
        scratch_shapes=[pltpu.VMEM((columns, columns), jnp.float32)],
    )(rank_index, bridge, raw)


def last_kernel(scale, joined_ref, middle_ref, carry_ref, out_ref, inverse_ref):
    columns = inverse_ref.shape[0]
    width = carry_ref.shape[1]
    factor(joined_ref[pl.ds(width, columns), :], inverse_ref)
    inverse = inverse_ref[...]
    carry_ref[...] = exact(inverse, joined_ref[pl.ds(0, width), :], NT)
    out_ref[...] = exact(middle_ref[...], scale * inverse, NT)


def last_factor(joined, middle, scale, width):
    columns = joined.shape[1]
    whole = pl.BlockSpec(memory_space=pltpu.VMEM)
    return call(
        functools.partial(last_kernel, scale),
        8 * middle.size * columns,
        8 * middle.size,
        in_specs=[whole, whole],
        out_specs=[whole, whole],
        out_shape=[shape(columns, width), shape(*middle.shape)],
        scratch_shapes=[pltpu.VMEM((columns, columns), jnp.float32)],
    )(joined, middle)


def swap(value, axis, offset):
    return lax.ppermute(value, axis, [(i, i ^ offset) for i in range(lax.axis_size(axis))])


def exchange(value, axes, groups=None):
    return lax.all_to_all(value, axes, 0, 0, axis_index_groups=groups, tiled=True)


def gather_all(value, axes):
    parts = lax.axis_size(axes)
    return exchange(jnp.broadcast_to(value[None], (parts,) + value.shape), axes)


def after(value, others):
    return lax.optimization_barrier((value, others))


def on_device(core_one, core_two, right_sketch, sketch_core):
    local_rows, slices, width = core_one.shape
    columns = right_sketch.shape[1]
    ranks, cuts = lax.axis_size("rank"), lax.axis_size("cuts")
    rank, cut = lax.axis_index("rank"), lax.axis_index("cuts")
    rank_index = rank.astype(jnp.int32).reshape(1)
    core_index = lax.rem(cut, 2).astype(jnp.int32).reshape(1)
    both = ("cuts", "rank")
    parts = ranks * cuts
    band = columns // ranks
    share = -(-slices // ranks)
    room = share * ranks
    halves = [share // 2, share - share // 2]
    core_groups = [
        [z * ranks + place for z in range(core, cuts, 2) for place in range(ranks)] for core in range(2)
    ]
    filler = ((0, 0), (0, room - slices), (0, 0))
    core_two, sketch_core = jnp.pad(core_two, filler), jnp.pad(sketch_core, filler)
    flat_one = core_one.reshape(local_rows * slices, width)
    flat_two = core_two.reshape(local_rows * room, width)

    sketched, part = sketch(core_two, right_sketch, sketch_core)

    def piece(half, offset):
        start = (rank ^ offset) * share + half * halves[0]
        return lax.dynamic_slice_in_dim(sketched, start, halves[half], 0)

    def send(names, behind):
        found = [piece(*name) for name in names]
        if behind is not None:
            found, _ = after(found, behind)
        return {name: swap(value, "rank", name[1]) for name, value in zip(names, found)}

    far = ranks - 1
    pieces = {(half, 0): piece(half, 0) for half in range(2)}
    near = [[(half, offset) for offset in range(1, far)] for half in range(2)]

    moved = send(near[0], None)
    bridge_rows = jnp.sum(exchange(part.reshape(cuts, local_rows // cuts, columns), "cuts"), axis=0)
    flat_late, part = after(flat_one, part)
    keep, give = square_of(flat_late, core_index)
    bridge_rows, moved = after(bridge_rows, moved)
    pieces.update(moved)

    moved = send(near[1], bridge_rows)
    bridge = gather_all(bridge_rows, both)
    bridge = bridge.reshape(cuts, ranks, -1, columns).swapaxes(0, 1).reshape(width, columns)
    square = keep + swap(give, "cuts", 1)
    square, moved = after(square, moved)
    pieces.update(moved)

    moved = send([(0, far)], square)
    square = exchange(square.reshape(parts // 2, -1, width), both, core_groups)
    raw_rows = exact(jnp.sum(square, axis=0), bridge, NN)
    raw_rows, moved = after(raw_rows, moved)
    pieces.update(moved)

    pieces.update(send([(1, far)], raw_rows))
    raw = gather_all(raw_rows, both).reshape(cuts // 2, 2, ranks, -1, columns)
    raw = raw.transpose(1, 0, 2, 3, 4).reshape(width, columns)

    ordered = [pieces[(half, offset)] for half in range(2) for offset in range(ranks)]
    loose = loosen(rank_index, raw, ordered, halves)
    loose, (bridge, raw) = after(loose, (bridge, raw))

    bits = [1 << bit for bit in range((ranks - 1).bit_length())]
    everyone = []
    for value, order in zip(loose, (bits, bits[::-1])):
        found = {0: value}
        for bit in order:
            found.update({offset ^ bit: swap(held, "rank", bit) for offset, held in list(found.items())})
        everyone += [found[offset] for offset in range(ranks)]

    scale = math.sqrt(local_rows * ranks * slices * cuts)
    weight, solve = first_factor(rank_index, bridge, raw, scale, local_rows, band)
    joined, middle = carry_rows(rank_index, weight, flat_two, everyone, halves, share, band)
    total = joined.shape[0]
    joined = jnp.pad(joined, ((0, -total % parts), (0, 0))).reshape(parts, -1, columns)
    joined = jnp.sum(exchange(joined, both), axis=0)
    joined = lax.all_gather(joined, both, axis=0, tiled=True)[:total]
    left_core = apply_to(flat_one, solve).reshape(local_rows, slices, columns)
    scale = math.sqrt(columns * slices * cuts)
    carry, middle = last_factor(joined, middle, scale, width)
    middle_core = middle.reshape(band, room, columns)[:, :slices]
    return (left_core, middle_core, carry)


def solution(mesh):
    placed = (P("rank", "cuts", None), P("rank", "cuts", None), P(), P(None, "cuts", None))
    return jax.shard_map(
        on_device,
        mesh=mesh,
        in_specs=placed,
        out_specs=(P("rank", "cuts", None), P("rank", "cuts", None), P()),
        check_vma=False,
    )
```

time: 565 us -> 229 us (0.41); the launches traced: 558 us -> 228 us
  waiting for transfers between devices: 403 us -> 46.2 us
  matrix products: 78.1 us -> 0.24 us
  Pallas kernels: 0 us -> 61.8 us
  blocking collectives: 9.62 us -> 66.7 us
  other arithmetic: 47.6 us -> 2 us
  starting transfers between devices: 0.74 us -> 41.5 us
  between operations: 14.1 us -> 0.79 us
    psum x3 -> x0, waiting for transfers between devices: 299 us -> none  [the longest x2 242 us: orthonormalize(): gram, raw = lax.psum((local_gram, carry_of(all_rows)), ('cuts', 'rank'))]
    reduce_scatter x1 -> x0, waiting for transfers between devices: 104 us -> none  [on_device(): lax.psum_scatter(jnp.einsum('ba,ank->bnk', local_carry, core_two, precisi...]
    dot_general x9 -> x1, matrix products: 65.7 us -> 0.24 us  [exact(): lax.dot_general(a, b, form, precision=lax.Precision.HIGHEST, preferred_el...]
    pallas_call x0 -> x7, Pallas kernels: none -> 61.8 us  [the longest x1 11.1 us: square_of(): call(square_kernel, 4 * rows * width * width, 4 * flat_one.size, grid=(ro...]
    all_gather x1, blocking collectives: 9.62 us -> 66.7 us  [on_device(): joined = lax.all_gather(joined, both, axis=0, tiled=True)[:total]]
    another operation x10 -> x0, other arithmetic: 45.9 us -> none  [the longest x6 25 us: orthonormalize(): factor = jnp.linalg.cholesky(gram)]
    all_to_all x0 -> x5, waiting for transfers between devices: none -> 25.8 us  [exchange(): lax.all_to_all(value, axes, 0, 0, axis_index_groups=groups, tiled=True)]
    all_to_all x0 -> x5, starting transfers between devices: none -> 23.9 us  [exchange(): lax.all_to_all(value, axes, 0, 0, axis_index_groups=groups, tiled=True)]
  transfers between devices with their start and end apart: 4 -> 18, of which waited for: 4 -> 10; matrix products, arithmetic and copies ran while one was open for 1% -> 3% of each run, Pallas kernels for 0% -> 13%
where the time goes in v1:
time: 229 us; the launch traced here: 228 us
  blocking collectives  66.7 us (29%)
  Pallas kernels  61.8 us (27%)
  waiting for transfers between devices  46.2 us (20%)
  starting transfers between devices  41.5 us (18%)
  local copies, waits for them, and re-layouts  9.11 us (4%)
    all_gather x1, blocking collectives, on_device(): joined = lax.all_gather(joined, both, axis=0, tiled=True)[:total]  66.7 us
    all_to_all x5, waiting for transfers between devices, exchange(): lax.all_to_all(value, axes, 0, 0, axis_index_groups=groups, tiled=True)  25.8 us
    all_to_all x5, starting transfers between devices, exchange(): lax.all_to_all(value, axes, 0, 0, axis_index_groups=groups, tiled=True)  23.9 us
    ppermute x13, waiting for transfers between devices, swap(): lax.ppermute(value, axis, [(i, i ^ offset) for i in range(lax.axis_size(a...  20.4 us
    ppermute x13, starting transfers between devices, swap(): lax.ppermute(value, axis, [(i, i ^ offset) for i in range(lax.axis_size(a...  17.6 us
    pallas_call x1, Pallas kernels, square_of(): call(square_kernel, 4 * rows * width * width, 4 * flat_one.size, grid=(ro...  11.1 us
    pallas_call x1, Pallas kernels, carry_rows(): call(functools.partial(carry_kernel, halves, share), 8 * flat_two.size *...  10.6 us
    pallas_call x1, Pallas kernels, sketch(): call(sketch_kernel, 2 * core_two.size * columns * 4, 4 * (core_two.size +...  9.82 us
  transfers between devices with their start and end apart: 18, of which 10 were waited for; matrix products, arithmetic and copies ran while one was open for 3% of the time, Pallas kernels for 13%

profile of v1, /device:TPU:0, one launch (start us, length us, event | category | flops | bytes accessed | tf_op | source)
XLA Modules:
  0.0 228.5 jit_solution(15091700801966993710)
XLA Ops:
  0.6 9.8 %shard_map.67 = (f32[40,128,128]{2,1,0:T(8,128)}, f32[128,128]{1,0:T(8,128)}) custom-call(f32[128,40,512]{2,1,0:T(8,128)} %core_ref.1, f32[512,128]{1,0:T(8,128)} %right_ref.1, f32[128,40,128]{2,1,0:T(8,128)} %left_ref.1), custom_call_target="tpu_custom_call" | custom-call | flops 2684354560 | bytes 15728640 | tf_op jit(solution)/shard_map/pallas_call | solution.py:86
  10.4 6.3 %all-to-all-start = ((f32[8,16,128]{2,1,0:T(8,128)}), f32[8,16,128]{2,1,0:T(8,128)S(1)}, u32[]{:S(2)}, u32[]{:S(2)}) async-start(f32[8,16,128]{2,1,0:T(8,128)} %bitcast.29), calls=%async_computation | async-start | bytes 131072 | tf_op jit(solution)/shard_map/all_to_all | solution.py:380
  16.8 2.7 %constant_dynamic-slice_fusion = (f32[5,128,128]{2,1,0:T(8,128)S(1)}, f32[5,128,128]{2,1,0:T(8,128)}, f32[5,128,128]{2,1,0:T(8,128)}, f32[5,128,128]{2,1,0:T(8,1...) fusion(f32[40,128,128]{2,1,0:T(8,128)} %get-tuple-element.36, ...), kind=kLoop, calls=%fused_computation | loop fusion | bytes 5242912 | tf_op jit(solution)/shard_map/dynamic_slice | solution.py:417
  19.5 1.5 collective-permute-start.2
  21.0 1.5 collective-permute-start.1
  22.5 11.1 %shard_map.68 = (f32[256,512]{1,0:T(8,128)}, f32[256,512]{1,0:T(8,128)}) custom-call(f32[5120,512]{1,0:T(8,128)} %bitcast.20, s32[1]{0:T(128)} %bitcast.2.core_index_ref), custom_call_target="tpu_custom_call" | custom-call | flops 5368709120 | bytes 10485760 | tf_op jit(solution)/shard_map/pallas_call | solution.py:137
  33.6 0.0 collective-permute-start
  33.6 0.0 all-to-all-done
  33.6 0.0 collective-permute-done.2.refs_2_
  33.6 0.0 copy-start.7
  33.6 0.0 collective-permute-done.1.refs_1_
  33.6 0.0 copy-start.8
  33.7 0.8 broadcast_in_dim.4
  34.4 4.3 %all-to-all-start.2 = ((f32[32,16,128]{2,1,0:T(8,128)}), f32[32,16,128]{2,1,0:T(8,128)S(1)}, u32[]{:S(2)}, u32[]{:S(2)}) async-start(f32[32,16,128]{2,1,0:T(8,128)} %broadcast_in_dim.4), calls=%async_computation.2 | async-start | bytes 524288 | tf_op jit(solution)/shard_map/all_to_all | solution.py:380
  38.7 1.8 collective-permute-start.3
  40.6 1.5 collective-permute-start.4
  42.0 0.0 collective-permute-done
  42.1 1.9 add.47
  44.0 7.5 %collective-permute-done.3.refs_5_ = f32[5,128,128]{2,1,0:T(8,128)S(1)} collective-permute-done((f32[5,128,128]{2,1,0:T(8,128)S(1)}, f32[5,128,128]{2,1,0:T(8,128)S(1)}, u32[]{:S(2)}, u32[]{:S(2)}) %collective-permute-start.3) | collective-permute-done | bytes 327712 | tf_op jit(solution)/shard_map/ppermute | solution.py:376
  51.4 0.9 collective-permute-done.4.refs_6_
  52.4 0.0 all-to-all-done.2
  52.4 4.8 %all-to-all-start.1 = ((f32[16,16,512]{2,1,0:T(8,128)}), f32[16,16,512]{2,1,0:T(8,128)S(1)}, u32[]{:S(2)}, u32[]{:S(2)}) async-start(f32[16,16,512]{2,1,0:T(8,128)} %bitcast.4), calls=%async_computation.1 | async-start | bytes 1048576 | tf_op jit(solution)/shard_map/all_to_all | solution.py:380
  57.2 2.8 %collective-permute-start.5 = (f32[5,128,128]{2,1,0:T(8,128)S(1)}, f32[5,128,128]{2,1,0:T(8,128)S(1)}, u32[]{:S(2)}, u32[]{:S(2)}) collective-permute-start(f32[5,128,128]{2,1,0:T(8,128)S(1)} %get-tuple-element.41), channel_id=1, source_target_pairs={{0,3},{1,2},{2,1},{3,0},{4,7},{5,6},{6,5},{7,4},{8,11},{9,10},{10,... | collective-permute-start | bytes 983048 | tf_op jit(solution)/shard_map/ppermute | solution.py:376
  60.1 0.0 copy-start
  60.1 12.4 %all-to-all-done.1 = f32[16,16,512]{2,1,0:T(8,128)S(1)} async-done(((f32[16,16,512]{2,1,0:T(8,128)}), f32[16,16,512]{2,1,0:T(8,128)S(1)}, u32[]{:S(2)}, u32[]{:S(2)}) %all-to-all-start.1) | async-done | bytes 524320 | tf_op jit(solution)/shard_map/all_to_all | solution.py:380
  72.5 0.2 fusion
  72.8 1.0 collective-permute-done.5.refs_3_
  73.7 0.8 broadcast_in_dim.5
  74.5 0.0 copy-done.7
  74.5 0.0 copy-done.8
  74.5 4.2 %all-to-all-start.3 = ((f32[32,16,128]{2,1,0:T(8,128)}), f32[32,16,128]{2,1,0:T(8,128)S(1)}, u32[]{:S(2)}, u32[]{:S(2)}) async-start(f32[32,16,128]{2,1,0:T(8,128)} %broadcast_in_dim.5), calls=%async_computation.3 | async-start | bytes 524288 | tf_op jit(solution)/shard_map/all_to_all | solution.py:380
  78.7 2.6 %collective-permute-start.6 = (f32[5,128,128]{2,1,0:T(8,128)S(1)}, f32[5,128,128]{2,1,0:T(8,128)S(1)}, u32[]{:S(2)}, u32[]{:S(2)}) collective-permute-start(f32[5,128,128]{2,1,0:T(8,128)S(1)} %get-tuple-element.48), channel_id=1, source_target_pairs={{0,3},{1,2},{2,1},{3,0},{4,7},{5,6},{6,5},{7,4},{8,11},{9,10},{10,... | collective-permute-start | bytes 983048 | tf_op jit(solution)/shard_map/ppermute | solution.py:376
  81.2 8.3 %all-to-all-done.3 = f32[32,16,128]{2,1,0:T(8,128)S(1)} async-done(((f32[32,16,128]{2,1,0:T(8,128)}), f32[32,16,128]{2,1,0:T(8,128)S(1)}, u32[]{:S(2)}, u32[]{:S(2)}) %all-to-all-start.3) | async-done | bytes 262176 | tf_op jit(solution)/shard_map/all_to_all | solution.py:380
  89.5 0.7 copy.10
  90.3 1.8 collective-permute-done.6.refs_7_
  92.1 0.0 copy-done.9
  92.1 0.0 copy-done.10
  92.1 0.7 copy-done.11
  92.8 3.3 %shard_map.69 = (f32[5,128,128]{2,1,0:T(8,128)}, f32[5,128,128]{2,1,0:T(8,128)}) custom-call(s32[1]{0:T(128)} %bitcast.1.rank_ref, f32[512,128]{1,0:T(8,128)} %bitcast.25, f32[5,128,128]{2,1,0:T(8,128)} %get-tuple-element.63.refs_0_, f32[5,128,128]{2,1,0:T(8,128)} %copy-done.8, f32[5,128,128]{2,1,0:T(8,128)} %copy-done.7, f32[5,128,128]{2,1,0:T(8,128)} %copy-done.10, ...), custom_call_target="tpu_custom_call" | custom-call | flops 671088640 | bytes 2883584 | tf_op jit(solution)/shard_map/pallas_call | solution.py:173
  96.2 1.1 collective-permute-start.7
  97.2 0.9 collective-permute-start.11
  98.1 1.1 collective-permute-start.8
  99.2 1.0 collective-permute-start.10
  100.2 6.8 %collective-permute-done.7.refs_1_ = f32[5,128,128]{2,1,0:T(8,128)S(1)} collective-permute-done((f32[5,128,128]{2,1,0:T(8,128)}, f32[5,128,128]{2,1,0:T(8,128)S(1)}, u32[]{:S(2)}, u32[]{:S(2)}) %collective-permute-start.7) | collective-permute-done | bytes 327712 | tf_op jit(solution)/shard_map/ppermute | solution.py:376
  107.0 0.9 collective-permute-start.9
  107.9 0.2 collective-permute-done.11.refs_6_
  108.1 1.0 collective-permute-start.12
  109.0 0.0 copy-done
  109.1 9.2 %shard_map.70 = (f32[160,128]{1,0:T(8,128)}, f32[512,128]{1,0:T(8,128)}) custom-call(s32[1]{0:T(128)} %bitcast.1.rank_ref, f32[512,128]{1,0:T(8,128)} %bitcast.24, f32[512,128]{1,0:T(8,128)} %bitcast.26), custom_call_target="tpu_custom_call" | custom-call | flops 67108864 | bytes 1048576 | tf_op jit(solution)/shard_map/pallas_call | solution.py:341
  118.3 0.0 collective-permute-done.8.refs_2_
  118.3 0.0 collective-permute-done.10.refs_5_
  118.3 2.3 collective-permute-done.9.refs_3_
  120.6 0.0 collective-permute-done.12.refs_7_
  120.6 0.0 copy-done.1
  120.6 0.7 copy-done.5
  121.3 0.1 copy-done.6
  121.5 10.6 %shard_map.72 = (f32[640,128]{1,0:T(8,128)}, f32[1280,128]{1,0:T(8,128)}) custom-call(s32[1]{0:T(128)} %bitcast.1.rank_ref, f32[160,128]{1,0:T(8,128)} %get-tuple-element.54.weight_ref, f32[5120,512]{1,0:T(8,128)} %bitcast.19, f32[5,128,128]{2,1,0:T(8,128)} %get-tuple-element.55.refs_0_, f32[5,128,128]{2,1,0:T(8,128)} %copy-done.1, ...), custom_call_target="tpu_custom_call" | custom-call | flops 2684354560 | bytes 13107200 | tf_op jit(solution)/shard_map/pallas_call | solution.py:228
  132.1 1.7 reshape.58
  133.8 4.2 %all-to-all-start.4 = ((f32[32,20,128]{2,1,0:T(8,128)}), f32[32,20,128]{2,1,0:T(8,128)S(1)}, u32[]{:S(2)}, u32[]{:S(2)}) async-start(f32[32,20,128]{2,1,0:T(8,128)} %reshape.58), calls=%async_computation.4 | async-start | bytes 786432 | tf_op jit(solution)/shard_map/all_to_all | solution.py:380
  138.1 8.5 %shard_map.71 = f32[5120,128]{1,0:T(8,128)} custom-call(f32[5120,512]{1,0:T(8,128)} %bitcast.21, f32[512,128]{1,0:T(8,128)} %get-tuple-element.53.weight_ref), custom_call_target="tpu_custom_call" | custom-call | flops 2684354560 | bytes 13107200 | tf_op jit(solution)/shard_map/pallas_call | solution.py:258
  146.5 5.1 %all-to-all-done.4 = f32[32,20,128]{2,1,0:T(8,128)S(1)} async-done(((f32[32,20,128]{2,1,0:T(8,128)}), f32[32,20,128]{2,1,0:T(8,128)S(1)}, u32[]{:S(2)}, u32[]{:S(2)}) %all-to-all-start.4) | async-done | bytes 327712 | tf_op jit(solution)/shard_map/all_to_all | solution.py:380
  151.7 66.7 %all-gather = f32[32,20,128]{2,1,0:T(8,128)S(1)} all-gather(f32[1,20,128]{2,1,0:T(8,128)S(1)} %bitcast.30), channel_id=1, replica_groups=mesh['cuts'=8,'rank'=4] {'cuts','rank'}, dimensions={0}, use_global_device_ids=true | all-gather | bytes 337920 | tf_op jit(solution)/shard_map/all_gather | solution.py:471
  218.4 0.8 reshape.61.joined_ref
  219.2 9.2 %shard_map.73 = (f32[128,512]{1,0:T(8,128)}, f32[1280,128]{1,0:T(8,128)}) custom-call(f32[640,128]{1,0:T(8,128)} %reshape.61.joined_ref, f32[1280,128]{1,0:T(8,128)} %get-tuple-element.58.middle_ref), custom_call_target="tpu_custom_call" | custom-call | flops 167772160 | bytes 1310720 | tf_op jit(solution)/shard_map/pallas_call | solution.py:364
  (16 shorter events, 0.1 us)
Async XLA Ops:
  10.4 23.2 %all-to-all-start = ((f32[8,16,128]{2,1,0:T(8,128)}), f32[8,16,128]{2,1,0:T(8,128)S(1)}, u32[]{:S(2)}, u32[]{:S(2)}) async-start(f32[8,16,128]{2,1,0:T(8,128)} %bitcast.29), calls=%async_computation | async-start | bytes 131072 | tf_op jit(solution)/shard_map/all_to_all | solution.py:380
  19.5 14.1 %collective-permute-start.2 = (f32[5,128,128]{2,1,0:T(8,128)S(1)}, f32[5,128,128]{2,1,0:T(8,128)S(1)}, u32[]{:S(2)}, u32[]{:S(2)}) collective-permute-start(f32[5,128,128]{2,1,0:T(8,128)S(1)} %get-tuple-element.65), channel_id=1, source_target_pairs={{0,2},{1,3},{2,0},{3,1},{4,6},{5,7},{6,4},{7,5},{8,10},{9,11},{10,... | collective-permute-start | bytes 983048 | tf_op jit(solution)/shard_map/ppermute | solution.py:376
  21.0 12.6 %collective-permute-start.1 = (f32[5,128,128]{2,1,0:T(8,128)S(1)}, f32[5,128,128]{2,1,0:T(8,128)S(1)}, u32[]{:S(2)}, u32[]{:S(2)}) collective-permute-start(f32[5,128,128]{2,1,0:T(8,128)S(1)} %get-tuple-element.66), channel_id=1, source_target_pairs={{0,1},{1,0},{2,3},{3,2},{4,5},{5,4},{6,7},{7,6},{8,9},{9,8},{10,11... | collective-permute-start | bytes 983048 | tf_op jit(solution)/shard_map/ppermute | solution.py:376
  33.6 8.5 %collective-permute-start = (f32[256,512]{1,0:T(8,128)}, f32[256,512]{1,0:T(8,128)S(1)}, u32[]{:S(2)}, u32[]{:S(2)}) collective-permute-start(f32[256,512]{1,0:T(8,128)} %get-tuple-element.35), channel_id=1, source_target_pairs={{0,4},{4,0},{8,12},{12,8},{16,20},{20,16},{24,28},{28,24},{1,5},{5... | collective-permute-start | bytes 1572872 | tf_op jit(solution)/shard_map/ppermute | solution.py:376
  33.6 40.9 %copy-start.7 = (f32[5,128,128]{2,1,0:T(8,128)}, f32[5,128,128]{2,1,0:T(8,128)S(1)}, u32[]{:S(2)}) copy-start(f32[5,128,128]{2,1,0:T(8,128)S(1)} %collective-permute-done.2.refs_2_) | copy-start | bytes 983044
  33.6 40.8 %copy-start.8 = (f32[5,128,128]{2,1,0:T(8,128)}, f32[5,128,128]{2,1,0:T(8,128)S(1)}, u32[]{:S(2)}) copy-start(f32[5,128,128]{2,1,0:T(8,128)S(1)} %collective-permute-done.1.refs_1_) | copy-start | bytes 983044
  34.4 17.9 %all-to-all-start.2 = ((f32[32,16,128]{2,1,0:T(8,128)}), f32[32,16,128]{2,1,0:T(8,128)S(1)}, u32[]{:S(2)}, u32[]{:S(2)}) async-start(f32[32,16,128]{2,1,0:T(8,128)} %broadcast_in_dim.4), calls=%async_computation.2 | async-start | bytes 524288 | tf_op jit(solution)/shard_map/all_to_all | solution.py:380
  38.7 12.7 %collective-permute-start.3 = (f32[5,128,128]{2,1,0:T(8,128)S(1)}, f32[5,128,128]{2,1,0:T(8,128)S(1)}, u32[]{:S(2)}, u32[]{:S(2)}) collective-permute-start(f32[5,128,128]{2,1,0:T(8,128)S(1)} %get-tuple-element.38), channel_id=1, source_target_pairs={{0,1},{1,0},{2,3},{3,2},{4,5},{5,4},{6,7},{7,6},{8,9},{9,8},{10,11... | collective-permute-start | bytes 983048 | tf_op jit(solution)/shard_map/ppermute | solution.py:376
  40.6 11.8 %collective-permute-start.4 = (f32[5,128,128]{2,1,0:T(8,128)S(1)}, f32[5,128,128]{2,1,0:T(8,128)}, u32[]{:S(2)}, u32[]{:S(2)}) collective-permute-start(f32[5,128,128]{2,1,0:T(8,128)S(1)} %get-tuple-element.39), channel_id=1, source_target_pairs={{0,2},{1,3},{2,0},{3,1},{4,6},{5,7},{6,4},{7,5},{8,10},{9,11},{10,... | collective-permute-start | bytes 983048 | tf_op jit(solution)/shard_map/ppermute | solution.py:376
  51.4 40.6 %copy-start.9 = (f32[5,128,128]{2,1,0:T(8,128)}, f32[5,128,128]{2,1,0:T(8,128)S(1)}, u32[]{:S(2)}) copy-start(f32[5,128,128]{2,1,0:T(8,128)S(1)} %collective-permute-done.3.refs_5_) | copy-start | bytes 983044
  52.4 20.1 %all-to-all-start.1 = ((f32[16,16,512]{2,1,0:T(8,128)}), f32[16,16,512]{2,1,0:T(8,128)S(1)}, u32[]{:S(2)}, u32[]{:S(2)}) async-start(f32[16,16,512]{2,1,0:T(8,128)} %bitcast.4), calls=%async_computation.1 | async-start | bytes 1048576 | tf_op jit(solution)/shard_map/all_to_all | solution.py:380
  57.2 16.5 %collective-permute-start.5 = (f32[5,128,128]{2,1,0:T(8,128)S(1)}, f32[5,128,128]{2,1,0:T(8,128)S(1)}, u32[]{:S(2)}, u32[]{:S(2)}) collective-permute-start(f32[5,128,128]{2,1,0:T(8,128)S(1)} %get-tuple-element.41), channel_id=1, source_target_pairs={{0,3},{1,2},{2,1},{3,0},{4,7},{5,6},{6,5},{7,4},{8,11},{9,10},{10,... | collective-permute-start | bytes 983048 | tf_op jit(solution)/shard_map/ppermute | solution.py:376
  60.1 49.0 %copy-start = (f32[4,8,16,128]{3,2,1,0:T(8,128)}, f32[4,8,16,128]{3,2,1,0:T(8,128)S(1)}, u32[]{:S(2)}) copy-start(f32[4,8,16,128]{3,2,1,0:T(8,128)S(1)} %copy.9) | copy-start | bytes 786436
  73.7 18.4 %copy-start.10 = (f32[5,128,128]{2,1,0:T(8,128)}, f32[5,128,128]{2,1,0:T(8,128)S(1)}, u32[]{:S(2)}) copy-start(f32[5,128,128]{2,1,0:T(8,128)S(1)} %collective-permute-done.5.refs_3_) | copy-start | bytes 983044
  74.5 15.1 %all-to-all-start.3 = ((f32[32,16,128]{2,1,0:T(8,128)}), f32[32,16,128]{2,1,0:T(8,128)S(1)}, u32[]{:S(2)}, u32[]{:S(2)}) async-start(f32[32,16,128]{2,1,0:T(8,128)} %broadcast_in_dim.5), calls=%async_computation.3 | async-start | bytes 524288 | tf_op jit(solution)/shard_map/all_to_all | solution.py:380
  78.7 13.4 %collective-permute-start.6 = (f32[5,128,128]{2,1,0:T(8,128)S(1)}, f32[5,128,128]{2,1,0:T(8,128)S(1)}, u32[]{:S(2)}, u32[]{:S(2)}) collective-permute-start(f32[5,128,128]{2,1,0:T(8,128)S(1)} %get-tuple-element.48), channel_id=1, source_target_pairs={{0,3},{1,2},{2,1},{3,0},{4,7},{5,6},{6,5},{7,4},{8,11},{9,10},{10,... | collective-permute-start | bytes 983048 | tf_op jit(solution)/shard_map/ppermute | solution.py:376
  92.1 0.7 copy-start.11
  96.2 10.8 %collective-permute-start.7 = (f32[5,128,128]{2,1,0:T(8,128)}, f32[5,128,128]{2,1,0:T(8,128)S(1)}, u32[]{:S(2)}, u32[]{:S(2)}) collective-permute-start(f32[5,128,128]{2,1,0:T(8,128)} %get-tuple-element.55.refs_0_), channel_id=1, source_target_pairs={{0,1},{1,0},{2,3},{3,2},{4,5},{5,4},{6,7},{7,6},{8,9},{9,8},{10,11... | collective-permute-start | bytes 983048 | tf_op jit(solution)/shard_map/ppermute | solution.py:376
  97.2 10.9 %collective-permute-start.11 = (f32[5,128,128]{2,1,0:T(8,128)}, f32[5,128,128]{2,1,0:T(8,128)S(1)}, u32[]{:S(2)}, u32[]{:S(2)}) collective-permute-start(f32[5,128,128]{2,1,0:T(8,128)} %get-tuple-element.56.refs_4_), channel_id=1, source_target_pairs={{0,2},{1,3},{2,0},{3,1},{4,6},{5,7},{6,4},{7,5},{8,10},{9,11},{10,... | collective-permute-start | bytes 983048 | tf_op jit(solution)/shard_map/ppermute | solution.py:376
  98.1 20.2 %collective-permute-start.8 = (f32[5,128,128]{2,1,0:T(8,128)}, f32[5,128,128]{2,1,0:T(8,128)S(1)}, u32[]{:S(2)}, u32[]{:S(2)}) collective-permute-start(f32[5,128,128]{2,1,0:T(8,128)} %get-tuple-element.55.refs_0_), channel_id=1, source_target_pairs={{0,2},{1,3},{2,0},{3,1},{4,6},{5,7},{6,4},{7,5},{8,10},{9,11},{10,... | collective-permute-start | bytes 983048 | tf_op jit(solution)/shard_map/ppermute | solution.py:376
  99.2 19.1 %collective-permute-start.10 = (f32[5,128,128]{2,1,0:T(8,128)}, f32[5,128,128]{2,1,0:T(8,128)S(1)}, u32[]{:S(2)}, u32[]{:S(2)}) collective-permute-start(f32[5,128,128]{2,1,0:T(8,128)} %get-tuple-element.56.refs_4_), channel_id=1, source_target_pairs={{0,1},{1,0},{2,3},{3,2},{4,5},{5,4},{6,7},{7,6},{8,9},{9,8},{10,11... | collective-permute-start | bytes 983048 | tf_op jit(solution)/shard_map/ppermute | solution.py:376
  107.0 13.6 %copy-start.1 = (f32[5,128,128]{2,1,0:T(8,128)}, f32[5,128,128]{2,1,0:T(8,128)S(1)}, u32[]{:S(2)}) copy-start(f32[5,128,128]{2,1,0:T(8,128)S(1)} %collective-permute-done.7.refs_1_) | copy-start | bytes 983044
  107.0 13.6 %collective-permute-start.9 = (f32[5,128,128]{2,1,0:T(8,128)S(1)}, f32[5,128,128]{2,1,0:T(8,128)S(1)}, u32[]{:S(2)}, u32[]{:S(2)}) collective-permute-start(f32[5,128,128]{2,1,0:T(8,128)S(1)} %collective-permute-done.7.refs_1_), channel_id=1, source_target_pairs={{0,2},{1,3},{2,0},{3,1},{4,6},{5,7},{6,4},{7,5},{8,10},{9,11},{10,... | collective-permute-start | bytes 983048 | tf_op jit(solution)/shard_map/ppermute | solution.py:376
  108.1 12.5 %copy-start.2 = (f32[5,128,128]{2,1,0:T(8,128)}, f32[5,128,128]{2,1,0:T(8,128)S(1)}, u32[]{:S(2)}) copy-start(f32[5,128,128]{2,1,0:T(8,128)S(1)} %collective-permute-done.11.refs_6_) | copy-start | bytes 983044
  108.1 12.5 %collective-permute-start.12 = (f32[5,128,128]{2,1,0:T(8,128)S(1)}, f32[5,128,128]{2,1,0:T(8,128)S(1)}, u32[]{:S(2)}, u32[]{:S(2)}) collective-permute-start(f32[5,128,128]{2,1,0:T(8,128)S(1)} %collective-permute-done.11.refs_6_), channel_id=1, source_target_pairs={{0,1},{1,0},{2,3},{3,2},{4,5},{5,4},{6,7},{7,6},{8,9},{9,8},{10,11... | collective-permute-start | bytes 983048 | tf_op jit(solution)/shard_map/ppermute | solution.py:376
  118.3 2.3 %copy-start.3 = (f32[5,128,128]{2,1,0:T(8,128)}, f32[5,128,128]{2,1,0:T(8,128)S(1)}, u32[]{:S(2)}) copy-start(f32[5,128,128]{2,1,0:T(8,128)S(1)} %collective-permute-done.8.refs_2_) | copy-start | bytes 983044
  118.3 2.3 %copy-start.4 = (f32[5,128,128]{2,1,0:T(8,128)}, f32[5,128,128]{2,1,0:T(8,128)S(1)}, u32[]{:S(2)}) copy-start(f32[5,128,128]{2,1,0:T(8,128)S(1)} %collective-permute-done.10.refs_5_) | copy-start | bytes 983044
  120.6 0.7 copy-start.5
  120.6 0.9 copy-start.6
  133.8 17.9 %all-to-all-start.4 = ((f32[32,20,128]{2,1,0:T(8,128)}), f32[32,20,128]{2,1,0:T(8,128)S(1)}, u32[]{:S(2)}, u32[]{:S(2)}) async-start(f32[32,20,128]{2,1,0:T(8,128)} %reshape.58), calls=%async_computation.4 | async-start | bytes 786432 | tf_op jit(solution)/shard_map/all_to_all | solution.py:380

commit v2 on v1

--- a/solution.py
+++ b/solution.py
@@ -45,6 +45,10 @@
     return jnp.concatenate(split(value), axis=axis)
 
 
+def twice(value, axis):
+    return jnp.concatenate([value, value], axis=axis)
+
+
 def fold(value, axis):
     half = value.shape[axis] // 2
     return lax.slice_in_dim(value, 0, half, axis=axis) + lax.slice_in_dim(value, half, 2 * half, axis=axis)
@@ -57,27 +61,23 @@
 def sketch_kernel(core_ref, right_ref, left_ref, sketched_ref, part_ref, rows_ref):
     local_rows, block, _ = core_ref.shape
     columns = right_ref.shape[1]
-    right = both_parts(right_ref[...], 1)
-    product = mxu(both_parts(rows_of(core_ref)[...], 0), right, NN)
-    rows_ref[...] = fold(fold(product, 0), 1)
+    right = twice(both_parts(right_ref[...], 1), 0)
+    rows_ref[...] = fold(mxu(both_parts(rows_of(core_ref)[...], 1), right, NN), 1)
     left_rows = rows_of(left_ref)
 
     @pl.when(pl.program_id(0) == 0)
     def _():
         part_ref[...] = jnp.zeros_like(part_ref)
 
-    total = jnp.zeros(part_ref.shape, jnp.float32)
-    for pair in range(0, block, 2):
-        sides, lefts = [], []
-        for n in (pair, pair + 1):
-            rows = rows_ref[pl.ds(n, local_rows, stride=block), :]
-            sketched_ref[n] = rows
-            sides.append(rows)
-            lefts.append(left_rows[pl.ds(n, columns, stride=block), :])
-        side = both_parts(jnp.concatenate(sides, axis=1), 0)
-        left = both_parts(jnp.concatenate(lefts, axis=1), 0)
-        total = total + fold(fold(mxu(side, left, NT), 0), 1)
-    part_ref[...] += total
+    sides, lefts = [], []
+    for n in range(block):
+        rows = rows_ref[pl.ds(n, local_rows, stride=block), :]
+        sketched_ref[n] = rows
+        sides.append(rows)
+        lefts.append(left_rows[pl.ds(n, columns, stride=block), :])
+    side = both_parts(jnp.concatenate(sides, axis=1), 1)
+    left = twice(both_parts(jnp.concatenate(lefts, axis=1), 0), 1)
+    part_ref[...] += fold(mxu(side, left, NT), 1)
 
 
 def sketch(core_two, right_sketch, sketch_core):
@@ -157,13 +157,14 @@
     for offset in range(ranks):
         start = pl.multiple_of((rank_ref[0] ^ offset) * local_rows, local_rows)
         rows.append(raw_ref[pl.ds(start, local_rows), :])
-    raw = both_parts(jnp.concatenate(rows, axis=0), 1).T
+    raw = twice(both_parts(jnp.concatenate(rows, axis=0), 1).T, 1)
+    columns = raw_ref.shape[1]
     for half, count in enumerate(halves):
         refs = piece_refs[half * ranks:(half + 1) * ranks]
+        value = [jnp.concatenate([ref[n] for n in range(count)], axis=1) for ref in refs]
+        product = fold(mxu(raw, both_parts(jnp.concatenate(value, axis=0), 0), NN), 0)
         for n in range(count):
-            value = jnp.concatenate([ref[n] for ref in refs], axis=0)
-            product = mxu(raw, jnp.concatenate(split(value), axis=1), NN)
-            out_refs[half][n] = fold(fold(product, 0), 1)
+            out_refs[half][n] = product[:, n * columns:(n + 1) * columns]
 
 
 def loosen(rank_index, raw, pieces, halves):
@@ -194,32 +195,31 @@
     @pl.when(step == 0)
     def _():
         sum_ref[...] = jnp.zeros_like(sum_ref)
-        weight_high, weight_low = split(weight_ref[...])
-        weight = jnp.concatenate([weight_high, weight_low], axis=0)
+        weight = twice(both_parts(weight_ref[...], 0), 1)
         for half, count in enumerate(halves):
             for offset in range(ranks):
                 ref = piece_refs[half * ranks + offset]
                 first = (rank_ref[0] ^ offset) * share + sum(halves[:half])
-                high, low = split(jnp.concatenate([ref[n] for n in range(count)], axis=1))
-                spread = fold(mxu(weight, high, NN), 0) + mxu(weight_high, low, NN)
+                value = both_parts(jnp.concatenate([ref[n] for n in range(count)], axis=1), 0)
+                spread = fold(mxu(weight, value, NN), 0)
                 for n in range(count):
                     piece = lax.slice_in_dim(spread, n * columns, (n + 1) * columns, axis=1)
                     rows_ref[pl.ds(first + n, local_rows, stride=room), :] = piece[:local_rows]
                     middle_ref[pl.ds(first + n, band, stride=room), :] = piece[local_rows:]
 
-    rows = both_parts(rows_ref[pl.ds(pl.multiple_of(step * block, block), block), :], 1)
-    product = mxu(rows, both_parts(core_ref[...], 1), TN)
-    product = fold(fold(product, 0), 1)
+    rows = both_parts(rows_ref[pl.ds(pl.multiple_of(step * block, block), block), :], 1).T
+    product = fold(mxu(twice(rows, 1), both_parts(core_ref[...], 0), NN), 0)
     sum_ref[...] += product
 
     @pl.when(step == pl.num_programs(0) - 1)
     def _():
         joined_ref[:width, :] = sum_ref[...].T
         middle = both_parts(middle_ref[...], 1)
-        joined_ref[width:, :] = fold(fold(mxu(middle, middle, TN), 0), 1)
-
-
-def carry_rows(rank_index, weight, flat_two, pieces, halves, share, band):
+        joined_ref[width:width + columns, :] = fold(fold(mxu(middle, middle, TN), 0), 1)
+        joined_ref[width + columns:, :] = jnp.zeros_like(joined_ref[width + columns:, :])
+
+
+def carry_rows(rank_index, weight, flat_two, pieces, halves, share, band, total):
     rows, width = flat_two.shape
     columns = weight.shape[1]
     block = block_of(rows)
@@ -237,18 +237,17 @@
         ]
         + [pl.BlockSpec(piece.shape, lambda i: (0, 0, 0)) for piece in pieces],
         out_specs=[
-            pl.BlockSpec((width + columns, columns), lambda i: (0, 0)),
+            pl.BlockSpec((total, columns), lambda i: (0, 0)),
             pl.BlockSpec((band * share * ranks, columns), lambda i: (0, 0)),
         ],
-        out_shape=[shape(width + columns, columns), shape(band * share * ranks, columns)],
+        out_shape=[shape(total, columns), shape(band * share * ranks, columns)],
         scratch_shapes=[pltpu.VMEM((rows, columns), jnp.float32), pltpu.VMEM((columns, width), jnp.float32)],
     )(rank_index, weight, flat_two, *pieces)
 
 
 def apply_kernel(rows_ref, weight_ref, out_ref):
-    weight = both_parts(weight_ref[...], 1)
-    product = mxu(both_parts(rows_ref[...], 0), weight, NN)
-    out_ref[...] = fold(fold(product, 0), 1)
+    weight = twice(both_parts(weight_ref[...], 1), 0)
+    out_ref[...] = fold(mxu(both_parts(rows_ref[...], 1), weight, NN), 1)
 
 
 def apply_to(rows, weight):
@@ -412,41 +411,36 @@
 
     sketched, part = sketch(core_two, right_sketch, sketch_core)
 
-    def piece(half, offset):
-        start = (rank ^ offset) * share + half * halves[0]
-        return lax.dynamic_slice_in_dim(sketched, start, halves[half], 0)
-
-    def send(names, behind):
-        found = [piece(*name) for name in names]
+    def send(names, source, behind):
+        found = []
+        for half, offset in names:
+            start = (rank ^ offset) * share + half * halves[0]
+            found.append(lax.dynamic_slice_in_dim(source, start, halves[half], 0))
         if behind is not None:
             found, _ = after(found, behind)
-        return {name: swap(value, "rank", name[1]) for name, value in zip(names, found)}
+        return {name: swap(value, "rank", name[1]) if name[1] else value for name, value in zip(names, found)}
 
     far = ranks - 1
-    pieces = {(half, 0): piece(half, 0) for half in range(2)}
     near = [[(half, offset) for offset in range(1, far)] for half in range(2)]
 
-    moved = send(near[0], None)
+    moved = send(near[0], sketched, None)
     bridge_rows = jnp.sum(exchange(part.reshape(cuts, local_rows // cuts, columns), "cuts"), axis=0)
     flat_late, part = after(flat_one, part)
     keep, give = square_of(flat_late, core_index)
-    bridge_rows, moved = after(bridge_rows, moved)
-    pieces.update(moved)
-
-    moved = send(near[1], bridge_rows)
+    bridge_rows, pieces = after(bridge_rows, moved)
+    sketched, bridge_rows = after(sketched, bridge_rows)
+    pieces.update(send([(0, 0), (1, 0)], sketched, None))
+
     bridge = gather_all(bridge_rows, both)
     bridge = bridge.reshape(cuts, ranks, -1, columns).swapaxes(0, 1).reshape(width, columns)
     square = keep + swap(give, "cuts", 1)
-    square, moved = after(square, moved)
-    pieces.update(moved)
-
-    moved = send([(0, far)], square)
+    moved = send(near[1] + [(0, far)], sketched, square)
     square = exchange(square.reshape(parts // 2, -1, width), both, core_groups)
     raw_rows = exact(jnp.sum(square, axis=0), bridge, NN)
     raw_rows, moved = after(raw_rows, moved)
     pieces.update(moved)
 
-    pieces.update(send([(1, far)], raw_rows))
+    pieces.update(send([(1, far)], sketched, raw_rows))
     raw = gather_all(raw_rows, both).reshape(cuts // 2, 2, ranks, -1, columns)
     raw = raw.transpose(1, 0, 2, 3, 4).reshape(width, columns)
 
@@ -464,11 +458,10 @@
 
     scale = math.sqrt(local_rows * ranks * slices * cuts)
     weight, solve = first_factor(rank_index, bridge, raw, scale, local_rows, band)
-    joined, middle = carry_rows(rank_index, weight, flat_two, everyone, halves, share, band)
-    total = joined.shape[0]
-    joined = jnp.pad(joined, ((0, -total % parts), (0, 0))).reshape(parts, -1, columns)
-    joined = jnp.sum(exchange(joined, both), axis=0)
-    joined = lax.all_gather(joined, both, axis=0, tiled=True)[:total]
+    total = -(-(width + columns) // (BLOCK * parts)) * BLOCK * parts
+    joined, middle = carry_rows(rank_index, weight, flat_two, everyone, halves, share, band, total)
+    joined = jnp.sum(exchange(joined.reshape(parts, -1, columns), both), axis=0)
+    joined = gather_all(joined, both).reshape(total, columns)
     left_core = apply_to(flat_one, solve).reshape(local_rows, slices, columns)
     scale = math.sqrt(columns * slices * cuts)
     carry, middle = last_factor(joined, middle, scale, width)

time: 229 us -> 182 us (0.79)
  blocking collectives: 66.7 us -> 17.9 us
  waiting for transfers between devices: 46.2 us -> 50.5 us
  starting transfers between devices: 41.5 us -> 37.3 us
    all_gather x1 -> x0, blocking collectives: 66.7 us -> none  [on_device(): joined = lax.all_gather(joined, both, axis=0, tiled=True)[:total]]
    all_to_all x0 -> x1, blocking collectives: none -> 17.9 us  [exchange(): lax.all_to_all(value, axes, 0, 0, axis_index_groups=groups, tiled=True)]
    all_to_all x5, waiting for transfers between devices: 25.8 us -> 32.1 us  [exchange(): lax.all_to_all(value, axes, 0, 0, axis_index_groups=groups, tiled=True)]
    all_to_all x5, starting transfers between devices: 23.9 us -> 20.2 us  [exchange(): lax.all_to_all(value, axes, 0, 0, axis_index_groups=groups, tiled=True)]
  transfers between devices with their start and end apart: 18 -> 18, of which waited for: 10 -> 9; matrix products, arithmetic and copies ran while one was open for 3% -> 3% of each run, Pallas kernels for 13% -> 16%
where the time goes in v2:
time: 182 us; the launch traced here: 181 us
  Pallas kernels  63.1 us (35%)
  waiting for transfers between devices  50.5 us (28%)
  starting transfers between devices  37.3 us (20%)
  blocking collectives  17.9 us (10%)
  local copies, waits for them, and re-layouts  8.66 us (5%)
  other arithmetic  2 us (1%)
    all_to_all x5, waiting for transfers between devices, exchange(): lax.all_to_all(value, axes, 0, 0, axis_index_groups=groups, tiled=True)  32.1 us
    all_to_all x5, starting transfers between devices, exchange(): lax.all_to_all(value, axes, 0, 0, axis_index_groups=groups, tiled=True)  20.2 us
    ppermute x13, waiting for transfers between devices, swap(): lax.ppermute(value, axis, [(i, i ^ offset) for i in range(lax.axis_size(a...  18.3 us
    all_to_all x1, blocking collectives, exchange(): lax.all_to_all(value, axes, 0, 0, axis_index_groups=groups, tiled=True)  17.9 us
    ppermute x13, starting transfers between devices, swap(): lax.ppermute(value, axis, [(i, i ^ offset) for i in range(lax.axis_size(a...  17.1 us
    pallas_call x1, Pallas kernels, square_of(): call(square_kernel, 4 * rows * width * width, 4 * flat_one.size, grid=(ro...  11.1 us
    pallas_call x1, Pallas kernels, sketch(): call(sketch_kernel, 2 * core_two.size * columns * 4, 4 * (core_two.size +...  10.9 us
    pallas_call x1, Pallas kernels, carry_rows(): call(functools.partial(carry_kernel, halves, share), 8 * flat_two.size *...  10.6 us
  transfers between devices with their start and end apart: 18, of which 9 were waited for; matrix products, arithmetic and copies ran while one was open for 3% of the time, Pallas kernels for 16%

profile of v2, /device:TPU:0, one launch (start us, length us, event | category | flops | bytes accessed | tf_op | source)
XLA Modules:
  0.0 180.6 jit_solution(1095042011591209563)
XLA Ops:
  0.7 10.9 %shard_map.67 = (f32[40,128,128]{2,1,0:T(8,128)}, f32[128,128]{1,0:T(8,128)}) custom-call(f32[128,40,512]{2,1,0:T(8,128)} %core_ref.1, f32[512,128]{1,0:T(8,128)} %right_ref.1, f32[128,40,128]{2,1,0:T(8,128)} %left_ref.1), custom_call_target="tpu_custom_call" | custom-call | flops 2684354560 | bytes 15728640 | tf_op jit(solution)/shard_map/pallas_call | solution.py:86
  11.6 2.0 %constant_dynamic-slice_fusion.6 = (f32[5,128,128]{2,1,0:T(8,128)}, f32[5,128,128]{2,1,0:T(8,128)}) fusion(f32[40,128,128]{2,1,0:T(8,128)} %get-tuple-element.40, s32[]{:T(128)S(6)} %select_n.25, s32[]{:T(128)S(6)} %select_n.24), kind=kLoop, calls=%fused_computation.6 | loop fusion | bytes 1310728 | tf_op jit(solution)/shard_map/dynamic_slice | solution.py:418
  13.6 2.9 %collective-permute-start.1 = (f32[5,128,128]{2,1,0:T(8,128)}, f32[5,128,128]{2,1,0:T(8,128)}, u32[]{:S(2)}, u32[]{:S(2)}) collective-permute-start(f32[5,128,128]{2,1,0:T(8,128)} %get-tuple-element.70), channel_id=1, source_target_pairs={{0,1},{1,0},{2,3},{3,2},{4,5},{5,4},{6,7},{7,6},{8,9},{9,8},{10,11... | collective-permute-start | bytes 983048 | tf_op jit(solution)/shard_map/ppermute | solution.py:375
  16.5 1.5 collective-permute-start.2
  18.0 4.9 %all-to-all-start.1 = ((f32[8,16,128]{2,1,0:T(8,128)}), f32[8,16,128]{2,1,0:T(8,128)S(1)}, u32[]{:S(2)}, u32[]{:S(2)}) async-start(f32[8,16,128]{2,1,0:T(8,128)} %bitcast.32), calls=%async_computation.1 | async-start | bytes 131072 | tf_op jit(solution)/shard_map/all_to_all | solution.py:379
  22.9 11.1 %shard_map.68 = (f32[256,512]{1,0:T(8,128)}, f32[256,512]{1,0:T(8,128)}) custom-call(f32[5120,512]{1,0:T(8,128)} %bitcast.21, s32[1]{0:T(128)} %bitcast.2.core_index_ref), custom_call_target="tpu_custom_call" | custom-call | flops 5368709120 | bytes 10485760 | tf_op jit(solution)/shard_map/pallas_call | solution.py:137
  34.0 0.5 collective-permute-start
  34.5 0.0 all-to-all-done.1
  34.6 0.0 collective-permute-done.1.refs_1_
  34.6 0.0 collective-permute-done.2.refs_2_
  34.6 0.7 broadcast_in_dim.6
  35.3 3.8 %all-to-all-start.2 = ((f32[32,16,128]{2,1,0:T(8,128)}), f32[32,16,128]{2,1,0:T(8,128)S(1)}, u32[]{:S(2)}, u32[]{:S(2)}) async-start(f32[32,16,128]{2,1,0:T(8,128)} %broadcast_in_dim.6), calls=%async_computation.2 | async-start | bytes 524288 | tf_op jit(solution)/shard_map/all_to_all | solution.py:379
  39.2 0.0 collective-permute-done
  39.2 1.9 %add.47 = f32[256,512]{1,0:T(8,128)} add(f32[256,512]{1,0:T(8,128)} %get-tuple-element.35, f32[256,512]{1,0:T(8,128)S(1)} %collective-permute-done) | non-fusion elementwise | flops 131072 | bytes 1572864 | tf_op jit(solution)/shard_map/add | solution.py:436
  41.1 9.0 %all-to-all-done.2 = f32[32,16,128]{2,1,0:T(8,128)S(1)} async-done(((f32[32,16,128]{2,1,0:T(8,128)}), f32[32,16,128]{2,1,0:T(8,128)S(1)}, u32[]{:S(2)}, u32[]{:S(2)}) %all-to-all-start.2) | async-done | bytes 262176 | tf_op jit(solution)/shard_map/all_to_all | solution.py:379
  50.1 3.6 %all-to-all-start = ((f32[16,16,512]{2,1,0:T(8,128)}), f32[16,16,512]{2,1,0:T(8,128)S(1)}, u32[]{:S(2)}, u32[]{:S(2)}) async-start(f32[16,16,512]{2,1,0:T(8,128)} %bitcast.3), calls=%async_computation | async-start | bytes 1048576 | tf_op jit(solution)/shard_map/all_to_all | solution.py:379
  53.7 0.0 copy-done
  53.7 1.3 constant_dynamic-slice_fusion
  55.0 2.7 %collective-permute-start.3 = (f32[5,128,128]{2,1,0:T(8,128)}, f32[5,128,128]{2,1,0:T(8,128)S(1)}, u32[]{:S(2)}, u32[]{:S(2)}) collective-permute-start(f32[5,128,128]{2,1,0:T(8,128)} %get-tuple-element.41), channel_id=1, source_target_pairs={{0,3},{1,2},{2,1},{3,0},{4,7},{5,6},{6,5},{7,4},{8,11},{9,10},{10,... | collective-permute-start | bytes 983048 | tf_op jit(solution)/shard_map/ppermute | solution.py:375
  57.7 0.6 collective-permute-start.4
  58.3 0.2 collective-permute-start.5
  58.6 0.0 copy-start.1
  58.6 9.9 %all-to-all-done = f32[16,16,512]{2,1,0:T(8,128)S(1)} async-done(((f32[16,16,512]{2,1,0:T(8,128)}), f32[16,16,512]{2,1,0:T(8,128)S(1)}, u32[]{:S(2)}, u32[]{:S(2)}) %all-to-all-start) | async-done | bytes 524320 | tf_op jit(solution)/shard_map/all_to_all | solution.py:379
  68.5 0.2 fusion
  68.8 2.3 %collective-permute-done.3.refs_3_ = f32[5,128,128]{2,1,0:T(8,128)S(1)} collective-permute-done((f32[5,128,128]{2,1,0:T(8,128)}, f32[5,128,128]{2,1,0:T(8,128)S(1)}, u32[]{:S(2)}, u32[]{:S(2)}) %collective-permute-start.3) | collective-permute-done | bytes 327712 | tf_op jit(solution)/shard_map/ppermute | solution.py:375
  71.1 5.2 %collective-permute-done.4.refs_5_ = f32[5,128,128]{2,1,0:T(8,128)S(1)} collective-permute-done((f32[5,128,128]{2,1,0:T(8,128)}, f32[5,128,128]{2,1,0:T(8,128)S(1)}, u32[]{:S(2)}, u32[]{:S(2)}) %collective-permute-start.4) | collective-permute-done | bytes 327712 | tf_op jit(solution)/shard_map/ppermute | solution.py:375
  76.3 0.0 collective-permute-done.5.refs_6_
  76.3 0.8 broadcast_in_dim.7
  77.1 5.0 %all-to-all-start.3 = ((f32[32,16,128]{2,1,0:T(8,128)}), f32[32,16,128]{2,1,0:T(8,128)S(1)}, u32[]{:S(2)}, u32[]{:S(2)}) async-start(f32[32,16,128]{2,1,0:T(8,128)} %broadcast_in_dim.7), calls=%async_computation.3 | async-start | bytes 524288 | tf_op jit(solution)/shard_map/all_to_all | solution.py:379
  82.2 2.6 %collective-permute-start.6 = (f32[5,128,128]{2,1,0:T(8,128)}, f32[5,128,128]{2,1,0:T(8,128)S(1)}, u32[]{:S(2)}, u32[]{:S(2)}) collective-permute-start(f32[5,128,128]{2,1,0:T(8,128)} %get-tuple-element.50), channel_id=1, source_target_pairs={{0,3},{1,2},{2,1},{3,0},{4,7},{5,6},{6,5},{7,4},{8,11},{9,10},{10,... | collective-permute-start | bytes 983048 | tf_op jit(solution)/shard_map/ppermute | solution.py:375
  84.7 8.3 %all-to-all-done.3 = f32[32,16,128]{2,1,0:T(8,128)S(1)} async-done(((f32[32,16,128]{2,1,0:T(8,128)}), f32[32,16,128]{2,1,0:T(8,128)S(1)}, u32[]{:S(2)}, u32[]{:S(2)}) %all-to-all-start.3) | async-done | bytes 262176 | tf_op jit(solution)/shard_map/all_to_all | solution.py:379
  93.0 0.8 copy.8
  93.8 1.8 collective-permute-done.6.refs_7_
  95.6 0.0 copy-done.9
  95.6 0.0 copy-done.10
  95.6 0.0 copy-done.11
  95.6 0.7 copy-done.12
  96.3 3.5 %shard_map.69 = (f32[5,128,128]{2,1,0:T(8,128)}, f32[5,128,128]{2,1,0:T(8,128)}) custom-call(s32[1]{0:T(128)} %bitcast.1.rank_ref, f32[512,128]{1,0:T(8,128)} %bitcast.26, f32[5,128,128]{2,1,0:T(8,128)} %get-tuple-element.65.refs_0_, f32[5,128,128]{2,1,0:T(8,128)} %collective-permute-done.1.refs_1_, f32[5,128,128]{2,1,0:T(8,128)} %collective-permute-done.2.refs_2_, ...), custom_call_target="tpu_custom_call" | custom-call | flops 671088640 | bytes 2883584 | tf_op jit(solution)/shard_map/pallas_call | solution.py:174
  99.8 1.0 collective-permute-start.11
  100.8 1.0 collective-permute-start.7
  101.8 1.0 collective-permute-start.10
  102.8 1.0 collective-permute-start.8
  103.8 6.8 %collective-permute-done.11.refs_6_ = f32[5,128,128]{2,1,0:T(8,128)S(1)} collective-permute-done((f32[5,128,128]{2,1,0:T(8,128)}, f32[5,128,128]{2,1,0:T(8,128)S(1)}, u32[]{:S(2)}, u32[]{:S(2)}) %collective-permute-start.11) | collective-permute-done | bytes 327712 | tf_op jit(solution)/shard_map/ppermute | solution.py:375
  110.6 1.1 collective-permute-start.12
  111.7 0.0 collective-permute-done.7.refs_1_
  111.7 0.9 collective-permute-start.9
  112.7 0.0 copy-done.1
  112.7 9.2 %shard_map.70 = (f32[160,128]{1,0:T(8,128)}, f32[512,128]{1,0:T(8,128)}) custom-call(s32[1]{0:T(128)} %bitcast.1.rank_ref, f32[512,128]{1,0:T(8,128)} %bitcast.25, f32[512,128]{1,0:T(8,128)} %bitcast.27), custom_call_target="tpu_custom_call" | custom-call | flops 67108864 | bytes 1048576 | tf_op jit(solution)/shard_map/pallas_call | solution.py:340
  121.9 0.0 collective-permute-done.10.refs_5_
  121.9 0.0 collective-permute-done.8.refs_2_
  121.9 0.0 copy-start.6
  122.0 2.2 %collective-permute-done.12.refs_7_ = f32[5,128,128]{2,1,0:T(8,128)S(1)} collective-permute-done((f32[5,128,128]{2,1,0:T(8,128)S(1)}, f32[5,128,128]{2,1,0:T(8,128)S(1)}, u32[]{:S(2)}, u32[]{:S(2)}) %collective-permute-start.12) | collective-permute-done | bytes 327712 | tf_op jit(solution)/shard_map/ppermute | solution.py:375
  124.2 0.0 collective-permute-done.9.refs_3_
  124.2 0.0 copy-done.3
  124.2 0.7 copy-done.7
  124.9 0.1 copy-done.8
  125.0 10.6 %shard_map.72 = (f32[768,128]{1,0:T(8,128)}, f32[1280,128]{1,0:T(8,128)}) custom-call(s32[1]{0:T(128)} %bitcast.1.rank_ref, f32[160,128]{1,0:T(8,128)} %get-tuple-element.56.weight_ref, f32[5120,512]{1,0:T(8,128)} %bitcast.20, f32[5,128,128]{2,1,0:T(8,128)} %get-tuple-element.57.refs_0_, f32[5,128,128]{2,1,0:T(8,128)} %copy-done.4, ...), custom_call_target="tpu_custom_call" | custom-call | flops 2684354560 | bytes 13107200 | tf_op jit(solution)/shard_map/pallas_call | solution.py:228
  135.6 17.9 %all_to_all.30 = f32[32,24,128]{2,1,0:T(8,128)S(1)} all-to-all(f32[32,24,128]{2,1,0:T(8,128)} %bitcast.31), channel_id=1, replica_groups=mesh['cuts'=8,'rank'=4] {'cuts','rank'}, dimensions={0} | all-to-all | bytes 786432 | tf_op jit(solution)/shard_map/all_to_all | solution.py:379
  153.6 0.8 broadcast_in_dim.8
  154.3 2.8 %all-to-all-start.5 = ((f32[32,24,128]{2,1,0:T(8,128)}), f32[32,24,128]{2,1,0:T(8,128)S(1)}, u32[]{:S(2)}, u32[]{:S(2)}) async-start(f32[32,24,128]{2,1,0:T(8,128)} %broadcast_in_dim.8), calls=%async_computation.5 | async-start | bytes 786432 | tf_op jit(solution)/shard_map/all_to_all | solution.py:379
  157.2 8.5 %shard_map.71 = f32[5120,128]{1,0:T(8,128)} custom-call(f32[5120,512]{1,0:T(8,128)} %bitcast.22, f32[512,128]{1,0:T(8,128)} %get-tuple-element.55.weight_ref), custom_call_target="tpu_custom_call" | custom-call | flops 2684354560 | bytes 13107200 | tf_op jit(solution)/shard_map/pallas_call | solution.py:257
  165.7 4.9 %all-to-all-done.5 = f32[32,24,128]{2,1,0:T(8,128)S(1)} async-done(((f32[32,24,128]{2,1,0:T(8,128)}), f32[32,24,128]{2,1,0:T(8,128)S(1)}, u32[]{:S(2)}, u32[]{:S(2)}) %all-to-all-start.5) | async-done | bytes 393248 | tf_op jit(solution)/shard_map/all_to_all | solution.py:379
  170.6 0.7 copy-done.2
  171.3 9.3 %shard_map.73 = (f32[128,512]{1,0:T(8,128)}, f32[1280,128]{1,0:T(8,128)}) custom-call(f32[768,128]{1,0:T(8,128)} %bitcast.28, f32[1280,128]{1,0:T(8,128)} %get-tuple-element.60.middle_ref), custom_call_target="tpu_custom_call" | custom-call | flops 167772160 | bytes 1310720 | tf_op jit(solution)/shard_map/pallas_call | solution.py:363
  (18 shorter events, 0.1 us)
Async XLA Ops:
  13.6 21.0 %collective-permute-start.1 = (f32[5,128,128]{2,1,0:T(8,128)}, f32[5,128,128]{2,1,0:T(8,128)}, u32[]{:S(2)}, u32[]{:S(2)}) collective-permute-start(f32[5,128,128]{2,1,0:T(8,128)} %get-tuple-element.70), channel_id=1, source_target_pairs={{0,1},{1,0},{2,3},{3,2},{4,5},{5,4},{6,7},{7,6},{8,9},{9,8},{10,11... | collective-permute-start | bytes 983048 | tf_op jit(solution)/shard_map/ppermute | solution.py:375
  16.5 18.1 %collective-permute-start.2 = (f32[5,128,128]{2,1,0:T(8,128)}, f32[5,128,128]{2,1,0:T(8,128)}, u32[]{:S(2)}, u32[]{:S(2)}) collective-permute-start(f32[5,128,128]{2,1,0:T(8,128)} %get-tuple-element.69), channel_id=1, source_target_pairs={{0,2},{1,3},{2,0},{3,1},{4,6},{5,7},{6,4},{7,5},{8,10},{9,11},{10,... | collective-permute-start | bytes 983048 | tf_op jit(solution)/shard_map/ppermute | solution.py:375
  18.0 16.5 %all-to-all-start.1 = ((f32[8,16,128]{2,1,0:T(8,128)}), f32[8,16,128]{2,1,0:T(8,128)S(1)}, u32[]{:S(2)}, u32[]{:S(2)}) async-start(f32[8,16,128]{2,1,0:T(8,128)} %bitcast.32), calls=%async_computation.1 | async-start | bytes 131072 | tf_op jit(solution)/shard_map/all_to_all | solution.py:379
  34.0 19.7 %copy-start = (f32[40,128,128]{2,1,0:T(8,128)S(1)}, f32[40,128,128]{2,1,0:T(8,128)}, u32[]{:S(2)}) copy-start(f32[40,128,128]{2,1,0:T(8,128)} %get-tuple-element.40) | copy-start | bytes 7864324
  34.0 5.1 %collective-permute-start = (f32[256,512]{1,0:T(8,128)}, f32[256,512]{1,0:T(8,128)S(1)}, u32[]{:S(2)}, u32[]{:S(2)}) collective-permute-start(f32[256,512]{1,0:T(8,128)} %get-tuple-element.36), channel_id=1, source_target_pairs={{0,4},{4,0},{8,12},{12,8},{16,20},{20,16},{24,28},{28,24},{1,5},{5... | collective-permute-start | bytes 1572872 | tf_op jit(solution)/shard_map/ppermute | solution.py:375
  35.3 14.8 %all-to-all-start.2 = ((f32[32,16,128]{2,1,0:T(8,128)}), f32[32,16,128]{2,1,0:T(8,128)S(1)}, u32[]{:S(2)}, u32[]{:S(2)}) async-start(f32[32,16,128]{2,1,0:T(8,128)} %broadcast_in_dim.6), calls=%async_computation.2 | async-start | bytes 524288 | tf_op jit(solution)/shard_map/all_to_all | solution.py:379
  50.1 18.4 %all-to-all-start = ((f32[16,16,512]{2,1,0:T(8,128)}), f32[16,16,512]{2,1,0:T(8,128)S(1)}, u32[]{:S(2)}, u32[]{:S(2)}) async-start(f32[16,16,512]{2,1,0:T(8,128)} %bitcast.3), calls=%async_computation | async-start | bytes 1048576 | tf_op jit(solution)/shard_map/all_to_all | solution.py:379
  55.0 16.0 %collective-permute-start.3 = (f32[5,128,128]{2,1,0:T(8,128)}, f32[5,128,128]{2,1,0:T(8,128)S(1)}, u32[]{:S(2)}, u32[]{:S(2)}) collective-permute-start(f32[5,128,128]{2,1,0:T(8,128)} %get-tuple-element.41), channel_id=1, source_target_pairs={{0,3},{1,2},{2,1},{3,0},{4,7},{5,6},{6,5},{7,4},{8,11},{9,10},{10,... | collective-permute-start | bytes 983048 | tf_op jit(solution)/shard_map/ppermute | solution.py:375
  57.7 18.6 %collective-permute-start.4 = (f32[5,128,128]{2,1,0:T(8,128)}, f32[5,128,128]{2,1,0:T(8,128)S(1)}, u32[]{:S(2)}, u32[]{:S(2)}) collective-permute-start(f32[5,128,128]{2,1,0:T(8,128)} %get-tuple-element.42), channel_id=1, source_target_pairs={{0,1},{1,0},{2,3},{3,2},{4,5},{5,4},{6,7},{7,6},{8,9},{9,8},{10,11... | collective-permute-start | bytes 983048 | tf_op jit(solution)/shard_map/ppermute | solution.py:375
  58.3 18.0 %collective-permute-start.5 = (f32[5,128,128]{2,1,0:T(8,128)}, f32[5,128,128]{2,1,0:T(8,128)S(1)}, u32[]{:S(2)}, u32[]{:S(2)}) collective-permute-start(f32[5,128,128]{2,1,0:T(8,128)} %get-tuple-element.43), channel_id=1, source_target_pairs={{0,2},{1,3},{2,0},{3,1},{4,6},{5,7},{6,4},{7,5},{8,10},{9,11},{10,... | collective-permute-start | bytes 983048 | tf_op jit(solution)/shard_map/ppermute | solution.py:375
  58.6 54.1 %copy-start.1 = (f32[4,8,16,128]{3,2,1,0:T(8,128)}, f32[4,8,16,128]{3,2,1,0:T(8,128)S(1)}, u32[]{:S(2)}) copy-start(f32[4,8,16,128]{3,2,1,0:T(8,128)S(1)} %copy.7) | copy-start | bytes 786436
  71.1 24.5 %copy-start.9 = (f32[5,128,128]{2,1,0:T(8,128)}, f32[5,128,128]{2,1,0:T(8,128)S(1)}, u32[]{:S(2)}) copy-start(f32[5,128,128]{2,1,0:T(8,128)S(1)} %collective-permute-done.3.refs_3_) | copy-start | bytes 983044
  76.3 19.3 %copy-start.10 = (f32[5,128,128]{2,1,0:T(8,128)}, f32[5,128,128]{2,1,0:T(8,128)S(1)}, u32[]{:S(2)}) copy-start(f32[5,128,128]{2,1,0:T(8,128)S(1)} %collective-permute-done.4.refs_5_) | copy-start | bytes 983044
  76.3 19.3 %copy-start.11 = (f32[5,128,128]{2,1,0:T(8,128)}, f32[5,128,128]{2,1,0:T(8,128)S(1)}, u32[]{:S(2)}) copy-start(f32[5,128,128]{2,1,0:T(8,128)S(1)} %collective-permute-done.5.refs_6_) | copy-start | bytes 983044
  77.1 15.9 %all-to-all-start.3 = ((f32[32,16,128]{2,1,0:T(8,128)}), f32[32,16,128]{2,1,0:T(8,128)S(1)}, u32[]{:S(2)}, u32[]{:S(2)}) async-start(f32[32,16,128]{2,1,0:T(8,128)} %broadcast_in_dim.7), calls=%async_computation.3 | async-start | bytes 524288 | tf_op jit(solution)/shard_map/all_to_all | solution.py:379
  82.2 13.4 %collective-permute-start.6 = (f32[5,128,128]{2,1,0:T(8,128)}, f32[5,128,128]{2,1,0:T(8,128)S(1)}, u32[]{:S(2)}, u32[]{:S(2)}) collective-permute-start(f32[5,128,128]{2,1,0:T(8,128)} %get-tuple-element.50), channel_id=1, source_target_pairs={{0,3},{1,2},{2,1},{3,0},{4,7},{5,6},{6,5},{7,4},{8,11},{9,10},{10,... | collective-permute-start | bytes 983048 | tf_op jit(solution)/shard_map/ppermute | solution.py:375
  95.6 0.7 copy-start.12
  99.8 10.8 %collective-permute-start.11 = (f32[5,128,128]{2,1,0:T(8,128)}, f32[5,128,128]{2,1,0:T(8,128)S(1)}, u32[]{:S(2)}, u32[]{:S(2)}) collective-permute-start(f32[5,128,128]{2,1,0:T(8,128)} %get-tuple-element.58.refs_4_), channel_id=1, source_target_pairs={{0,2},{1,3},{2,0},{3,1},{4,6},{5,7},{6,4},{7,5},{8,10},{9,11},{10,... | collective-permute-start | bytes 983048 | tf_op jit(solution)/shard_map/ppermute | solution.py:375
  100.8 10.9 %collective-permute-start.7 = (f32[5,128,128]{2,1,0:T(8,128)}, f32[5,128,128]{2,1,0:T(8,128)S(1)}, u32[]{:S(2)}, u32[]{:S(2)}) collective-permute-start(f32[5,128,128]{2,1,0:T(8,128)} %get-tuple-element.57.refs_0_), channel_id=1, source_target_pairs={{0,1},{1,0},{2,3},{3,2},{4,5},{5,4},{6,7},{7,6},{8,9},{9,8},{10,11... | collective-permute-start | bytes 983048 | tf_op jit(solution)/shard_map/ppermute | solution.py:375
  101.8 20.1 %collective-permute-start.10 = (f32[5,128,128]{2,1,0:T(8,128)}, f32[5,128,128]{2,1,0:T(8,128)S(1)}, u32[]{:S(2)}, u32[]{:S(2)}) collective-permute-start(f32[5,128,128]{2,1,0:T(8,128)} %get-tuple-element.58.refs_4_), channel_id=1, source_target_pairs={{0,1},{1,0},{2,3},{3,2},{4,5},{5,4},{6,7},{7,6},{8,9},{9,8},{10,11... | collective-permute-start | bytes 983048 | tf_op jit(solution)/shard_map/ppermute | solution.py:375
  102.8 19.1 %collective-permute-start.8 = (f32[5,128,128]{2,1,0:T(8,128)}, f32[5,128,128]{2,1,0:T(8,128)S(1)}, u32[]{:S(2)}, u32[]{:S(2)}) collective-permute-start(f32[5,128,128]{2,1,0:T(8,128)} %get-tuple-element.57.refs_0_), channel_id=1, source_target_pairs={{0,2},{1,3},{2,0},{3,1},{4,6},{5,7},{6,4},{7,5},{8,10},{9,11},{10,... | collective-permute-start | bytes 983048 | tf_op jit(solution)/shard_map/ppermute | solution.py:375
  110.6 13.6 %copy-start.3 = (f32[5,128,128]{2,1,0:T(8,128)}, f32[5,128,128]{2,1,0:T(8,128)S(1)}, u32[]{:S(2)}) copy-start(f32[5,128,128]{2,1,0:T(8,128)S(1)} %collective-permute-done.11.refs_6_) | copy-start | bytes 983044
  110.6 13.6 %collective-permute-start.12 = (f32[5,128,128]{2,1,0:T(8,128)S(1)}, f32[5,128,128]{2,1,0:T(8,128)S(1)}, u32[]{:S(2)}, u32[]{:S(2)}) collective-permute-start(f32[5,128,128]{2,1,0:T(8,128)S(1)} %collective-permute-done.11.refs_6_), channel_id=1, source_target_pairs={{0,1},{1,0},{2,3},{3,2},{4,5},{5,4},{6,7},{7,6},{8,9},{9,8},{10,11... | collective-permute-start | bytes 983048 | tf_op jit(solution)/shard_map/ppermute | solution.py:375
  111.7 12.5 %copy-start.4 = (f32[5,128,128]{2,1,0:T(8,128)}, f32[5,128,128]{2,1,0:T(8,128)S(1)}, u32[]{:S(2)}) copy-start(f32[5,128,128]{2,1,0:T(8,128)S(1)} %collective-permute-done.7.refs_1_) | copy-start | bytes 983044
  111.7 12.4 %collective-permute-start.9 = (f32[5,128,128]{2,1,0:T(8,128)S(1)}, f32[5,128,128]{2,1,0:T(8,128)S(1)}, u32[]{:S(2)}, u32[]{:S(2)}) collective-permute-start(f32[5,128,128]{2,1,0:T(8,128)S(1)} %collective-permute-done.7.refs_1_), channel_id=1, source_target_pairs={{0,2},{1,3},{2,0},{3,1},{4,6},{5,7},{6,4},{7,5},{8,10},{9,11},{10,... | collective-permute-start | bytes 983048 | tf_op jit(solution)/shard_map/ppermute | solution.py:375
  121.9 2.3 %copy-start.5 = (f32[5,128,128]{2,1,0:T(8,128)}, f32[5,128,128]{2,1,0:T(8,128)S(1)}, u32[]{:S(2)}) copy-start(f32[5,128,128]{2,1,0:T(8,128)S(1)} %collective-permute-done.10.refs_5_) | copy-start | bytes 983044
  121.9 2.3 %copy-start.6 = (f32[5,128,128]{2,1,0:T(8,128)}, f32[5,128,128]{2,1,0:T(8,128)S(1)}, u32[]{:S(2)}) copy-start(f32[5,128,128]{2,1,0:T(8,128)S(1)} %collective-permute-done.8.refs_2_) | copy-start | bytes 983044
  124.2 0.7 copy-start.7
  124.2 0.9 copy-start.8
  154.3 16.2 %all-to-all-start.5 = ((f32[32,24,128]{2,1,0:T(8,128)}), f32[32,24,128]{2,1,0:T(8,128)S(1)}, u32[]{:S(2)}, u32[]{:S(2)}) async-start(f32[32,24,128]{2,1,0:T(8,128)} %broadcast_in_dim.8), calls=%async_computation.5 | async-start | bytes 786432 | tf_op jit(solution)/shard_map/all_to_all | solution.py:379
  170.6 0.7 copy-start.2

commit v3 on v2

--- a/solution.py
+++ b/solution.py
@@ -13,6 +13,18 @@
 TN = (((0,), (0,)), ((), ()))
 VMEM_LIMIT = 56 * 1024 * 1024
 BLOCK = 8
+
+
+PARTS = 4
+
+
+def tiles(block, width):
+    size = block // PARTS
+    return [pl.BlockSpec((size, width), lambda i, q=q: (i * PARTS + q, 0)) for q in range(PARTS)]
+
+
+def joined_rows(refs):
+    return jnp.concatenate([ref[...] for ref in refs], axis=0)
 
 
 def call(kernel, flops, size, **more):
@@ -58,11 +70,13 @@
     return ref.reshape(ref.shape[0] * ref.shape[1], ref.shape[2])
 
 
-def sketch_kernel(core_ref, right_ref, left_ref, sketched_ref, part_ref, rows_ref):
-    local_rows, block, _ = core_ref.shape
+def sketch_kernel(*refs):
+    core_refs, (right_ref, left_ref, sketched_ref, part_ref, rows_ref) = refs[:PARTS], refs[PARTS:]
+    block = left_ref.shape[1]
+    local_rows = rows_ref.shape[0] // block
     columns = right_ref.shape[1]
     right = twice(both_parts(right_ref[...], 1), 0)
-    rows_ref[...] = fold(mxu(both_parts(rows_of(core_ref)[...], 1), right, NN), 1)
+    rows_ref[...] = fold(mxu(both_parts(jnp.concatenate([rows_of(ref)[...] for ref in core_refs], axis=0), 1), right, NN), 1)
     left_rows = rows_of(left_ref)
 
     @pl.when(pl.program_id(0) == 0)
@@ -89,7 +103,7 @@
         4 * (core_two.size + 2 * sketch_core.size),
         grid=(slices // BLOCK,),
         in_specs=[
-            pl.BlockSpec((local_rows, BLOCK, width), lambda i: (0, i, 0)),
+            *[pl.BlockSpec((local_rows // PARTS, BLOCK, width), lambda i, q=q: (q, i, 0)) for q in range(PARTS)],
             pl.BlockSpec((width, columns), lambda i: (0, 0)),
             pl.BlockSpec((columns, BLOCK, columns), lambda i: (0, i, 0)),
         ],
@@ -99,7 +113,7 @@
         ],
         out_shape=[shape(slices, local_rows, columns), shape(local_rows, columns)],
         scratch_shapes=[pltpu.VMEM((local_rows * BLOCK, columns), jnp.float32)],
-    )(core_two, right_sketch, sketch_core)
+    )(*[core_two] * PARTS, right_sketch, sketch_core)
 
 
 def block_of(rows):
@@ -109,44 +123,47 @@
     return block
 
 
-def square_kernel(core_ref, core_index_ref, keep_ref, give_ref, sum_ref):
+def rows_kernel(*refs):
+    core_refs, (bridge_ref, raw_ref, rows_ref, sum_ref) = refs[:PARTS], refs[PARTS:]
     step = pl.program_id(0)
-    width = core_ref.shape[1]
-    high, low = split(core_ref[...])
 
     @pl.when(step == 0)
     def _():
         sum_ref[...] = jnp.zeros_like(sum_ref)
 
-    sum_ref[...] += mxu(high, jnp.concatenate([high, low], axis=1), TN)
+    high, low = split(joined_rows(core_refs))
+    bridge = twice(both_parts(bridge_ref[...], 1), 0)
+    rows = fold(mxu(jnp.concatenate([high, low], axis=1), bridge, NN), 1)
+    rows_ref[...] = rows
+    turned = twice(both_parts(rows, 1).T, 1)
+    product = fold(mxu(turned, jnp.concatenate([high, low], axis=0), NN), 0)
+    sum_ref[...] += product
 
     @pl.when(step == pl.num_programs(0) - 1)
     def _():
-        cross = sum_ref[:, width:]
-        sum_ref[:, :width] = sum_ref[:, :width] + cross + cross.T
-        half = width // 2
-        own = core_index_ref[0]
-        keep_ref[...] = sum_ref[pl.ds(pl.multiple_of(own * half, half), half), :width]
-        give_ref[...] = sum_ref[pl.ds(pl.multiple_of((1 - own) * half, half), half), :width]
-
-
-def square_of(flat_one, core_index):
+        raw_ref[...] = sum_ref[...].T
+
+
+def first_rows_of(flat_one, bridge):
     rows, width = flat_one.shape
+    columns = bridge.shape[1]
     block = block_of(rows)
-    half = pl.BlockSpec((width // 2, width), lambda i: (0, 0))
-    return call(
-        square_kernel,
-        4 * rows * width * width,
+    return call(
+        rows_kernel,
+        16 * flat_one.size * columns,
         4 * flat_one.size,
         grid=(rows // block,),
         in_specs=[
-            pl.BlockSpec((block, width), lambda i: (i, 0)),
-            pl.BlockSpec(memory_space=pltpu.SMEM),
+            *tiles(block, width),
+            pl.BlockSpec((width, columns), lambda i: (0, 0)),
         ],
-        out_specs=[half, half],
-        out_shape=[shape(width // 2, width)] * 2,
-        scratch_shapes=[pltpu.VMEM((width, 2 * width), jnp.float32)],
-    )(flat_one, core_index)
+        out_specs=[
+            pl.BlockSpec((width, columns), lambda i: (0, 0)),
+            pl.BlockSpec((block, columns), lambda i: (i, 0)),
+        ],
+        out_shape=[shape(width, columns), shape(rows, columns)],
+        scratch_shapes=[pltpu.VMEM((columns, width), jnp.float32)],
+    )(*[flat_one] * PARTS, bridge)
 
 
 def loose_kernel(halves, rank_ref, raw_ref, *refs):
@@ -181,11 +198,11 @@
     )(rank_index, raw, *pieces)
 
 
-def carry_kernel(halves, share, rank_ref, weight_ref, core_ref, *refs):
-    piece_refs = refs[:-4]
+def carry_kernel(halves, share, rank_ref, weight_ref, *refs):
+    core_refs, piece_refs = refs[:PARTS], refs[PARTS:-4]
     joined_ref, middle_ref, rows_ref, sum_ref = refs[-4:]
     step = pl.program_id(0)
-    block, width = core_ref.shape
+    block, width = core_refs[0].shape[0] * PARTS, core_refs[0].shape[1]
     columns = weight_ref.shape[1]
     ranks = len(piece_refs) // len(halves)
     room = share * ranks
@@ -208,7 +225,7 @@
                     middle_ref[pl.ds(first + n, band, stride=room), :] = piece[local_rows:]
 
     rows = both_parts(rows_ref[pl.ds(pl.multiple_of(step * block, block), block), :], 1).T
-    product = fold(mxu(twice(rows, 1), both_parts(core_ref[...], 0), NN), 0)
+    product = fold(mxu(twice(rows, 1), both_parts(joined_rows(core_refs), 0), NN), 0)
     sum_ref[...] += product
 
     @pl.when(step == pl.num_programs(0) - 1)
@@ -233,7 +250,7 @@
         in_specs=[
             pl.BlockSpec(memory_space=pltpu.SMEM),
             pl.BlockSpec((weight.shape[0], columns), lambda i: (0, 0)),
-            pl.BlockSpec((block, width), lambda i: (i, 0)),
+            *tiles(block, width),
         ]
         + [pl.BlockSpec(piece.shape, lambda i: (0, 0, 0)) for piece in pieces],
         out_specs=[
@@ -242,27 +259,24 @@
         ],
         out_shape=[shape(total, columns), shape(band * share * ranks, columns)],
         scratch_shapes=[pltpu.VMEM((rows, columns), jnp.float32), pltpu.VMEM((columns, width), jnp.float32)],
-    )(rank_index, weight, flat_two, *pieces)
+    )(rank_index, weight, *[flat_two] * PARTS, *pieces)
 
 
 def apply_kernel(rows_ref, weight_ref, out_ref):
-    weight = twice(both_parts(weight_ref[...], 1), 0)
-    out_ref[...] = fold(mxu(both_parts(rows_ref[...], 1), weight, NN), 1)
+    weight = twice(both_parts(weight_ref[...], 0), 1)
+    out_ref[...] = fold(mxu(both_parts(rows_ref[...], 1), weight, NT), 1)
 
 
 def apply_to(rows, weight):
-    count, width = rows.shape
-    columns = weight.shape[1]
+    count, columns = rows.shape
     block = block_of(count)
+    tile = pl.BlockSpec((block, columns), lambda i: (i, 0))
     return call(
         apply_kernel,
         8 * rows.size * columns,
-        4 * (rows.size + count * columns),
+        8 * rows.size,
         grid=(count // block,),
-        in_specs=[
-            pl.BlockSpec((block, width), lambda i: (i, 0)),
-            pl.BlockSpec((width, columns), lambda i: (0, 0)),
-        ],
+        in_specs=[tile, pl.BlockSpec((columns, columns), lambda i: (0, 0))],
         out_specs=pl.BlockSpec((block, columns), lambda i: (i, 0)),
         out_shape=shape(count, columns),
     )(rows, weight)
@@ -331,7 +345,7 @@
     own = exact(raw_ref[pl.ds(start, local_rows), :], inverse, NT)
     weight_ref[:local_rows, :] = exact(own, inverse, NN)
     weight_ref[local_rows:, :] = inverse_ref[pl.ds(pl.multiple_of(rank_ref[0] * band, band), band), :]
-    solve_ref[...] = scale * exact(bridge_ref[...], inverse, NT)
+    solve_ref[...] = scale * inverse
 
 
 def first_factor(rank_index, bridge, raw, scale, local_rows, band):
@@ -343,7 +357,7 @@
         16 * raw.size,
         in_specs=[pl.BlockSpec(memory_space=pltpu.SMEM), whole, whole],
         out_specs=[whole, whole],
-        out_shape=[shape(local_rows + band, columns), shape(*raw.shape)],
+        out_shape=[shape(local_rows + band, columns), shape(columns, columns)],
         scratch_shapes=[pltpu.VMEM((columns, columns), jnp.float32)],
     )(rank_index, bridge, raw)
 
@@ -375,8 +389,8 @@
     return lax.ppermute(value, axis, [(i, i ^ offset) for i in range(lax.axis_size(axis))])
 
 
-def exchange(value, axes, groups=None):
-    return lax.all_to_all(value, axes, 0, 0, axis_index_groups=groups, tiled=True)
+def exchange(value, axes):
+    return lax.all_to_all(value, axes, 0, 0, tiled=True)
 
 
 def gather_all(value, axes):
@@ -392,18 +406,14 @@
     local_rows, slices, width = core_one.shape
     columns = right_sketch.shape[1]
     ranks, cuts = lax.axis_size("rank"), lax.axis_size("cuts")
-    rank, cut = lax.axis_index("rank"), lax.axis_index("cuts")
+    rank = lax.axis_index("rank")
     rank_index = rank.astype(jnp.int32).reshape(1)
-    core_index = lax.rem(cut, 2).astype(jnp.int32).reshape(1)
     both = ("cuts", "rank")
     parts = ranks * cuts
     band = columns // ranks
     share = -(-slices // ranks)
     room = share * ranks
     halves = [share // 2, share - share // 2]
-    core_groups = [
-        [z * ranks + place for z in range(core, cuts, 2) for place in range(ranks)] for core in range(2)
-    ]
     filler = ((0, 0), (0, room - slices), (0, 0))
     core_two, sketch_core = jnp.pad(core_two, filler), jnp.pad(sketch_core, filler)
     flat_one = core_one.reshape(local_rows * slices, width)
@@ -423,32 +433,31 @@
     far = ranks - 1
     near = [[(half, offset) for offset in range(1, far)] for half in range(2)]
 
-    moved = send(near[0], sketched, None)
-    bridge_rows = jnp.sum(exchange(part.reshape(cuts, local_rows // cuts, columns), "cuts"), axis=0)
-    flat_late, part = after(flat_one, part)
-    keep, give = square_of(flat_late, core_index)
-    bridge_rows, pieces = after(bridge_rows, moved)
-    sketched, bridge_rows = after(sketched, bridge_rows)
-    pieces.update(send([(0, 0), (1, 0)], sketched, None))
-
-    bridge = gather_all(bridge_rows, both)
-    bridge = bridge.reshape(cuts, ranks, -1, columns).swapaxes(0, 1).reshape(width, columns)
-    square = keep + swap(give, "cuts", 1)
-    moved = send(near[1] + [(0, far)], sketched, square)
-    square = exchange(square.reshape(parts // 2, -1, width), both, core_groups)
-    raw_rows = exact(jnp.sum(square, axis=0), bridge, NN)
-    raw_rows, moved = after(raw_rows, moved)
+    cut_bits = [1 << bit for bit in range((cuts - 1).bit_length())]
+    bits = [1 << bit for bit in range((ranks - 1).bit_length())]
+    for bit in cut_bits:
+        part = part + swap(part, "cuts", bit)
+    bridge = {0: part}
+    for bit in bits:
+        bridge.update({offset ^ bit: swap(held, "rank", bit) for offset, held in list(bridge.items())})
+    bridge = jnp.stack([bridge[offset] for offset in range(ranks)])
+    bridge = bridge[rank ^ jnp.arange(ranks)].reshape(width, columns)
+    sketched, bridge = after(sketched, bridge)
+    pieces = send([(0, 0), (1, 0)] + near[0] + near[1], sketched, None)
+    raw, first_rows = first_rows_of(flat_one, bridge)
+    raw, moved = after(raw, pieces)
     pieces.update(moved)
-
-    pieces.update(send([(1, far)], sketched, raw_rows))
-    raw = gather_all(raw_rows, both).reshape(cuts // 2, 2, ranks, -1, columns)
-    raw = raw.transpose(1, 0, 2, 3, 4).reshape(width, columns)
+    moved = send([(0, far)], sketched, raw)
+    raw = jnp.sum(exchange(raw.reshape(parts, -1, columns), both), axis=0)
+    raw, moved = after(raw, moved)
+    pieces.update(moved)
+    pieces.update(send([(1, far)], sketched, raw))
+    raw = gather_all(raw, both).reshape(width, columns)
 
     ordered = [pieces[(half, offset)] for half in range(2) for offset in range(ranks)]
     loose = loosen(rank_index, raw, ordered, halves)
     loose, (bridge, raw) = after(loose, (bridge, raw))
 
-    bits = [1 << bit for bit in range((ranks - 1).bit_length())]
     everyone = []
     for value, order in zip(loose, (bits, bits[::-1])):
         found = {0: value}
@@ -462,7 +471,7 @@
     joined, middle = carry_rows(rank_index, weight, flat_two, everyone, halves, share, band, total)
     joined = jnp.sum(exchange(joined.reshape(parts, -1, columns), both), axis=0)
     joined = gather_all(joined, both).reshape(total, columns)
-    left_core = apply_to(flat_one, solve).reshape(local_rows, slices, columns)
+    left_core = apply_to(first_rows, solve).reshape(local_rows, slices, columns)
     scale = math.sqrt(columns * slices * cuts)
     carry, middle = last_factor(joined, middle, scale, width)
     middle_core = middle.reshape(band, room, columns)[:, :slices]

time: 182 us -> 181 us (level)
  starting transfers between devices: 37.3 us -> 40.3 us
    all_to_all x5 -> x3, waiting for transfers between devices: 32.1 us -> 16.3 us  [exchange(): return lax.all_to_all(value, axes, 0, 0, tiled=True)]
    ppermute x13 -> x18, waiting for transfers between devices: 18.3 us -> 32.4 us  [swap(): lax.ppermute(value, axis, [(i, i ^ offset) for i in range(lax.axis_size(a...]
    ppermute x13 -> x18, starting transfers between devices: 17.1 us -> 26.6 us  [swap(): lax.ppermute(value, axis, [(i, i ^ offset) for i in range(lax.axis_size(a...]
    all_to_all x5 -> x3, starting transfers between devices: 20.2 us -> 13.6 us  [exchange(): return lax.all_to_all(value, axes, 0, 0, tiled=True)]
  transfers between devices with their start and end apart: 18 -> 21, of which waited for: 9 -> 12; matrix products, arithmetic and copies ran while one was open for 3% -> 0% of each run, Pallas kernels for 16% -> 16%
where the time goes in v3:
time: 181 us; the launch traced here: 180 us
  Pallas kernels  63.6 us (35%)
  waiting for transfers between devices  48.7 us (27%)
  starting transfers between devices  40.3 us (22%)
  blocking collectives  17.9 us (10%)
  local copies, waits for them, and re-layouts  7.95 us (4%)
    ppermute x18, waiting for transfers between devices, swap(): lax.ppermute(value, axis, [(i, i ^ offset) for i in range(lax.axis_size(a...  32.4 us
    ppermute x18, starting transfers between devices, swap(): lax.ppermute(value, axis, [(i, i ^ offset) for i in range(lax.axis_size(a...  26.6 us
    all_to_all x1, blocking collectives, exchange(): return lax.all_to_all(value, axes, 0, 0, tiled=True)  17.9 us
    all_to_all x3, waiting for transfers between devices, exchange(): return lax.all_to_all(value, axes, 0, 0, tiled=True)  16.3 us
    pallas_call x1, Pallas kernels, first_rows_of(): call(rows_kernel, 16 * flat_one.size * columns, 4 * flat_one.size, grid=(...  14.4 us
    all_to_all x3, starting transfers between devices, exchange(): return lax.all_to_all(value, axes, 0, 0, tiled=True)  13.6 us
    pallas_call x1, Pallas kernels, sketch(): call(sketch_kernel, 2 * core_two.size * columns * 4, 4 * (core_two.size +...  11.5 us
    pallas_call x1, Pallas kernels, carry_rows(): call(functools.partial(carry_kernel, halves, share), 8 * flat_two.size *...  10.6 us
  transfers between devices with their start and end apart: 21, of which 12 were waited for; matrix products, arithmetic and copies ran while one was open for 0% of the time, Pallas kernels for 16%

profile of v3, /device:TPU:0, one launch (start us, length us, event | category | flops | bytes accessed | tf_op | source)
XLA Modules:
  0.0 180.2 jit_solution(8797771898576818010)
XLA Ops:
  0.6 11.5 %shard_map.67 = (f32[40,128,128]{2,1,0:T(8,128)}, f32[128,128]{1,0:T(8,128)}) custom-call(f32[128,40,512]{2,1,0:T(8,128)} %refs_3_.1, f32[128,40,512]{2,1,0:T(8,128)} %refs_3_.1, f32[128,40,512]{2,1,0:T(8,128)} %refs_3_.1, f32[128,40,512]{2,1,0:T(8,128)} %refs_3_.1, f32[512,128]{1,0:T(8,128)} %refs_4_.1, f32[128,40,128]{2,1,0:T(8,128)} %refs_5_.1), custom_call_target="tpu_custom_call" | custom-call | flops 2684354560 | bytes 15728640 | tf_op jit(solution)/shard_map/pallas_call | solution.py:100
  12.1 0.5 collective-permute-start
  12.6 1.1 collective-permute-done
  13.7 0.9 add.63
  14.5 3.0 %collective-permute-start.1 = (f32[128,128]{1,0:T(8,128)S(1)}, f32[128,128]{1,0:T(8,128)S(1)}, u32[]{:S(2)}, u32[]{:S(2)}) collective-permute-start(f32[128,128]{1,0:T(8,128)S(1)} %add.63), channel_id=1, source_target_pairs={{0,8},{4,12},{8,0},{12,4},{16,24},{20,28},{24,16},{28,20},{1,9},{5... | collective-permute-start | bytes 196616 | tf_op jit(solution)/shard_map/ppermute | solution.py:389
  17.5 2.4 %collective-permute-done.1 = f32[128,128]{1,0:T(8,128)S(1)} collective-permute-done((f32[128,128]{1,0:T(8,128)S(1)}, f32[128,128]{1,0:T(8,128)S(1)}, u32[]{:S(2)}, u32[]{:S(2)}) %collective-permute-start.1) | collective-permute-done | bytes 65568 | tf_op jit(solution)/shard_map/ppermute | solution.py:389
  19.9 2.9 %collective-permute-start.2 = (f32[128,128]{1,0:T(8,128)S(1)}, f32[128,128]{1,0:T(8,128)S(1)}, u32[]{:S(2)}, u32[]{:S(2)}) collective-permute-start(f32[128,128]{1,0:T(8,128)S(1)} %add.64), channel_id=1, source_target_pairs={{0,16},{4,20},{8,24},{12,28},{16,0},{20,4},{24,8},{28,12},{1,17},{... | collective-permute-start | bytes 196616 | tf_op jit(solution)/shard_map/ppermute | solution.py:389
  22.9 2.4 %collective-permute-done.2 = f32[128,128]{1,0:T(8,128)S(1)} collective-permute-done((f32[128,128]{1,0:T(8,128)S(1)}, f32[128,128]{1,0:T(8,128)S(1)}, u32[]{:S(2)}, u32[]{:S(2)}) %collective-permute-start.2) | collective-permute-done | bytes 65568 | tf_op jit(solution)/shard_map/ppermute | solution.py:389
  25.3 1.8 collective-permute-start.3
  27.0 1.5 collective-permute-start.4
  28.5 1.1 collective-permute-done.3
  29.6 1.7 collective-permute-start.5
  31.3 0.0 collective-permute-done.4
  31.3 2.5 %collective-permute-done.5 = f32[128,128]{1,0:T(8,128)S(1)} collective-permute-done((f32[128,128]{1,0:T(8,128)S(1)}, f32[128,128]{1,0:T(8,128)S(1)}, u32[]{:S(2)}, u32[]{:S(2)}) %collective-permute-start.5) | collective-permute-done | bytes 65568 | tf_op jit(solution)/shard_map/ppermute | solution.py:389
  33.9 1.3 gather_fusion
  35.1 2.8 %constant_dynamic-slice_fusion = (f32[5,128,128]{2,1,0:T(8,128)S(1)}, f32[5,128,128]{2,1,0:T(8,128)S(1)}, f32[5,128,128]{2,1,0:T(8,128)S(1)}, f32[5,128,128]{2,1...) fusion(f32[40,128,128]{2,1,0:T(8,128)} %get-tuple-element.37, ...), kind=kLoop, calls=%fused_computation.4 | loop fusion | bytes 5242912 | tf_op jit(solution)/shard_map/dynamic_slice | solution.py:428
  37.9 1.7 collective-permute-start.9
  39.6 1.5 collective-permute-start.8
  41.1 0.5 collective-permute-start.7
  41.6 0.3 collective-permute-start.6
  42.0 14.4 %shard_map.68 = (f32[512,128]{1,0:T(8,128)}, f32[5120,128]{1,0:T(8,128)}) custom-call(f32[5120,512]{1,0:T(8,128)} %bitcast.20, f32[5120,512]{1,0:T(8,128)} %bitcast.21, f32[5120,512]{1,0:T(8,128)} %bitcast.22, f32[5120,512]{1,0:T(8,128)} %bitcast.23, f32[512,128]{1,0:T(8,128)} %bitcast.25), custom_call_target="tpu_custom_call" | custom-call | flops 5368709120 | bytes 10485760 | tf_op jit(solution)/shard_map/pallas_call | solution.py:151
  56.3 0.0 collective-permute-done.9.refs_6_
  56.3 0.0 collective-permute-done.8.refs_5_
  56.3 0.0 copy-start.9
  56.4 0.0 collective-permute-done.7.refs_2_
  56.4 0.0 collective-permute-done.6.refs_1_
  56.4 0.0 copy-start.11
  56.4 6.6 %all-to-all-start = ((f32[32,16,128]{2,1,0:T(8,128)}), f32[32,16,128]{2,1,0:T(8,128)S(1)}, u32[]{:S(2)}, u32[]{:S(2)}) async-start(f32[32,16,128]{2,1,0:T(8,128)} %bitcast.31), calls=%async_computation | async-start | bytes 524288 | tf_op jit(solution)/shard_map/all_to_all | solution.py:393
  63.0 2.7 %collective-permute-start.10 = (f32[5,128,128]{2,1,0:T(8,128)S(1)}, f32[5,128,128]{2,1,0:T(8,128)S(1)}, u32[]{:S(2)}, u32[]{:S(2)}) collective-permute-start(f32[5,128,128]{2,1,0:T(8,128)S(1)} %get-tuple-element.39), channel_id=1, source_target_pairs={{0,3},{1,2},{2,1},{3,0},{4,7},{5,6},{6,5},{7,4},{8,11},{9,10},{10,... | collective-permute-start | bytes 983048 | tf_op jit(solution)/shard_map/ppermute | solution.py:389
  65.8 8.3 %all-to-all-done = f32[32,16,128]{2,1,0:T(8,128)S(1)} async-done(((f32[32,16,128]{2,1,0:T(8,128)}), f32[32,16,128]{2,1,0:T(8,128)S(1)}, u32[]{:S(2)}, u32[]{:S(2)}) %all-to-all-start) | async-done | bytes 262176 | tf_op jit(solution)/shard_map/all_to_all | solution.py:393
  74.1 2.5 %collective-permute-done.10.refs_3_ = f32[5,128,128]{2,1,0:T(8,128)S(1)} collective-permute-done((f32[5,128,128]{2,1,0:T(8,128)S(1)}, f32[5,128,128]{2,1,0:T(8,128)S(1)}, u32[]{:S(2)}, u32[]{:S(2)}) %collective-permute-start.10) | collective-permute-done | bytes 327712 | tf_op jit(solution)/shard_map/ppermute | solution.py:389
  76.6 0.8 broadcast_in_dim.4
  77.4 4.2 %all-to-all-start.1 = ((f32[32,16,128]{2,1,0:T(8,128)}), f32[32,16,128]{2,1,0:T(8,128)S(1)}, u32[]{:S(2)}, u32[]{:S(2)}) async-start(f32[32,16,128]{2,1,0:T(8,128)} %broadcast_in_dim.4), calls=%async_computation.1 | async-start | bytes 524288 | tf_op jit(solution)/shard_map/all_to_all | solution.py:393
  81.6 2.6 %collective-permute-start.11 = (f32[5,128,128]{2,1,0:T(8,128)S(1)}, f32[5,128,128]{2,1,0:T(8,128)S(1)}, u32[]{:S(2)}, u32[]{:S(2)}) collective-permute-start(f32[5,128,128]{2,1,0:T(8,128)S(1)} %get-tuple-element.48), channel_id=1, source_target_pairs={{0,3},{1,2},{2,1},{3,0},{4,7},{5,6},{6,5},{7,4},{8,11},{9,10},{10,... | collective-permute-start | bytes 983048 | tf_op jit(solution)/shard_map/ppermute | solution.py:389
  84.1 10.8 %collective-permute-done.11.refs_7_ = f32[5,128,128]{2,1,0:T(8,128)S(1)} collective-permute-done((f32[5,128,128]{2,1,0:T(8,128)S(1)}, f32[5,128,128]{2,1,0:T(8,128)S(1)}, u32[]{:S(2)}, u32[]{:S(2)}) %collective-permute-start.11) | collective-permute-done | bytes 327712 | tf_op jit(solution)/shard_map/ppermute | solution.py:389
  95.0 0.0 all-to-all-done.1
  95.0 0.0 copy-done.9
  95.0 0.0 copy-done.10
  95.1 0.7 copy-done.13
  95.7 0.1 copy-done
  95.8 3.5 %shard_map.69 = (f32[5,128,128]{2,1,0:T(8,128)}, f32[5,128,128]{2,1,0:T(8,128)}) custom-call(s32[1]{0:T(128)} %bitcast.7.rank_ref, f32[512,128]{1,0:T(8,128)} %bitcast.27, f32[5,128,128]{2,1,0:T(8,128)} %get-tuple-element.41.refs_0_, f32[5,128,128]{2,1,0:T(8,128)} %copy-done.11, f32[5,128,128]{2,1,0:T(8,128)} %copy-done.10, f32[5,128,128]{2,1,0:T(8,128)} %copy-done.12, ...), custom_call_target="tpu_custom_call" | custom-call | flops 671088640 | bytes 2883584 | tf_op jit(solution)/shard_map/pallas_call | solution.py:191
  99.3 1.0 collective-permute-start.12
  100.4 0.9 collective-permute-start.16
  101.3 1.1 collective-permute-start.13
  102.4 1.0 collective-permute-start.15
  103.4 6.8 %collective-permute-done.12.refs_5_ = f32[5,128,128]{2,1,0:T(8,128)S(1)} collective-permute-done((f32[5,128,128]{2,1,0:T(8,128)}, f32[5,128,128]{2,1,0:T(8,128)S(1)}, u32[]{:S(2)}, u32[]{:S(2)}) %collective-permute-start.12) | collective-permute-done | bytes 327712 | tf_op jit(solution)/shard_map/ppermute | solution.py:389
  110.2 0.9 collective-permute-start.14
  111.1 0.2 collective-permute-done.16.refs_10_
  111.2 1.0 collective-permute-start.17
  112.2 8.9 %shard_map.70 = (f32[160,128]{1,0:T(8,128)}, f32[128,128]{1,0:T(8,128)}) custom-call(s32[1]{0:T(128)} %bitcast.7.rank_ref, f32[512,128]{1,0:T(8,128)} %bitcast.26, f32[512,128]{1,0:T(8,128)} %bitcast.28), custom_call_target="tpu_custom_call" | custom-call | flops 67108864 | bytes 1048576 | tf_op jit(solution)/shard_map/pallas_call | solution.py:354
  121.2 0.0 collective-permute-done.13.refs_6_
  121.2 0.0 collective-permute-done.15.refs_9_
  121.2 2.6 %collective-permute-done.14.refs_7_ = f32[5,128,128]{2,1,0:T(8,128)S(1)} collective-permute-done((f32[5,128,128]{2,1,0:T(8,128)S(1)}, f32[5,128,128]{2,1,0:T(8,128)S(1)}, u32[]{:S(2)}, u32[]{:S(2)}) %collective-permute-start.14) | collective-permute-done | bytes 327712 | tf_op jit(solution)/shard_map/ppermute | solution.py:389
  123.8 0.0 collective-permute-done.17.refs_11_
  123.8 0.7 copy-done.6
  124.5 0.1 copy-done.7
  124.6 10.6 %shard_map.72 = (f32[768,128]{1,0:T(8,128)}, f32[1280,128]{1,0:T(8,128)}) custom-call(s32[1]{0:T(128)} %bitcast.7.rank_ref, f32[160,128]{1,0:T(8,128)} %get-tuple-element.54.weight_ref, f32[5120,512]{1,0:T(8,128)} %bitcast.16, f32[5120,512]{1,0:T(8,128)} %bitcast.17, f32[5120,512]{1,0:T(8,128)} %bitcast.18, f32[5120,512]{1,0:T(8,128)} %bitcast.19, ...), custom_call_target="tpu_custom_call" | custom-call | flops 2684354560 | bytes 13107200 | tf_op jit(solution)/shard_map/pallas_call | solution.py:245
  135.2 17.9 %all_to_all.20 = f32[32,24,128]{2,1,0:T(8,128)S(1)} all-to-all(f32[32,24,128]{2,1,0:T(8,128)} %bitcast.30), channel_id=1, replica_groups=mesh['cuts'=8,'rank'=4] {'cuts','rank'}, dimensions={0} | all-to-all | bytes 786432 | tf_op jit(solution)/shard_map/all_to_all | solution.py:393
  153.1 0.8 broadcast_in_dim.5
  153.9 2.8 %all-to-all-start.3 = ((f32[32,24,128]{2,1,0:T(8,128)}), f32[32,24,128]{2,1,0:T(8,128)S(1)}, u32[]{:S(2)}, u32[]{:S(2)}) async-start(f32[32,24,128]{2,1,0:T(8,128)} %broadcast_in_dim.5), calls=%async_computation.3 | async-start | bytes 786432 | tf_op jit(solution)/shard_map/all_to_all | solution.py:393
  156.7 5.4 %shard_map.71 = f32[5120,128]{1,0:T(8,128)} custom-call(f32[5120,128]{1,0:T(8,128)} %get-tuple-element.35.rows_ref, f32[128,128]{1,0:T(8,128)} %get-tuple-element.53.weight_ref), custom_call_target="tpu_custom_call" | custom-call | flops 671088640 | bytes 5242880 | tf_op jit(solution)/shard_map/pallas_call | solution.py:274
  162.1 8.0 %all-to-all-done.3 = f32[32,24,128]{2,1,0:T(8,128)S(1)} async-done(((f32[32,24,128]{2,1,0:T(8,128)}), f32[32,24,128]{2,1,0:T(8,128)S(1)}, u32[]{:S(2)}, u32[]{:S(2)}) %all-to-all-start.3) | async-done | bytes 393248 | tf_op jit(solution)/shard_map/all_to_all | solution.py:393
  170.1 0.8 copy-done.1
  170.9 9.3 %shard_map.73 = (f32[128,512]{1,0:T(8,128)}, f32[1280,128]{1,0:T(8,128)}) custom-call(f32[768,128]{1,0:T(8,128)} %bitcast.29, f32[1280,128]{1,0:T(8,128)} %get-tuple-element.58.middle_ref), custom_call_target="tpu_custom_call" | custom-call | flops 167772160 | bytes 1310720 | tf_op jit(solution)/shard_map/pallas_call | solution.py:377
  (26 shorter events, 0.2 us)
Async XLA Ops:
  12.1 1.6 collective-permute-start
  14.5 5.4 %collective-permute-start.1 = (f32[128,128]{1,0:T(8,128)S(1)}, f32[128,128]{1,0:T(8,128)S(1)}, u32[]{:S(2)}, u32[]{:S(2)}) collective-permute-start(f32[128,128]{1,0:T(8,128)S(1)} %add.63), channel_id=1, source_target_pairs={{0,8},{4,12},{8,0},{12,4},{16,24},{20,28},{24,16},{28,20},{1,9},{5... | collective-permute-start | bytes 196616 | tf_op jit(solution)/shard_map/ppermute | solution.py:389
  19.9 5.3 %collective-permute-start.2 = (f32[128,128]{1,0:T(8,128)S(1)}, f32[128,128]{1,0:T(8,128)S(1)}, u32[]{:S(2)}, u32[]{:S(2)}) collective-permute-start(f32[128,128]{1,0:T(8,128)S(1)} %add.64), channel_id=1, source_target_pairs={{0,16},{4,20},{8,24},{12,28},{16,0},{20,4},{24,8},{28,12},{1,17},{... | collective-permute-start | bytes 196616 | tf_op jit(solution)/shard_map/ppermute | solution.py:389
  25.3 4.3 %collective-permute-start.3 = (f32[128,128]{1,0:T(8,128)S(1)}, f32[128,128]{1,0:T(8,128)S(1)}, u32[]{:S(2)}, u32[]{:S(2)}) collective-permute-start(f32[128,128]{1,0:T(8,128)S(1)} %add.65), channel_id=1, source_target_pairs={{0,1},{1,0},{2,3},{3,2},{4,5},{5,4},{6,7},{7,6},{8,9},{9,8},{10,11... | collective-permute-start | bytes 196616 | tf_op jit(solution)/shard_map/ppermute | solution.py:389
  27.0 4.3 %collective-permute-start.4 = (f32[128,128]{1,0:T(8,128)S(1)}, f32[128,128]{1,0:T(8,128)S(1)}, u32[]{:S(2)}, u32[]{:S(2)}) collective-permute-start(f32[128,128]{1,0:T(8,128)S(1)} %add.65), channel_id=1, source_target_pairs={{0,2},{1,3},{2,0},{3,1},{4,6},{5,7},{6,4},{7,5},{8,10},{9,11},{10,... | collective-permute-start | bytes 196616 | tf_op jit(solution)/shard_map/ppermute | solution.py:389
  29.6 4.3 %collective-permute-start.5 = (f32[128,128]{1,0:T(8,128)S(1)}, f32[128,128]{1,0:T(8,128)S(1)}, u32[]{:S(2)}, u32[]{:S(2)}) collective-permute-start(f32[128,128]{1,0:T(8,128)S(1)} %collective-permute-done.3), channel_id=1, source_target_pairs={{0,2},{1,3},{2,0},{3,1},{4,6},{5,7},{6,4},{7,5},{8,10},{9,11},{10,... | collective-permute-start | bytes 196616 | tf_op jit(solution)/shard_map/ppermute | solution.py:389
  37.9 18.4 %collective-permute-start.9 = (f32[5,128,128]{2,1,0:T(8,128)S(1)}, f32[5,128,128]{2,1,0:T(8,128)S(1)}, u32[]{:S(2)}, u32[]{:S(2)}) collective-permute-start(f32[5,128,128]{2,1,0:T(8,128)S(1)} %get-tuple-element.63), channel_id=1, source_target_pairs={{0,2},{1,3},{2,0},{3,1},{4,6},{5,7},{6,4},{7,5},{8,10},{9,11},{10,... | collective-permute-start | bytes 983048 | tf_op jit(solution)/shard_map/ppermute | solution.py:389
  39.6 16.7 %collective-permute-start.8 = (f32[5,128,128]{2,1,0:T(8,128)S(1)}, f32[5,128,128]{2,1,0:T(8,128)S(1)}, u32[]{:S(2)}, u32[]{:S(2)}) collective-permute-start(f32[5,128,128]{2,1,0:T(8,128)S(1)} %get-tuple-element.64), channel_id=1, source_target_pairs={{0,1},{1,0},{2,3},{3,2},{4,5},{5,4},{6,7},{7,6},{8,9},{9,8},{10,11... | collective-permute-start | bytes 983048 | tf_op jit(solution)/shard_map/ppermute | solution.py:389
  41.1 15.2 %collective-permute-start.7 = (f32[5,128,128]{2,1,0:T(8,128)S(1)}, f32[5,128,128]{2,1,0:T(8,128)S(1)}, u32[]{:S(2)}, u32[]{:S(2)}) collective-permute-start(f32[5,128,128]{2,1,0:T(8,128)S(1)} %get-tuple-element.66), channel_id=1, source_target_pairs={{0,2},{1,3},{2,0},{3,1},{4,6},{5,7},{6,4},{7,5},{8,10},{9,11},{10,... | collective-permute-start | bytes 983048 | tf_op jit(solution)/shard_map/ppermute | solution.py:389
  41.6 14.8 %collective-permute-start.6 = (f32[5,128,128]{2,1,0:T(8,128)S(1)}, f32[5,128,128]{2,1,0:T(8,128)S(1)}, u32[]{:S(2)}, u32[]{:S(2)}) collective-permute-start(f32[5,128,128]{2,1,0:T(8,128)S(1)} %get-tuple-element.67), channel_id=1, source_target_pairs={{0,1},{1,0},{2,3},{3,2},{4,5},{5,4},{6,7},{7,6},{8,9},{9,8},{10,11... | collective-permute-start | bytes 983048 | tf_op jit(solution)/shard_map/ppermute | solution.py:389
  56.3 38.7 %copy-start.8 = (f32[5,128,128]{2,1,0:T(8,128)}, f32[5,128,128]{2,1,0:T(8,128)S(1)}, u32[]{:S(2)}) copy-start(f32[5,128,128]{2,1,0:T(8,128)S(1)} %collective-permute-done.9.refs_6_) | copy-start | bytes 983044
  56.3 38.7 %copy-start.9 = (f32[5,128,128]{2,1,0:T(8,128)}, f32[5,128,128]{2,1,0:T(8,128)S(1)}, u32[]{:S(2)}) copy-start(f32[5,128,128]{2,1,0:T(8,128)S(1)} %collective-permute-done.8.refs_5_) | copy-start | bytes 983044
  56.4 38.7 %copy-start.10 = (f32[5,128,128]{2,1,0:T(8,128)}, f32[5,128,128]{2,1,0:T(8,128)S(1)}, u32[]{:S(2)}) copy-start(f32[5,128,128]{2,1,0:T(8,128)S(1)} %collective-permute-done.7.refs_2_) | copy-start | bytes 983044
  56.4 38.6 %copy-start.11 = (f32[5,128,128]{2,1,0:T(8,128)}, f32[5,128,128]{2,1,0:T(8,128)S(1)}, u32[]{:S(2)}) copy-start(f32[5,128,128]{2,1,0:T(8,128)S(1)} %collective-permute-done.6.refs_1_) | copy-start | bytes 983044
  56.4 17.7 %all-to-all-start = ((f32[32,16,128]{2,1,0:T(8,128)}), f32[32,16,128]{2,1,0:T(8,128)S(1)}, u32[]{:S(2)}, u32[]{:S(2)}) async-start(f32[32,16,128]{2,1,0:T(8,128)} %bitcast.31), calls=%async_computation | async-start | bytes 524288 | tf_op jit(solution)/shard_map/all_to_all | solution.py:393
  63.0 13.6 %collective-permute-start.10 = (f32[5,128,128]{2,1,0:T(8,128)S(1)}, f32[5,128,128]{2,1,0:T(8,128)S(1)}, u32[]{:S(2)}, u32[]{:S(2)}) collective-permute-start(f32[5,128,128]{2,1,0:T(8,128)S(1)} %get-tuple-element.39), channel_id=1, source_target_pairs={{0,3},{1,2},{2,1},{3,0},{4,7},{5,6},{6,5},{7,4},{8,11},{9,10},{10,... | collective-permute-start | bytes 983048 | tf_op jit(solution)/shard_map/ppermute | solution.py:389
  76.6 18.4 %copy-start.12 = (f32[5,128,128]{2,1,0:T(8,128)}, f32[5,128,128]{2,1,0:T(8,128)S(1)}, u32[]{:S(2)}) copy-start(f32[5,128,128]{2,1,0:T(8,128)S(1)} %collective-permute-done.10.refs_3_) | copy-start | bytes 983044
  77.4 17.6 %all-to-all-start.1 = ((f32[32,16,128]{2,1,0:T(8,128)}), f32[32,16,128]{2,1,0:T(8,128)S(1)}, u32[]{:S(2)}, u32[]{:S(2)}) async-start(f32[32,16,128]{2,1,0:T(8,128)} %broadcast_in_dim.4), calls=%async_computation.1 | async-start | bytes 524288 | tf_op jit(solution)/shard_map/all_to_all | solution.py:393
  81.6 13.4 %collective-permute-start.11 = (f32[5,128,128]{2,1,0:T(8,128)S(1)}, f32[5,128,128]{2,1,0:T(8,128)S(1)}, u32[]{:S(2)}, u32[]{:S(2)}) collective-permute-start(f32[5,128,128]{2,1,0:T(8,128)S(1)} %get-tuple-element.48), channel_id=1, source_target_pairs={{0,3},{1,2},{2,1},{3,0},{4,7},{5,6},{6,5},{7,4},{8,11},{9,10},{10,... | collective-permute-start | bytes 983048 | tf_op jit(solution)/shard_map/ppermute | solution.py:389
  95.0 0.7 copy-start.13
  95.0 0.8 copy-start
  99.3 10.8 %collective-permute-start.12 = (f32[5,128,128]{2,1,0:T(8,128)}, f32[5,128,128]{2,1,0:T(8,128)S(1)}, u32[]{:S(2)}, u32[]{:S(2)}) collective-permute-start(f32[5,128,128]{2,1,0:T(8,128)} %get-tuple-element.55.refs_4_), channel_id=1, source_target_pairs={{0,1},{1,0},{2,3},{3,2},{4,5},{5,4},{6,7},{7,6},{8,9},{9,8},{10,11... | collective-permute-start | bytes 983048 | tf_op jit(solution)/shard_map/ppermute | solution.py:389
  100.4 10.9 %collective-permute-start.16 = (f32[5,128,128]{2,1,0:T(8,128)}, f32[5,128,128]{2,1,0:T(8,128)S(1)}, u32[]{:S(2)}, u32[]{:S(2)}) collective-permute-start(f32[5,128,128]{2,1,0:T(8,128)} %get-tuple-element.56.refs_8_), channel_id=1, source_target_pairs={{0,2},{1,3},{2,0},{3,1},{4,6},{5,7},{6,4},{7,5},{8,10},{9,11},{10,... | collective-permute-start | bytes 983048 | tf_op jit(solution)/shard_map/ppermute | solution.py:389
  101.3 19.9 %collective-permute-start.13 = (f32[5,128,128]{2,1,0:T(8,128)}, f32[5,128,128]{2,1,0:T(8,128)S(1)}, u32[]{:S(2)}, u32[]{:S(2)}) collective-permute-start(f32[5,128,128]{2,1,0:T(8,128)} %get-tuple-element.55.refs_4_), channel_id=1, source_target_pairs={{0,2},{1,3},{2,0},{3,1},{4,6},{5,7},{6,4},{7,5},{8,10},{9,11},{10,... | collective-permute-start | bytes 983048 | tf_op jit(solution)/shard_map/ppermute | solution.py:389
  102.4 18.8 %collective-permute-start.15 = (f32[5,128,128]{2,1,0:T(8,128)}, f32[5,128,128]{2,1,0:T(8,128)S(1)}, u32[]{:S(2)}, u32[]{:S(2)}) collective-permute-start(f32[5,128,128]{2,1,0:T(8,128)} %get-tuple-element.56.refs_8_), channel_id=1, source_target_pairs={{0,1},{1,0},{2,3},{3,2},{4,5},{5,4},{6,7},{7,6},{8,9},{9,8},{10,11... | collective-permute-start | bytes 983048 | tf_op jit(solution)/shard_map/ppermute | solution.py:389
  110.2 13.6 %copy-start.2 = (f32[5,128,128]{2,1,0:T(8,128)}, f32[5,128,128]{2,1,0:T(8,128)S(1)}, u32[]{:S(2)}) copy-start(f32[5,128,128]{2,1,0:T(8,128)S(1)} %collective-permute-done.12.refs_5_) | copy-start | bytes 983044
  110.2 13.6 %collective-permute-start.14 = (f32[5,128,128]{2,1,0:T(8,128)S(1)}, f32[5,128,128]{2,1,0:T(8,128)S(1)}, u32[]{:S(2)}, u32[]{:S(2)}) collective-permute-start(f32[5,128,128]{2,1,0:T(8,128)S(1)} %collective-permute-done.12.refs_5_), channel_id=1, source_target_pairs={{0,2},{1,3},{2,0},{3,1},{4,6},{5,7},{6,4},{7,5},{8,10},{9,11},{10,... | collective-permute-start | bytes 983048 | tf_op jit(solution)/shard_map/ppermute | solution.py:389
  111.2 12.5 %copy-start.3 = (f32[5,128,128]{2,1,0:T(8,128)}, f32[5,128,128]{2,1,0:T(8,128)S(1)}, u32[]{:S(2)}) copy-start(f32[5,128,128]{2,1,0:T(8,128)S(1)} %collective-permute-done.16.refs_10_) | copy-start | bytes 983044
  111.2 12.5 %collective-permute-start.17 = (f32[5,128,128]{2,1,0:T(8,128)S(1)}, f32[5,128,128]{2,1,0:T(8,128)S(1)}, u32[]{:S(2)}, u32[]{:S(2)}) collective-permute-start(f32[5,128,128]{2,1,0:T(8,128)S(1)} %collective-permute-done.16.refs_10_), channel_id=1, source_target_pairs={{0,1},{1,0},{2,3},{3,2},{4,5},{5,4},{6,7},{7,6},{8,9},{9,8},{10,11... | collective-permute-start | bytes 983048 | tf_op jit(solution)/shard_map/ppermute | solution.py:389
  121.2 2.6 %copy-start.4 = (f32[5,128,128]{2,1,0:T(8,128)}, f32[5,128,128]{2,1,0:T(8,128)S(1)}, u32[]{:S(2)}) copy-start(f32[5,128,128]{2,1,0:T(8,128)S(1)} %collective-permute-done.13.refs_6_) | copy-start | bytes 983044
  121.2 2.6 %copy-start.5 = (f32[5,128,128]{2,1,0:T(8,128)}, f32[5,128,128]{2,1,0:T(8,128)S(1)}, u32[]{:S(2)}) copy-start(f32[5,128,128]{2,1,0:T(8,128)S(1)} %collective-permute-done.15.refs_9_) | copy-start | bytes 983044
  123.8 0.7 copy-start.6
  123.8 0.8 copy-start.7
  153.9 16.2 %all-to-all-start.3 = ((f32[32,24,128]{2,1,0:T(8,128)}), f32[32,24,128]{2,1,0:T(8,128)S(1)}, u32[]{:S(2)}, u32[]{:S(2)}) async-start(f32[32,24,128]{2,1,0:T(8,128)} %broadcast_in_dim.5), calls=%async_computation.3 | async-start | bytes 786432 | tf_op jit(solution)/shard_map/all_to_all | solution.py:393
  170.1 0.8 copy-start.1

commit v4 on v2

--- a/solution.py
+++ b/solution.py
@@ -13,6 +13,18 @@
 TN = (((0,), (0,)), ((), ()))
 VMEM_LIMIT = 56 * 1024 * 1024
 BLOCK = 8
+
+
+PARTS = 4
+
+
+def tiles(block, width):
+    size = block // PARTS
+    return [pl.BlockSpec((size, width), lambda i, q=q: (i * PARTS + q, 0)) for q in range(PARTS)]
+
+
+def joined_rows(refs):
+    return jnp.concatenate([ref[...] for ref in refs], axis=0)
 
 
 def call(kernel, flops, size, **more):
@@ -58,11 +70,13 @@
     return ref.reshape(ref.shape[0] * ref.shape[1], ref.shape[2])
 
 
-def sketch_kernel(core_ref, right_ref, left_ref, sketched_ref, part_ref, rows_ref):
-    local_rows, block, _ = core_ref.shape
+def sketch_kernel(*refs):
+    core_refs, (right_ref, left_ref, sketched_ref, part_ref, rows_ref) = refs[:PARTS], refs[PARTS:]
+    block = left_ref.shape[1]
+    local_rows = rows_ref.shape[0] // block
     columns = right_ref.shape[1]
     right = twice(both_parts(right_ref[...], 1), 0)
-    rows_ref[...] = fold(mxu(both_parts(rows_of(core_ref)[...], 1), right, NN), 1)
+    rows_ref[...] = fold(mxu(both_parts(jnp.concatenate([rows_of(ref)[...] for ref in core_refs], axis=0), 1), right, NN), 1)
     left_rows = rows_of(left_ref)
 
     @pl.when(pl.program_id(0) == 0)
@@ -89,7 +103,7 @@
         4 * (core_two.size + 2 * sketch_core.size),
         grid=(slices // BLOCK,),
         in_specs=[
-            pl.BlockSpec((local_rows, BLOCK, width), lambda i: (0, i, 0)),
+            *[pl.BlockSpec((local_rows // PARTS, BLOCK, width), lambda i, q=q: (q, i, 0)) for q in range(PARTS)],
             pl.BlockSpec((width, columns), lambda i: (0, 0)),
             pl.BlockSpec((columns, BLOCK, columns), lambda i: (0, i, 0)),
         ],
@@ -99,7 +113,7 @@
         ],
         out_shape=[shape(slices, local_rows, columns), shape(local_rows, columns)],
         scratch_shapes=[pltpu.VMEM((local_rows * BLOCK, columns), jnp.float32)],
-    )(core_two, right_sketch, sketch_core)
+    )(*[core_two] * PARTS, right_sketch, sketch_core)
 
 
 def block_of(rows):
@@ -109,7 +123,7 @@
     return block
 
 
-def square_kernel(core_ref, core_index_ref, keep_ref, give_ref, sum_ref):
+def square_kernel(core_ref, square_ref, sum_ref):
     step = pl.program_id(0)
     width = core_ref.shape[1]
     high, low = split(core_ref[...])
@@ -123,69 +137,57 @@
     @pl.when(step == pl.num_programs(0) - 1)
     def _():
         cross = sum_ref[:, width:]
-        sum_ref[:, :width] = sum_ref[:, :width] + cross + cross.T
-        half = width // 2
-        own = core_index_ref[0]
-        keep_ref[...] = sum_ref[pl.ds(pl.multiple_of(own * half, half), half), :width]
-        give_ref[...] = sum_ref[pl.ds(pl.multiple_of((1 - own) * half, half), half), :width]
-
-
-def square_of(flat_one, core_index):
+        square_ref[...] = sum_ref[:, :width] + cross + cross.T
+
+
+def square_of(flat_one):
     rows, width = flat_one.shape
     block = block_of(rows)
-    half = pl.BlockSpec((width // 2, width), lambda i: (0, 0))
     return call(
         square_kernel,
         4 * rows * width * width,
         4 * flat_one.size,
         grid=(rows // block,),
-        in_specs=[
-            pl.BlockSpec((block, width), lambda i: (i, 0)),
-            pl.BlockSpec(memory_space=pltpu.SMEM),
-        ],
-        out_specs=[half, half],
-        out_shape=[shape(width // 2, width)] * 2,
+        in_specs=[pl.BlockSpec((block, width), lambda i: (i, 0))],
+        out_specs=pl.BlockSpec((width, width), lambda i: (0, 0)),
+        out_shape=shape(width, width),
         scratch_shapes=[pltpu.VMEM((width, 2 * width), jnp.float32)],
-    )(flat_one, core_index)
-
-
-def loose_kernel(halves, rank_ref, raw_ref, *refs):
-    piece_refs, out_refs = refs[:-len(halves)], refs[-len(halves):]
-    ranks = len(piece_refs) // len(halves)
-    local_rows = piece_refs[0].shape[1]
+    )(flat_one)
+
+
+def loose_kernel(rank_ref, raw_ref, *refs):
+    piece_refs, out_ref = refs[:-1], refs[-1]
+    count, local_rows, columns = piece_refs[0].shape
     rows = []
-    for offset in range(ranks):
+    for offset in range(len(piece_refs)):
         start = pl.multiple_of((rank_ref[0] ^ offset) * local_rows, local_rows)
         rows.append(raw_ref[pl.ds(start, local_rows), :])
     raw = twice(both_parts(jnp.concatenate(rows, axis=0), 1).T, 1)
-    columns = raw_ref.shape[1]
-    for half, count in enumerate(halves):
-        refs = piece_refs[half * ranks:(half + 1) * ranks]
-        value = [jnp.concatenate([ref[n] for n in range(count)], axis=1) for ref in refs]
-        product = fold(mxu(raw, both_parts(jnp.concatenate(value, axis=0), 0), NN), 0)
-        for n in range(count):
-            out_refs[half][n] = product[:, n * columns:(n + 1) * columns]
-
-
-def loosen(rank_index, raw, pieces, halves):
+    value = [jnp.concatenate([ref[n] for n in range(count)], axis=1) for ref in piece_refs]
+    product = fold(mxu(raw, both_parts(jnp.concatenate(value, axis=0), 0), NN), 0)
+    for n in range(count):
+        out_ref[n] = product[:, n * columns:(n + 1) * columns]
+
+
+def loosen(rank_index, raw, pieces):
     columns = raw.shape[1]
-    size = sum(piece.size for piece in pieces)
+    size = len(pieces) * pieces[0].size
     whole = pl.BlockSpec(memory_space=pltpu.VMEM)
     return call(
-        functools.partial(loose_kernel, halves),
+        loose_kernel,
         8 * size * columns,
         4 * raw.size + 4 * size,
         in_specs=[pl.BlockSpec(memory_space=pltpu.SMEM)] + [whole] * (len(pieces) + 1),
-        out_specs=[whole] * len(halves),
-        out_shape=[shape(count, columns, columns) for count in halves],
+        out_specs=whole,
+        out_shape=shape(pieces[0].shape[0], columns, columns),
     )(rank_index, raw, *pieces)
 
 
-def carry_kernel(halves, share, rank_ref, weight_ref, core_ref, *refs):
-    piece_refs = refs[:-4]
+def carry_kernel(halves, share, rank_ref, weight_ref, *refs):
+    core_refs, piece_refs = refs[:PARTS], refs[PARTS:-4]
     joined_ref, middle_ref, rows_ref, sum_ref = refs[-4:]
     step = pl.program_id(0)
-    block, width = core_ref.shape
+    block, width = core_refs[0].shape[0] * PARTS, core_refs[0].shape[1]
     columns = weight_ref.shape[1]
     ranks = len(piece_refs) // len(halves)
     room = share * ranks
@@ -208,7 +210,7 @@
                     middle_ref[pl.ds(first + n, band, stride=room), :] = piece[local_rows:]
 
     rows = both_parts(rows_ref[pl.ds(pl.multiple_of(step * block, block), block), :], 1).T
-    product = fold(mxu(twice(rows, 1), both_parts(core_ref[...], 0), NN), 0)
+    product = fold(mxu(twice(rows, 1), both_parts(joined_rows(core_refs), 0), NN), 0)
     sum_ref[...] += product
 
     @pl.when(step == pl.num_programs(0) - 1)
@@ -233,7 +235,7 @@
         in_specs=[
             pl.BlockSpec(memory_space=pltpu.SMEM),
             pl.BlockSpec((weight.shape[0], columns), lambda i: (0, 0)),
-            pl.BlockSpec((block, width), lambda i: (i, 0)),
+            *tiles(block, width),
         ]
         + [pl.BlockSpec(piece.shape, lambda i: (0, 0, 0)) for piece in pieces],
         out_specs=[
@@ -242,7 +244,7 @@
         ],
         out_shape=[shape(total, columns), shape(band * share * ranks, columns)],
         scratch_shapes=[pltpu.VMEM((rows, columns), jnp.float32), pltpu.VMEM((columns, width), jnp.float32)],
-    )(rank_index, weight, flat_two, *pieces)
+    )(rank_index, weight, *[flat_two] * PARTS, *pieces)
 
 
 def apply_kernel(rows_ref, weight_ref, out_ref):
@@ -375,8 +377,8 @@
     return lax.ppermute(value, axis, [(i, i ^ offset) for i in range(lax.axis_size(axis))])
 
 
-def exchange(value, axes, groups=None):
-    return lax.all_to_all(value, axes, 0, 0, axis_index_groups=groups, tiled=True)
+def exchange(value, axes):
+    return lax.all_to_all(value, axes, 0, 0, tiled=True)
 
 
 def gather_all(value, axes):
@@ -392,18 +394,14 @@
     local_rows, slices, width = core_one.shape
     columns = right_sketch.shape[1]
     ranks, cuts = lax.axis_size("rank"), lax.axis_size("cuts")
-    rank, cut = lax.axis_index("rank"), lax.axis_index("cuts")
+    rank = lax.axis_index("rank")
     rank_index = rank.astype(jnp.int32).reshape(1)
-    core_index = lax.rem(cut, 2).astype(jnp.int32).reshape(1)
     both = ("cuts", "rank")
     parts = ranks * cuts
     band = columns // ranks
     share = -(-slices // ranks)
     room = share * ranks
     halves = [share // 2, share - share // 2]
-    core_groups = [
-        [z * ranks + place for z in range(core, cuts, 2) for place in range(ranks)] for core in range(2)
-    ]
     filler = ((0, 0), (0, room - slices), (0, 0))
     core_two, sketch_core = jnp.pad(core_two, filler), jnp.pad(sketch_core, filler)
     flat_one = core_one.reshape(local_rows * slices, width)
@@ -423,32 +421,27 @@
     far = ranks - 1
     near = [[(half, offset) for offset in range(1, far)] for half in range(2)]
 
-    moved = send(near[0], sketched, None)
+    bits = [1 << bit for bit in range((ranks - 1).bit_length())]
+    moved = send(near[0] + near[1], sketched, None)
     bridge_rows = jnp.sum(exchange(part.reshape(cuts, local_rows // cuts, columns), "cuts"), axis=0)
     flat_late, part = after(flat_one, part)
-    keep, give = square_of(flat_late, core_index)
-    bridge_rows, pieces = after(bridge_rows, moved)
+    square = square_of(flat_late)
+    bridge_rows, (pieces, square) = after(bridge_rows, (moved, square))
     sketched, bridge_rows = after(sketched, bridge_rows)
     pieces.update(send([(0, 0), (1, 0)], sketched, None))
-
     bridge = gather_all(bridge_rows, both)
     bridge = bridge.reshape(cuts, ranks, -1, columns).swapaxes(0, 1).reshape(width, columns)
-    square = keep + swap(give, "cuts", 1)
-    moved = send(near[1] + [(0, far)], sketched, square)
-    square = exchange(square.reshape(parts // 2, -1, width), both, core_groups)
-    raw_rows = exact(jnp.sum(square, axis=0), bridge, NN)
-    raw_rows, moved = after(raw_rows, moved)
-    pieces.update(moved)
-
-    pieces.update(send([(1, far)], sketched, raw_rows))
-    raw = gather_all(raw_rows, both).reshape(cuts // 2, 2, ranks, -1, columns)
-    raw = raw.transpose(1, 0, 2, 3, 4).reshape(width, columns)
-
-    ordered = [pieces[(half, offset)] for half in range(2) for offset in range(ranks)]
-    loose = loosen(rank_index, raw, ordered, halves)
-    loose, (bridge, raw) = after(loose, (bridge, raw))
-
-    bits = [1 << bit for bit in range((ranks - 1).bit_length())]
+
+    raw = exact(square, bridge, NN)
+    far_piece = send([(0, far)], sketched, raw)
+    raw = jnp.sum(exchange(raw.reshape(parts, -1, columns), both), axis=0)
+    raw, far_piece = after(raw, far_piece)
+    pieces.update(far_piece)
+    pieces.update(send([(1, far)], sketched, raw))
+    raw = gather_all(raw, both).reshape(width, columns)
+
+    loose = [loosen(rank_index, raw, [pieces[(half, offset)] for offset in range(ranks)]) for half in range(2)]
+    loose[1], (bridge, raw) = after(loose[1], (bridge, raw))
     everyone = []
     for value, order in zip(loose, (bits, bits[::-1])):
         found = {0: value}

time: 182 us -> 177 us (0.973)
  waiting for transfers between devices: 50.5 us -> 35 us
  blocking collectives: 17.9 us -> 32.1 us
  starting transfers between devices: 37.3 us -> 32.1 us
  matrix products: 0.24 us -> 3.01 us
  Pallas kernels: 63.1 us -> 65.5 us
  other arithmetic: 2 us -> 0.09 us
    all_to_all x1 -> x2, blocking collectives: 17.9 us -> 32.1 us  [exchange(): return lax.all_to_all(value, axes, 0, 0, tiled=True)]
    all_to_all x5 -> x4, waiting for transfers between devices: 32.1 us -> 20.7 us  [exchange(): return lax.all_to_all(value, axes, 0, 0, tiled=True)]
    ppermute x13 -> x12, waiting for transfers between devices: 18.3 us -> 14.3 us  [swap(): lax.ppermute(value, axis, [(i, i ^ offset) for i in range(lax.axis_size(a...]
    all_to_all x5 -> x4, starting transfers between devices: 20.2 us -> 16.3 us  [exchange(): return lax.all_to_all(value, axes, 0, 0, tiled=True)]
    dot_general x1, matrix products: 0.24 us -> 3.01 us  [exact(): lax.dot_general(a, b, form, precision=lax.Precision.HIGHEST, preferred_el...]
    add x1 -> x0, other arithmetic: 1.92 us -> none  [on_device(): square = keep + swap(give, 'cuts', 1)]
    pallas_call x1 -> x2, Pallas kernels: 3.49 us -> 5.36 us  [loosen(): call(loose_kernel, 8 * size * columns, 4 * raw.size + 4 * size, in_specs=...]
    ppermute x13 -> x12, starting transfers between devices: 17.1 us -> 15.8 us  [swap(): lax.ppermute(value, axis, [(i, i ^ offset) for i in range(lax.axis_size(a...]
  transfers between devices with their start and end apart: 18 -> 16, of which waited for: 9 -> 9; matrix products, arithmetic and copies ran while one was open for 3% -> 2% of each run, Pallas kernels for 16% -> 19%
where the time goes in v4:
time: 177 us; the launch traced here: 176 us
  Pallas kernels  65.5 us (37%)
  waiting for transfers between devices  35 us (20%)
  starting transfers between devices  32.1 us (18%)
  blocking collectives  32.1 us (18%)
  local copies, waits for them, and re-layouts  7.79 us (4%)
  matrix products  3.01 us (2%)
    all_to_all x2, blocking collectives, exchange(): return lax.all_to_all(value, axes, 0, 0, tiled=True)  32.1 us
    all_to_all x4, waiting for transfers between devices, exchange(): return lax.all_to_all(value, axes, 0, 0, tiled=True)  20.7 us
    all_to_all x4, starting transfers between devices, exchange(): return lax.all_to_all(value, axes, 0, 0, tiled=True)  16.3 us
    ppermute x12, starting transfers between devices, swap(): lax.ppermute(value, axis, [(i, i ^ offset) for i in range(lax.axis_size(a...  15.8 us
    ppermute x12, waiting for transfers between devices, swap(): lax.ppermute(value, axis, [(i, i ^ offset) for i in range(lax.axis_size(a...  14.3 us
    pallas_call x1, Pallas kernels, sketch(): call(sketch_kernel, 2 * core_two.size * columns * 4, 4 * (core_two.size +...  11.5 us
    pallas_call x1, Pallas kernels, square_of(): call(square_kernel, 4 * rows * width * width, 4 * flat_one.size, grid=(ro...  11 us
    pallas_call x1, Pallas kernels, carry_rows(): call(functools.partial(carry_kernel, halves, share), 8 * flat_two.size *...  10.6 us
  transfers between devices with their start and end apart: 16, of which 9 were waited for; matrix products, arithmetic and copies ran while one was open for 2% of the time, Pallas kernels for 19%

profile of v4, /device:TPU:0, one launch (start us, length us, event | category | flops | bytes accessed | tf_op | source)
XLA Modules:
  0.0 176.4 jit_solution(8143665803479243936)
XLA Ops:
  0.6 11.5 %shard_map.67 = (f32[40,128,128]{2,1,0:T(8,128)}, f32[128,128]{1,0:T(8,128)}) custom-call(f32[128,40,512]{2,1,0:T(8,128)} %refs_3_.1, f32[128,40,512]{2,1,0:T(8,128)} %refs_3_.1, f32[128,40,512]{2,1,0:T(8,128)} %refs_3_.1, f32[128,40,512]{2,1,0:T(8,128)} %refs_3_.1, f32[512,128]{1,0:T(8,128)} %refs_4_.1, f32[128,40,128]{2,1,0:T(8,128)} %refs_5_.1), custom_call_target="tpu_custom_call" | custom-call | flops 2684354560 | bytes 15728640 | tf_op jit(solution)/shard_map/pallas_call | solution.py:100
  12.1 6.3 %all-to-all-start = ((f32[8,16,128]{2,1,0:T(8,128)}), f32[8,16,128]{2,1,0:T(8,128)S(1)}, u32[]{:S(2)}, u32[]{:S(2)}) async-start(f32[8,16,128]{2,1,0:T(8,128)} %bitcast.31), calls=%async_computation | async-start | bytes 131072 | tf_op jit(solution)/shard_map/all_to_all | solution.py:381
  18.4 2.2 %constant_dynamic-slice_fusion.4 = (f32[5,128,128]{2,1,0:T(8,128)}, f32[5,128,128]{2,1,0:T(8,128)}, f32[5,128,128]{2,1,0:T(8,128)S(1)}, f32[5,128,128]{2,1,0:T(8,128)S(1)}) fusion(f32[40,128,128]{2,1,0:T(8,128)} %get-tuple-element.33, s32[]{:T(128)S(6)} %select_n.27, s32[]{:T(128)S(6)} %select_n.26, s32[]{:T(128)S(6)} %select_n.25, s32[]{:T(128)S(6)} %select_n.24), kind=kLoop, calls=%fused_computation.4 | loop fusion | bytes 2621456 | tf_op jit(solution)/shard_map/dynamic_slice | solution.py:416
  20.7 1.5 collective-permute-start.3
  22.2 1.5 collective-permute-start.2
  23.7 0.5 collective-permute-start.1
  24.2 0.5 collective-permute-start
  24.7 11.0 %shard_map.68 = f32[512,512]{1,0:T(8,128)} custom-call(f32[5120,512]{1,0:T(8,128)} %bitcast.20), custom_call_target="tpu_custom_call" | custom-call | flops 5368709120 | bytes 10485760 | tf_op jit(solution)/shard_map/pallas_call | solution.py:146
  35.8 0.0 copy-start.1
  35.8 0.0 all-to-all-done
  35.8 0.0 collective-permute-done.3.refs_2_
  35.8 0.0 collective-permute-done.2.refs_1_
  35.8 2.3 %collective-permute-done.1.refs_2_ = f32[5,128,128]{2,1,0:T(8,128)} collective-permute-done((f32[5,128,128]{2,1,0:T(8,128)S(1)}, f32[5,128,128]{2,1,0:T(8,128)}, u32[]{:S(2)}, u32[]{:S(2)}) %collective-permute-start.1) | collective-permute-done | bytes 327712 | tf_op jit(solution)/shard_map/ppermute | solution.py:377
  38.1 1.2 collective-permute-done.refs_1_
  39.4 15.5 %all_to_all.30 = f32[32,16,128]{2,1,0:T(8,128)S(1)} all-to-all(f32[32,16,128]{2,1,0:T(8,128)S(1)} %broadcast_in_dim.6), channel_id=1, replica_groups=mesh['cuts'=8,'rank'=4] {'cuts','rank'}, dimensions={0} | all-to-all | bytes 524288 | tf_op jit(solution)/shard_map/all_to_all | solution.py:381
  54.9 0.0 copy-start.2
  54.9 3.0 %fusion = f32[512,128]{1,0:T(8,128)} fusion(f32[512,512]{1,0:T(8,128)} %shard_map.68, f32[512,128]{1,0:T(8,128)S(1)} %bitcast.26), kind=kOutput, calls=%fused_computation.8 | convolution fusion | flops 402653184 | bytes 1572864 | tf_op jit(solution)/shard_map/dot_general | solution.py:53
  57.9 2.6 %all-to-all-start.2 = ((f32[32,16,128]{2,1,0:T(8,128)}), f32[32,16,128]{2,1,0:T(8,128)S(1)}, u32[]{:S(2)}, u32[]{:S(2)}) async-start(f32[32,16,128]{2,1,0:T(8,128)} %bitcast.6), calls=%async_computation.2 | async-start | bytes 524288 | tf_op jit(solution)/shard_map/all_to_all | solution.py:381
  60.5 0.0 copy-done.1
  60.6 1.0 constant_dynamic-slice_fusion
  61.5 2.6 %collective-permute-start.4 = (f32[5,128,128]{2,1,0:T(8,128)}, f32[5,128,128]{2,1,0:T(8,128)S(1)}, u32[]{:S(2)}, u32[]{:S(2)}) collective-permute-start(f32[5,128,128]{2,1,0:T(8,128)} %get-tuple-element.34), channel_id=1, source_target_pairs={{0,3},{1,2},{2,1},{3,0},{4,7},{5,6},{6,5},{7,4},{8,11},{9,10},{10,... | collective-permute-start | bytes 983048 | tf_op jit(solution)/shard_map/ppermute | solution.py:377
  64.1 7.5 %all-to-all-done.2 = f32[32,16,128]{2,1,0:T(8,128)S(1)} async-done(((f32[32,16,128]{2,1,0:T(8,128)}), f32[32,16,128]{2,1,0:T(8,128)S(1)}, u32[]{:S(2)}, u32[]{:S(2)}) %all-to-all-start.2) | async-done | bytes 262176 | tf_op jit(solution)/shard_map/all_to_all | solution.py:381
  71.6 2.8 %collective-permute-done.4.refs_3_ = f32[5,128,128]{2,1,0:T(8,128)S(1)} collective-permute-done((f32[5,128,128]{2,1,0:T(8,128)}, f32[5,128,128]{2,1,0:T(8,128)S(1)}, u32[]{:S(2)}, u32[]{:S(2)}) %collective-permute-start.4) | collective-permute-done | bytes 327712 | tf_op jit(solution)/shard_map/ppermute | solution.py:377
  74.4 0.0 copy-start.10
  74.4 0.8 broadcast_in_dim.7
  75.2 0.0 copy-done.2
  75.2 4.6 %all-to-all-start.3 = ((f32[32,16,128]{2,1,0:T(8,128)}), f32[32,16,128]{2,1,0:T(8,128)S(1)}, u32[]{:S(2)}, u32[]{:S(2)}) async-start(f32[32,16,128]{2,1,0:T(8,128)} %broadcast_in_dim.7), calls=%async_computation.3 | async-start | bytes 524288 | tf_op jit(solution)/shard_map/all_to_all | solution.py:381
  79.8 2.6 %collective-permute-start.5 = (f32[5,128,128]{2,1,0:T(8,128)S(1)}, f32[5,128,128]{2,1,0:T(8,128)S(1)}, u32[]{:S(2)}, u32[]{:S(2)}) collective-permute-start(f32[5,128,128]{2,1,0:T(8,128)S(1)} %get-tuple-element.38), channel_id=1, source_target_pairs={{0,3},{1,2},{2,1},{3,0},{4,7},{5,6},{6,5},{7,4},{8,11},{9,10},{10,... | collective-permute-start | bytes 983048 | tf_op jit(solution)/shard_map/ppermute | solution.py:377
  82.3 8.3 %all-to-all-done.3 = f32[32,16,128]{2,1,0:T(8,128)S(1)} async-done(((f32[32,16,128]{2,1,0:T(8,128)}), f32[32,16,128]{2,1,0:T(8,128)S(1)}, u32[]{:S(2)}, u32[]{:S(2)}) %all-to-all-start.3) | async-done | bytes 262176 | tf_op jit(solution)/shard_map/all_to_all | solution.py:381
  90.6 0.0 copy-start
  90.6 0.0 copy-done.10
  90.7 0.7 copy-done
  91.3 2.7 %shard_map.72.refs_4_ = f32[5,128,128]{2,1,0:T(8,128)} custom-call(s32[1]{0:T(128)} %bitcast.1.rank_ref, f32[512,128]{1,0:T(8,128)} %bitcast.22, f32[5,128,128]{2,1,0:T(8,128)} %get-tuple-element.51.refs_0_, f32[5,128,128]{2,1,0:T(8,128)} %collective-permute-done.refs_1_, f32[5,128,128]{2,1,0:T(8,128)} %collective-permute-done.1.refs_2_, ...), custom_call_target="tpu_custom_call" | custom-call | flops 335544320 | bytes 1572864 | tf_op jit(solution)/shard_map/pallas_call | solution.py:176
  94.0 0.0 collective-permute-start.6
  94.0 0.0 collective-permute-done.5.refs_3_
  94.0 0.7 copy-done.11
  94.8 2.7 %shard_map.69.refs_8_ = f32[5,128,128]{2,1,0:T(8,128)} custom-call(s32[1]{0:T(128)} %bitcast.1.rank_ref, f32[512,128]{1,0:T(8,128)} %bitcast.23, f32[5,128,128]{2,1,0:T(8,128)} %get-tuple-element.53.refs_0_, f32[5,128,128]{2,1,0:T(8,128)} %collective-permute-done.2.refs_1_, f32[5,128,128]{2,1,0:T(8,128)} %collective-permute-done.3.refs_2_, ...), custom_call_target="tpu_custom_call" | custom-call | flops 335544320 | bytes 1572864 | tf_op jit(solution)/shard_map/pallas_call | solution.py:176
  97.4 1.3 collective-permute-start.10
  98.7 0.7 collective-permute-start.7
  99.5 2.0 %collective-permute-start.9 = (f32[5,128,128]{2,1,0:T(8,128)}, f32[5,128,128]{2,1,0:T(8,128)S(1)}, u32[]{:S(2)}, u32[]{:S(2)}) collective-permute-start(f32[5,128,128]{2,1,0:T(8,128)} %shard_map.69.refs_8_), channel_id=1, source_target_pairs={{0,1},{1,0},{2,3},{3,2},{4,5},{5,4},{6,7},{7,6},{8,9},{9,8},{10,11... | collective-permute-start | bytes 983048 | tf_op jit(solution)/shard_map/ppermute | solution.py:377
  101.5 2.7 %collective-permute-done.6.refs_5_ = f32[5,128,128]{2,1,0:T(8,128)S(1)} collective-permute-done((f32[5,128,128]{2,1,0:T(8,128)}, f32[5,128,128]{2,1,0:T(8,128)S(1)}, u32[]{:S(2)}, u32[]{:S(2)}) %collective-permute-start.6) | collective-permute-done | bytes 327712 | tf_op jit(solution)/shard_map/ppermute | solution.py:377
  104.1 0.5 collective-permute-start.8
  104.6 3.6 %collective-permute-done.10.refs_10_ = f32[5,128,128]{2,1,0:T(8,128)S(1)} collective-permute-done((f32[5,128,128]{2,1,0:T(8,128)}, f32[5,128,128]{2,1,0:T(8,128)S(1)}, u32[]{:S(2)}, u32[]{:S(2)}) %collective-permute-start.10) | collective-permute-done | bytes 327712 | tf_op jit(solution)/shard_map/ppermute | solution.py:377
  108.2 2.1 %collective-permute-start.11 = (f32[5,128,128]{2,1,0:T(8,128)S(1)}, f32[5,128,128]{2,1,0:T(8,128)S(1)}, u32[]{:S(2)}, u32[]{:S(2)}) collective-permute-start(f32[5,128,128]{2,1,0:T(8,128)S(1)} %collective-permute-done.10.refs_10_), channel_id=1, source_target_pairs={{0,1},{1,0},{2,3},{3,2},{4,5},{5,4},{6,7},{7,6},{8,9},{9,8},{10,11... | collective-permute-start | bytes 983048 | tf_op jit(solution)/shard_map/ppermute | solution.py:377
  110.3 9.2 %shard_map.70 = (f32[160,128]{1,0:T(8,128)}, f32[512,128]{1,0:T(8,128)}) custom-call(s32[1]{0:T(128)} %bitcast.1.rank_ref, f32[512,128]{1,0:T(8,128)} %bitcast.27, f32[512,128]{1,0:T(8,128)} %bitcast.24), custom_call_target="tpu_custom_call" | custom-call | flops 67108864 | bytes 1048576 | tf_op jit(solution)/shard_map/pallas_call | solution.py:342
  119.6 0.0 collective-permute-done.7.refs_6_
  119.6 0.0 collective-permute-done.9.refs_9_
  119.6 0.0 copy-start.7
  119.6 1.7 collective-permute-done.8.refs_7_
  121.3 0.0 collective-permute-done.11.refs_11_
  121.3 0.0 copy-done.4
  121.3 0.0 copy-done.5
  121.3 0.0 copy-done.6
  121.3 0.0 copy-done.7
  121.3 0.7 copy-done.8
  122.0 0.1 copy-done.9
  122.2 10.6 %shard_map.73 = (f32[768,128]{1,0:T(8,128)}, f32[1280,128]{1,0:T(8,128)}) custom-call(s32[1]{0:T(128)} %bitcast.1.rank_ref, f32[160,128]{1,0:T(8,128)} %get-tuple-element.42.weight_ref, f32[5120,512]{1,0:T(8,128)} %bitcast.16, f32[5120,512]{1,0:T(8,128)} %bitcast.17, f32[5120,512]{1,0:T(8,128)} %bitcast.18, f32[5120,512]{1,0:T(8,128)} %bitcast.19, ...), custom_call_target="tpu_custom_call" | custom-call | flops 2684354560 | bytes 13107200 | tf_op jit(solution)/shard_map/pallas_call | solution.py:230
  132.8 16.6 %all_to_all.31 = f32[32,24,128]{2,1,0:T(8,128)S(1)} all-to-all(f32[32,24,128]{2,1,0:T(8,128)} %bitcast.30), channel_id=1, replica_groups=mesh['cuts'=8,'rank'=4] {'cuts','rank'}, dimensions={0} | all-to-all | bytes 786432 | tf_op jit(solution)/shard_map/all_to_all | solution.py:381
  149.4 0.8 broadcast_in_dim.8
  150.2 2.8 %all-to-all-start.5 = ((f32[32,24,128]{2,1,0:T(8,128)}), f32[32,24,128]{2,1,0:T(8,128)S(1)}, u32[]{:S(2)}, u32[]{:S(2)}) async-start(f32[32,24,128]{2,1,0:T(8,128)} %broadcast_in_dim.8), calls=%async_computation.5 | async-start | bytes 786432 | tf_op jit(solution)/shard_map/all_to_all | solution.py:381
  153.0 8.5 %shard_map.71 = f32[5120,128]{1,0:T(8,128)} custom-call(f32[5120,512]{1,0:T(8,128)} %bitcast.21, f32[512,128]{1,0:T(8,128)} %get-tuple-element.41.weight_ref), custom_call_target="tpu_custom_call" | custom-call | flops 2684354560 | bytes 13107200 | tf_op jit(solution)/shard_map/pallas_call | solution.py:259
  161.5 4.9 %all-to-all-done.5 = f32[32,24,128]{2,1,0:T(8,128)S(1)} async-done(((f32[32,24,128]{2,1,0:T(8,128)}), f32[32,24,128]{2,1,0:T(8,128)S(1)}, u32[]{:S(2)}, u32[]{:S(2)}) %all-to-all-start.5) | async-done | bytes 393248 | tf_op jit(solution)/shard_map/all_to_all | solution.py:381
  166.4 0.8 copy-done.3
  167.2 9.3 %shard_map.74 = (f32[128,512]{1,0:T(8,128)}, f32[1280,128]{1,0:T(8,128)}) custom-call(f32[768,128]{1,0:T(8,128)} %bitcast.28, f32[1280,128]{1,0:T(8,128)} %get-tuple-element.48.middle_ref), custom_call_target="tpu_custom_call" | custom-call | flops 167772160 | bytes 1310720 | tf_op jit(solution)/shard_map/pallas_call | solution.py:365
  (12 shorter events, 0.1 us)
Async XLA Ops:
  12.1 23.7 %all-to-all-start = ((f32[8,16,128]{2,1,0:T(8,128)}), f32[8,16,128]{2,1,0:T(8,128)S(1)}, u32[]{:S(2)}, u32[]{:S(2)}) async-start(f32[8,16,128]{2,1,0:T(8,128)} %bitcast.31), calls=%async_computation | async-start | bytes 131072 | tf_op jit(solution)/shard_map/all_to_all | solution.py:381
  20.7 15.1 %collective-permute-start.3 = (f32[5,128,128]{2,1,0:T(8,128)}, f32[5,128,128]{2,1,0:T(8,128)}, u32[]{:S(2)}, u32[]{:S(2)}) collective-permute-start(f32[5,128,128]{2,1,0:T(8,128)} %get-tuple-element.55), channel_id=1, source_target_pairs={{0,2},{1,3},{2,0},{3,1},{4,6},{5,7},{6,4},{7,5},{8,10},{9,11},{10,... | collective-permute-start | bytes 983048 | tf_op jit(solution)/shard_map/ppermute | solution.py:377
  22.2 13.6 %collective-permute-start.2 = (f32[5,128,128]{2,1,0:T(8,128)}, f32[5,128,128]{2,1,0:T(8,128)}, u32[]{:S(2)}, u32[]{:S(2)}) collective-permute-start(f32[5,128,128]{2,1,0:T(8,128)} %get-tuple-element.56), channel_id=1, source_target_pairs={{0,1},{1,0},{2,3},{3,2},{4,5},{5,4},{6,7},{7,6},{8,9},{9,8},{10,11... | collective-permute-start | bytes 983048 | tf_op jit(solution)/shard_map/ppermute | solution.py:377
  23.7 14.4 %collective-permute-start.1 = (f32[5,128,128]{2,1,0:T(8,128)S(1)}, f32[5,128,128]{2,1,0:T(8,128)}, u32[]{:S(2)}, u32[]{:S(2)}) collective-permute-start(f32[5,128,128]{2,1,0:T(8,128)S(1)} %get-tuple-element.57), channel_id=1, source_target_pairs={{0,2},{1,3},{2,0},{3,1},{4,6},{5,7},{6,4},{7,5},{8,10},{9,11},{10,... | collective-permute-start | bytes 983048 | tf_op jit(solution)/shard_map/ppermute | solution.py:377
  24.2 15.2 %collective-permute-start = (f32[5,128,128]{2,1,0:T(8,128)S(1)}, f32[5,128,128]{2,1,0:T(8,128)}, u32[]{:S(2)}, u32[]{:S(2)}) collective-permute-start(f32[5,128,128]{2,1,0:T(8,128)S(1)} %get-tuple-element.58), channel_id=1, source_target_pairs={{0,1},{1,0},{2,3},{3,2},{4,5},{5,4},{6,7},{7,6},{8,9},{9,8},{10,11... | collective-permute-start | bytes 983048 | tf_op jit(solution)/shard_map/ppermute | solution.py:377
  35.8 24.8 %copy-start.1 = (f32[40,128,128]{2,1,0:T(8,128)S(1)}, f32[40,128,128]{2,1,0:T(8,128)}, u32[]{:S(2)}) copy-start(f32[40,128,128]{2,1,0:T(8,128)} %get-tuple-element.33) | copy-start | bytes 7864324
  54.9 20.2 %copy-start.2 = (f32[4,8,16,128]{3,2,1,0:T(8,128)}, f32[4,8,16,128]{3,2,1,0:T(8,128)S(1)}, u32[]{:S(2)}) copy-start(f32[4,8,16,128]{3,2,1,0:T(8,128)S(1)} %copy.7) | copy-start | bytes 786436
  57.9 13.6 %all-to-all-start.2 = ((f32[32,16,128]{2,1,0:T(8,128)}), f32[32,16,128]{2,1,0:T(8,128)S(1)}, u32[]{:S(2)}, u32[]{:S(2)}) async-start(f32[32,16,128]{2,1,0:T(8,128)} %bitcast.6), calls=%async_computation.2 | async-start | bytes 524288 | tf_op jit(solution)/shard_map/all_to_all | solution.py:381
  61.5 12.9 %collective-permute-start.4 = (f32[5,128,128]{2,1,0:T(8,128)}, f32[5,128,128]{2,1,0:T(8,128)S(1)}, u32[]{:S(2)}, u32[]{:S(2)}) collective-permute-start(f32[5,128,128]{2,1,0:T(8,128)} %get-tuple-element.34), channel_id=1, source_target_pairs={{0,3},{1,2},{2,1},{3,0},{4,7},{5,6},{6,5},{7,4},{8,11},{9,10},{10,... | collective-permute-start | bytes 983048 | tf_op jit(solution)/shard_map/ppermute | solution.py:377
  74.4 16.3 %copy-start.10 = (f32[5,128,128]{2,1,0:T(8,128)}, f32[5,128,128]{2,1,0:T(8,128)S(1)}, u32[]{:S(2)}) copy-start(f32[5,128,128]{2,1,0:T(8,128)S(1)} %collective-permute-done.4.refs_3_) | copy-start | bytes 983044
  75.2 15.5 %all-to-all-start.3 = ((f32[32,16,128]{2,1,0:T(8,128)}), f32[32,16,128]{2,1,0:T(8,128)S(1)}, u32[]{:S(2)}, u32[]{:S(2)}) async-start(f32[32,16,128]{2,1,0:T(8,128)} %broadcast_in_dim.7), calls=%async_computation.3 | async-start | bytes 524288 | tf_op jit(solution)/shard_map/all_to_all | solution.py:381
  79.8 14.3 %collective-permute-start.5 = (f32[5,128,128]{2,1,0:T(8,128)S(1)}, f32[5,128,128]{2,1,0:T(8,128)S(1)}, u32[]{:S(2)}, u32[]{:S(2)}) collective-permute-start(f32[5,128,128]{2,1,0:T(8,128)S(1)} %get-tuple-element.38), channel_id=1, source_target_pairs={{0,3},{1,2},{2,1},{3,0},{4,7},{5,6},{6,5},{7,4},{8,11},{9,10},{10,... | collective-permute-start | bytes 983048 | tf_op jit(solution)/shard_map/ppermute | solution.py:377
  90.6 0.7 copy-start
  94.0 10.1 %collective-permute-start.6 = (f32[5,128,128]{2,1,0:T(8,128)}, f32[5,128,128]{2,1,0:T(8,128)S(1)}, u32[]{:S(2)}, u32[]{:S(2)}) collective-permute-start(f32[5,128,128]{2,1,0:T(8,128)} %shard_map.72.refs_4_), channel_id=1, source_target_pairs={{0,1},{1,0},{2,3},{3,2},{4,5},{5,4},{6,7},{7,6},{8,9},{9,8},{10,11... | collective-permute-start | bytes 983048 | tf_op jit(solution)/shard_map/ppermute | solution.py:377
  94.0 0.7 copy-start.11
  97.4 10.8 %collective-permute-start.10 = (f32[5,128,128]{2,1,0:T(8,128)}, f32[5,128,128]{2,1,0:T(8,128)S(1)}, u32[]{:S(2)}, u32[]{:S(2)}) collective-permute-start(f32[5,128,128]{2,1,0:T(8,128)} %shard_map.69.refs_8_), channel_id=1, source_target_pairs={{0,2},{1,3},{2,0},{3,1},{4,6},{5,7},{6,4},{7,5},{8,10},{9,11},{10,... | collective-permute-start | bytes 983048 | tf_op jit(solution)/shard_map/ppermute | solution.py:377
  98.7 20.8 %collective-permute-start.7 = (f32[5,128,128]{2,1,0:T(8,128)}, f32[5,128,128]{2,1,0:T(8,128)S(1)}, u32[]{:S(2)}, u32[]{:S(2)}) collective-permute-start(f32[5,128,128]{2,1,0:T(8,128)} %shard_map.72.refs_4_), channel_id=1, source_target_pairs={{0,2},{1,3},{2,0},{3,1},{4,6},{5,7},{6,4},{7,5},{8,10},{9,11},{10,... | collective-permute-start | bytes 983048 | tf_op jit(solution)/shard_map/ppermute | solution.py:377
  99.5 20.1 %collective-permute-start.9 = (f32[5,128,128]{2,1,0:T(8,128)}, f32[5,128,128]{2,1,0:T(8,128)S(1)}, u32[]{:S(2)}, u32[]{:S(2)}) collective-permute-start(f32[5,128,128]{2,1,0:T(8,128)} %shard_map.69.refs_8_), channel_id=1, source_target_pairs={{0,1},{1,0},{2,3},{3,2},{4,5},{5,4},{6,7},{7,6},{8,9},{9,8},{10,11... | collective-permute-start | bytes 983048 | tf_op jit(solution)/shard_map/ppermute | solution.py:377
  104.1 17.2 %copy-start.4 = (f32[5,128,128]{2,1,0:T(8,128)}, f32[5,128,128]{2,1,0:T(8,128)S(1)}, u32[]{:S(2)}) copy-start(f32[5,128,128]{2,1,0:T(8,128)S(1)} %collective-permute-done.6.refs_5_) | copy-start | bytes 983044
  104.1 17.2 %collective-permute-start.8 = (f32[5,128,128]{2,1,0:T(8,128)S(1)}, f32[5,128,128]{2,1,0:T(8,128)S(1)}, u32[]{:S(2)}, u32[]{:S(2)}) collective-permute-start(f32[5,128,128]{2,1,0:T(8,128)S(1)} %collective-permute-done.6.refs_5_), channel_id=1, source_target_pairs={{0,2},{1,3},{2,0},{3,1},{4,6},{5,7},{6,4},{7,5},{8,10},{9,11},{10,... | collective-permute-start | bytes 983048 | tf_op jit(solution)/shard_map/ppermute | solution.py:377
  108.2 13.1 %copy-start.5 = (f32[5,128,128]{2,1,0:T(8,128)}, f32[5,128,128]{2,1,0:T(8,128)S(1)}, u32[]{:S(2)}) copy-start(f32[5,128,128]{2,1,0:T(8,128)S(1)} %collective-permute-done.10.refs_10_) | copy-start | bytes 983044
  108.2 13.1 %collective-permute-start.11 = (f32[5,128,128]{2,1,0:T(8,128)S(1)}, f32[5,128,128]{2,1,0:T(8,128)S(1)}, u32[]{:S(2)}, u32[]{:S(2)}) collective-permute-start(f32[5,128,128]{2,1,0:T(8,128)S(1)} %collective-permute-done.10.refs_10_), channel_id=1, source_target_pairs={{0,1},{1,0},{2,3},{3,2},{4,5},{5,4},{6,7},{7,6},{8,9},{9,8},{10,11... | collective-permute-start | bytes 983048 | tf_op jit(solution)/shard_map/ppermute | solution.py:377
  119.6 1.8 %copy-start.6 = (f32[5,128,128]{2,1,0:T(8,128)}, f32[5,128,128]{2,1,0:T(8,128)S(1)}, u32[]{:S(2)}) copy-start(f32[5,128,128]{2,1,0:T(8,128)S(1)} %collective-permute-done.7.refs_6_) | copy-start | bytes 983044
  119.6 1.8 %copy-start.7 = (f32[5,128,128]{2,1,0:T(8,128)}, f32[5,128,128]{2,1,0:T(8,128)S(1)}, u32[]{:S(2)}) copy-start(f32[5,128,128]{2,1,0:T(8,128)S(1)} %collective-permute-done.9.refs_9_) | copy-start | bytes 983044
  121.3 0.7 copy-start.8
  121.3 0.8 copy-start.9
  150.2 16.2 %all-to-all-start.5 = ((f32[32,24,128]{2,1,0:T(8,128)}), f32[32,24,128]{2,1,0:T(8,128)S(1)}, u32[]{:S(2)}, u32[]{:S(2)}) async-start(f32[32,24,128]{2,1,0:T(8,128)} %broadcast_in_dim.8), calls=%async_computation.5 | async-start | bytes 786432 | tf_op jit(solution)/shard_map/all_to_all | solution.py:381
  166.4 0.8 copy-start.3

commit v5 on v4

--- a/solution.py
+++ b/solution.py
@@ -153,6 +153,20 @@
         out_shape=shape(width, width),
         scratch_shapes=[pltpu.VMEM((width, 2 * width), jnp.float32)],
     )(flat_one)
+
+
+def product_kernel(square_ref, bridge_ref, out_ref):
+    bridge = twice(both_parts(bridge_ref[...], 1), 0)
+    out_ref[...] = fold(mxu(both_parts(square_ref[...], 1), bridge, NN), 1)
+
+
+def product_of(square, bridge):
+    return call(
+        product_kernel,
+        8 * square.size * bridge.shape[1],
+        4 * square.size + 8 * bridge.size,
+        out_shape=shape(*bridge.shape),
+    )(square, bridge)
 
 
 def loose_kernel(rank_ref, raw_ref, *refs):
@@ -277,7 +291,6 @@
     for k in range(size):
         pivot = entry[k][k]
         root = lax.rsqrt(pivot)
-        root = root * (1.5 - 0.5 * pivot * root * root)
         inverse[k][k] = root
         for i in range(k + 1, size):
             entry[i][k] = entry[i][k] * root
@@ -422,22 +435,23 @@
     near = [[(half, offset) for offset in range(1, far)] for half in range(2)]
 
     bits = [1 << bit for bit in range((ranks - 1).bit_length())]
-    moved = send(near[0] + near[1], sketched, None)
+    moved = send(near[0], sketched, None)
     bridge_rows = jnp.sum(exchange(part.reshape(cuts, local_rows // cuts, columns), "cuts"), axis=0)
-    flat_late, part = after(flat_one, part)
+    bridge_rows, pieces = after(bridge_rows, moved)
+    flat_late, bridge_rows = after(flat_one, bridge_rows)
+    sketched, bridge_rows = after(sketched, bridge_rows)
+    moved = send(near[1] + [(0, far)], sketched, None)
+    bridge = gather_all(bridge_rows, ("rank", "cuts")).reshape(width, columns)
     square = square_of(flat_late)
-    bridge_rows, (pieces, square) = after(bridge_rows, (moved, square))
-    sketched, bridge_rows = after(sketched, bridge_rows)
     pieces.update(send([(0, 0), (1, 0)], sketched, None))
-    bridge = gather_all(bridge_rows, both)
-    bridge = bridge.reshape(cuts, ranks, -1, columns).swapaxes(0, 1).reshape(width, columns)
-
-    raw = exact(square, bridge, NN)
-    far_piece = send([(0, far)], sketched, raw)
+
+    raw = product_of(square, bridge)
+    raw, moved = after(raw, moved)
+    pieces.update(moved)
+    far_piece = send([(1, far)], sketched, raw)
     raw = jnp.sum(exchange(raw.reshape(parts, -1, columns), both), axis=0)
     raw, far_piece = after(raw, far_piece)
     pieces.update(far_piece)
-    pieces.update(send([(1, far)], sketched, raw))
     raw = gather_all(raw, both).reshape(width, columns)
 
     loose = [loosen(rank_index, raw, [pieces[(half, offset)] for offset in range(ranks)]) for half in range(2)]

time: 177 us -> 172 us (0.972)
  waiting for transfers between devices: 35 us -> 31.5 us
  matrix products: 3.01 us -> 0 us
  Pallas kernels: 65.5 us -> 67.7 us
    dot_general x1 -> x0, matrix products: 3.01 us -> none  [exact(): lax.dot_general(a, b, form, precision=lax.Precision.HIGHEST, preferred_el...]
    pallas_call x0 -> x1, Pallas kernels: none -> 2.43 us  [product_of(): call(product_kernel, 8 * square.size * bridge.shape[1], 4 * square.size +...]
    ppermute x12, waiting for transfers between devices: 14.3 us -> 12.4 us  [swap(): lax.ppermute(value, axis, [(i, i ^ offset) for i in range(lax.axis_size(a...]
  transfers between devices with their start and end apart: 16 -> 16, of which waited for: 9 -> 8; matrix products, arithmetic and copies ran while one was open for 2% -> 1% of each run, Pallas kernels for 19% -> 20%
where the time goes in v5:
time: 172 us; the launch traced here: 171 us
  Pallas kernels  67.7 us (39%)
  starting transfers between devices  31.8 us (18%)
  waiting for transfers between devices  31.5 us (18%)
  blocking collectives  31.4 us (18%)
  local copies, waits for them, and re-layouts  7.45 us (4%)
    all_to_all x2, blocking collectives, exchange(): return lax.all_to_all(value, axes, 0, 0, tiled=True)  31.4 us
    all_to_all x4, waiting for transfers between devices, exchange(): return lax.all_to_all(value, axes, 0, 0, tiled=True)  19.1 us
    ppermute x12, starting transfers between devices, swap(): lax.ppermute(value, axis, [(i, i ^ offset) for i in range(lax.axis_size(a...  16.9 us
    all_to_all x4, starting transfers between devices, exchange(): return lax.all_to_all(value, axes, 0, 0, tiled=True)  14.9 us
    ppermute x12, waiting for transfers between devices, swap(): lax.ppermute(value, axis, [(i, i ^ offset) for i in range(lax.axis_size(a...  12.4 us
    pallas_call x1, Pallas kernels, sketch(): call(sketch_kernel, 2 * core_two.size * columns * 4, 4 * (core_two.size +...  11.5 us
    pallas_call x1, Pallas kernels, square_of(): call(square_kernel, 4 * rows * width * width, 4 * flat_one.size, grid=(ro...  11 us
    pallas_call x1, Pallas kernels, carry_rows(): call(functools.partial(carry_kernel, halves, share), 8 * flat_two.size *...  10.6 us
  transfers between devices with their start and end apart: 16, of which 8 were waited for; matrix products, arithmetic and copies ran while one was open for 1% of the time, Pallas kernels for 20%

profile of v5, /device:TPU:0, one launch (start us, length us, event | category | flops | bytes accessed | tf_op | source)
XLA Modules:
  0.0 170.8 jit_solution(4095398645677613535)
XLA Ops:
  0.6 11.5 %shard_map.67 = (f32[40,128,128]{2,1,0:T(8,128)}, f32[128,128]{1,0:T(8,128)}) custom-call(f32[128,40,512]{2,1,0:T(8,128)} %refs_3_.1, f32[128,40,512]{2,1,0:T(8,128)} %refs_3_.1, f32[128,40,512]{2,1,0:T(8,128)} %refs_3_.1, f32[128,40,512]{2,1,0:T(8,128)} %refs_3_.1, f32[512,128]{1,0:T(8,128)} %refs_4_.1, f32[128,40,128]{2,1,0:T(8,128)} %refs_5_.1), custom_call_target="tpu_custom_call" | custom-call | flops 2684354560 | bytes 15728640 | tf_op jit(solution)/shard_map/pallas_call | solution.py:100
  12.1 1.1 constant_dynamic-slice_fusion.6
  13.2 3.0 %collective-permute-start = (f32[5,128,128]{2,1,0:T(8,128)S(1)}, f32[5,128,128]{2,1,0:T(8,128)S(1)}, u32[]{:S(2)}, u32[]{:S(2)}) collective-permute-start(f32[5,128,128]{2,1,0:T(8,128)S(1)} %get-tuple-element.60), channel_id=1, source_target_pairs={{0,1},{1,0},{2,3},{3,2},{4,5},{5,4},{6,7},{7,6},{8,9},{9,8},{10,11... | collective-permute-start | bytes 983048 | tf_op jit(solution)/shard_map/ppermute | solution.py:390
  16.2 1.5 collective-permute-start.1
  17.8 4.9 %all-to-all-start = ((f32[8,16,128]{2,1,0:T(8,128)}), f32[8,16,128]{2,1,0:T(8,128)S(1)}, u32[]{:S(2)}, u32[]{:S(2)}) async-start(f32[8,16,128]{2,1,0:T(8,128)} %bitcast.26), calls=%async_computation | async-start | bytes 131072 | tf_op jit(solution)/shard_map/all_to_all | solution.py:394
  22.6 5.9 %all-to-all-done = f32[8,16,128]{2,1,0:T(8,128)S(1)} async-done(((f32[8,16,128]{2,1,0:T(8,128)}), f32[8,16,128]{2,1,0:T(8,128)S(1)}, u32[]{:S(2)}, u32[]{:S(2)}) %all-to-all-start) | async-done | bytes 65568 | tf_op jit(solution)/shard_map/all_to_all | solution.py:394
  28.6 0.0 collective-permute-done.refs_1_
  28.6 0.0 copy-start.8
  28.6 0.0 collective-permute-done.1.refs_2_
  28.6 0.0 copy-start.9
  28.6 0.8 broadcast_in_dim.6
  29.4 2.6 %all-to-all-start.1 = ((f32[32,16,128]{2,1,0:T(8,128)}), f32[32,16,128]{2,1,0:T(8,128)S(1)}, u32[]{:S(2)}, u32[]{:S(2)}) async-start(f32[32,16,128]{2,1,0:T(8,128)} %broadcast_in_dim.6), calls=%async_computation.1 | async-start | bytes 524288 | tf_op jit(solution)/shard_map/all_to_all | solution.py:394
  32.0 2.5 %constant_dynamic-slice_fusion = (f32[5,128,128]{2,1,0:T(8,128)}, f32[5,128,128]{2,1,0:T(8,128)}, f32[5,128,128]{2,1,0:T(8,128)S(1)}, f32[5,128,128]{2,1,0:T(8,1...) fusion(f32[40,128,128]{2,1,0:T(8,128)} %get-tuple-element.34, s32[]{:T(128)S(6)} %select_n.31, ...), kind=kLoop, calls=%fused_computation | loop fusion | bytes 3932184 | tf_op jit(solution)/shard_map/dynamic_slice | solution.py:429
  34.5 2.6 %collective-permute-start.2 = (f32[5,128,128]{2,1,0:T(8,128)S(1)}, f32[5,128,128]{2,1,0:T(8,128)S(1)}, u32[]{:S(2)}, u32[]{:S(2)}) collective-permute-start(f32[5,128,128]{2,1,0:T(8,128)S(1)} %get-tuple-element.58), channel_id=1, source_target_pairs={{0,3},{1,2},{2,1},{3,0},{4,7},{5,6},{6,5},{7,4},{8,11},{9,10},{10,... | collective-permute-start | bytes 983048 | tf_op jit(solution)/shard_map/ppermute | solution.py:390
  37.0 0.5 collective-permute-start.3
  37.6 0.4 collective-permute-start.4
  37.9 11.0 %shard_map.68.square_ref = f32[512,512]{1,0:T(8,128)} custom-call(f32[5120,512]{1,0:T(8,128)} %bitcast.15), custom_call_target="tpu_custom_call" | custom-call | flops 5368709120 | bytes 10485760 | tf_op jit(solution)/shard_map/pallas_call | solution.py:146
  49.0 0.0 copy-done.8
  49.0 0.0 copy-done.9
  49.0 0.0 all-to-all-done.1
  49.0 0.0 copy-start
  49.0 0.7 copy-done
  49.7 2.4 %shard_map.69 = f32[512,128]{1,0:T(8,128)} custom-call(f32[512,512]{1,0:T(8,128)} %shard_map.68.square_ref, f32[512,128]{1,0:T(8,128)} %bitcast.21), custom_call_target="tpu_custom_call" | custom-call | flops 268435456 | bytes 1572864 | tf_op jit(solution)/shard_map/pallas_call | solution.py:164
  52.1 0.0 collective-permute-done.2.refs_3_
  52.1 1.4 collective-permute-done.3.refs_1_
  53.5 0.0 collective-permute-done.4.refs_2_
  53.5 4.6 %all-to-all-start.2 = ((f32[32,16,128]{2,1,0:T(8,128)}), f32[32,16,128]{2,1,0:T(8,128)S(1)}, u32[]{:S(2)}, u32[]{:S(2)}) async-start(f32[32,16,128]{2,1,0:T(8,128)} %bitcast.24), calls=%async_computation.2 | async-start | bytes 524288 | tf_op jit(solution)/shard_map/all_to_all | solution.py:394
  58.2 2.7 %collective-permute-start.5 = (f32[5,128,128]{2,1,0:T(8,128)S(1)}, f32[5,128,128]{2,1,0:T(8,128)S(1)}, u32[]{:S(2)}, u32[]{:S(2)}) collective-permute-start(f32[5,128,128]{2,1,0:T(8,128)S(1)} %get-tuple-element.36), channel_id=1, source_target_pairs={{0,3},{1,2},{2,1},{3,0},{4,7},{5,6},{6,5},{7,4},{8,11},{9,10},{10,... | collective-permute-start | bytes 983048 | tf_op jit(solution)/shard_map/ppermute | solution.py:390
  60.9 8.3 %all-to-all-done.2 = f32[32,16,128]{2,1,0:T(8,128)S(1)} async-done(((f32[32,16,128]{2,1,0:T(8,128)}), f32[32,16,128]{2,1,0:T(8,128)S(1)}, u32[]{:S(2)}, u32[]{:S(2)}) %all-to-all-start.2) | async-done | bytes 262176 | tf_op jit(solution)/shard_map/all_to_all | solution.py:394
  69.3 2.5 %collective-permute-done.5.refs_3_ = f32[5,128,128]{2,1,0:T(8,128)S(1)} collective-permute-done((f32[5,128,128]{2,1,0:T(8,128)S(1)}, f32[5,128,128]{2,1,0:T(8,128)S(1)}, u32[]{:S(2)}, u32[]{:S(2)}) %collective-permute-start.5) | collective-permute-done | bytes 327712 | tf_op jit(solution)/shard_map/ppermute | solution.py:390
  71.8 14.8 %all_to_all.30 = f32[32,16,128]{2,1,0:T(8,128)} all-to-all(f32[32,16,128]{2,1,0:T(8,128)S(1)} %broadcast_in_dim.7), channel_id=1, replica_groups=mesh['cuts'=8,'rank'=4] {'cuts','rank'}, dimensions={0} | all-to-all | bytes 524288 | tf_op jit(solution)/shard_map/all_to_all | solution.py:394
  86.6 0.0 copy-done.12
  86.6 2.7 %shard_map.73.refs_4_ = f32[5,128,128]{2,1,0:T(8,128)} custom-call(s32[1]{0:T(128)} %bitcast.1.rank_ref, f32[512,128]{1,0:T(8,128)} %bitcast.17, f32[5,128,128]{2,1,0:T(8,128)} %get-tuple-element.53.refs_0_, f32[5,128,128]{2,1,0:T(8,128)} %copy-done.8, f32[5,128,128]{2,1,0:T(8,128)} %copy-done.9, f32[5,128,128]{2,1,0:T(8,128)} %copy-done.12), custom_call_target="tpu_custom_call" | custom-call | flops 335544320 | bytes 1572864 | tf_op jit(solution)/shard_map/pallas_call | solution.py:190
  89.3 0.0 collective-permute-start.6
  89.3 0.0 copy-done.10
  89.3 0.0 copy-done.11
  89.3 0.0 copy-done.13
  89.3 2.7 %shard_map.70.refs_8_ = f32[5,128,128]{2,1,0:T(8,128)} custom-call(s32[1]{0:T(128)} %bitcast.1.rank_ref, f32[512,128]{1,0:T(8,128)} %bitcast.18, f32[5,128,128]{2,1,0:T(8,128)} %get-tuple-element.54.refs_0_, f32[5,128,128]{2,1,0:T(8,128)} %copy-done.10, f32[5,128,128]{2,1,0:T(8,128)} %copy-done.11, f32[5,128,128]{2,1,0:T(8,128)} %copy-done.13), custom_call_target="tpu_custom_call" | custom-call | flops 335544320 | bytes 1572864 | tf_op jit(solution)/shard_map/pallas_call | solution.py:190
  92.0 1.4 collective-permute-start.10
  93.4 0.6 collective-permute-start.7
  94.1 2.0 %collective-permute-start.9 = (f32[5,128,128]{2,1,0:T(8,128)}, f32[5,128,128]{2,1,0:T(8,128)S(1)}, u32[]{:S(2)}, u32[]{:S(2)}) collective-permute-start(f32[5,128,128]{2,1,0:T(8,128)} %shard_map.70.refs_8_), channel_id=1, source_target_pairs={{0,1},{1,0},{2,3},{3,2},{4,5},{5,4},{6,7},{7,6},{8,9},{9,8},{10,11... | collective-permute-start | bytes 983048 | tf_op jit(solution)/shard_map/ppermute | solution.py:390
  96.1 4.1 %collective-permute-done.6.refs_5_ = f32[5,128,128]{2,1,0:T(8,128)S(1)} collective-permute-done((f32[5,128,128]{2,1,0:T(8,128)}, f32[5,128,128]{2,1,0:T(8,128)S(1)}, u32[]{:S(2)}, u32[]{:S(2)}) %collective-permute-start.6) | collective-permute-done | bytes 327712 | tf_op jit(solution)/shard_map/ppermute | solution.py:390
  100.2 0.0 collective-permute-start.8
  100.2 2.6 %collective-permute-done.10.refs_10_ = f32[5,128,128]{2,1,0:T(8,128)S(1)} collective-permute-done((f32[5,128,128]{2,1,0:T(8,128)}, f32[5,128,128]{2,1,0:T(8,128)S(1)}, u32[]{:S(2)}, u32[]{:S(2)}) %collective-permute-start.10) | collective-permute-done | bytes 327712 | tf_op jit(solution)/shard_map/ppermute | solution.py:390
  102.8 2.1 %collective-permute-start.11 = (f32[5,128,128]{2,1,0:T(8,128)S(1)}, f32[5,128,128]{2,1,0:T(8,128)S(1)}, u32[]{:S(2)}, u32[]{:S(2)}) collective-permute-start(f32[5,128,128]{2,1,0:T(8,128)S(1)} %collective-permute-done.10.refs_10_), channel_id=1, source_target_pairs={{0,1},{1,0},{2,3},{3,2},{4,5},{5,4},{6,7},{7,6},{8,9},{9,8},{10,11... | collective-permute-start | bytes 983048 | tf_op jit(solution)/shard_map/ppermute | solution.py:390
  104.9 9.2 %shard_map.71 = (f32[160,128]{1,0:T(8,128)}, f32[512,128]{1,0:T(8,128)}) custom-call(s32[1]{0:T(128)} %bitcast.1.rank_ref, f32[512,128]{1,0:T(8,128)} %bitcast.22, f32[512,128]{1,0:T(8,128)} %bitcast.19), custom_call_target="tpu_custom_call" | custom-call | flops 67108864 | bytes 1048576 | tf_op jit(solution)/shard_map/pallas_call | solution.py:355
  114.1 0.0 collective-permute-done.7.refs_6_
  114.1 0.0 collective-permute-done.9.refs_9_
  114.1 0.0 copy-start.5
  114.1 1.8 %collective-permute-done.8.refs_7_ = f32[5,128,128]{2,1,0:T(8,128)S(1)} collective-permute-done((f32[5,128,128]{2,1,0:T(8,128)S(1)}, f32[5,128,128]{2,1,0:T(8,128)S(1)}, u32[]{:S(2)}, u32[]{:S(2)}) %collective-permute-start.8) | collective-permute-done | bytes 327712 | tf_op jit(solution)/shard_map/ppermute | solution.py:390
  115.9 0.0 collective-permute-done.11.refs_11_
  115.9 0.0 copy-done.2
  115.9 0.0 copy-done.3
  115.9 0.0 copy-done.4
  115.9 0.7 copy-done.6
  116.6 0.1 copy-done.7
  116.7 10.6 %shard_map.74 = (f32[768,128]{1,0:T(8,128)}, f32[1280,128]{1,0:T(8,128)}) custom-call(s32[1]{0:T(128)} %bitcast.1.rank_ref, f32[160,128]{1,0:T(8,128)} %get-tuple-element.44.weight_ref, f32[5120,512]{1,0:T(8,128)} %bitcast.11, f32[5120,512]{1,0:T(8,128)} %bitcast.12, f32[5120,512]{1,0:T(8,128)} %bitcast.13, f32[5120,512]{1,0:T(8,128)} %bitcast.14, ...), custom_call_target="tpu_custom_call" | custom-call | flops 2684354560 | bytes 13107200 | tf_op jit(solution)/shard_map/pallas_call | solution.py:244
  127.3 16.6 %all_to_all.31 = f32[32,24,128]{2,1,0:T(8,128)S(1)} all-to-all(f32[32,24,128]{2,1,0:T(8,128)} %bitcast.25), channel_id=1, replica_groups=mesh['cuts'=8,'rank'=4] {'cuts','rank'}, dimensions={0} | all-to-all | bytes 786432 | tf_op jit(solution)/shard_map/all_to_all | solution.py:394
  144.0 0.8 broadcast_in_dim.8
  144.7 2.8 %all-to-all-start.5 = ((f32[32,24,128]{2,1,0:T(8,128)}), f32[32,24,128]{2,1,0:T(8,128)S(1)}, u32[]{:S(2)}, u32[]{:S(2)}) async-start(f32[32,24,128]{2,1,0:T(8,128)} %broadcast_in_dim.8), calls=%async_computation.5 | async-start | bytes 786432 | tf_op jit(solution)/shard_map/all_to_all | solution.py:394
  147.6 8.5 %shard_map.72 = f32[5120,128]{1,0:T(8,128)} custom-call(f32[5120,512]{1,0:T(8,128)} %bitcast.16, f32[512,128]{1,0:T(8,128)} %get-tuple-element.43.weight_ref), custom_call_target="tpu_custom_call" | custom-call | flops 2684354560 | bytes 13107200 | tf_op jit(solution)/shard_map/pallas_call | solution.py:273
  156.1 4.9 %all-to-all-done.5 = f32[32,24,128]{2,1,0:T(8,128)S(1)} async-done(((f32[32,24,128]{2,1,0:T(8,128)}), f32[32,24,128]{2,1,0:T(8,128)S(1)}, u32[]{:S(2)}, u32[]{:S(2)}) %all-to-all-start.5) | async-done | bytes 393248 | tf_op jit(solution)/shard_map/all_to_all | solution.py:394
  161.0 0.8 copy-done.1
  161.7 9.1 %shard_map.75 = (f32[128,512]{1,0:T(8,128)}, f32[1280,128]{1,0:T(8,128)}) custom-call(f32[768,128]{1,0:T(8,128)} %bitcast.23, f32[1280,128]{1,0:T(8,128)} %get-tuple-element.50.middle_ref), custom_call_target="tpu_custom_call" | custom-call | flops 167772160 | bytes 1310720 | tf_op jit(solution)/shard_map/pallas_call | solution.py:378
  (15 shorter events, 0.1 us)
Async XLA Ops:
  13.2 15.3 %collective-permute-start = (f32[5,128,128]{2,1,0:T(8,128)S(1)}, f32[5,128,128]{2,1,0:T(8,128)S(1)}, u32[]{:S(2)}, u32[]{:S(2)}) collective-permute-start(f32[5,128,128]{2,1,0:T(8,128)S(1)} %get-tuple-element.60), channel_id=1, source_target_pairs={{0,1},{1,0},{2,3},{3,2},{4,5},{5,4},{6,7},{7,6},{8,9},{9,8},{10,11... | collective-permute-start | bytes 983048 | tf_op jit(solution)/shard_map/ppermute | solution.py:390
  16.2 12.4 %collective-permute-start.1 = (f32[5,128,128]{2,1,0:T(8,128)S(1)}, f32[5,128,128]{2,1,0:T(8,128)S(1)}, u32[]{:S(2)}, u32[]{:S(2)}) collective-permute-start(f32[5,128,128]{2,1,0:T(8,128)S(1)} %get-tuple-element.59), channel_id=1, source_target_pairs={{0,2},{1,3},{2,0},{3,1},{4,6},{5,7},{6,4},{7,5},{8,10},{9,11},{10,... | collective-permute-start | bytes 983048 | tf_op jit(solution)/shard_map/ppermute | solution.py:390
  17.8 10.8 %all-to-all-start = ((f32[8,16,128]{2,1,0:T(8,128)}), f32[8,16,128]{2,1,0:T(8,128)S(1)}, u32[]{:S(2)}, u32[]{:S(2)}) async-start(f32[8,16,128]{2,1,0:T(8,128)} %bitcast.26), calls=%async_computation | async-start | bytes 131072 | tf_op jit(solution)/shard_map/all_to_all | solution.py:394
  28.6 20.4 %copy-start.8 = (f32[5,128,128]{2,1,0:T(8,128)}, f32[5,128,128]{2,1,0:T(8,128)S(1)}, u32[]{:S(2)}) copy-start(f32[5,128,128]{2,1,0:T(8,128)S(1)} %collective-permute-done.refs_1_) | copy-start | bytes 983044
  28.6 20.4 %copy-start.9 = (f32[5,128,128]{2,1,0:T(8,128)}, f32[5,128,128]{2,1,0:T(8,128)S(1)}, u32[]{:S(2)}) copy-start(f32[5,128,128]{2,1,0:T(8,128)S(1)} %collective-permute-done.1.refs_2_) | copy-start | bytes 983044
  29.4 19.6 %all-to-all-start.1 = ((f32[32,16,128]{2,1,0:T(8,128)}), f32[32,16,128]{2,1,0:T(8,128)S(1)}, u32[]{:S(2)}, u32[]{:S(2)}) async-start(f32[32,16,128]{2,1,0:T(8,128)} %broadcast_in_dim.6), calls=%async_computation.1 | async-start | bytes 524288 | tf_op jit(solution)/shard_map/all_to_all | solution.py:394
  34.5 17.7 %collective-permute-start.2 = (f32[5,128,128]{2,1,0:T(8,128)S(1)}, f32[5,128,128]{2,1,0:T(8,128)S(1)}, u32[]{:S(2)}, u32[]{:S(2)}) collective-permute-start(f32[5,128,128]{2,1,0:T(8,128)S(1)} %get-tuple-element.58), channel_id=1, source_target_pairs={{0,3},{1,2},{2,1},{3,0},{4,7},{5,6},{6,5},{7,4},{8,11},{9,10},{10,... | collective-permute-start | bytes 983048 | tf_op jit(solution)/shard_map/ppermute | solution.py:390
  37.0 16.5 %collective-permute-start.3 = (f32[5,128,128]{2,1,0:T(8,128)S(1)}, f32[5,128,128]{2,1,0:T(8,128)S(1)}, u32[]{:S(2)}, u32[]{:S(2)}) collective-permute-start(f32[5,128,128]{2,1,0:T(8,128)S(1)} %get-tuple-element.57), channel_id=1, source_target_pairs={{0,1},{1,0},{2,3},{3,2},{4,5},{5,4},{6,7},{7,6},{8,9},{9,8},{10,11... | collective-permute-start | bytes 983048 | tf_op jit(solution)/shard_map/ppermute | solution.py:390
  37.6 15.9 %collective-permute-start.4 = (f32[5,128,128]{2,1,0:T(8,128)S(1)}, f32[5,128,128]{2,1,0:T(8,128)S(1)}, u32[]{:S(2)}, u32[]{:S(2)}) collective-permute-start(f32[5,128,128]{2,1,0:T(8,128)S(1)} %get-tuple-element.56), channel_id=1, source_target_pairs={{0,2},{1,3},{2,0},{3,1},{4,6},{5,7},{6,4},{7,5},{8,10},{9,11},{10,... | collective-permute-start | bytes 983048 | tf_op jit(solution)/shard_map/ppermute | solution.py:390
  49.0 0.7 copy-start
  52.1 34.5 %copy-start.12 = (f32[5,128,128]{2,1,0:T(8,128)}, f32[5,128,128]{2,1,0:T(8,128)S(1)}, u32[]{:S(2)}) copy-start(f32[5,128,128]{2,1,0:T(8,128)S(1)} %collective-permute-done.2.refs_3_) | copy-start | bytes 983044
  53.5 35.8 %copy-start.10 = (f32[5,128,128]{2,1,0:T(8,128)}, f32[5,128,128]{2,1,0:T(8,128)S(1)}, u32[]{:S(2)}) copy-start(f32[5,128,128]{2,1,0:T(8,128)S(1)} %collective-permute-done.3.refs_1_) | copy-start | bytes 983044
  53.5 35.8 %copy-start.11 = (f32[5,128,128]{2,1,0:T(8,128)}, f32[5,128,128]{2,1,0:T(8,128)S(1)}, u32[]{:S(2)}) copy-start(f32[5,128,128]{2,1,0:T(8,128)S(1)} %collective-permute-done.4.refs_2_) | copy-start | bytes 983044
  53.5 15.7 %all-to-all-start.2 = ((f32[32,16,128]{2,1,0:T(8,128)}), f32[32,16,128]{2,1,0:T(8,128)S(1)}, u32[]{:S(2)}, u32[]{:S(2)}) async-start(f32[32,16,128]{2,1,0:T(8,128)} %bitcast.24), calls=%async_computation.2 | async-start | bytes 524288 | tf_op jit(solution)/shard_map/all_to_all | solution.py:394
  58.2 13.6 %collective-permute-start.5 = (f32[5,128,128]{2,1,0:T(8,128)S(1)}, f32[5,128,128]{2,1,0:T(8,128)S(1)}, u32[]{:S(2)}, u32[]{:S(2)}) collective-permute-start(f32[5,128,128]{2,1,0:T(8,128)S(1)} %get-tuple-element.36), channel_id=1, source_target_pairs={{0,3},{1,2},{2,1},{3,0},{4,7},{5,6},{6,5},{7,4},{8,11},{9,10},{10,... | collective-permute-start | bytes 983048 | tf_op jit(solution)/shard_map/ppermute | solution.py:390
  71.8 17.6 %copy-start.13 = (f32[5,128,128]{2,1,0:T(8,128)}, f32[5,128,128]{2,1,0:T(8,128)S(1)}, u32[]{:S(2)}) copy-start(f32[5,128,128]{2,1,0:T(8,128)S(1)} %collective-permute-done.5.refs_3_) | copy-start | bytes 983044
  89.3 10.9 %collective-permute-start.6 = (f32[5,128,128]{2,1,0:T(8,128)}, f32[5,128,128]{2,1,0:T(8,128)S(1)}, u32[]{:S(2)}, u32[]{:S(2)}) collective-permute-start(f32[5,128,128]{2,1,0:T(8,128)} %shard_map.73.refs_4_), channel_id=1, source_target_pairs={{0,1},{1,0},{2,3},{3,2},{4,5},{5,4},{6,7},{7,6},{8,9},{9,8},{10,11... | collective-permute-start | bytes 983048 | tf_op jit(solution)/shard_map/ppermute | solution.py:390
  92.0 10.8 %collective-permute-start.10 = (f32[5,128,128]{2,1,0:T(8,128)}, f32[5,128,128]{2,1,0:T(8,128)S(1)}, u32[]{:S(2)}, u32[]{:S(2)}) collective-permute-start(f32[5,128,128]{2,1,0:T(8,128)} %shard_map.70.refs_8_), channel_id=1, source_target_pairs={{0,2},{1,3},{2,0},{3,1},{4,6},{5,7},{6,4},{7,5},{8,10},{9,11},{10,... | collective-permute-start | bytes 983048 | tf_op jit(solution)/shard_map/ppermute | solution.py:390
  93.4 20.7 %collective-permute-start.7 = (f32[5,128,128]{2,1,0:T(8,128)}, f32[5,128,128]{2,1,0:T(8,128)S(1)}, u32[]{:S(2)}, u32[]{:S(2)}) collective-permute-start(f32[5,128,128]{2,1,0:T(8,128)} %shard_map.73.refs_4_), channel_id=1, source_target_pairs={{0,2},{1,3},{2,0},{3,1},{4,6},{5,7},{6,4},{7,5},{8,10},{9,11},{10,... | collective-permute-start | bytes 983048 | tf_op jit(solution)/shard_map/ppermute | solution.py:390
  94.1 20.0 %collective-permute-start.9 = (f32[5,128,128]{2,1,0:T(8,128)}, f32[5,128,128]{2,1,0:T(8,128)S(1)}, u32[]{:S(2)}, u32[]{:S(2)}) collective-permute-start(f32[5,128,128]{2,1,0:T(8,128)} %shard_map.70.refs_8_), channel_id=1, source_target_pairs={{0,1},{1,0},{2,3},{3,2},{4,5},{5,4},{6,7},{7,6},{8,9},{9,8},{10,11... | collective-permute-start | bytes 983048 | tf_op jit(solution)/shard_map/ppermute | solution.py:390
  100.2 15.7 %copy-start.2 = (f32[5,128,128]{2,1,0:T(8,128)}, f32[5,128,128]{2,1,0:T(8,128)S(1)}, u32[]{:S(2)}) copy-start(f32[5,128,128]{2,1,0:T(8,128)S(1)} %collective-permute-done.6.refs_5_) | copy-start | bytes 983044
  100.2 15.7 %collective-permute-start.8 = (f32[5,128,128]{2,1,0:T(8,128)S(1)}, f32[5,128,128]{2,1,0:T(8,128)S(1)}, u32[]{:S(2)}, u32[]{:S(2)}) collective-permute-start(f32[5,128,128]{2,1,0:T(8,128)S(1)} %collective-permute-done.6.refs_5_), channel_id=1, source_target_pairs={{0,2},{1,3},{2,0},{3,1},{4,6},{5,7},{6,4},{7,5},{8,10},{9,11},{10,... | collective-permute-start | bytes 983048 | tf_op jit(solution)/shard_map/ppermute | solution.py:390
  102.8 13.1 %copy-start.3 = (f32[5,128,128]{2,1,0:T(8,128)}, f32[5,128,128]{2,1,0:T(8,128)S(1)}, u32[]{:S(2)}) copy-start(f32[5,128,128]{2,1,0:T(8,128)S(1)} %collective-permute-done.10.refs_10_) | copy-start | bytes 983044
  102.8 13.1 %collective-permute-start.11 = (f32[5,128,128]{2,1,0:T(8,128)S(1)}, f32[5,128,128]{2,1,0:T(8,128)S(1)}, u32[]{:S(2)}, u32[]{:S(2)}) collective-permute-start(f32[5,128,128]{2,1,0:T(8,128)S(1)} %collective-permute-done.10.refs_10_), channel_id=1, source_target_pairs={{0,1},{1,0},{2,3},{3,2},{4,5},{5,4},{6,7},{7,6},{8,9},{9,8},{10,11... | collective-permute-start | bytes 983048 | tf_op jit(solution)/shard_map/ppermute | solution.py:390
  114.1 1.8 %copy-start.4 = (f32[5,128,128]{2,1,0:T(8,128)}, f32[5,128,128]{2,1,0:T(8,128)S(1)}, u32[]{:S(2)}) copy-start(f32[5,128,128]{2,1,0:T(8,128)S(1)} %collective-permute-done.7.refs_6_) | copy-start | bytes 983044
  114.1 1.8 %copy-start.5 = (f32[5,128,128]{2,1,0:T(8,128)}, f32[5,128,128]{2,1,0:T(8,128)S(1)}, u32[]{:S(2)}) copy-start(f32[5,128,128]{2,1,0:T(8,128)S(1)} %collective-permute-done.9.refs_9_) | copy-start | bytes 983044
  115.9 0.7 copy-start.6
  115.9 0.8 copy-start.7
  144.7 16.2 %all-to-all-start.5 = ((f32[32,24,128]{2,1,0:T(8,128)}), f32[32,24,128]{2,1,0:T(8,128)S(1)}, u32[]{:S(2)}, u32[]{:S(2)}) async-start(f32[32,24,128]{2,1,0:T(8,128)} %broadcast_in_dim.8), calls=%async_computation.5 | async-start | bytes 786432 | tf_op jit(solution)/shard_map/all_to_all | solution.py:394
  161.0 0.8 copy-start.1

commit v6 on v5

--- a/solution.py
+++ b/solution.py
@@ -16,15 +16,6 @@
 
 
 PARTS = 4
-
-
-def tiles(block, width):
-    size = block // PARTS
-    return [pl.BlockSpec((size, width), lambda i, q=q: (i * PARTS + q, 0)) for q in range(PARTS)]
-
-
-def joined_rows(refs):
-    return jnp.concatenate([ref[...] for ref in refs], axis=0)
 
 
 def call(kernel, flops, size, **more):
@@ -137,7 +128,7 @@
     @pl.when(step == pl.num_programs(0) - 1)
     def _():
         cross = sum_ref[:, width:]
-        square_ref[...] = sum_ref[:, :width] + cross + cross.T
+        square_ref[...] = both_parts(sum_ref[:, :width] + cross + cross.T, 1)
 
 
 def square_of(flat_one):
@@ -149,116 +140,145 @@
         4 * flat_one.size,
         grid=(rows // block,),
         in_specs=[pl.BlockSpec((block, width), lambda i: (i, 0))],
-        out_specs=pl.BlockSpec((width, width), lambda i: (0, 0)),
-        out_shape=shape(width, width),
+        out_specs=pl.BlockSpec((width, 2 * width), lambda i: (0, 0)),
+        out_shape=jax.ShapeDtypeStruct((width, 2 * width), jnp.bfloat16),
         scratch_shapes=[pltpu.VMEM((width, 2 * width), jnp.float32)],
     )(flat_one)
 
 
 def product_kernel(square_ref, bridge_ref, out_ref):
     bridge = twice(both_parts(bridge_ref[...], 1), 0)
-    out_ref[...] = fold(mxu(both_parts(square_ref[...], 1), bridge, NN), 1)
+    out_ref[...] = fold(mxu(square_ref[...], bridge, NN), 1)
 
 
 def product_of(square, bridge):
     return call(
         product_kernel,
-        8 * square.size * bridge.shape[1],
-        4 * square.size + 8 * bridge.size,
+        4 * square.size * bridge.shape[1],
+        2 * square.size + 8 * bridge.size,
         out_shape=shape(*bridge.shape),
     )(square, bridge)
 
 
 def loose_kernel(rank_ref, raw_ref, *refs):
-    piece_refs, out_ref = refs[:-1], refs[-1]
-    count, local_rows, columns = piece_refs[0].shape
+    piece_refs, out_refs = refs[:-2], refs[-2:]
+    ranks = len(piece_refs) // 2
+    local_rows, columns = piece_refs[0].shape[1:]
     rows = []
-    for offset in range(len(piece_refs)):
+    for offset in range(ranks):
         start = pl.multiple_of((rank_ref[0] ^ offset) * local_rows, local_rows)
         rows.append(raw_ref[pl.ds(start, local_rows), :])
     raw = twice(both_parts(jnp.concatenate(rows, axis=0), 1).T, 1)
-    value = [jnp.concatenate([ref[n] for n in range(count)], axis=1) for ref in piece_refs]
-    product = fold(mxu(raw, both_parts(jnp.concatenate(value, axis=0), 0), NN), 0)
-    for n in range(count):
-        out_ref[n] = product[:, n * columns:(n + 1) * columns]
-
-
-def loosen(rank_index, raw, pieces):
+    for half, out_ref in enumerate(out_refs):
+        refs = piece_refs[half * ranks:(half + 1) * ranks]
+        count = out_ref.shape[0]
+        value = [jnp.concatenate([ref[n] for n in range(count)], axis=1) for ref in refs]
+        product = fold(mxu(raw, both_parts(jnp.concatenate(value, axis=0), 0), NN), 0)
+        for n in range(count):
+            out_ref[n] = product[:, n * columns:(n + 1) * columns]
+
+
+def loosen(rank_index, raw, pieces, halves):
     columns = raw.shape[1]
-    size = len(pieces) * pieces[0].size
+    size = sum(piece.size for piece in pieces)
     whole = pl.BlockSpec(memory_space=pltpu.VMEM)
     return call(
         loose_kernel,
         8 * size * columns,
         4 * raw.size + 4 * size,
         in_specs=[pl.BlockSpec(memory_space=pltpu.SMEM)] + [whole] * (len(pieces) + 1),
-        out_specs=whole,
-        out_shape=shape(pieces[0].shape[0], columns, columns),
+        out_specs=[whole] * 2,
+        out_shape=[shape(count, columns, columns) for count in halves],
     )(rank_index, raw, *pieces)
 
 
-def carry_kernel(halves, share, rank_ref, weight_ref, *refs):
-    core_refs, piece_refs = refs[:PARTS], refs[PARTS:-4]
-    joined_ref, middle_ref, rows_ref, sum_ref = refs[-4:]
+def slot_places(rank, places, pieces):
+    return [
+        (rank ^ offset) * stride + n
+        for (offset, stride, first), piece in zip(places, pieces)
+        for n in range(first, first + piece.shape[0])
+    ]
+
+
+def carry_kernel(places, room, last, tiles, rank_ref, weight_ref, *refs):
+    core_refs, refs = refs[:tiles], refs[tiles:]
+    piece_refs = refs[:len(places)]
+    if last:
+        before_ref, before_gram_ref, out_ref, middle_ref, spread_ref, sum_ref = refs[len(places):]
+    else:
+        out_ref, gram_ref, middle_ref, spread_ref, sum_ref = refs[len(places):]
     step = pl.program_id(0)
-    block, width = core_refs[0].shape[0] * PARTS, core_refs[0].shape[1]
     columns = weight_ref.shape[1]
-    ranks = len(piece_refs) // len(halves)
-    room = share * ranks
-    local_rows = rows_ref.shape[0] // room
-    band = middle_ref.shape[0] // room
+    local_rows = spread_ref.shape[1]
+    width = sum_ref.shape[1]
+    block = core_refs[0].shape[0] // room
+    slots = slot_places(rank_ref[0], places, piece_refs)
 
     @pl.when(step == 0)
     def _():
-        sum_ref[...] = jnp.zeros_like(sum_ref)
+        sum_ref[...] = before_ref[...] if last else jnp.zeros_like(sum_ref)
         weight = twice(both_parts(weight_ref[...], 0), 1)
-        for half, count in enumerate(halves):
-            for offset in range(ranks):
-                ref = piece_refs[half * ranks + offset]
-                first = (rank_ref[0] ^ offset) * share + sum(halves[:half])
-                value = both_parts(jnp.concatenate([ref[n] for n in range(count)], axis=1), 0)
-                spread = fold(mxu(weight, value, NN), 0)
-                for n in range(count):
-                    piece = lax.slice_in_dim(spread, n * columns, (n + 1) * columns, axis=1)
-                    rows_ref[pl.ds(first + n, local_rows, stride=room), :] = piece[:local_rows]
-                    middle_ref[pl.ds(first + n, band, stride=room), :] = piece[local_rows:]
-
-    rows = both_parts(rows_ref[pl.ds(pl.multiple_of(step * block, block), block), :], 1).T
-    product = fold(mxu(twice(rows, 1), both_parts(joined_rows(core_refs), 0), NN), 0)
+        slot = 0
+        for ref in piece_refs:
+            count = ref.shape[0]
+            value = both_parts(jnp.concatenate([ref[n] for n in range(count)], axis=1), 0)
+            spread = fold(mxu(weight, value, NN), 0)
+            for n in range(count):
+                piece = lax.slice_in_dim(spread, n * columns, (n + 1) * columns, axis=1)
+                spread_ref[slot] = piece[:local_rows]
+                middle_ref[slot] = piece[local_rows:]
+                slot += 1
+
+    start = pl.multiple_of(step * block, block)
+    rows = jnp.concatenate([spread_ref[slot, pl.ds(start, block), :] for slot in range(len(slots))], axis=0)
+    core = [[ref[pl.ds(place, block, stride=room), :] for ref in core_refs] for place in slots]
+    core = jnp.concatenate([jnp.concatenate(row, axis=1) for row in core], axis=0)
+    product = fold(mxu(twice(both_parts(rows, 1).T, 1), both_parts(core, 0), NN), 0)
     sum_ref[...] += product
 
     @pl.when(step == pl.num_programs(0) - 1)
     def _():
-        joined_ref[:width, :] = sum_ref[...].T
-        middle = both_parts(middle_ref[...], 1)
-        joined_ref[width:width + columns, :] = fold(fold(mxu(middle, middle, TN), 0), 1)
-        joined_ref[width + columns:, :] = jnp.zeros_like(joined_ref[width + columns:, :])
-
-
-def carry_rows(rank_index, weight, flat_two, pieces, halves, share, band, total):
+        middle = jnp.concatenate([middle_ref[slot] for slot in range(len(slots))], axis=0)
+        middle = both_parts(middle, 1)
+        gram = fold(fold(mxu(middle, middle, TN), 0), 1)
+        if last:
+            out_ref[:width, :] = sum_ref[...].T
+            out_ref[width:width + columns, :] = gram + before_gram_ref[...]
+            out_ref[width + columns:, :] = jnp.zeros_like(out_ref[width + columns:, :])
+        else:
+            out_ref[...] = sum_ref[...]
+            gram_ref[...] = gram
+
+
+def carry_rows(rank_index, weight, flat_two, pieces, places, room, band, before, total):
     rows, width = flat_two.shape
     columns = weight.shape[1]
-    block = block_of(rows)
-    ranks = len(pieces) // len(halves)
-    whole = pl.BlockSpec(memory_space=pltpu.VMEM)
-    return call(
-        functools.partial(carry_kernel, halves, share),
-        8 * flat_two.size * columns,
+    local_rows = rows // room
+    block = math.gcd(local_rows, 32)
+    tiles = max(width // 128, 1)
+    slots = sum(piece.shape[0] for piece in pieces)
+    last = before is not None
+    fixed = [pl.BlockSpec(piece.shape, lambda i: (0, 0, 0)) for piece in pieces]
+    outs = [shape(columns, width), shape(columns, columns)]
+    if last:
+        fixed += [pl.BlockSpec(value.shape, lambda i: (0, 0)) for value in before]
+        outs = [shape(total, columns)]
+    return call(
+        functools.partial(carry_kernel, places, room, last, tiles),
+        8 * slots * local_rows * width * columns,
         4 * flat_two.size + 4 * sum(piece.size for piece in pieces),
-        grid=(rows // block,),
+        grid=(local_rows // block,),
         in_specs=[
             pl.BlockSpec(memory_space=pltpu.SMEM),
             pl.BlockSpec((weight.shape[0], columns), lambda i: (0, 0)),
-            *tiles(block, width),
+            *[pl.BlockSpec((block * room, width // tiles), lambda i, q=q: (i, q)) for q in range(tiles)],
         ]
-        + [pl.BlockSpec(piece.shape, lambda i: (0, 0, 0)) for piece in pieces],
-        out_specs=[
-            pl.BlockSpec((total, columns), lambda i: (0, 0)),
-            pl.BlockSpec((band * share * ranks, columns), lambda i: (0, 0)),
-        ],
-        out_shape=[shape(total, columns), shape(band * share * ranks, columns)],
-        scratch_shapes=[pltpu.VMEM((rows, columns), jnp.float32), pltpu.VMEM((columns, width), jnp.float32)],
-    )(rank_index, weight, *[flat_two] * PARTS, *pieces)
+        + fixed,
+        out_specs=[pl.BlockSpec(out.shape, lambda i: (0, 0)) for out in outs]
+        + [pl.BlockSpec((slots, band, columns), lambda i: (0, 0, 0))],
+        out_shape=outs + [shape(slots, band, columns)],
+        scratch_shapes=[pltpu.VMEM((slots, local_rows, columns), jnp.float32), pltpu.VMEM((columns, width), jnp.float32)],
+    )(rank_index, weight, *[flat_two] * tiles, *pieces, *(before or ()))
 
 
 def apply_kernel(rows_ref, weight_ref, out_ref):
@@ -287,23 +307,24 @@
 def small_inverse(entry):
     size = len(entry)
     entry = [list(row) for row in entry]
+    unit = [[None] * size for _ in range(size)]
+    for k in range(size):
+        scaled = 1.0 / entry[k][k]
+        for i in range(k + 1, size):
+            unit[i][k] = entry[i][k] * scaled
+        for i in range(k + 1, size):
+            for m in range(k + 1, i + 1):
+                entry[i][m] = entry[i][m] - unit[i][k] * entry[m][k]
+    roots = [lax.rsqrt(entry[k][k]) for k in range(size)]
     inverse = [[None] * size for _ in range(size)]
     for k in range(size):
-        pivot = entry[k][k]
-        root = lax.rsqrt(pivot)
-        inverse[k][k] = root
+        inverse[k][k] = 1.0
         for i in range(k + 1, size):
-            entry[i][k] = entry[i][k] * root
-        for i in range(k + 1, size):
-            for m in range(k + 1, i + 1):
-                entry[i][m] = entry[i][m] - entry[i][k] * entry[m][k]
-    for k in range(size):
-        for i in range(k + 1, size):
-            total = entry[i][k] * inverse[k][k]
+            total = unit[i][k]
             for m in range(k + 1, i):
-                total = total + entry[i][m] * inverse[m][k]
-            inverse[i][k] = -total * inverse[i][i]
-    return inverse
+                total = total + unit[i][m] * inverse[m][k]
+            inverse[i][k] = -total
+    return [[inverse[i][k] * roots[i] for k in range(i + 1)] for i in range(size)]
 
 
 def factor(gram, inverse_ref):
@@ -363,27 +384,40 @@
     )(rank_index, bridge, raw)
 
 
-def last_kernel(scale, joined_ref, middle_ref, carry_ref, out_ref, inverse_ref):
+def last_kernel(scale, places, room, rank_ref, joined_ref, *refs):
+    middle_refs = refs[:len(places)]
+    carry_ref, out_ref, inverse_ref = refs[len(places):]
     columns = inverse_ref.shape[0]
     width = carry_ref.shape[1]
     factor(joined_ref[pl.ds(width, columns), :], inverse_ref)
     inverse = inverse_ref[...]
     carry_ref[...] = exact(inverse, joined_ref[pl.ds(0, width), :], NT)
-    out_ref[...] = exact(middle_ref[...], scale * inverse, NT)
-
-
-def last_factor(joined, middle, scale, width):
+    inverse = scale * inverse
+    for ref, group in zip(middle_refs, places):
+        count, band, _ = ref.shape
+        rows = jnp.concatenate([ref[slot] for slot in range(count)], axis=0)
+        rows = exact(rows, inverse, NT)
+        slot = 0
+        for offset, stride, first, pieces in group:
+            for n in range(first, first + pieces):
+                place = (rank_ref[0] ^ offset) * stride + n
+                out_ref[pl.ds(place, band, stride=room), :] = rows[slot * band:(slot + 1) * band]
+                slot += 1
+
+
+def last_factor(rank_index, joined, middles, scale, width, places, room):
     columns = joined.shape[1]
+    band = middles[0].shape[1]
     whole = pl.BlockSpec(memory_space=pltpu.VMEM)
     return call(
-        functools.partial(last_kernel, scale),
-        8 * middle.size * columns,
-        8 * middle.size,
-        in_specs=[whole, whole],
+        functools.partial(last_kernel, scale, places, room),
+        8 * room * band * columns * columns,
+        8 * room * band * columns,
+        in_specs=[pl.BlockSpec(memory_space=pltpu.SMEM), whole] + [whole] * len(middles),
         out_specs=[whole, whole],
-        out_shape=[shape(columns, width), shape(*middle.shape)],
+        out_shape=[shape(columns, width), shape(room * band, columns)],
         scratch_shapes=[pltpu.VMEM((columns, columns), jnp.float32)],
-    )(joined, middle)
+    )(rank_index, joined, *middles)
 
 
 def swap(value, axis, offset):
@@ -454,24 +488,34 @@
     pieces.update(far_piece)
     raw = gather_all(raw, both).reshape(width, columns)
 
-    loose = [loosen(rank_index, raw, [pieces[(half, offset)] for offset in range(ranks)]) for half in range(2)]
-    loose[1], (bridge, raw) = after(loose[1], (bridge, raw))
-    everyone = []
-    for value, order in zip(loose, (bits, bits[::-1])):
-        found = {0: value}
+    ordered = [pieces[(half, offset)] for half in range(2) for offset in range(ranks)]
+    loose = loosen(rank_index, raw, ordered, halves)
+    loose, (bridge, raw) = after(loose, (bridge, raw))
+    groups = [[], []]
+    for half, order in enumerate((bits, bits[::-1])):
+        found = {0: loose[half]}
         for bit in order:
             found.update({offset ^ bit: swap(held, "rank", bit) for offset, held in list(found.items())})
-        everyone += [found[offset] for offset in range(ranks)]
+        for offset, held in found.items():
+            late = offset not in (0, *order[:1])
+            groups[late].append((held, (offset, share, half * halves[0])))
+    groups = [group for group in groups if group]
 
     scale = math.sqrt(local_rows * ranks * slices * cuts)
     weight, solve = first_factor(rank_index, bridge, raw, scale, local_rows, band)
     total = -(-(width + columns) // (BLOCK * parts)) * BLOCK * parts
-    joined, middle = carry_rows(rank_index, weight, flat_two, everyone, halves, share, band, total)
+    joined, middles = None, []
+    for group in groups:
+        held, places = zip(*group)
+        *joined, middle = carry_rows(rank_index, weight, flat_two, held, places, room, band, joined, total)
+        middles.append(middle)
+    joined = joined[0]
     joined = jnp.sum(exchange(joined.reshape(parts, -1, columns), both), axis=0)
     joined = gather_all(joined, both).reshape(total, columns)
     left_core = apply_to(flat_one, solve).reshape(local_rows, slices, columns)
     scale = math.sqrt(columns * slices * cuts)
-    carry, middle = last_factor(joined, middle, scale, width)
+    places = [[(*place, held.shape[0]) for held, place in group] for group in groups]
+    carry, middle = last_factor(rank_index, joined, middles, scale, width, places, room)
     middle_core = middle.reshape(band, room, columns)[:, :slices]
     return (left_core, middle_core, carry)
 

time: 172 us -> 174 us (1.012)
  Pallas kernels: 67.7 us -> 72 us
    pallas_call x3 -> x4, Pallas kernels: 22.1 us -> 28.3 us  [the longest x2 16.8 us: carry_rows(): call(functools.partial(carry_kernel, places, room, last, tiles), 8 * slot...]
    pallas_call x2 -> x1, Pallas kernels: 5.39 us -> 3.51 us  [loosen(): call(loose_kernel, 8 * size * columns, 4 * raw.size + 4 * size, in_specs=...]
    ppermute x12, waiting for transfers between devices: 12.4 us -> 10.7 us  [swap(): lax.ppermute(value, axis, [(i, i ^ offset) for i in range(lax.axis_size(a...]
  transfers between devices with their start and end apart: 16 -> 16, of which waited for: 8 -> 6; matrix products, arithmetic and copies ran while one was open for 1% -> 1% of each run, Pallas kernels for 20% -> 23%
where the time goes in v6:
time: 174 us; the launch traced here: 173 us
  Pallas kernels  72 us (41%)
  starting transfers between devices  31.8 us (18%)
  blocking collectives  31.3 us (18%)
  waiting for transfers between devices  29.8 us (17%)
  local copies, waits for them, and re-layouts  7.6 us (4%)
    all_to_all x2, blocking collectives, exchange(): return lax.all_to_all(value, axes, 0, 0, tiled=True)  31.3 us
    all_to_all x4, waiting for transfers between devices, exchange(): return lax.all_to_all(value, axes, 0, 0, tiled=True)  19.2 us
    ppermute x12, starting transfers between devices, swap(): lax.ppermute(value, axis, [(i, i ^ offset) for i in range(lax.axis_size(a...  16.8 us
    pallas_call x2, Pallas kernels, carry_rows(): call(functools.partial(carry_kernel, places, room, last, tiles), 8 * slot...  16.8 us
    all_to_all x4, starting transfers between devices, exchange(): return lax.all_to_all(value, axes, 0, 0, tiled=True)  14.9 us
    pallas_call x1, Pallas kernels, sketch(): call(sketch_kernel, 2 * core_two.size * columns * 4, 4 * (core_two.size +...  11.5 us
    pallas_call x1, Pallas kernels, square_of(): call(square_kernel, 4 * rows * width * width, 4 * flat_one.size, grid=(ro...  11.1 us
    ppermute x12, waiting for transfers between devices, swap(): lax.ppermute(value, axis, [(i, i ^ offset) for i in range(lax.axis_size(a...  10.7 us
  transfers between devices with their start and end apart: 16, of which 6 were waited for; matrix products, arithmetic and copies ran while one was open for 1% of the time, Pallas kernels for 23%

profile of v6, /device:TPU:0, one launch (start us, length us, event | category | flops | bytes accessed | tf_op | source)
XLA Modules:
  0.0 173.4 jit_solution(8873987856988478158)
XLA Ops:
  0.6 11.5 %shard_map.67 = (f32[40,128,128]{2,1,0:T(8,128)}, f32[128,128]{1,0:T(8,128)}) custom-call(f32[128,40,512]{2,1,0:T(8,128)} %refs_3_.1, f32[128,40,512]{2,1,0:T(8,128)} %refs_3_.1, f32[128,40,512]{2,1,0:T(8,128)} %refs_3_.1, f32[128,40,512]{2,1,0:T(8,128)} %refs_3_.1, f32[512,128]{1,0:T(8,128)} %refs_4_.1, f32[128,40,128]{2,1,0:T(8,128)} %refs_5_.1), custom_call_target="tpu_custom_call" | custom-call | flops 2684354560 | bytes 15728640 | tf_op jit(solution)/shard_map/pallas_call | solution.py:91
  12.1 1.1 constant_dynamic-slice_fusion.6
  13.2 3.0 %collective-permute-start = (f32[5,128,128]{2,1,0:T(8,128)S(1)}, f32[5,128,128]{2,1,0:T(8,128)S(1)}, u32[]{:S(2)}, u32[]{:S(2)}) collective-permute-start(f32[5,128,128]{2,1,0:T(8,128)S(1)} %get-tuple-element.72), channel_id=1, source_target_pairs={{0,1},{1,0},{2,3},{3,2},{4,5},{5,4},{6,7},{7,6},{8,9},{9,8},{10,11... | collective-permute-start | bytes 983048 | tf_op jit(solution)/shard_map/ppermute | solution.py:424
  16.2 1.5 collective-permute-start.1
  17.8 4.9 %all-to-all-start = ((f32[8,16,128]{2,1,0:T(8,128)}), f32[8,16,128]{2,1,0:T(8,128)S(1)}, u32[]{:S(2)}, u32[]{:S(2)}) async-start(f32[8,16,128]{2,1,0:T(8,128)} %bitcast.29), calls=%async_computation | async-start | bytes 131072 | tf_op jit(solution)/shard_map/all_to_all | solution.py:428
  22.6 5.9 %all-to-all-done = f32[8,16,128]{2,1,0:T(8,128)S(1)} async-done(((f32[8,16,128]{2,1,0:T(8,128)}), f32[8,16,128]{2,1,0:T(8,128)S(1)}, u32[]{:S(2)}, u32[]{:S(2)}) %all-to-all-start) | async-done | bytes 65568 | tf_op jit(solution)/shard_map/all_to_all | solution.py:428
  28.6 0.0 collective-permute-done.refs_1_
  28.6 0.0 copy-start.8
  28.6 0.0 collective-permute-done.1.refs_2_
  28.6 0.0 copy-start.9
  28.6 0.8 broadcast_in_dim.6
  29.4 2.6 %all-to-all-start.1 = ((f32[32,16,128]{2,1,0:T(8,128)}), f32[32,16,128]{2,1,0:T(8,128)S(1)}, u32[]{:S(2)}, u32[]{:S(2)}) async-start(f32[32,16,128]{2,1,0:T(8,128)} %broadcast_in_dim.6), calls=%async_computation.1 | async-start | bytes 524288 | tf_op jit(solution)/shard_map/all_to_all | solution.py:428
  32.0 2.5 %constant_dynamic-slice_fusion = (f32[5,128,128]{2,1,0:T(8,128)}, f32[5,128,128]{2,1,0:T(8,128)}, f32[5,128,128]{2,1,0:T(8,128)S(1)}, f32[5,128,128]{2,1,0:T(8,1...) fusion(f32[40,128,128]{2,1,0:T(8,128)} %get-tuple-element.40, s32[]{:T(128)S(6)} %select_n.31, ...), kind=kLoop, calls=%fused_computation | loop fusion | bytes 3932184 | tf_op jit(solution)/shard_map/dynamic_slice | solution.py:463
  34.4 2.6 %collective-permute-start.2 = (f32[5,128,128]{2,1,0:T(8,128)S(1)}, f32[5,128,128]{2,1,0:T(8,128)S(1)}, u32[]{:S(2)}, u32[]{:S(2)}) collective-permute-start(f32[5,128,128]{2,1,0:T(8,128)S(1)} %get-tuple-element.70), channel_id=1, source_target_pairs={{0,3},{1,2},{2,1},{3,0},{4,7},{5,6},{6,5},{7,4},{8,11},{9,10},{10,... | collective-permute-start | bytes 983048 | tf_op jit(solution)/shard_map/ppermute | solution.py:424
  37.0 0.5 collective-permute-start.3
  37.6 0.4 collective-permute-start.4
  37.9 11.1 %shard_map.68.square_ref = bf16[512,1024]{1,0:T(8,128)(2,1)} custom-call(f32[5120,512]{1,0:T(8,128)} %bitcast.19), custom_call_target="tpu_custom_call" | custom-call | flops 5368709120 | bytes 10485760 | tf_op jit(solution)/shard_map/pallas_call | solution.py:137
  49.0 0.0 copy-done.8
  49.0 0.0 copy-done.9
  49.0 0.0 all-to-all-done.1
  49.0 0.0 copy-start
  49.0 0.7 copy-done
  49.7 2.4 %shard_map.69 = f32[512,128]{1,0:T(8,128)} custom-call(bf16[512,1024]{1,0:T(8,128)(2,1)} %shard_map.68.square_ref, f32[512,128]{1,0:T(8,128)} %bitcast.24), custom_call_target="tpu_custom_call" | custom-call | flops 268435456 | bytes 1572864 | tf_op jit(solution)/shard_map/pallas_call | solution.py:155
  52.1 0.0 collective-permute-done.2.refs_3_
  52.1 1.4 collective-permute-done.3.refs_5_
  53.5 0.0 collective-permute-done.4.refs_6_
  53.5 4.6 %all-to-all-start.2 = ((f32[32,16,128]{2,1,0:T(8,128)}), f32[32,16,128]{2,1,0:T(8,128)S(1)}, u32[]{:S(2)}, u32[]{:S(2)}) async-start(f32[32,16,128]{2,1,0:T(8,128)} %bitcast.27), calls=%async_computation.2 | async-start | bytes 524288 | tf_op jit(solution)/shard_map/all_to_all | solution.py:428
  58.2 2.7 %collective-permute-start.5 = (f32[5,128,128]{2,1,0:T(8,128)S(1)}, f32[5,128,128]{2,1,0:T(8,128)S(1)}, u32[]{:S(2)}, u32[]{:S(2)}) collective-permute-start(f32[5,128,128]{2,1,0:T(8,128)S(1)} %get-tuple-element.42), channel_id=1, source_target_pairs={{0,3},{1,2},{2,1},{3,0},{4,7},{5,6},{6,5},{7,4},{8,11},{9,10},{10,... | collective-permute-start | bytes 983048 | tf_op jit(solution)/shard_map/ppermute | solution.py:424
  60.9 8.3 %all-to-all-done.2 = f32[32,16,128]{2,1,0:T(8,128)S(1)} async-done(((f32[32,16,128]{2,1,0:T(8,128)}), f32[32,16,128]{2,1,0:T(8,128)S(1)}, u32[]{:S(2)}, u32[]{:S(2)}) %all-to-all-start.2) | async-done | bytes 262176 | tf_op jit(solution)/shard_map/all_to_all | solution.py:428
  69.2 2.5 %collective-permute-done.5.refs_7_ = f32[5,128,128]{2,1,0:T(8,128)S(1)} collective-permute-done((f32[5,128,128]{2,1,0:T(8,128)S(1)}, f32[5,128,128]{2,1,0:T(8,128)S(1)}, u32[]{:S(2)}, u32[]{:S(2)}) %collective-permute-start.5) | collective-permute-done | bytes 327712 | tf_op jit(solution)/shard_map/ppermute | solution.py:424
  71.8 14.8 %all_to_all.30 = f32[32,16,128]{2,1,0:T(8,128)} all-to-all(f32[32,16,128]{2,1,0:T(8,128)S(1)} %broadcast_in_dim.7), channel_id=1, replica_groups=mesh['cuts'=8,'rank'=4] {'cuts','rank'}, dimensions={0} | all-to-all | bytes 524288 | tf_op jit(solution)/shard_map/all_to_all | solution.py:428
  86.6 0.0 copy-done.10
  86.6 0.0 copy-done.11
  86.6 0.0 copy-done.12
  86.6 0.0 copy-done.13
  86.6 3.5 %shard_map.70 = (f32[5,128,128]{2,1,0:T(8,128)}, f32[5,128,128]{2,1,0:T(8,128)}) custom-call(s32[1]{0:T(128)} %bitcast.1.rank_ref, f32[512,128]{1,0:T(8,128)} %bitcast.22, f32[5,128,128]{2,1,0:T(8,128)} %get-tuple-element.66.refs_0_, f32[5,128,128]{2,1,0:T(8,128)} %copy-done.8, f32[5,128,128]{2,1,0:T(8,128)} %copy-done.9, f32[5,128,128]{2,1,0:T(8,128)} %copy-done.10, ...), custom_call_target="tpu_custom_call" | custom-call | flops 671088640 | bytes 2883584 | tf_op jit(solution)/shard_map/pallas_call | solution.py:185
  90.1 0.0 collective-permute-start.10
  90.2 1.4 collective-permute-start.7
  91.5 0.6 collective-permute-start.6
  92.2 2.0 %collective-permute-start.9 = (f32[5,128,128]{2,1,0:T(8,128)}, f32[5,128,128]{2,1,0:T(8,128)S(1)}, u32[]{:S(2)}, u32[]{:S(2)}) collective-permute-start(f32[5,128,128]{2,1,0:T(8,128)} %get-tuple-element.57.refs_6_), channel_id=1, source_target_pairs={{0,1},{1,0},{2,3},{3,2},{4,5},{5,4},{6,7},{7,6},{8,9},{9,8},{10,11... | collective-permute-start | bytes 983048 | tf_op jit(solution)/shard_map/ppermute | solution.py:424
  94.2 6.8 %collective-permute-done.10.refs_7_ = f32[5,128,128]{2,1,0:T(8,128)S(1)} collective-permute-done((f32[5,128,128]{2,1,0:T(8,128)}, f32[5,128,128]{2,1,0:T(8,128)S(1)}, u32[]{:S(2)}, u32[]{:S(2)}) %collective-permute-start.10) | collective-permute-done | bytes 327712 | tf_op jit(solution)/shard_map/ppermute | solution.py:424
  101.0 0.0 collective-permute-start.11
  101.0 0.0 collective-permute-done.7.refs_5_
  101.0 0.0 copy-start.4
  101.0 2.0 %collective-permute-start.8 = (f32[5,128,128]{2,1,0:T(8,128)S(1)}, f32[5,128,128]{2,1,0:T(8,128)S(1)}, u32[]{:S(2)}, u32[]{:S(2)}) collective-permute-start(f32[5,128,128]{2,1,0:T(8,128)S(1)} %collective-permute-done.7.refs_5_), channel_id=1, source_target_pairs={{0,2},{1,3},{2,0},{3,1},{4,6},{5,7},{6,4},{7,5},{8,10},{9,11},{10,... | collective-permute-start | bytes 983048 | tf_op jit(solution)/shard_map/ppermute | solution.py:424
  103.0 9.2 %shard_map.71 = (f32[160,128]{1,0:T(8,128)}, f32[512,128]{1,0:T(8,128)}) custom-call(s32[1]{0:T(128)} %bitcast.1.rank_ref, f32[512,128]{1,0:T(8,128)} %bitcast.25, f32[512,128]{1,0:T(8,128)} %bitcast.23), custom_call_target="tpu_custom_call" | custom-call | flops 67108864 | bytes 1048576 | tf_op jit(solution)/shard_map/pallas_call | solution.py:376
  112.2 8.3 %shard_map.73 = (f32[128,512]{1,0:T(8,128)}, f32[128,128]{1,0:T(8,128)}, f32[20,32,128]{2,1,0:T(8,128)}) custom-call(s32[1]{0:T(128)} %bitcast.1.rank_ref, f32[160,128]{1,0:T(8,128)} %get-tuple-element.55.weight_ref, f32[5120,512]{1,0:T(8,128)} %bitcast.11, f32[5120,512]{1,0:T(8,128)} %bitcast.12, f32[5120,512]{1,0:T(8,128)} %bitcast.13, ...), custom_call_target="tpu_custom_call" | custom-call | flops 1342177280 | bytes 11796480 | tf_op jit(solution)/shard_map/pallas_call | solution.py:266
  120.6 0.0 collective-permute-done.6.refs_4_
  120.6 0.0 copy-start.2
  120.6 0.0 collective-permute-done.9.refs_6_
  120.6 0.0 collective-permute-done.11.refs_7_
  120.6 0.0 collective-permute-done.8.refs_5_
  120.6 0.7 copy-done.2
  121.3 0.1 copy-done.5
  121.4 0.1 copy-done.6
  121.5 0.1 copy-done.7
  121.6 8.4 %shard_map.74 = (f32[768,128]{1,0:T(8,128)}, f32[20,32,128]{2,1,0:T(8,128)}) custom-call(s32[1]{0:T(128)} %bitcast.1.rank_ref, f32[160,128]{1,0:T(8,128)} %get-tuple-element.55.weight_ref, f32[5120,512]{1,0:T(8,128)} %bitcast.15, f32[5120,512]{1,0:T(8,128)} %bitcast.16, f32[5120,512]{1,0:T(8,128)} %bitcast.17, f32[5120,512]{1,0:T(8,128)} %bitcast.18, ...), custom_call_target="tpu_custom_call" | custom-call | flops 1342177280 | bytes 11796480 | tf_op jit(solution)/shard_map/pallas_call | solution.py:266
  130.1 16.4 %all_to_all.31 = f32[32,24,128]{2,1,0:T(8,128)S(1)} all-to-all(f32[32,24,128]{2,1,0:T(8,128)} %bitcast.28), channel_id=1, replica_groups=mesh['cuts'=8,'rank'=4] {'cuts','rank'}, dimensions={0} | all-to-all | bytes 786432 | tf_op jit(solution)/shard_map/all_to_all | solution.py:428
  146.5 0.8 broadcast_in_dim.8
  147.3 2.8 %all-to-all-start.5 = ((f32[32,24,128]{2,1,0:T(8,128)}), f32[32,24,128]{2,1,0:T(8,128)S(1)}, u32[]{:S(2)}, u32[]{:S(2)}) async-start(f32[32,24,128]{2,1,0:T(8,128)} %broadcast_in_dim.8), calls=%async_computation.5 | async-start | bytes 786432 | tf_op jit(solution)/shard_map/all_to_all | solution.py:428
  150.1 8.5 %shard_map.72 = f32[5120,128]{1,0:T(8,128)} custom-call(f32[5120,512]{1,0:T(8,128)} %bitcast.20, f32[512,128]{1,0:T(8,128)} %get-tuple-element.54.weight_ref), custom_call_target="tpu_custom_call" | custom-call | flops 2684354560 | bytes 13107200 | tf_op jit(solution)/shard_map/pallas_call | solution.py:293
  158.6 4.9 %all-to-all-done.5 = f32[32,24,128]{2,1,0:T(8,128)S(1)} async-done(((f32[32,24,128]{2,1,0:T(8,128)}), f32[32,24,128]{2,1,0:T(8,128)S(1)}, u32[]{:S(2)}, u32[]{:S(2)}) %all-to-all-start.5) | async-done | bytes 393248 | tf_op jit(solution)/shard_map/all_to_all | solution.py:428
  163.5 0.7 copy-done.1
  164.3 9.1 %shard_map.75 = (f32[128,512]{1,0:T(8,128)}, f32[1280,128]{1,0:T(8,128)}) custom-call(s32[1]{0:T(128)} %bitcast.1.rank_ref, f32[768,128]{1,0:T(8,128)} %bitcast.26, f32[20,32,128]{2,1,0:T(8,128)} %get-tuple-element.61.refs_0_, f32[20,32,128]{2,1,0:T(8,128)} %get-tuple-element.62.refs_1_), custom_call_target="tpu_custom_call" | custom-call | flops 167772160 | bytes 1310720 | tf_op jit(solution)/shard_map/pallas_call | solution.py:412
  (15 shorter events, 0.1 us)
Async XLA Ops:
  13.2 15.3 %collective-permute-start = (f32[5,128,128]{2,1,0:T(8,128)S(1)}, f32[5,128,128]{2,1,0:T(8,128)S(1)}, u32[]{:S(2)}, u32[]{:S(2)}) collective-permute-start(f32[5,128,128]{2,1,0:T(8,128)S(1)} %get-tuple-element.72), channel_id=1, source_target_pairs={{0,1},{1,0},{2,3},{3,2},{4,5},{5,4},{6,7},{7,6},{8,9},{9,8},{10,11... | collective-permute-start | bytes 983048 | tf_op jit(solution)/shard_map/ppermute | solution.py:424
  16.2 12.4 %collective-permute-start.1 = (f32[5,128,128]{2,1,0:T(8,128)S(1)}, f32[5,128,128]{2,1,0:T(8,128)S(1)}, u32[]{:S(2)}, u32[]{:S(2)}) collective-permute-start(f32[5,128,128]{2,1,0:T(8,128)S(1)} %get-tuple-element.71), channel_id=1, source_target_pairs={{0,2},{1,3},{2,0},{3,1},{4,6},{5,7},{6,4},{7,5},{8,10},{9,11},{10,... | collective-permute-start | bytes 983048 | tf_op jit(solution)/shard_map/ppermute | solution.py:424
  17.8 10.8 %all-to-all-start = ((f32[8,16,128]{2,1,0:T(8,128)}), f32[8,16,128]{2,1,0:T(8,128)S(1)}, u32[]{:S(2)}, u32[]{:S(2)}) async-start(f32[8,16,128]{2,1,0:T(8,128)} %bitcast.29), calls=%async_computation | async-start | bytes 131072 | tf_op jit(solution)/shard_map/all_to_all | solution.py:428
  28.6 20.4 %copy-start.8 = (f32[5,128,128]{2,1,0:T(8,128)}, f32[5,128,128]{2,1,0:T(8,128)S(1)}, u32[]{:S(2)}) copy-start(f32[5,128,128]{2,1,0:T(8,128)S(1)} %collective-permute-done.refs_1_) | copy-start | bytes 983044
  28.6 20.4 %copy-start.9 = (f32[5,128,128]{2,1,0:T(8,128)}, f32[5,128,128]{2,1,0:T(8,128)S(1)}, u32[]{:S(2)}) copy-start(f32[5,128,128]{2,1,0:T(8,128)S(1)} %collective-permute-done.1.refs_2_) | copy-start | bytes 983044
  29.4 19.6 %all-to-all-start.1 = ((f32[32,16,128]{2,1,0:T(8,128)}), f32[32,16,128]{2,1,0:T(8,128)S(1)}, u32[]{:S(2)}, u32[]{:S(2)}) async-start(f32[32,16,128]{2,1,0:T(8,128)} %broadcast_in_dim.6), calls=%async_computation.1 | async-start | bytes 524288 | tf_op jit(solution)/shard_map/all_to_all | solution.py:428
  34.4 17.7 %collective-permute-start.2 = (f32[5,128,128]{2,1,0:T(8,128)S(1)}, f32[5,128,128]{2,1,0:T(8,128)S(1)}, u32[]{:S(2)}, u32[]{:S(2)}) collective-permute-start(f32[5,128,128]{2,1,0:T(8,128)S(1)} %get-tuple-element.70), channel_id=1, source_target_pairs={{0,3},{1,2},{2,1},{3,0},{4,7},{5,6},{6,5},{7,4},{8,11},{9,10},{10,... | collective-permute-start | bytes 983048 | tf_op jit(solution)/shard_map/ppermute | solution.py:424
  37.0 16.5 %collective-permute-start.3 = (f32[5,128,128]{2,1,0:T(8,128)S(1)}, f32[5,128,128]{2,1,0:T(8,128)S(1)}, u32[]{:S(2)}, u32[]{:S(2)}) collective-permute-start(f32[5,128,128]{2,1,0:T(8,128)S(1)} %get-tuple-element.69), channel_id=1, source_target_pairs={{0,1},{1,0},{2,3},{3,2},{4,5},{5,4},{6,7},{7,6},{8,9},{9,8},{10,11... | collective-permute-start | bytes 983048 | tf_op jit(solution)/shard_map/ppermute | solution.py:424
  37.6 15.9 %collective-permute-start.4 = (f32[5,128,128]{2,1,0:T(8,128)S(1)}, f32[5,128,128]{2,1,0:T(8,128)S(1)}, u32[]{:S(2)}, u32[]{:S(2)}) collective-permute-start(f32[5,128,128]{2,1,0:T(8,128)S(1)} %get-tuple-element.68), channel_id=1, source_target_pairs={{0,2},{1,3},{2,0},{3,1},{4,6},{5,7},{6,4},{7,5},{8,10},{9,11},{10,... | collective-permute-start | bytes 983048 | tf_op jit(solution)/shard_map/ppermute | solution.py:424
  49.0 0.7 copy-start
  52.1 34.5 %copy-start.10 = (f32[5,128,128]{2,1,0:T(8,128)}, f32[5,128,128]{2,1,0:T(8,128)S(1)}, u32[]{:S(2)}) copy-start(f32[5,128,128]{2,1,0:T(8,128)S(1)} %collective-permute-done.2.refs_3_) | copy-start | bytes 983044
  53.5 33.1 %copy-start.11 = (f32[5,128,128]{2,1,0:T(8,128)}, f32[5,128,128]{2,1,0:T(8,128)S(1)}, u32[]{:S(2)}) copy-start(f32[5,128,128]{2,1,0:T(8,128)S(1)} %collective-permute-done.3.refs_5_) | copy-start | bytes 983044
  53.5 33.1 %copy-start.12 = (f32[5,128,128]{2,1,0:T(8,128)}, f32[5,128,128]{2,1,0:T(8,128)S(1)}, u32[]{:S(2)}) copy-start(f32[5,128,128]{2,1,0:T(8,128)S(1)} %collective-permute-done.4.refs_6_) | copy-start | bytes 983044
  53.5 15.7 %all-to-all-start.2 = ((f32[32,16,128]{2,1,0:T(8,128)}), f32[32,16,128]{2,1,0:T(8,128)S(1)}, u32[]{:S(2)}, u32[]{:S(2)}) async-start(f32[32,16,128]{2,1,0:T(8,128)} %bitcast.27), calls=%async_computation.2 | async-start | bytes 524288 | tf_op jit(solution)/shard_map/all_to_all | solution.py:428
  58.2 13.6 %collective-permute-start.5 = (f32[5,128,128]{2,1,0:T(8,128)S(1)}, f32[5,128,128]{2,1,0:T(8,128)S(1)}, u32[]{:S(2)}, u32[]{:S(2)}) collective-permute-start(f32[5,128,128]{2,1,0:T(8,128)S(1)} %get-tuple-element.42), channel_id=1, source_target_pairs={{0,3},{1,2},{2,1},{3,0},{4,7},{5,6},{6,5},{7,4},{8,11},{9,10},{10,... | collective-permute-start | bytes 983048 | tf_op jit(solution)/shard_map/ppermute | solution.py:424
  71.7 14.9 %copy-start.13 = (f32[5,128,128]{2,1,0:T(8,128)}, f32[5,128,128]{2,1,0:T(8,128)S(1)}, u32[]{:S(2)}) copy-start(f32[5,128,128]{2,1,0:T(8,128)S(1)} %collective-permute-done.5.refs_7_) | copy-start | bytes 983044
  90.1 10.9 %collective-permute-start.10 = (f32[5,128,128]{2,1,0:T(8,128)}, f32[5,128,128]{2,1,0:T(8,128)S(1)}, u32[]{:S(2)}, u32[]{:S(2)}) collective-permute-start(f32[5,128,128]{2,1,0:T(8,128)} %get-tuple-element.57.refs_6_), channel_id=1, source_target_pairs={{0,2},{1,3},{2,0},{3,1},{4,6},{5,7},{6,4},{7,5},{8,10},{9,11},{10,... | collective-permute-start | bytes 983048 | tf_op jit(solution)/shard_map/ppermute | solution.py:424
  90.2 10.9 %collective-permute-start.7 = (f32[5,128,128]{2,1,0:T(8,128)}, f32[5,128,128]{2,1,0:T(8,128)S(1)}, u32[]{:S(2)}, u32[]{:S(2)}) collective-permute-start(f32[5,128,128]{2,1,0:T(8,128)} %get-tuple-element.56.refs_4_), channel_id=1, source_target_pairs={{0,1},{1,0},{2,3},{3,2},{4,5},{5,4},{6,7},{7,6},{8,9},{9,8},{10,11... | collective-permute-start | bytes 983048 | tf_op jit(solution)/shard_map/ppermute | solution.py:424
  91.5 29.0 %collective-permute-start.6 = (f32[5,128,128]{2,1,0:T(8,128)}, f32[5,128,128]{2,1,0:T(8,128)S(1)}, u32[]{:S(2)}, u32[]{:S(2)}) collective-permute-start(f32[5,128,128]{2,1,0:T(8,128)} %get-tuple-element.56.refs_4_), channel_id=1, source_target_pairs={{0,2},{1,3},{2,0},{3,1},{4,6},{5,7},{6,4},{7,5},{8,10},{9,11},{10,... | collective-permute-start | bytes 983048 | tf_op jit(solution)/shard_map/ppermute | solution.py:424
  92.2 28.4 %collective-permute-start.9 = (f32[5,128,128]{2,1,0:T(8,128)}, f32[5,128,128]{2,1,0:T(8,128)S(1)}, u32[]{:S(2)}, u32[]{:S(2)}) collective-permute-start(f32[5,128,128]{2,1,0:T(8,128)} %get-tuple-element.57.refs_6_), channel_id=1, source_target_pairs={{0,1},{1,0},{2,3},{3,2},{4,5},{5,4},{6,7},{7,6},{8,9},{9,8},{10,11... | collective-permute-start | bytes 983048 | tf_op jit(solution)/shard_map/ppermute | solution.py:424
  101.0 11.2 %copy-start.3 = (f32[5,128,128]{2,1,0:T(8,128)}, f32[5,128,128]{2,1,0:T(8,128)S(1)}, u32[]{:S(2)}) copy-start(f32[5,128,128]{2,1,0:T(8,128)S(1)} %collective-permute-done.10.refs_7_) | copy-start | bytes 983044
  101.0 19.6 %collective-permute-start.11 = (f32[5,128,128]{2,1,0:T(8,128)S(1)}, f32[5,128,128]{2,1,0:T(8,128)S(1)}, u32[]{:S(2)}, u32[]{:S(2)}) collective-permute-start(f32[5,128,128]{2,1,0:T(8,128)S(1)} %collective-permute-done.10.refs_7_), channel_id=1, source_target_pairs={{0,1},{1,0},{2,3},{3,2},{4,5},{5,4},{6,7},{7,6},{8,9},{9,8},{10,11... | collective-permute-start | bytes 983048 | tf_op jit(solution)/shard_map/ppermute | solution.py:424
  101.0 11.2 %copy-start.4 = (f32[5,128,128]{2,1,0:T(8,128)}, f32[5,128,128]{2,1,0:T(8,128)S(1)}, u32[]{:S(2)}) copy-start(f32[5,128,128]{2,1,0:T(8,128)S(1)} %collective-permute-done.7.refs_5_) | copy-start | bytes 983044
  101.0 19.6 %collective-permute-start.8 = (f32[5,128,128]{2,1,0:T(8,128)S(1)}, f32[5,128,128]{2,1,0:T(8,128)S(1)}, u32[]{:S(2)}, u32[]{:S(2)}) collective-permute-start(f32[5,128,128]{2,1,0:T(8,128)S(1)} %collective-permute-done.7.refs_5_), channel_id=1, source_target_pairs={{0,2},{1,3},{2,0},{3,1},{4,6},{5,7},{6,4},{7,5},{8,10},{9,11},{10,... | collective-permute-start | bytes 983048 | tf_op jit(solution)/shard_map/ppermute | solution.py:424
  120.6 0.7 copy-start.2
  120.6 0.8 copy-start.5
  120.6 0.9 copy-start.6
  120.6 1.0 copy-start.7
  147.3 16.2 %all-to-all-start.5 = ((f32[32,24,128]{2,1,0:T(8,128)}), f32[32,24,128]{2,1,0:T(8,128)S(1)}, u32[]{:S(2)}, u32[]{:S(2)}) async-start(f32[32,24,128]{2,1,0:T(8,128)} %broadcast_in_dim.8), calls=%async_computation.5 | async-start | bytes 786432 | tf_op jit(solution)/shard_map/all_to_all | solution.py:428
  163.5 0.7 copy-start.1

commit v7 on v5

--- a/solution.py
+++ b/solution.py
@@ -137,7 +137,7 @@
     @pl.when(step == pl.num_programs(0) - 1)
     def _():
         cross = sum_ref[:, width:]
-        square_ref[...] = sum_ref[:, :width] + cross + cross.T
+        square_ref[...] = both_parts(sum_ref[:, :width] + cross + cross.T, 1)
 
 
 def square_of(flat_one):
@@ -149,57 +149,61 @@
         4 * flat_one.size,
         grid=(rows // block,),
         in_specs=[pl.BlockSpec((block, width), lambda i: (i, 0))],
-        out_specs=pl.BlockSpec((width, width), lambda i: (0, 0)),
-        out_shape=shape(width, width),
+        out_specs=pl.BlockSpec((width, 2 * width), lambda i: (0, 0)),
+        out_shape=jax.ShapeDtypeStruct((width, 2 * width), jnp.bfloat16),
         scratch_shapes=[pltpu.VMEM((width, 2 * width), jnp.float32)],
     )(flat_one)
 
 
 def product_kernel(square_ref, bridge_ref, out_ref):
     bridge = twice(both_parts(bridge_ref[...], 1), 0)
-    out_ref[...] = fold(mxu(both_parts(square_ref[...], 1), bridge, NN), 1)
+    out_ref[...] = fold(mxu(square_ref[...], bridge, NN), 1)
 
 
 def product_of(square, bridge):
     return call(
         product_kernel,
-        8 * square.size * bridge.shape[1],
-        4 * square.size + 8 * bridge.size,
+        4 * square.size * bridge.shape[1],
+        2 * square.size + 8 * bridge.size,
         out_shape=shape(*bridge.shape),
     )(square, bridge)
 
 
 def loose_kernel(rank_ref, raw_ref, *refs):
-    piece_refs, out_ref = refs[:-1], refs[-1]
-    count, local_rows, columns = piece_refs[0].shape
+    piece_refs, out_refs = refs[:-2], refs[-2:]
+    ranks = len(piece_refs) // 2
+    local_rows, columns = piece_refs[0].shape[1:]
     rows = []
-    for offset in range(len(piece_refs)):
+    for offset in range(ranks):
         start = pl.multiple_of((rank_ref[0] ^ offset) * local_rows, local_rows)
         rows.append(raw_ref[pl.ds(start, local_rows), :])
     raw = twice(both_parts(jnp.concatenate(rows, axis=0), 1).T, 1)
-    value = [jnp.concatenate([ref[n] for n in range(count)], axis=1) for ref in piece_refs]
-    product = fold(mxu(raw, both_parts(jnp.concatenate(value, axis=0), 0), NN), 0)
-    for n in range(count):
-        out_ref[n] = product[:, n * columns:(n + 1) * columns]
-
-
-def loosen(rank_index, raw, pieces):
+    for half, out_ref in enumerate(out_refs):
+        refs = piece_refs[half * ranks:(half + 1) * ranks]
+        count = out_ref.shape[0]
+        value = [jnp.concatenate([ref[n] for n in range(count)], axis=1) for ref in refs]
+        product = fold(mxu(raw, both_parts(jnp.concatenate(value, axis=0), 0), NN), 0)
+        for n in range(count):
+            out_ref[n] = product[:, n * columns:(n + 1) * columns]
+
+
+def loosen(rank_index, raw, pieces, halves):
     columns = raw.shape[1]
-    size = len(pieces) * pieces[0].size
+    size = sum(piece.size for piece in pieces)
     whole = pl.BlockSpec(memory_space=pltpu.VMEM)
     return call(
         loose_kernel,
         8 * size * columns,
         4 * raw.size + 4 * size,
         in_specs=[pl.BlockSpec(memory_space=pltpu.SMEM)] + [whole] * (len(pieces) + 1),
-        out_specs=whole,
-        out_shape=shape(pieces[0].shape[0], columns, columns),
+        out_specs=[whole] * 2,
+        out_shape=[shape(count, columns, columns) for count in halves],
     )(rank_index, raw, *pieces)
 
 
 def carry_kernel(halves, share, rank_ref, weight_ref, *refs):
-    core_refs, piece_refs = refs[:PARTS], refs[PARTS:-4]
-    joined_ref, middle_ref, rows_ref, sum_ref = refs[-4:]
+    core_refs, piece_refs = refs[:PARTS], refs[PARTS:-5]
+    raw_ref, gram_ref, middle_ref, rows_ref, sum_ref = refs[-5:]
     step = pl.program_id(0)
     block, width = core_refs[0].shape[0] * PARTS, core_refs[0].shape[1]
     columns = weight_ref.shape[1]
@@ -229,13 +233,12 @@
 
     @pl.when(step == pl.num_programs(0) - 1)
     def _():
-        joined_ref[:width, :] = sum_ref[...].T
+        raw_ref[...] = sum_ref[...].T
         middle = both_parts(middle_ref[...], 1)
-        joined_ref[width:width + columns, :] = fold(fold(mxu(middle, middle, TN), 0), 1)
-        joined_ref[width + columns:, :] = jnp.zeros_like(joined_ref[width + columns:, :])
-
-
-def carry_rows(rank_index, weight, flat_two, pieces, halves, share, band, total):
+        gram_ref[...] = fold(fold(mxu(middle, middle, TN), 0), 1)
+
+
+def carry_rows(rank_index, weight, flat_two, pieces, halves, share, band):
     rows, width = flat_two.shape
     columns = weight.shape[1]
     block = block_of(rows)
@@ -253,10 +256,11 @@
         ]
         + [pl.BlockSpec(piece.shape, lambda i: (0, 0, 0)) for piece in pieces],
         out_specs=[
-            pl.BlockSpec((total, columns), lambda i: (0, 0)),
+            pl.BlockSpec((width, columns), lambda i: (0, 0)),
+            pl.BlockSpec((columns, columns), lambda i: (0, 0)),
             pl.BlockSpec((band * share * ranks, columns), lambda i: (0, 0)),
         ],
-        out_shape=[shape(total, columns), shape(band * share * ranks, columns)],
+        out_shape=[shape(width, columns), shape(columns, columns), shape(band * share * ranks, columns)],
         scratch_shapes=[pltpu.VMEM((rows, columns), jnp.float32), pltpu.VMEM((columns, width), jnp.float32)],
     )(rank_index, weight, *[flat_two] * PARTS, *pieces)
 
@@ -363,17 +367,13 @@
     )(rank_index, bridge, raw)
 
 
-def last_kernel(scale, joined_ref, middle_ref, carry_ref, out_ref, inverse_ref):
-    columns = inverse_ref.shape[0]
-    width = carry_ref.shape[1]
-    factor(joined_ref[pl.ds(width, columns), :], inverse_ref)
-    inverse = inverse_ref[...]
-    carry_ref[...] = exact(inverse, joined_ref[pl.ds(0, width), :], NT)
-    out_ref[...] = exact(middle_ref[...], scale * inverse, NT)
-
-
-def last_factor(joined, middle, scale, width):
-    columns = joined.shape[1]
+def last_kernel(scale, gram_ref, middle_ref, inverse_ref, out_ref):
+    factor(gram_ref[...], inverse_ref)
+    out_ref[...] = exact(middle_ref[...], scale * inverse_ref[...], NT)
+
+
+def last_factor(gram, middle, scale):
+    columns = gram.shape[0]
     whole = pl.BlockSpec(memory_space=pltpu.VMEM)
     return call(
         functools.partial(last_kernel, scale),
@@ -381,9 +381,8 @@
         8 * middle.size,
         in_specs=[whole, whole],
         out_specs=[whole, whole],
-        out_shape=[shape(columns, width), shape(*middle.shape)],
-        scratch_shapes=[pltpu.VMEM((columns, columns), jnp.float32)],
-    )(joined, middle)
+        out_shape=[shape(columns, columns), shape(*middle.shape)],
+    )(gram, middle)
 
 
 def swap(value, axis, offset):
@@ -434,44 +433,52 @@
     far = ranks - 1
     near = [[(half, offset) for offset in range(1, far)] for half in range(2)]
 
+    cut_bits = [1 << bit for bit in range((cuts - 1).bit_length())]
     bits = [1 << bit for bit in range((ranks - 1).bit_length())]
-    moved = send(near[0], sketched, None)
+    first = send(near[0], sketched, None)
     bridge_rows = jnp.sum(exchange(part.reshape(cuts, local_rows // cuts, columns), "cuts"), axis=0)
-    bridge_rows, pieces = after(bridge_rows, moved)
-    flat_late, bridge_rows = after(flat_one, bridge_rows)
+    flat_late, (bridge_rows, pieces) = after(flat_one, (bridge_rows, first))
     sketched, bridge_rows = after(sketched, bridge_rows)
     moved = send(near[1] + [(0, far)], sketched, None)
     bridge = gather_all(bridge_rows, ("rank", "cuts")).reshape(width, columns)
     square = square_of(flat_late)
-    pieces.update(send([(0, 0), (1, 0)], sketched, None))
 
     raw = product_of(square, bridge)
     raw, moved = after(raw, moved)
     pieces.update(moved)
-    far_piece = send([(1, far)], sketched, raw)
+    sketched, raw = after(sketched, raw)
+    pieces.update(send([(0, 0), (1, 0)], sketched, None))
     raw = jnp.sum(exchange(raw.reshape(parts, -1, columns), both), axis=0)
-    raw, far_piece = after(raw, far_piece)
-    pieces.update(far_piece)
+    pieces.update(send([(1, far)], sketched, raw))
     raw = gather_all(raw, both).reshape(width, columns)
 
-    loose = [loosen(rank_index, raw, [pieces[(half, offset)] for offset in range(ranks)]) for half in range(2)]
-    loose[1], (bridge, raw) = after(loose[1], (bridge, raw))
-    everyone = []
-    for value, order in zip(loose, (bits, bits[::-1])):
-        found = {0: value}
-        for bit in order:
-            found.update({offset ^ bit: swap(held, "rank", bit) for offset, held in list(found.items())})
-        everyone += [found[offset] for offset in range(ranks)]
-
+    ordered = [pieces[(half, offset)] for half in range(2) for offset in range(ranks)]
+    loose = loosen(rank_index, raw, ordered, halves)
+    loose, (bridge, raw) = after(loose, (bridge, raw))
     scale = math.sqrt(local_rows * ranks * slices * cuts)
     weight, solve = first_factor(rank_index, bridge, raw, scale, local_rows, band)
-    total = -(-(width + columns) // (BLOCK * parts)) * BLOCK * parts
-    joined, middle = carry_rows(rank_index, weight, flat_two, everyone, halves, share, band, total)
-    joined = jnp.sum(exchange(joined.reshape(parts, -1, columns), both), axis=0)
-    joined = gather_all(joined, both).reshape(total, columns)
+    everyone = []
+    for half, order in enumerate((bits, bits[::-1])):
+        found = {0: loose[half]}
+        for bit in order:
+            moved = {bit: swap(found[0], "rank", bit)}
+            if len(found) > 1:
+                late, weight = after({offset: found[offset] for offset in found if offset}, weight)
+                moved.update({offset ^ bit: swap(held, "rank", bit) for offset, held in late.items()})
+            found.update(moved)
+        everyone += [found[offset] for offset in range(ranks)]
+
     left_core = apply_to(flat_one, solve).reshape(local_rows, slices, columns)
+    weight, left_core = after(weight, left_core)
+    raw, gram, middle = carry_rows(rank_index, weight, flat_two, everyone, halves, share, band)
+    raw = jnp.sum(exchange(raw.reshape(parts, -1, columns), both), axis=0)
+    for axis, bit in [("cuts", 1)] + [("rank", bit) for bit in bits] + [("cuts", bit) for bit in cut_bits[1:]]:
+        gram = gram + swap(gram, axis, bit)
+    raw, gram = after(raw, gram)
+    raw = gather_all(raw, both).reshape(width, columns)
     scale = math.sqrt(columns * slices * cuts)
-    carry, middle = last_factor(joined, middle, scale, width)
+    inverse, middle = last_factor(gram, middle, scale)
+    carry = exact(inverse, raw, NT)
     middle_core = middle.reshape(band, room, columns)[:, :slices]
     return (left_core, middle_core, carry)
 

time: 172 us -> 173 us (level)
  blocking collectives: 31.4 us -> 15.4 us
  starting transfers between devices: 31.8 us -> 46.1 us
  Pallas kernels: 67.7 us -> 65.5 us
  matrix products: 0 us -> 1.92 us
    all_to_all x2 -> x1, blocking collectives: 31.4 us -> 15.4 us  [exchange(): return lax.all_to_all(value, axes, 0, 0, tiled=True)]
    all_to_all x4 -> x5, waiting for transfers between devices: 19.1 us -> 7.85 us  [exchange(): return lax.all_to_all(value, axes, 0, 0, tiled=True)]
    ppermute x12 -> x17, waiting for transfers between devices: 12.4 us -> 23.5 us  [swap(): lax.ppermute(value, axis, [(i, i ^ offset) for i in range(lax.axis_size(a...]
    ppermute x12 -> x17, starting transfers between devices: 16.9 us -> 25.6 us  [swap(): lax.ppermute(value, axis, [(i, i ^ offset) for i in range(lax.axis_size(a...]
    all_to_all x4 -> x5, starting transfers between devices: 14.9 us -> 20.5 us  [exchange(): return lax.all_to_all(value, axes, 0, 0, tiled=True)]
    dot_general x0 -> x1, matrix products: none -> 1.92 us  [exact(): lax.dot_general(a, b, form, precision=lax.Precision.HIGHEST, preferred_el...]
    pallas_call x2 -> x1, Pallas kernels: 5.39 us -> 3.48 us  [loosen(): call(loose_kernel, 8 * size * columns, 4 * raw.size + 4 * size, in_specs=...]
    dynamic_slice x2 -> x3, local copies, waits for them, and re-layouts: 3.58 us -> 4.47 us  [send(): found.append(lax.dynamic_slice_in_dim(source, start, halves[half], 0))]
  transfers between devices with their start and end apart: 16 -> 22, of which waited for: 8 -> 11; matrix products, arithmetic and copies ran while one was open for 1% -> 3% of each run, Pallas kernels for 20% -> 23%
where the time goes in v7:
time: 173 us; the launch traced here: 172 us
  Pallas kernels  65.5 us (38%)
  starting transfers between devices  46.1 us (27%)
  waiting for transfers between devices  31.3 us (18%)
  blocking collectives  15.4 us (9%)
  local copies, waits for them, and re-layouts  9.09 us (5%)
  matrix products  1.92 us (1%)
    ppermute x17, starting transfers between devices, swap(): lax.ppermute(value, axis, [(i, i ^ offset) for i in range(lax.axis_size(a...  25.6 us
    ppermute x17, waiting for transfers between devices, swap(): lax.ppermute(value, axis, [(i, i ^ offset) for i in range(lax.axis_size(a...  23.5 us
    all_to_all x5, starting transfers between devices, exchange(): return lax.all_to_all(value, axes, 0, 0, tiled=True)  20.5 us
    all_to_all x1, blocking collectives, exchange(): return lax.all_to_all(value, axes, 0, 0, tiled=True)  15.4 us
    pallas_call x1, Pallas kernels, sketch(): call(sketch_kernel, 2 * core_two.size * columns * 4, 4 * (core_two.size +...  11.5 us
    pallas_call x1, Pallas kernels, square_of(): call(square_kernel, 4 * rows * width * width, 4 * flat_one.size, grid=(ro...  11.1 us
    pallas_call x1, Pallas kernels, carry_rows(): call(functools.partial(carry_kernel, halves, share), 8 * flat_two.size *...  10.6 us
    pallas_call x1, Pallas kernels, first_factor(): call(functools.partial(first_kernel, scale, band), 8 * raw.size * columns...  9.18 us
  transfers between devices with their start and end apart: 22, of which 11 were waited for; matrix products, arithmetic and copies ran while one was open for 3% of the time, Pallas kernels for 23%

profile of v7, /device:TPU:0, one launch (start us, length us, event | category | flops | bytes accessed | tf_op | source)
XLA Modules:
  0.0 171.9 jit_solution(13817136393667522)
XLA Ops:
  0.6 11.5 %shard_map.67 = (f32[40,128,128]{2,1,0:T(8,128)}, f32[128,128]{1,0:T(8,128)}) custom-call(f32[128,40,512]{2,1,0:T(8,128)} %refs_3_.1, f32[128,40,512]{2,1,0:T(8,128)} %refs_3_.1, f32[128,40,512]{2,1,0:T(8,128)} %refs_3_.1, f32[128,40,512]{2,1,0:T(8,128)} %refs_3_.1, f32[512,128]{1,0:T(8,128)} %refs_4_.1, f32[128,40,128]{2,1,0:T(8,128)} %refs_5_.1), custom_call_target="tpu_custom_call" | custom-call | flops 2684354560 | bytes 15728640 | tf_op jit(solution)/shard_map/pallas_call | solution.py:100
  12.1 1.1 constant_dynamic-slice_fusion.6
  13.2 3.0 %collective-permute-start = (f32[5,128,128]{2,1,0:T(8,128)S(1)}, f32[5,128,128]{2,1,0:T(8,128)S(1)}, u32[]{:S(2)}, u32[]{:S(2)}) collective-permute-start(f32[5,128,128]{2,1,0:T(8,128)S(1)} %get-tuple-element.82), channel_id=1, source_target_pairs={{0,1},{1,0},{2,3},{3,2},{4,5},{5,4},{6,7},{7,6},{8,9},{9,8},{10,11... | collective-permute-start | bytes 983048 | tf_op jit(solution)/shard_map/ppermute | solution.py:389
  16.2 1.5 collective-permute-start.1
  17.8 4.9 %all-to-all-start = ((f32[8,16,128]{2,1,0:T(8,128)}), f32[8,16,128]{2,1,0:T(8,128)S(1)}, u32[]{:S(2)}, u32[]{:S(2)}) async-start(f32[8,16,128]{2,1,0:T(8,128)} %bitcast.27), calls=%async_computation | async-start | bytes 131072 | tf_op jit(solution)/shard_map/all_to_all | solution.py:393
  22.6 5.9 %all-to-all-done = f32[8,16,128]{2,1,0:T(8,128)S(1)} async-done(((f32[8,16,128]{2,1,0:T(8,128)}), f32[8,16,128]{2,1,0:T(8,128)S(1)}, u32[]{:S(2)}, u32[]{:S(2)}) %all-to-all-start) | async-done | bytes 65568 | tf_op jit(solution)/shard_map/all_to_all | solution.py:393
  28.6 0.0 collective-permute-done.refs_1_
  28.6 0.8 broadcast_in_dim.6
  29.4 2.6 %all-to-all-start.1 = ((f32[32,16,128]{2,1,0:T(8,128)}), f32[32,16,128]{2,1,0:T(8,128)S(1)}, u32[]{:S(2)}, u32[]{:S(2)}) async-start(f32[32,16,128]{2,1,0:T(8,128)} %broadcast_in_dim.6), calls=%async_computation.1 | async-start | bytes 524288 | tf_op jit(solution)/shard_map/all_to_all | solution.py:393
  32.0 1.2 constant_dynamic-slice_fusion.3
  33.3 2.6 %collective-permute-start.2 = (f32[5,128,128]{2,1,0:T(8,128)S(1)}, f32[5,128,128]{2,1,0:T(8,128)S(1)}, u32[]{:S(2)}, u32[]{:S(2)}) collective-permute-start(f32[5,128,128]{2,1,0:T(8,128)S(1)} %get-tuple-element.80), channel_id=1, source_target_pairs={{0,3},{1,2},{2,1},{3,0},{4,7},{5,6},{6,5},{7,4},{8,11},{9,10},{10,... | collective-permute-start | bytes 983048 | tf_op jit(solution)/shard_map/ppermute | solution.py:389
  35.9 0.5 collective-permute-start.3
  36.4 0.4 collective-permute-start.4
  36.8 11.1 %shard_map.68.square_ref = bf16[512,1024]{1,0:T(8,128)(2,1)} custom-call(f32[5120,512]{1,0:T(8,128)} %bitcast.17), custom_call_target="tpu_custom_call" | custom-call | flops 5368709120 | bytes 10485760 | tf_op jit(solution)/shard_map/pallas_call | solution.py:146
  47.9 0.0 copy-start.1
  47.9 0.7 copy-done.1
  48.6 2.4 %shard_map.69 = f32[512,128]{1,0:T(8,128)} custom-call(bf16[512,1024]{1,0:T(8,128)(2,1)} %shard_map.68.square_ref, f32[512,128]{1,0:T(8,128)} %bitcast.22), custom_call_target="tpu_custom_call" | custom-call | flops 268435456 | bytes 1572864 | tf_op jit(solution)/shard_map/pallas_call | solution.py:164
  51.0 1.7 %collective-permute-done.3.refs_5_ = f32[5,128,128]{2,1,0:T(8,128)S(1)} collective-permute-done((f32[5,128,128]{2,1,0:T(8,128)S(1)}, f32[5,128,128]{2,1,0:T(8,128)S(1)}, u32[]{:S(2)}, u32[]{:S(2)}) %collective-permute-start.3) | collective-permute-done | bytes 327712 | tf_op jit(solution)/shard_map/ppermute | solution.py:389
  52.7 0.1 collective-permute-done.4.refs_6_
  52.9 15.4 %all_to_all.30 = f32[32,16,128]{2,1,0:T(8,128)S(1)} all-to-all(f32[32,16,128]{2,1,0:T(8,128)} %bitcast.25), channel_id=1, replica_groups=mesh['cuts'=8,'rank'=4] {'cuts','rank'}, dimensions={0} | all-to-all | bytes 524288 | tf_op jit(solution)/shard_map/all_to_all | solution.py:393
  68.4 0.7 broadcast_in_dim.7
  69.1 2.8 %all-to-all-start.3 = ((f32[32,16,128]{2,1,0:T(8,128)}), f32[32,16,128]{2,1,0:T(8,128)S(1)}, u32[]{:S(2)}, u32[]{:S(2)}) async-start(f32[32,16,128]{2,1,0:T(8,128)} %broadcast_in_dim.7), calls=%async_computation.3 | async-start | bytes 524288 | tf_op jit(solution)/shard_map/all_to_all | solution.py:393
  71.9 2.1 %constant_dynamic-slice_fusion = (f32[5,128,128]{2,1,0:T(8,128)S(1)}, f32[5,128,128]{2,1,0:T(8,128)}, f32[5,128,128]{2,1,0:T(8,128)}) fusion(f32[40,128,128]{2,1,0:T(8,128)} %get-tuple-element.47, s32[]{:T(128)S(6)} %select_n.31, s32[]{:T(128)S(6)} %select_n.30, s32[]{:T(128)S(6)} %select_n.29), kind=kLoop, calls=%fused_computation | loop fusion | bytes 1966092 | tf_op jit(solution)/shard_map/dynamic_slice | solution.py:428
  74.0 2.4 %collective-permute-start.5 = (f32[5,128,128]{2,1,0:T(8,128)S(1)}, f32[5,128,128]{2,1,0:T(8,128)S(1)}, u32[]{:S(2)}, u32[]{:S(2)}) collective-permute-start(f32[5,128,128]{2,1,0:T(8,128)S(1)} %get-tuple-element.53), channel_id=1, source_target_pairs={{0,3},{1,2},{2,1},{3,0},{4,7},{5,6},{6,5},{7,4},{8,11},{9,10},{10,... | collective-permute-start | bytes 983048 | tf_op jit(solution)/shard_map/ppermute | solution.py:389
  76.4 9.6 %collective-permute-done.5.refs_7_ = f32[5,128,128]{2,1,0:T(8,128)S(1)} collective-permute-done((f32[5,128,128]{2,1,0:T(8,128)S(1)}, f32[5,128,128]{2,1,0:T(8,128)S(1)}, u32[]{:S(2)}, u32[]{:S(2)}) %collective-permute-start.5) | collective-permute-done | bytes 327712 | tf_op jit(solution)/shard_map/ppermute | solution.py:389
  86.0 0.0 all-to-all-done.3
  86.0 0.7 copy-done.13
  86.7 0.1 copy-done
  86.8 3.5 %shard_map.70 = (f32[5,128,128]{2,1,0:T(8,128)}, f32[5,128,128]{2,1,0:T(8,128)}) custom-call(s32[1]{0:T(128)} %bitcast.rank_ref, f32[512,128]{1,0:T(8,128)} %bitcast.20, f32[5,128,128]{2,1,0:T(8,128)} %get-tuple-element.77.refs_0_, f32[5,128,128]{2,1,0:T(8,128)} %copy-done.8, f32[5,128,128]{2,1,0:T(8,128)} %copy-done.9, f32[5,128,128]{2,1,0:T(8,128)} %copy-done.10, ...), custom_call_target="tpu_custom_call" | custom-call | flops 671088640 | bytes 2883584 | tf_op jit(solution)/shard_map/pallas_call | solution.py:194
  90.3 1.3 collective-permute-start.7
  91.6 1.1 collective-permute-start.6
  92.7 0.9 collective-permute-start.8
  93.6 0.8 collective-permute-start.10
  94.3 9.2 %shard_map.71 = (f32[160,128]{1,0:T(8,128)}, f32[512,128]{1,0:T(8,128)}) custom-call(s32[1]{0:T(128)} %bitcast.rank_ref, f32[512,128]{1,0:T(8,128)} %bitcast.23, f32[512,128]{1,0:T(8,128)} %bitcast.21), custom_call_target="tpu_custom_call" | custom-call | flops 67108864 | bytes 1048576 | tf_op jit(solution)/shard_map/pallas_call | solution.py:359
  103.5 0.0 collective-permute-done.6.refs_10_
  103.5 1.3 collective-permute-start.9
  104.9 1.1 collective-permute-start.11
  106.0 8.5 %shard_map.72 = f32[5120,128]{1,0:T(8,128)} custom-call(f32[5120,512]{1,0:T(8,128)} %bitcast.18, f32[512,128]{1,0:T(8,128)} %get-tuple-element.63.weight_ref), custom_call_target="tpu_custom_call" | custom-call | flops 2684354560 | bytes 13107200 | tf_op jit(solution)/shard_map/pallas_call | solution.py:277
  114.5 0.0 collective-permute-done.8.refs_6_
  114.5 0.2 collective-permute-done.9.refs_7_
  114.7 0.5 copy-done.4
  115.2 0.1 copy-done.5
  115.4 0.1 copy-done.6
  115.5 0.1 copy-done.7
  115.6 10.6 %shard_map.73 = (f32[512,128]{1,0:T(8,128)}, f32[128,128]{1,0:T(8,128)}, f32[1280,128]{1,0:T(8,128)}) custom-call(s32[1]{0:T(128)} %bitcast.rank_ref, f32[160,128]{1,0:T(8,128)} %get-tuple-element.65.weight_ref, f32[5120,512]{1,0:T(8,128)} %bitcast.13, f32[5120,512]{1,0:T(8,128)} %bitcast.14, f32[5120,512]{1,0:T(8,128)} %bitcast.15, f32[5120,512]{1,0:T(8,128)} %bitcast.16, ...), custom_call_target="tpu_custom_call" | custom-call | flops 2684354560 | bytes 13107200 | tf_op jit(solution)/shard_map/pallas_call | solution.py:247
  126.2 4.0 %all-to-all-start.4 = ((f32[32,16,128]{2,1,0:T(8,128)}), f32[32,16,128]{2,1,0:T(8,128)S(1)}, u32[]{:S(2)}, u32[]{:S(2)}) async-start(f32[32,16,128]{2,1,0:T(8,128)} %bitcast.26), calls=%async_computation.4 | async-start | bytes 524288 | tf_op jit(solution)/shard_map/all_to_all | solution.py:393
  130.2 0.3 collective-permute-start.12
  130.5 1.2 collective-permute-done.12
  131.8 0.9 add.71
  132.6 1.8 %collective-permute-start.13 = (f32[128,128]{1,0:T(8,128)S(1)}, f32[128,128]{1,0:T(8,128)S(1)}, u32[]{:S(2)}, u32[]{:S(2)}) collective-permute-start(f32[128,128]{1,0:T(8,128)S(1)} %add.71), channel_id=1, source_target_pairs={{0,1},{1,0},{2,3},{3,2},{4,5},{5,4},{6,7},{7,6},{8,9},{9,8},{10,11... | collective-permute-start | bytes 196616 | tf_op jit(solution)/shard_map/ppermute | solution.py:389
  134.4 3.2 %collective-permute-done.13 = f32[128,128]{1,0:T(8,128)S(1)} collective-permute-done((f32[128,128]{1,0:T(8,128)S(1)}, f32[128,128]{1,0:T(8,128)S(1)}, u32[]{:S(2)}, u32[]{:S(2)}) %collective-permute-start.13) | collective-permute-done | bytes 65568 | tf_op jit(solution)/shard_map/ppermute | solution.py:389
  137.6 1.6 collective-permute-start.14
  139.2 2.7 %collective-permute-done.14 = f32[128,128]{1,0:T(8,128)S(1)} collective-permute-done((f32[128,128]{1,0:T(8,128)S(1)}, f32[128,128]{1,0:T(8,128)S(1)}, u32[]{:S(2)}, u32[]{:S(2)}) %collective-permute-start.14) | collective-permute-done | bytes 65568 | tf_op jit(solution)/shard_map/ppermute | solution.py:389
  142.0 2.0 %collective-permute-start.15 = (f32[128,128]{1,0:T(8,128)S(1)}, f32[128,128]{1,0:T(8,128)S(1)}, u32[]{:S(2)}, u32[]{:S(2)}) collective-permute-start(f32[128,128]{1,0:T(8,128)S(1)} %add.73), channel_id=1, source_target_pairs={{0,8},{4,12},{8,0},{12,4},{16,24},{20,28},{24,16},{28,20},{1,9},{5... | collective-permute-start | bytes 196616 | tf_op jit(solution)/shard_map/ppermute | solution.py:389
  144.0 2.3 %collective-permute-done.15 = f32[128,128]{1,0:T(8,128)S(1)} collective-permute-done((f32[128,128]{1,0:T(8,128)S(1)}, f32[128,128]{1,0:T(8,128)S(1)}, u32[]{:S(2)}, u32[]{:S(2)}) %collective-permute-start.15) | collective-permute-done | bytes 65568 | tf_op jit(solution)/shard_map/ppermute | solution.py:389
  146.3 2.9 %collective-permute-start.16 = (f32[128,128]{1,0:T(8,128)S(1)}, f32[128,128]{1,0:T(8,128)S(1)}, u32[]{:S(2)}, u32[]{:S(2)}) collective-permute-start(f32[128,128]{1,0:T(8,128)S(1)} %add.74), channel_id=1, source_target_pairs={{0,16},{4,20},{8,24},{12,28},{16,0},{20,4},{24,8},{28,12},{1,17},{... | collective-permute-start | bytes 196616 | tf_op jit(solution)/shard_map/ppermute | solution.py:389
  149.2 2.3 %collective-permute-done.16 = f32[128,128]{1,0:T(8,128)S(1)} collective-permute-done((f32[128,128]{1,0:T(8,128)S(1)}, f32[128,128]{1,0:T(8,128)S(1)}, u32[]{:S(2)}, u32[]{:S(2)}) %collective-permute-start.16) | collective-permute-done | bytes 65568 | tf_op jit(solution)/shard_map/ppermute | solution.py:389
  151.5 0.6 add.75.gram_ref
  152.2 0.0 all-to-all-done.4
  152.2 0.7 broadcast_in_dim.8
  152.9 6.3 %all-to-all-start.5 = ((f32[32,16,128]{2,1,0:T(8,128)}), f32[32,16,128]{2,1,0:T(8,128)S(1)}, u32[]{:S(2)}, u32[]{:S(2)}) async-start(f32[32,16,128]{2,1,0:T(8,128)} %broadcast_in_dim.8), calls=%async_computation.5 | async-start | bytes 524288 | tf_op jit(solution)/shard_map/all_to_all | solution.py:393
  159.2 8.8 %shard_map.74 = (f32[128,128]{1,0:T(8,128)}, f32[1280,128]{1,0:T(8,128)}) custom-call(f32[128,128]{1,0:T(8,128)} %add.75.gram_ref, f32[1280,128]{1,0:T(8,128)} %get-tuple-element.71.middle_ref), custom_call_target="tpu_custom_call" | custom-call | flops 167772160 | bytes 1310720 | tf_op jit(solution)/shard_map/pallas_call | solution.py:378
  168.0 1.9 %all-to-all-done.5 = f32[32,16,128]{2,1,0:T(8,128)S(1)} async-done(((f32[32,16,128]{2,1,0:T(8,128)}), f32[32,16,128]{2,1,0:T(8,128)S(1)}, u32[]{:S(2)}, u32[]{:S(2)}) %all-to-all-start.5) | async-done | bytes 262176 | tf_op jit(solution)/shard_map/all_to_all | solution.py:393
  169.9 1.9 %fusion = f32[128,512]{1,0:T(8,128)} fusion(f32[128,128]{1,0:T(8,128)} %get-tuple-element.73, f32[512,128]{1,0:T(8,128)S(1)} %bitcast.24), kind=kOutput, calls=%fused_computation.8 | convolution fusion | flops 100663296 | bytes 589824 | tf_op jit(solution)/shard_map/dot_general | solution.py:53
  (32 shorter events, 0.2 us)
Async XLA Ops:
  13.2 15.3 %collective-permute-start = (f32[5,128,128]{2,1,0:T(8,128)S(1)}, f32[5,128,128]{2,1,0:T(8,128)S(1)}, u32[]{:S(2)}, u32[]{:S(2)}) collective-permute-start(f32[5,128,128]{2,1,0:T(8,128)S(1)} %get-tuple-element.82), channel_id=1, source_target_pairs={{0,1},{1,0},{2,3},{3,2},{4,5},{5,4},{6,7},{7,6},{8,9},{9,8},{10,11... | collective-permute-start | bytes 983048 | tf_op jit(solution)/shard_map/ppermute | solution.py:389
  16.2 12.4 %collective-permute-start.1 = (f32[5,128,128]{2,1,0:T(8,128)S(1)}, f32[5,128,128]{2,1,0:T(8,128)S(1)}, u32[]{:S(2)}, u32[]{:S(2)}) collective-permute-start(f32[5,128,128]{2,1,0:T(8,128)S(1)} %get-tuple-element.81), channel_id=1, source_target_pairs={{0,2},{1,3},{2,0},{3,1},{4,6},{5,7},{6,4},{7,5},{8,10},{9,11},{10,... | collective-permute-start | bytes 983048 | tf_op jit(solution)/shard_map/ppermute | solution.py:389
  17.8 10.8 %all-to-all-start = ((f32[8,16,128]{2,1,0:T(8,128)}), f32[8,16,128]{2,1,0:T(8,128)S(1)}, u32[]{:S(2)}, u32[]{:S(2)}) async-start(f32[8,16,128]{2,1,0:T(8,128)} %bitcast.27), calls=%async_computation | async-start | bytes 131072 | tf_op jit(solution)/shard_map/all_to_all | solution.py:393
  28.6 19.3 %copy-start.8 = (f32[5,128,128]{2,1,0:T(8,128)}, f32[5,128,128]{2,1,0:T(8,128)S(1)}, u32[]{:S(2)}) copy-start(f32[5,128,128]{2,1,0:T(8,128)S(1)} %collective-permute-done.refs_1_) | copy-start | bytes 983044
  28.6 19.3 %copy-start.9 = (f32[5,128,128]{2,1,0:T(8,128)}, f32[5,128,128]{2,1,0:T(8,128)S(1)}, u32[]{:S(2)}) copy-start(f32[5,128,128]{2,1,0:T(8,128)S(1)} %collective-permute-done.1.refs_2_) | copy-start | bytes 983044
  29.4 18.5 %all-to-all-start.1 = ((f32[32,16,128]{2,1,0:T(8,128)}), f32[32,16,128]{2,1,0:T(8,128)S(1)}, u32[]{:S(2)}, u32[]{:S(2)}) async-start(f32[32,16,128]{2,1,0:T(8,128)} %broadcast_in_dim.6), calls=%async_computation.1 | async-start | bytes 524288 | tf_op jit(solution)/shard_map/all_to_all | solution.py:393
  33.3 17.8 %collective-permute-start.2 = (f32[5,128,128]{2,1,0:T(8,128)S(1)}, f32[5,128,128]{2,1,0:T(8,128)S(1)}, u32[]{:S(2)}, u32[]{:S(2)}) collective-permute-start(f32[5,128,128]{2,1,0:T(8,128)S(1)} %get-tuple-element.80), channel_id=1, source_target_pairs={{0,3},{1,2},{2,1},{3,0},{4,7},{5,6},{6,5},{7,4},{8,11},{9,10},{10,... | collective-permute-start | bytes 983048 | tf_op jit(solution)/shard_map/ppermute | solution.py:389
  35.9 16.9 %collective-permute-start.3 = (f32[5,128,128]{2,1,0:T(8,128)S(1)}, f32[5,128,128]{2,1,0:T(8,128)S(1)}, u32[]{:S(2)}, u32[]{:S(2)}) collective-permute-start(f32[5,128,128]{2,1,0:T(8,128)S(1)} %get-tuple-element.79), channel_id=1, source_target_pairs={{0,1},{1,0},{2,3},{3,2},{4,5},{5,4},{6,7},{7,6},{8,9},{9,8},{10,11... | collective-permute-start | bytes 983048 | tf_op jit(solution)/shard_map/ppermute | solution.py:389
  36.4 16.5 %collective-permute-start.4 = (f32[5,128,128]{2,1,0:T(8,128)S(1)}, f32[5,128,128]{2,1,0:T(8,128)S(1)}, u32[]{:S(2)}, u32[]{:S(2)}) collective-permute-start(f32[5,128,128]{2,1,0:T(8,128)S(1)} %get-tuple-element.78), channel_id=1, source_target_pairs={{0,2},{1,3},{2,0},{3,1},{4,6},{5,7},{6,4},{7,5},{8,10},{9,11},{10,... | collective-permute-start | bytes 983048 | tf_op jit(solution)/shard_map/ppermute | solution.py:389
  47.9 0.7 copy-start.1
  51.0 35.0 %copy-start.10 = (f32[5,128,128]{2,1,0:T(8,128)}, f32[5,128,128]{2,1,0:T(8,128)S(1)}, u32[]{:S(2)}) copy-start(f32[5,128,128]{2,1,0:T(8,128)S(1)} %collective-permute-done.2.refs_3_) | copy-start | bytes 983044
  52.7 33.3 %copy-start.11 = (f32[5,128,128]{2,1,0:T(8,128)}, f32[5,128,128]{2,1,0:T(8,128)S(1)}, u32[]{:S(2)}) copy-start(f32[5,128,128]{2,1,0:T(8,128)S(1)} %collective-permute-done.3.refs_5_) | copy-start | bytes 983044
  52.9 33.1 %copy-start.12 = (f32[5,128,128]{2,1,0:T(8,128)}, f32[5,128,128]{2,1,0:T(8,128)S(1)}, u32[]{:S(2)}) copy-start(f32[5,128,128]{2,1,0:T(8,128)S(1)} %collective-permute-done.4.refs_6_) | copy-start | bytes 983044
  69.1 16.9 %all-to-all-start.3 = ((f32[32,16,128]{2,1,0:T(8,128)}), f32[32,16,128]{2,1,0:T(8,128)S(1)}, u32[]{:S(2)}, u32[]{:S(2)}) async-start(f32[32,16,128]{2,1,0:T(8,128)} %broadcast_in_dim.7), calls=%async_computation.3 | async-start | bytes 524288 | tf_op jit(solution)/shard_map/all_to_all | solution.py:393
  74.0 12.0 %collective-permute-start.5 = (f32[5,128,128]{2,1,0:T(8,128)S(1)}, f32[5,128,128]{2,1,0:T(8,128)S(1)}, u32[]{:S(2)}, u32[]{:S(2)}) collective-permute-start(f32[5,128,128]{2,1,0:T(8,128)S(1)} %get-tuple-element.53), channel_id=1, source_target_pairs={{0,3},{1,2},{2,1},{3,0},{4,7},{5,6},{6,5},{7,4},{8,11},{9,10},{10,... | collective-permute-start | bytes 983048 | tf_op jit(solution)/shard_map/ppermute | solution.py:389
  86.0 0.7 copy-start.13
  86.0 0.8 copy-start
  90.3 13.2 %collective-permute-start.7 = (f32[5,128,128]{2,1,0:T(8,128)}, f32[5,128,128]{2,1,0:T(8,128)S(1)}, u32[]{:S(2)}, u32[]{:S(2)}) collective-permute-start(f32[5,128,128]{2,1,0:T(8,128)} %get-tuple-element.57.refs_4_), channel_id=1, source_target_pairs={{0,1},{1,0},{2,3},{3,2},{4,5},{5,4},{6,7},{7,6},{8,9},{9,8},{10,11... | collective-permute-start | bytes 983048 | tf_op jit(solution)/shard_map/ppermute | solution.py:389
  91.6 12.0 %collective-permute-start.6 = (f32[5,128,128]{2,1,0:T(8,128)}, f32[5,128,128]{2,1,0:T(8,128)S(1)}, u32[]{:S(2)}, u32[]{:S(2)}) collective-permute-start(f32[5,128,128]{2,1,0:T(8,128)} %get-tuple-element.56.refs_8_), channel_id=1, source_target_pairs={{0,2},{1,3},{2,0},{3,1},{4,6},{5,7},{6,4},{7,5},{8,10},{9,11},{10,... | collective-permute-start | bytes 983048 | tf_op jit(solution)/shard_map/ppermute | solution.py:389
  92.7 21.8 %collective-permute-start.8 = (f32[5,128,128]{2,1,0:T(8,128)}, f32[5,128,128]{2,1,0:T(8,128)S(1)}, u32[]{:S(2)}, u32[]{:S(2)}) collective-permute-start(f32[5,128,128]{2,1,0:T(8,128)} %get-tuple-element.57.refs_4_), channel_id=1, source_target_pairs={{0,2},{1,3},{2,0},{3,1},{4,6},{5,7},{6,4},{7,5},{8,10},{9,11},{10,... | collective-permute-start | bytes 983048 | tf_op jit(solution)/shard_map/ppermute | solution.py:389
  93.6 20.9 %collective-permute-start.10 = (f32[5,128,128]{2,1,0:T(8,128)}, f32[5,128,128]{2,1,0:T(8,128)S(1)}, u32[]{:S(2)}, u32[]{:S(2)}) collective-permute-start(f32[5,128,128]{2,1,0:T(8,128)} %get-tuple-element.56.refs_8_), channel_id=1, source_target_pairs={{0,1},{1,0},{2,3},{3,2},{4,5},{5,4},{6,7},{7,6},{8,9},{9,8},{10,11... | collective-permute-start | bytes 983048 | tf_op jit(solution)/shard_map/ppermute | solution.py:389
  103.5 11.0 %copy-start.2 = (f32[5,128,128]{2,1,0:T(8,128)}, f32[5,128,128]{2,1,0:T(8,128)S(1)}, u32[]{:S(2)}) copy-start(f32[5,128,128]{2,1,0:T(8,128)S(1)} %collective-permute-done.7.refs_5_) | copy-start | bytes 983044
  103.5 11.0 %copy-start.3 = (f32[5,128,128]{2,1,0:T(8,128)}, f32[5,128,128]{2,1,0:T(8,128)S(1)}, u32[]{:S(2)}) copy-start(f32[5,128,128]{2,1,0:T(8,128)S(1)} %collective-permute-done.6.refs_10_) | copy-start | bytes 983044
  103.5 11.2 %collective-permute-start.9 = (f32[5,128,128]{2,1,0:T(8,128)S(1)}, f32[5,128,128]{2,1,0:T(8,128)S(1)}, u32[]{:S(2)}, u32[]{:S(2)}) collective-permute-start(f32[5,128,128]{2,1,0:T(8,128)S(1)} %collective-permute-done.7.refs_5_), channel_id=1, source_target_pairs={{0,2},{1,3},{2,0},{3,1},{4,6},{5,7},{6,4},{7,5},{8,10},{9,11},{10,... | collective-permute-start | bytes 983048 | tf_op jit(solution)/shard_map/ppermute | solution.py:389
  104.9 9.9 %collective-permute-start.11 = (f32[5,128,128]{2,1,0:T(8,128)S(1)}, f32[5,128,128]{2,1,0:T(8,128)S(1)}, u32[]{:S(2)}, u32[]{:S(2)}) collective-permute-start(f32[5,128,128]{2,1,0:T(8,128)S(1)} %collective-permute-done.6.refs_10_), channel_id=1, source_target_pairs={{0,1},{1,0},{2,3},{3,2},{4,5},{5,4},{6,7},{7,6},{8,9},{9,8},{10,11... | collective-permute-start | bytes 983048 | tf_op jit(solution)/shard_map/ppermute | solution.py:389
  114.5 0.7 copy-start.4
  114.5 0.8 copy-start.5
  114.7 0.7 copy-start.6
  114.7 0.9 copy-start.7
  126.2 26.0 %all-to-all-start.4 = ((f32[32,16,128]{2,1,0:T(8,128)}), f32[32,16,128]{2,1,0:T(8,128)S(1)}, u32[]{:S(2)}, u32[]{:S(2)}) async-start(f32[32,16,128]{2,1,0:T(8,128)} %bitcast.26), calls=%async_computation.4 | async-start | bytes 524288 | tf_op jit(solution)/shard_map/all_to_all | solution.py:393
  130.2 1.5 collective-permute-start.12
  132.6 5.0 %collective-permute-start.13 = (f32[128,128]{1,0:T(8,128)S(1)}, f32[128,128]{1,0:T(8,128)S(1)}, u32[]{:S(2)}, u32[]{:S(2)}) collective-permute-start(f32[128,128]{1,0:T(8,128)S(1)} %add.71), channel_id=1, source_target_pairs={{0,1},{1,0},{2,3},{3,2},{4,5},{5,4},{6,7},{7,6},{8,9},{9,8},{10,11... | collective-permute-start | bytes 196616 | tf_op jit(solution)/shard_map/ppermute | solution.py:389
  137.6 4.3 %collective-permute-start.14 = (f32[128,128]{1,0:T(8,128)S(1)}, f32[128,128]{1,0:T(8,128)S(1)}, u32[]{:S(2)}, u32[]{:S(2)}) collective-permute-start(f32[128,128]{1,0:T(8,128)S(1)} %add.72), channel_id=1, source_target_pairs={{0,2},{1,3},{2,0},{3,1},{4,6},{5,7},{6,4},{7,5},{8,10},{9,11},{10,... | collective-permute-start | bytes 196616 | tf_op jit(solution)/shard_map/ppermute | solution.py:389
  142.0 4.3 %collective-permute-start.15 = (f32[128,128]{1,0:T(8,128)S(1)}, f32[128,128]{1,0:T(8,128)S(1)}, u32[]{:S(2)}, u32[]{:S(2)}) collective-permute-start(f32[128,128]{1,0:T(8,128)S(1)} %add.73), channel_id=1, source_target_pairs={{0,8},{4,12},{8,0},{12,4},{16,24},{20,28},{24,16},{28,20},{1,9},{5... | collective-permute-start | bytes 196616 | tf_op jit(solution)/shard_map/ppermute | solution.py:389
  146.3 5.2 %collective-permute-start.16 = (f32[128,128]{1,0:T(8,128)S(1)}, f32[128,128]{1,0:T(8,128)S(1)}, u32[]{:S(2)}, u32[]{:S(2)}) collective-permute-start(f32[128,128]{1,0:T(8,128)S(1)} %add.74), channel_id=1, source_target_pairs={{0,16},{4,20},{8,24},{12,28},{16,0},{20,4},{24,8},{28,12},{1,17},{... | collective-permute-start | bytes 196616 | tf_op jit(solution)/shard_map/ppermute | solution.py:389
  152.9 17.0 %all-to-all-start.5 = ((f32[32,16,128]{2,1,0:T(8,128)}), f32[32,16,128]{2,1,0:T(8,128)S(1)}, u32[]{:S(2)}, u32[]{:S(2)}) async-start(f32[32,16,128]{2,1,0:T(8,128)} %broadcast_in_dim.8), calls=%async_computation.5 | async-start | bytes 524288 | tf_op jit(solution)/shard_map/all_to_all | solution.py:393

commit v8 on v7

--- a/solution.py
+++ b/solution.py
@@ -171,20 +171,20 @@
 
 def loose_kernel(rank_ref, raw_ref, *refs):
     piece_refs, out_refs = refs[:-2], refs[-2:]
-    ranks = len(piece_refs) // 2
     local_rows, columns = piece_refs[0].shape[1:]
     rows = []
-    for offset in range(ranks):
+    for offset in range(len(piece_refs)):
         start = pl.multiple_of((rank_ref[0] ^ offset) * local_rows, local_rows)
         rows.append(raw_ref[pl.ds(start, local_rows), :])
     raw = twice(both_parts(jnp.concatenate(rows, axis=0), 1).T, 1)
-    for half, out_ref in enumerate(out_refs):
-        refs = piece_refs[half * ranks:(half + 1) * ranks]
+    first = 0
+    for out_ref in out_refs:
         count = out_ref.shape[0]
-        value = [jnp.concatenate([ref[n] for n in range(count)], axis=1) for ref in refs]
+        value = [jnp.concatenate([ref[first + n] for n in range(count)], axis=1) for ref in piece_refs]
         product = fold(mxu(raw, both_parts(jnp.concatenate(value, axis=0), 0), NN), 0)
         for n in range(count):
             out_ref[n] = product[:, n * columns:(n + 1) * columns]
+        first += count
 
 
 def loosen(rank_index, raw, pieces, halves):
@@ -398,6 +398,10 @@
     return exchange(jnp.broadcast_to(value[None], (parts,) + value.shape), axes)
 
 
+def pairs_of(axis, bits):
+    return [(axis, bits[start:start + 2]) for start in range(0, len(bits), 2)]
+
+
 def after(value, others):
     return lax.optimization_barrier((value, others))
 
@@ -421,39 +425,26 @@
 
     sketched, part = sketch(core_two, right_sketch, sketch_core)
 
-    def send(names, source, behind):
-        found = []
-        for half, offset in names:
-            start = (rank ^ offset) * share + half * halves[0]
-            found.append(lax.dynamic_slice_in_dim(source, start, halves[half], 0))
-        if behind is not None:
-            found, _ = after(found, behind)
-        return {name: swap(value, "rank", name[1]) if name[1] else value for name, value in zip(names, found)}
-
-    far = ranks - 1
-    near = [[(half, offset) for offset in range(1, far)] for half in range(2)]
+    def part_for(offset, source):
+        return lax.dynamic_slice_in_dim(source, (rank ^ offset) * share, share, 0)
 
     cut_bits = [1 << bit for bit in range((cuts - 1).bit_length())]
     bits = [1 << bit for bit in range((ranks - 1).bit_length())]
-    first = send(near[0], sketched, None)
     bridge_rows = jnp.sum(exchange(part.reshape(cuts, local_rows // cuts, columns), "cuts"), axis=0)
-    flat_late, (bridge_rows, pieces) = after(flat_one, (bridge_rows, first))
+    flat_late, bridge_rows = after(flat_one, bridge_rows)
     sketched, bridge_rows = after(sketched, bridge_rows)
-    moved = send(near[1] + [(0, far)], sketched, None)
+    moved = [swap(part_for(offset, sketched), "rank", offset) for offset in range(1, ranks)]
     bridge = gather_all(bridge_rows, ("rank", "cuts")).reshape(width, columns)
     square = square_of(flat_late)
 
     raw = product_of(square, bridge)
+    sketched, raw = after(sketched, raw)
+    own = part_for(0, sketched)
+    raw = jnp.sum(exchange(raw.reshape(parts, -1, columns), both), axis=0)
     raw, moved = after(raw, moved)
-    pieces.update(moved)
-    sketched, raw = after(sketched, raw)
-    pieces.update(send([(0, 0), (1, 0)], sketched, None))
-    raw = jnp.sum(exchange(raw.reshape(parts, -1, columns), both), axis=0)
-    pieces.update(send([(1, far)], sketched, raw))
     raw = gather_all(raw, both).reshape(width, columns)
 
-    ordered = [pieces[(half, offset)] for half in range(2) for offset in range(ranks)]
-    loose = loosen(rank_index, raw, ordered, halves)
+    loose = loosen(rank_index, raw, [own] + moved, halves)
     loose, (bridge, raw) = after(loose, (bridge, raw))
     scale = math.sqrt(local_rows * ranks * slices * cuts)
     weight, solve = first_factor(rank_index, bridge, raw, scale, local_rows, band)
@@ -472,8 +463,11 @@
     weight, left_core = after(weight, left_core)
     raw, gram, middle = carry_rows(rank_index, weight, flat_two, everyone, halves, share, band)
     raw = jnp.sum(exchange(raw.reshape(parts, -1, columns), both), axis=0)
-    for axis, bit in [("cuts", 1)] + [("rank", bit) for bit in bits] + [("cuts", bit) for bit in cut_bits[1:]]:
-        gram = gram + swap(gram, axis, bit)
+    for axis, pair in [("cuts", [1])] + pairs_of("rank", bits) + pairs_of("cuts", cut_bits[1:]):
+        other = gram + swap(gram, axis, pair[0])
+        if len(pair) > 1:
+            other = other + (swap(gram, axis, pair[1]) + swap(gram, axis, pair[0] ^ pair[1]))
+        gram = other
     raw, gram = after(raw, gram)
     raw = gather_all(raw, both).reshape(width, columns)
     scale = math.sqrt(columns * slices * cuts)

time: 173 us -> 164 us (0.948)
  starting transfers between devices: 46.1 us -> 37 us
  blocking collectives: 15.4 us -> 18.5 us
  waiting for transfers between devices: 31.3 us -> 28.8 us
    ppermute x17 -> x16, waiting for transfers between devices: 23.5 us -> 12.2 us  [swap(): lax.ppermute(value, axis, [(i, i ^ offset) for i in range(lax.axis_size(a...]
    ppermute x17 -> x16, starting transfers between devices: 25.6 us -> 16.5 us  [swap(): lax.ppermute(value, axis, [(i, i ^ offset) for i in range(lax.axis_size(a...]
    all_to_all x5, waiting for transfers between devices: 7.85 us -> 16.6 us  [exchange(): return lax.all_to_all(value, axes, 0, 0, tiled=True)]
    all_to_all x1, blocking collectives: 15.4 us -> 18.5 us  [exchange(): return lax.all_to_all(value, axes, 0, 0, tiled=True)]
    dynamic_slice x3 -> x2, local copies, waits for them, and re-layouts: 4.47 us -> 4.71 us  [part_for(): return lax.dynamic_slice_in_dim(source, (rank ^ offset) * share, share, 0)]
  transfers between devices with their start and end apart: 22 -> 21, of which waited for: 11 -> 7; matrix products, arithmetic and copies ran while one was open for 3% -> 3% of each run, Pallas kernels for 23% -> 24%
where the time goes in v8:
time: 164 us; the launch traced here: 163 us
  Pallas kernels  65.5 us (40%)
  starting transfers between devices  37 us (23%)
  waiting for transfers between devices  28.8 us (18%)
  blocking collectives  18.5 us (11%)
  local copies, waits for them, and re-layouts  9.2 us (6%)
  matrix products  1.92 us (1%)
    all_to_all x5, starting transfers between devices, exchange(): return lax.all_to_all(value, axes, 0, 0, tiled=True)  20.5 us
    all_to_all x1, blocking collectives, exchange(): return lax.all_to_all(value, axes, 0, 0, tiled=True)  18.5 us
    all_to_all x5, waiting for transfers between devices, exchange(): return lax.all_to_all(value, axes, 0, 0, tiled=True)  16.6 us
    ppermute x16, starting transfers between devices, swap(): lax.ppermute(value, axis, [(i, i ^ offset) for i in range(lax.axis_size(a...  16.5 us
    ppermute x16, waiting for transfers between devices, swap(): lax.ppermute(value, axis, [(i, i ^ offset) for i in range(lax.axis_size(a...  12.2 us
    pallas_call x1, Pallas kernels, sketch(): call(sketch_kernel, 2 * core_two.size * columns * 4, 4 * (core_two.size +...  11.5 us
    pallas_call x1, Pallas kernels, square_of(): call(square_kernel, 4 * rows * width * width, 4 * flat_one.size, grid=(ro...  11.1 us
    pallas_call x1, Pallas kernels, carry_rows(): call(functools.partial(carry_kernel, halves, share), 8 * flat_two.size *...  10.6 us
  transfers between devices with their start and end apart: 21, of which 7 were waited for; matrix products, arithmetic and copies ran while one was open for 3% of the time, Pallas kernels for 24%

profile of v8, /device:TPU:0, one launch (start us, length us, event | category | flops | bytes accessed | tf_op | source)
XLA Modules:
  0.0 163.4 jit_solution(15887608581545062924)
XLA Ops:
  0.6 11.5 %shard_map.67 = (f32[40,128,128]{2,1,0:T(8,128)}, f32[128,128]{1,0:T(8,128)}) custom-call(f32[128,40,512]{2,1,0:T(8,128)} %refs_3_.1, f32[128,40,512]{2,1,0:T(8,128)} %refs_3_.1, f32[128,40,512]{2,1,0:T(8,128)} %refs_3_.1, f32[128,40,512]{2,1,0:T(8,128)} %refs_3_.1, f32[512,128]{1,0:T(8,128)} %refs_4_.1, f32[128,40,128]{2,1,0:T(8,128)} %refs_5_.1), custom_call_target="tpu_custom_call" | custom-call | flops 2684354560 | bytes 15728640 | tf_op jit(solution)/shard_map/pallas_call | solution.py:100
  12.1 6.3 %all-to-all-start = ((f32[8,16,128]{2,1,0:T(8,128)}), f32[8,16,128]{2,1,0:T(8,128)S(1)}, u32[]{:S(2)}, u32[]{:S(2)}) async-start(f32[8,16,128]{2,1,0:T(8,128)} %bitcast.27), calls=%async_computation | async-start | bytes 131072 | tf_op jit(solution)/shard_map/all_to_all | solution.py:393
  18.4 5.9 %all-to-all-done = f32[8,16,128]{2,1,0:T(8,128)S(1)} async-done(((f32[8,16,128]{2,1,0:T(8,128)}), f32[8,16,128]{2,1,0:T(8,128)S(1)}, u32[]{:S(2)}, u32[]{:S(2)}) %all-to-all-start) | async-done | bytes 65568 | tf_op jit(solution)/shard_map/all_to_all | solution.py:393
  24.4 0.7 broadcast_in_dim.6
  25.1 3.1 %all-to-all-start.1 = ((f32[32,16,128]{2,1,0:T(8,128)}), f32[32,16,128]{2,1,0:T(8,128)S(1)}, u32[]{:S(2)}, u32[]{:S(2)}) async-start(f32[32,16,128]{2,1,0:T(8,128)} %broadcast_in_dim.6), calls=%async_computation.1 | async-start | bytes 524288 | tf_op jit(solution)/shard_map/all_to_all | solution.py:393
  28.2 2.7 %constant_dynamic-slice_fusion.1 = (f32[10,128,128]{2,1,0:T(8,128)S(1)}, f32[10,128,128]{2,1,0:T(8,128)}, f32[10,128,128]{2,1,0:T(8,128)}) fusion(f32[40,128,128]{2,1,0:T(8,128)} %get-tuple-element.44, s32[]{:T(128)S(6)} %select_n.14, s32[]{:T(128)S(6)} %select_n.13, s32[]{:T(128)S(6)} %select_n.12), kind=kLoop, calls=%fused_computation.3 | loop fusion | bytes 3932172 | tf_op jit(solution)/shard_map/dynamic_slice | solution.py:429
  31.0 1.8 %collective-permute-start = (f32[10,128,128]{2,1,0:T(8,128)}, f32[10,128,128]{2,1,0:T(8,128)S(1)}, u32[]{:S(2)}, u32[]{:S(2)}) collective-permute-start(f32[10,128,128]{2,1,0:T(8,128)} %get-tuple-element.71), channel_id=1, source_target_pairs={{0,1},{1,0},{2,3},{3,2},{4,5},{5,4},{6,7},{7,6},{8,9},{9,8},{10,11... | collective-permute-start | bytes 1966088 | tf_op jit(solution)/shard_map/ppermute | solution.py:389
  32.7 1.5 collective-permute-start.1
  34.2 0.3 collective-permute-start.2
  34.4 11.1 %shard_map.68.square_ref = bf16[512,1024]{1,0:T(8,128)(2,1)} custom-call(f32[5120,512]{1,0:T(8,128)} %bitcast.17), custom_call_target="tpu_custom_call" | custom-call | flops 5368709120 | bytes 10485760 | tf_op jit(solution)/shard_map/pallas_call | solution.py:146
  45.5 0.0 all-to-all-done.1
  45.5 0.7 copy-done.1
  46.2 2.4 %shard_map.69 = f32[512,128]{1,0:T(8,128)} custom-call(bf16[512,1024]{1,0:T(8,128)(2,1)} %shard_map.68.square_ref, f32[512,128]{1,0:T(8,128)} %bitcast.22), custom_call_target="tpu_custom_call" | custom-call | flops 268435456 | bytes 1572864 | tf_op jit(solution)/shard_map/pallas_call | solution.py:164
  48.6 18.5 %all_to_all.30 = f32[32,16,128]{2,1,0:T(8,128)S(1)} all-to-all(f32[32,16,128]{2,1,0:T(8,128)} %bitcast.25), channel_id=1, replica_groups=mesh['cuts'=8,'rank'=4] {'cuts','rank'}, dimensions={0} | all-to-all | bytes 524288 | tf_op jit(solution)/shard_map/all_to_all | solution.py:393
  67.2 0.0 collective-permute-done.refs_1_
  67.2 0.0 collective-permute-done.1.refs_2_
  67.2 0.0 collective-permute-done.2.refs_3_
  67.2 0.8 broadcast_in_dim.7
  68.0 4.2 %all-to-all-start.3 = ((f32[32,16,128]{2,1,0:T(8,128)}), f32[32,16,128]{2,1,0:T(8,128)S(1)}, u32[]{:S(2)}, u32[]{:S(2)}) async-start(f32[32,16,128]{2,1,0:T(8,128)} %broadcast_in_dim.7), calls=%async_computation.3 | async-start | bytes 524288 | tf_op jit(solution)/shard_map/all_to_all | solution.py:393
  72.2 2.0 %constant_dynamic-slice_fusion.refs_0_ = f32[10,128,128]{2,1,0:T(8,128)} fusion(f32[40,128,128]{2,1,0:T(8,128)} %get-tuple-element.44, s32[]{:T(128)S(6)} %select_n.15), kind=kLoop, calls=%fused_computation.2 | loop fusion | bytes 1310724 | tf_op jit(solution)/shard_map/dynamic_slice | solution.py:429
  74.2 8.8 %all-to-all-done.3 = f32[32,16,128]{2,1,0:T(8,128)S(1)} async-done(((f32[32,16,128]{2,1,0:T(8,128)}), f32[32,16,128]{2,1,0:T(8,128)S(1)}, u32[]{:S(2)}, u32[]{:S(2)}) %all-to-all-start.3) | async-done | bytes 262176 | tf_op jit(solution)/shard_map/all_to_all | solution.py:393
  83.0 0.7 copy-done
  83.7 3.5 %shard_map.70 = (f32[5,128,128]{2,1,0:T(8,128)}, f32[5,128,128]{2,1,0:T(8,128)}) custom-call(s32[1]{0:T(128)} %bitcast.rank_ref, f32[512,128]{1,0:T(8,128)} %bitcast.20, f32[10,128,128]{2,1,0:T(8,128)} %constant_dynamic-slice_fusion.refs_0_, f32[10,128,128]{2,1,0:T(8,128)} %copy-done.2, f32[10,128,128]{2,1,0:T(8,128)} %copy-done.3, f32[10,128,128]{2,1,0:T(8,128)} %copy-done.4), custom_call_target="tpu_custom_call" | custom-call | flops 671088640 | bytes 2883584 | tf_op jit(solution)/shard_map/pallas_call | solution.py:194
  87.2 0.0 collective-permute-start.4
  87.2 1.4 collective-permute-start.3
  88.6 0.6 collective-permute-start.5
  89.2 2.0 %collective-permute-start.7 = (f32[5,128,128]{2,1,0:T(8,128)}, f32[5,128,128]{2,1,0:T(8,128)S(1)}, u32[]{:S(2)}, u32[]{:S(2)}) collective-permute-start(f32[5,128,128]{2,1,0:T(8,128)} %get-tuple-element.50.refs_8_), channel_id=1, source_target_pairs={{0,1},{1,0},{2,3},{3,2},{4,5},{5,4},{6,7},{7,6},{8,9},{9,8},{10,11... | collective-permute-start | bytes 983048 | tf_op jit(solution)/shard_map/ppermute | solution.py:389
  91.2 9.2 %shard_map.71 = (f32[160,128]{1,0:T(8,128)}, f32[512,128]{1,0:T(8,128)}) custom-call(s32[1]{0:T(128)} %bitcast.rank_ref, f32[512,128]{1,0:T(8,128)} %bitcast.23, f32[512,128]{1,0:T(8,128)} %bitcast.21), custom_call_target="tpu_custom_call" | custom-call | flops 67108864 | bytes 1048576 | tf_op jit(solution)/shard_map/pallas_call | solution.py:359
  100.4 0.0 collective-permute-done.4.refs_5_
  100.4 0.0 collective-permute-done.3.refs_10_
  100.4 0.1 collective-permute-start.6
  100.5 1.4 collective-permute-start.8
  101.9 8.5 %shard_map.72 = f32[5120,128]{1,0:T(8,128)} custom-call(f32[5120,512]{1,0:T(8,128)} %bitcast.18, f32[512,128]{1,0:T(8,128)} %get-tuple-element.57.weight_ref), custom_call_target="tpu_custom_call" | custom-call | flops 2684354560 | bytes 13107200 | tf_op jit(solution)/shard_map/pallas_call | solution.py:277
  110.4 0.0 collective-permute-done.5.refs_6_
  110.4 0.0 collective-permute-done.7.refs_9_
  110.5 0.6 collective-permute-done.6.refs_7_
  111.1 0.0 collective-permute-done.8.refs_11_
  111.1 0.1 copy-done.7
  111.1 0.1 copy-done.8
  111.3 0.5 copy-done.9
  111.8 0.1 copy-done.10
  111.9 10.6 %shard_map.73 = (f32[512,128]{1,0:T(8,128)}, f32[128,128]{1,0:T(8,128)}, f32[1280,128]{1,0:T(8,128)}) custom-call(s32[1]{0:T(128)} %bitcast.rank_ref, f32[160,128]{1,0:T(8,128)} %get-tuple-element.59.weight_ref, f32[5120,512]{1,0:T(8,128)} %bitcast.13, f32[5120,512]{1,0:T(8,128)} %bitcast.14, f32[5120,512]{1,0:T(8,128)} %bitcast.15, f32[5120,512]{1,0:T(8,128)} %bitcast.16, ...), custom_call_target="tpu_custom_call" | custom-call | flops 2684354560 | bytes 13107200 | tf_op jit(solution)/shard_map/pallas_call | solution.py:247
  122.5 0.0 collective-permute-start.9
  122.5 1.5 collective-permute-done.9
  124.0 0.9 add.37
  124.8 1.0 collective-permute-start.11
  125.8 1.5 collective-permute-start.12
  127.3 1.1 collective-permute-start.10
  128.4 3.0 %all-to-all-start.4 = ((f32[32,16,128]{2,1,0:T(8,128)}), f32[32,16,128]{2,1,0:T(8,128)S(1)}, u32[]{:S(2)}, u32[]{:S(2)}) async-start(f32[32,16,128]{2,1,0:T(8,128)} %bitcast.26), calls=%async_computation.4 | async-start | bytes 524288 | tf_op jit(solution)/shard_map/all_to_all | solution.py:393
  131.3 0.0 collective-permute-done.11
  131.3 0.3 collective-permute-done.12
  131.7 2.5 %collective-permute-start.14 = (f32[128,128]{1,0:T(8,128)S(1)}, f32[128,128]{1,0:T(8,128)S(1)}, u32[]{:S(2)}, u32[]{:S(2)}) collective-permute-start(f32[128,128]{1,0:T(8,128)S(1)} %add_add_fusion.1), channel_id=1, source_target_pairs={{0,16},{4,20},{8,24},{12,28},{16,0},{20,4},{24,8},{28,12},{1,17},{... | collective-permute-start | bytes 196616 | tf_op jit(solution)/shard_map/ppermute | solution.py:389
  134.1 1.5 collective-permute-start.15
  135.6 0.1 collective-permute-start.13
  135.6 9.8 %collective-permute-done.14 = f32[128,128]{1,0:T(8,128)S(1)} collective-permute-done((f32[128,128]{1,0:T(8,128)S(1)}, f32[128,128]{1,0:T(8,128)S(1)}, u32[]{:S(2)}, u32[]{:S(2)}) %collective-permute-start.14) | collective-permute-done | bytes 65568 | tf_op jit(solution)/shard_map/ppermute | solution.py:389
  145.4 0.0 collective-permute-done.15
  145.4 0.0 collective-permute-done.13
  145.4 0.7 add_add_fusion.gram_ref
  146.1 0.0 all-to-all-done.4
  146.1 0.7 broadcast_in_dim.8
  146.8 3.9 %all-to-all-start.5 = ((f32[32,16,128]{2,1,0:T(8,128)}), f32[32,16,128]{2,1,0:T(8,128)S(1)}, u32[]{:S(2)}, u32[]{:S(2)}) async-start(f32[32,16,128]{2,1,0:T(8,128)} %broadcast_in_dim.8), calls=%async_computation.5 | async-start | bytes 524288 | tf_op jit(solution)/shard_map/all_to_all | solution.py:393
  150.7 8.8 %shard_map.74 = (f32[128,128]{1,0:T(8,128)}, f32[1280,128]{1,0:T(8,128)}) custom-call(f32[128,128]{1,0:T(8,128)} %add_add_fusion.gram_ref, f32[1280,128]{1,0:T(8,128)} %get-tuple-element.65.middle_ref), custom_call_target="tpu_custom_call" | custom-call | flops 167772160 | bytes 1310720 | tf_op jit(solution)/shard_map/pallas_call | solution.py:378
  159.5 1.9 %all-to-all-done.5 = f32[32,16,128]{2,1,0:T(8,128)S(1)} async-done(((f32[32,16,128]{2,1,0:T(8,128)}), f32[32,16,128]{2,1,0:T(8,128)S(1)}, u32[]{:S(2)}, u32[]{:S(2)}) %all-to-all-start.5) | async-done | bytes 262176 | tf_op jit(solution)/shard_map/all_to_all | solution.py:393
  161.5 1.9 %fusion = f32[128,512]{1,0:T(8,128)} fusion(f32[128,128]{1,0:T(8,128)} %get-tuple-element.67, f32[512,128]{1,0:T(8,128)S(1)} %bitcast.24), kind=kOutput, calls=%fused_computation.6 | convolution fusion | flops 100663296 | bytes 589824 | tf_op jit(solution)/shard_map/dot_general | solution.py:53
  (21 shorter events, 0.1 us)
Async XLA Ops:
  12.1 12.2 %all-to-all-start = ((f32[8,16,128]{2,1,0:T(8,128)}), f32[8,16,128]{2,1,0:T(8,128)S(1)}, u32[]{:S(2)}, u32[]{:S(2)}) async-start(f32[8,16,128]{2,1,0:T(8,128)} %bitcast.27), calls=%async_computation | async-start | bytes 131072 | tf_op jit(solution)/shard_map/all_to_all | solution.py:393
  25.1 20.4 %all-to-all-start.1 = ((f32[32,16,128]{2,1,0:T(8,128)}), f32[32,16,128]{2,1,0:T(8,128)S(1)}, u32[]{:S(2)}, u32[]{:S(2)}) async-start(f32[32,16,128]{2,1,0:T(8,128)} %broadcast_in_dim.6), calls=%async_computation.1 | async-start | bytes 524288 | tf_op jit(solution)/shard_map/all_to_all | solution.py:393
  31.0 36.2 %collective-permute-start = (f32[10,128,128]{2,1,0:T(8,128)}, f32[10,128,128]{2,1,0:T(8,128)S(1)}, u32[]{:S(2)}, u32[]{:S(2)}) collective-permute-start(f32[10,128,128]{2,1,0:T(8,128)} %get-tuple-element.71), channel_id=1, source_target_pairs={{0,1},{1,0},{2,3},{3,2},{4,5},{5,4},{6,7},{7,6},{8,9},{9,8},{10,11... | collective-permute-start | bytes 1966088 | tf_op jit(solution)/shard_map/ppermute | solution.py:389
  32.7 34.5 %collective-permute-start.1 = (f32[10,128,128]{2,1,0:T(8,128)}, f32[10,128,128]{2,1,0:T(8,128)S(1)}, u32[]{:S(2)}, u32[]{:S(2)}) collective-permute-start(f32[10,128,128]{2,1,0:T(8,128)} %get-tuple-element.70), channel_id=1, source_target_pairs={{0,2},{1,3},{2,0},{3,1},{4,6},{5,7},{6,4},{7,5},{8,10},{9,11},{10,... | collective-permute-start | bytes 1966088 | tf_op jit(solution)/shard_map/ppermute | solution.py:389
  34.2 33.0 %collective-permute-start.2 = (f32[10,128,128]{2,1,0:T(8,128)S(1)}, f32[10,128,128]{2,1,0:T(8,128)S(1)}, u32[]{:S(2)}, u32[]{:S(2)}) collective-permute-start(f32[10,128,128]{2,1,0:T(8,128)S(1)} %get-tuple-element.69), channel_id=1, source_target_pairs={{0,3},{1,2},{2,1},{3,0},{4,7},{5,6},{6,5},{7,4},{8,11},{9,10},{10,... | collective-permute-start | bytes 1966088 | tf_op jit(solution)/shard_map/ppermute | solution.py:389
  45.5 0.7 copy-start.1
  67.2 15.8 %copy-start.2 = (f32[10,128,128]{2,1,0:T(8,128)}, f32[10,128,128]{2,1,0:T(8,128)S(1)}, u32[]{:S(2)}) copy-start(f32[10,128,128]{2,1,0:T(8,128)S(1)} %collective-permute-done.refs_1_) | copy-start | bytes 1966084
  67.2 15.8 %copy-start.3 = (f32[10,128,128]{2,1,0:T(8,128)}, f32[10,128,128]{2,1,0:T(8,128)S(1)}, u32[]{:S(2)}) copy-start(f32[10,128,128]{2,1,0:T(8,128)S(1)} %collective-permute-done.1.refs_2_) | copy-start | bytes 1966084
  67.2 15.8 %copy-start.4 = (f32[10,128,128]{2,1,0:T(8,128)}, f32[10,128,128]{2,1,0:T(8,128)S(1)}, u32[]{:S(2)}) copy-start(f32[10,128,128]{2,1,0:T(8,128)S(1)} %collective-permute-done.2.refs_3_) | copy-start | bytes 1966084
  68.0 14.9 %all-to-all-start.3 = ((f32[32,16,128]{2,1,0:T(8,128)}), f32[32,16,128]{2,1,0:T(8,128)S(1)}, u32[]{:S(2)}, u32[]{:S(2)}) async-start(f32[32,16,128]{2,1,0:T(8,128)} %broadcast_in_dim.7), calls=%async_computation.3 | async-start | bytes 524288 | tf_op jit(solution)/shard_map/all_to_all | solution.py:393
  83.0 0.7 copy-start
  87.2 13.2 %collective-permute-start.4 = (f32[5,128,128]{2,1,0:T(8,128)}, f32[5,128,128]{2,1,0:T(8,128)S(1)}, u32[]{:S(2)}, u32[]{:S(2)}) collective-permute-start(f32[5,128,128]{2,1,0:T(8,128)} %get-tuple-element.51.refs_4_), channel_id=1, source_target_pairs={{0,1},{1,0},{2,3},{3,2},{4,5},{5,4},{6,7},{7,6},{8,9},{9,8},{10,11... | collective-permute-start | bytes 983048 | tf_op jit(solution)/shard_map/ppermute | solution.py:389
  87.2 13.2 %collective-permute-start.3 = (f32[5,128,128]{2,1,0:T(8,128)}, f32[5,128,128]{2,1,0:T(8,128)S(1)}, u32[]{:S(2)}, u32[]{:S(2)}) collective-permute-start(f32[5,128,128]{2,1,0:T(8,128)} %get-tuple-element.50.refs_8_), channel_id=1, source_target_pairs={{0,2},{1,3},{2,0},{3,1},{4,6},{5,7},{6,4},{7,5},{8,10},{9,11},{10,... | collective-permute-start | bytes 983048 | tf_op jit(solution)/shard_map/ppermute | solution.py:389
  88.6 21.8 %collective-permute-start.5 = (f32[5,128,128]{2,1,0:T(8,128)}, f32[5,128,128]{2,1,0:T(8,128)S(1)}, u32[]{:S(2)}, u32[]{:S(2)}) collective-permute-start(f32[5,128,128]{2,1,0:T(8,128)} %get-tuple-element.51.refs_4_), channel_id=1, source_target_pairs={{0,2},{1,3},{2,0},{3,1},{4,6},{5,7},{6,4},{7,5},{8,10},{9,11},{10,... | collective-permute-start | bytes 983048 | tf_op jit(solution)/shard_map/ppermute | solution.py:389
  89.2 21.2 %collective-permute-start.7 = (f32[5,128,128]{2,1,0:T(8,128)}, f32[5,128,128]{2,1,0:T(8,128)S(1)}, u32[]{:S(2)}, u32[]{:S(2)}) collective-permute-start(f32[5,128,128]{2,1,0:T(8,128)} %get-tuple-element.50.refs_8_), channel_id=1, source_target_pairs={{0,1},{1,0},{2,3},{3,2},{4,5},{5,4},{6,7},{7,6},{8,9},{9,8},{10,11... | collective-permute-start | bytes 983048 | tf_op jit(solution)/shard_map/ppermute | solution.py:389
  100.4 10.0 %copy-start.5 = (f32[5,128,128]{2,1,0:T(8,128)}, f32[5,128,128]{2,1,0:T(8,128)S(1)}, u32[]{:S(2)}) copy-start(f32[5,128,128]{2,1,0:T(8,128)S(1)} %collective-permute-done.4.refs_5_) | copy-start | bytes 983044
  100.4 10.0 %copy-start.6 = (f32[5,128,128]{2,1,0:T(8,128)}, f32[5,128,128]{2,1,0:T(8,128)S(1)}, u32[]{:S(2)}) copy-start(f32[5,128,128]{2,1,0:T(8,128)S(1)} %collective-permute-done.3.refs_10_) | copy-start | bytes 983044
  100.4 10.6 %collective-permute-start.6 = (f32[5,128,128]{2,1,0:T(8,128)S(1)}, f32[5,128,128]{2,1,0:T(8,128)S(1)}, u32[]{:S(2)}, u32[]{:S(2)}) collective-permute-start(f32[5,128,128]{2,1,0:T(8,128)S(1)} %collective-permute-done.4.refs_5_), channel_id=1, source_target_pairs={{0,2},{1,3},{2,0},{3,1},{4,6},{5,7},{6,4},{7,5},{8,10},{9,11},{10,... | collective-permute-start | bytes 983048 | tf_op jit(solution)/shard_map/ppermute | solution.py:389
  100.5 10.6 %collective-permute-start.8 = (f32[5,128,128]{2,1,0:T(8,128)S(1)}, f32[5,128,128]{2,1,0:T(8,128)S(1)}, u32[]{:S(2)}, u32[]{:S(2)}) collective-permute-start(f32[5,128,128]{2,1,0:T(8,128)S(1)} %collective-permute-done.3.refs_10_), channel_id=1, source_target_pairs={{0,1},{1,0},{2,3},{3,2},{4,5},{5,4},{6,7},{7,6},{8,9},{9,8},{10,11... | collective-permute-start | bytes 983048 | tf_op jit(solution)/shard_map/ppermute | solution.py:389
  110.4 0.7 copy-start.7
  110.4 0.8 copy-start.8
  111.1 0.7 copy-start.9
  111.1 0.8 copy-start.10
  122.5 1.5 collective-permute-start.9
  124.8 6.5 %collective-permute-start.11 = (f32[128,128]{1,0:T(8,128)S(1)}, f32[128,128]{1,0:T(8,128)S(1)}, u32[]{:S(2)}, u32[]{:S(2)}) collective-permute-start(f32[128,128]{1,0:T(8,128)S(1)} %add.37), channel_id=1, source_target_pairs={{0,2},{1,3},{2,0},{3,1},{4,6},{5,7},{6,4},{7,5},{8,10},{9,11},{10,... | collective-permute-start | bytes 196616 | tf_op jit(solution)/shard_map/ppermute | solution.py:389
  125.8 5.8 %collective-permute-start.12 = (f32[128,128]{1,0:T(8,128)S(1)}, f32[128,128]{1,0:T(8,128)S(1)}, u32[]{:S(2)}, u32[]{:S(2)}) collective-permute-start(f32[128,128]{1,0:T(8,128)S(1)} %add.37), channel_id=1, source_target_pairs={{0,3},{1,2},{2,1},{3,0},{4,7},{5,6},{6,5},{7,4},{8,11},{9,10},{10,... | collective-permute-start | bytes 196616 | tf_op jit(solution)/shard_map/ppermute | solution.py:389
  127.3 4.4 %collective-permute-start.10 = (f32[128,128]{1,0:T(8,128)S(1)}, f32[128,128]{1,0:T(8,128)S(1)}, u32[]{:S(2)}, u32[]{:S(2)}) collective-permute-start(f32[128,128]{1,0:T(8,128)S(1)} %add.37), channel_id=1, source_target_pairs={{0,1},{1,0},{2,3},{3,2},{4,5},{5,4},{6,7},{7,6},{8,9},{9,8},{10,11... | collective-permute-start | bytes 196616 | tf_op jit(solution)/shard_map/ppermute | solution.py:389
  128.4 17.7 %all-to-all-start.4 = ((f32[32,16,128]{2,1,0:T(8,128)}), f32[32,16,128]{2,1,0:T(8,128)S(1)}, u32[]{:S(2)}, u32[]{:S(2)}) async-start(f32[32,16,128]{2,1,0:T(8,128)} %bitcast.26), calls=%async_computation.4 | async-start | bytes 524288 | tf_op jit(solution)/shard_map/all_to_all | solution.py:393
  131.7 13.7 %collective-permute-start.14 = (f32[128,128]{1,0:T(8,128)S(1)}, f32[128,128]{1,0:T(8,128)S(1)}, u32[]{:S(2)}, u32[]{:S(2)}) collective-permute-start(f32[128,128]{1,0:T(8,128)S(1)} %add_add_fusion.1), channel_id=1, source_target_pairs={{0,16},{4,20},{8,24},{12,28},{16,0},{20,4},{24,8},{28,12},{1,17},{... | collective-permute-start | bytes 196616 | tf_op jit(solution)/shard_map/ppermute | solution.py:389
  134.1 11.3 %collective-permute-start.15 = (f32[128,128]{1,0:T(8,128)S(1)}, f32[128,128]{1,0:T(8,128)S(1)}, u32[]{:S(2)}, u32[]{:S(2)}) collective-permute-start(f32[128,128]{1,0:T(8,128)S(1)} %add_add_fusion.1), channel_id=1, source_target_pairs={{0,24},{4,28},{8,16},{12,20},{16,8},{20,12},{24,0},{28,4},{1,25},{... | collective-permute-start | bytes 196616 | tf_op jit(solution)/shard_map/ppermute | solution.py:389
  135.6 9.8 %collective-permute-start.13 = (f32[128,128]{1,0:T(8,128)S(1)}, f32[128,128]{1,0:T(8,128)S(1)}, u32[]{:S(2)}, u32[]{:S(2)}) collective-permute-start(f32[128,128]{1,0:T(8,128)S(1)} %add_add_fusion.1), channel_id=1, source_target_pairs={{0,8},{4,12},{8,0},{12,4},{16,24},{20,28},{24,16},{28,20},{1,9},{5... | collective-permute-start | bytes 196616 | tf_op jit(solution)/shard_map/ppermute | solution.py:389
  146.8 14.6 %all-to-all-start.5 = ((f32[32,16,128]{2,1,0:T(8,128)}), f32[32,16,128]{2,1,0:T(8,128)S(1)}, u32[]{:S(2)}, u32[]{:S(2)}) async-start(f32[32,16,128]{2,1,0:T(8,128)} %broadcast_in_dim.8), calls=%async_computation.5 | async-start | bytes 524288 | tf_op jit(solution)/shard_map/all_to_all | solution.py:393

commit v9 on v8

--- a/solution.py
+++ b/solution.py
@@ -75,8 +75,9 @@
     block = left_ref.shape[1]
     local_rows = rows_ref.shape[0] // block
     columns = right_ref.shape[1]
-    right = twice(both_parts(right_ref[...], 1), 0)
-    rows_ref[...] = fold(mxu(both_parts(jnp.concatenate([rows_of(ref)[...] for ref in core_refs], axis=0), 1), right, NN), 1)
+    right = both_parts(right_ref[...], 1)
+    core = jnp.concatenate([rows_of(ref)[...] for ref in core_refs], axis=0)
+    rows_ref[...] = fold(fold(mxu(both_parts(core, 0), right, NN), 0), 1)
     left_rows = rows_of(left_ref)
 
     @pl.when(pl.program_id(0) == 0)
@@ -89,9 +90,10 @@
         sketched_ref[n] = rows
         sides.append(rows)
         lefts.append(left_rows[pl.ds(n, columns, stride=block), :])
-    side = both_parts(jnp.concatenate(sides, axis=1), 1)
-    left = twice(both_parts(jnp.concatenate(lefts, axis=1), 0), 1)
-    part_ref[...] += fold(mxu(side, left, NT), 1)
+    side = both_parts(jnp.concatenate(sides, axis=1), 0)
+    left = both_parts(jnp.concatenate(lefts, axis=1), 0)
+    part = fold(fold(mxu(side, left, NT), 0), 1)
+    part_ref[...] += part
 
 
 def sketch(core_two, right_sketch, sketch_core):
@@ -123,36 +125,41 @@
     return block
 
 
-def square_kernel(core_ref, square_ref, sum_ref):
+def square_kernel(last, core_ref, *refs):
     step = pl.program_id(0)
+    before_refs, out_ref, sum_ref = refs[:-2], refs[-2], refs[-1]
     width = core_ref.shape[1]
     high, low = split(core_ref[...])
 
     @pl.when(step == 0)
     def _():
-        sum_ref[...] = jnp.zeros_like(sum_ref)
+        sum_ref[...] = before_refs[0][...] if before_refs else jnp.zeros_like(sum_ref)
 
     sum_ref[...] += mxu(high, jnp.concatenate([high, low], axis=1), TN)
 
     @pl.when(step == pl.num_programs(0) - 1)
     def _():
-        cross = sum_ref[:, width:]
-        square_ref[...] = both_parts(sum_ref[:, :width] + cross + cross.T, 1)
-
-
-def square_of(flat_one):
+        if last:
+            cross = sum_ref[:, width:]
+            out_ref[...] = both_parts(sum_ref[:, :width] + cross + cross.T, 1)
+        else:
+            out_ref[...] = sum_ref[...]
+
+
+def square_of(flat_one, first, count, before, last):
     rows, width = flat_one.shape
     block = block_of(rows)
-    return call(
-        square_kernel,
-        4 * rows * width * width,
-        4 * flat_one.size,
-        grid=(rows // block,),
-        in_specs=[pl.BlockSpec((block, width), lambda i: (i, 0))],
-        out_specs=pl.BlockSpec((width, 2 * width), lambda i: (0, 0)),
-        out_shape=jax.ShapeDtypeStruct((width, 2 * width), jnp.bfloat16),
+    whole = pl.BlockSpec((width, 2 * width), lambda i: (0, 0))
+    return call(
+        functools.partial(square_kernel, last),
+        4 * count * block * width * width,
+        4 * count * block * width,
+        grid=(count,),
+        in_specs=[pl.BlockSpec((block, width), lambda i: (i + first, 0))] + [whole] * len(before),
+        out_specs=whole,
+        out_shape=jax.ShapeDtypeStruct((width, 2 * width), jnp.bfloat16 if last else jnp.float32),
         scratch_shapes=[pltpu.VMEM((width, 2 * width), jnp.float32)],
-    )(flat_one)
+    )(flat_one, *before)
 
 
 def product_kernel(square_ref, bridge_ref, out_ref):
@@ -169,30 +176,29 @@
     )(square, bridge)
 
 
-def loose_kernel(rank_ref, raw_ref, *refs):
+def loose_kernel(plan, rank_ref, raw_ref, *refs):
     piece_refs, out_refs = refs[:-2], refs[-2:]
+    ranks = len(plan[0])
     local_rows, columns = piece_refs[0].shape[1:]
     rows = []
-    for offset in range(len(piece_refs)):
+    for offset in range(ranks):
         start = pl.multiple_of((rank_ref[0] ^ offset) * local_rows, local_rows)
         rows.append(raw_ref[pl.ds(start, local_rows), :])
     raw = twice(both_parts(jnp.concatenate(rows, axis=0), 1).T, 1)
-    first = 0
-    for out_ref in out_refs:
+    for places, out_ref in zip(plan, out_refs):
         count = out_ref.shape[0]
-        value = [jnp.concatenate([ref[first + n] for n in range(count)], axis=1) for ref in piece_refs]
+        value = [jnp.concatenate([piece_refs[ref][first + n] for n in range(count)], axis=1) for ref, first in places]
         product = fold(mxu(raw, both_parts(jnp.concatenate(value, axis=0), 0), NN), 0)
         for n in range(count):
             out_ref[n] = product[:, n * columns:(n + 1) * columns]
-        first += count
-
-
-def loosen(rank_index, raw, pieces, halves):
+
+
+def loosen(rank_index, raw, pieces, plan, halves):
     columns = raw.shape[1]
     size = sum(piece.size for piece in pieces)
     whole = pl.BlockSpec(memory_space=pltpu.VMEM)
     return call(
-        loose_kernel,
+        functools.partial(loose_kernel, plan),
         8 * size * columns,
         4 * raw.size + 4 * size,
         in_specs=[pl.BlockSpec(memory_space=pltpu.SMEM)] + [whole] * (len(pieces) + 1),
@@ -425,26 +431,37 @@
 
     sketched, part = sketch(core_two, right_sketch, sketch_core)
 
-    def part_for(offset, source):
-        return lax.dynamic_slice_in_dim(source, (rank ^ offset) * share, share, 0)
+    def part_for(offset, source, half=None):
+        start = (rank ^ offset) * share + (halves[0] if half else 0)
+        return lax.dynamic_slice_in_dim(source, start, share if half is None else halves[half], 0)
 
     cut_bits = [1 << bit for bit in range((cuts - 1).bit_length())]
     bits = [1 << bit for bit in range((ranks - 1).bit_length())]
+    far = ranks - 1
+    blocks = flat_one.shape[0] // block_of(flat_one.shape[0])
+    early = 2 * blocks // 5
     bridge_rows = jnp.sum(exchange(part.reshape(cuts, local_rows // cuts, columns), "cuts"), axis=0)
-    flat_late, bridge_rows = after(flat_one, bridge_rows)
+    flat_late, part = after(flat_one, part)
+    square = [square_of(flat_late, 0, early, [], False)] if early else []
+    flat_late, (bridge_rows, square) = after(flat_one, (bridge_rows, square))
     sketched, bridge_rows = after(sketched, bridge_rows)
-    moved = [swap(part_for(offset, sketched), "rank", offset) for offset in range(1, ranks)]
+    moved = [swap(part_for(offset, sketched), "rank", offset) for offset in range(1, far)]
+    moved.append(swap(part_for(far, sketched, 0), "rank", far))
     bridge = gather_all(bridge_rows, ("rank", "cuts")).reshape(width, columns)
-    square = square_of(flat_late)
+    square = square_of(flat_late, early, blocks - early, square, True)
 
     raw = product_of(square, bridge)
     sketched, raw = after(sketched, raw)
     own = part_for(0, sketched)
     raw = jnp.sum(exchange(raw.reshape(parts, -1, columns), both), axis=0)
     raw, moved = after(raw, moved)
+    sketched, raw = after(sketched, raw)
+    pieces = [own] + moved + [swap(part_for(far, sketched, 1), "rank", far)]
     raw = gather_all(raw, both).reshape(width, columns)
 
-    loose = loosen(rank_index, raw, [own] + moved, halves)
+    near = list(range(far))
+    plan = [[(ref, 0) for ref in near + [far]], [(ref, halves[0]) for ref in near] + [(ranks, 0)]]
+    loose = loosen(rank_index, raw, pieces, plan, halves)
     loose, (bridge, raw) = after(loose, (bridge, raw))
     scale = math.sqrt(local_rows * ranks * slices * cuts)
     weight, solve = first_factor(rank_index, bridge, raw, scale, local_rows, band)
@@ -459,16 +476,17 @@
             found.update(moved)
         everyone += [found[offset] for offset in range(ranks)]
 
-    left_core = apply_to(flat_one, solve).reshape(local_rows, slices, columns)
-    weight, left_core = after(weight, left_core)
     raw, gram, middle = carry_rows(rank_index, weight, flat_two, everyone, halves, share, band)
+    flat_late, raw = after(flat_one, raw)
+    left_core = apply_to(flat_late, solve)
     raw = jnp.sum(exchange(raw.reshape(parts, -1, columns), both), axis=0)
     for axis, pair in [("cuts", [1])] + pairs_of("rank", bits) + pairs_of("cuts", cut_bits[1:]):
         other = gram + swap(gram, axis, pair[0])
         if len(pair) > 1:
             other = other + (swap(gram, axis, pair[1]) + swap(gram, axis, pair[0] ^ pair[1]))
         gram = other
-    raw, gram = after(raw, gram)
+    raw, (gram, left_core) = after(raw, (gram, left_core))
+    left_core = left_core.reshape(local_rows, slices, columns)
     raw = gather_all(raw, both).reshape(width, columns)
     scale = math.sqrt(columns * slices * cuts)
     inverse, middle = last_factor(gram, middle, scale)

time: 164 us -> 167 us (1.018)
  blocking collectives: 18.5 us -> 0 us
  starting transfers between devices: 37 us -> 51.2 us
  waiting for transfers between devices: 28.8 us -> 33.8 us
  Pallas kernels: 65.5 us -> 68.3 us
    all_to_all x1 -> x0, blocking collectives: 18.5 us -> none  [exchange(): return lax.all_to_all(value, axes, 0, 0, tiled=True)]
    ppermute x16 -> x17, waiting for transfers between devices: 12.2 us -> 24.2 us  [swap(): lax.ppermute(value, axis, [(i, i ^ offset) for i in range(lax.axis_size(a...]
    all_to_all x5 -> x6, starting transfers between devices: 20.5 us -> 28.8 us  [exchange(): return lax.all_to_all(value, axes, 0, 0, tiled=True)]
    all_to_all x5 -> x6, waiting for transfers between devices: 16.6 us -> 9.55 us  [exchange(): return lax.all_to_all(value, axes, 0, 0, tiled=True)]
    ppermute x16 -> x17, starting transfers between devices: 16.5 us -> 22.4 us  [swap(): lax.ppermute(value, axis, [(i, i ^ offset) for i in range(lax.axis_size(a...]
    pallas_call x2 -> x3, Pallas kernels: 14.6 us -> 18.5 us  [the longest x2 15 us: square_of(): call(functools.partial(square_kernel, last), 4 * count * block * width *...]
    dynamic_slice x2 -> x4, local copies, waits for them, and re-layouts: 4.71 us -> 3.56 us  [part_for(): lax.dynamic_slice_in_dim(source, start, share if half is None else halves...]
  transfers between devices with their start and end apart: 21 -> 23, of which waited for: 7 -> 8; matrix products, arithmetic and copies ran while one was open for 3% -> 3% of each run, Pallas kernels for 24% -> 26%
where the time goes in v9:
time: 167 us; the launch traced here: 166 us
  Pallas kernels  68.3 us (41%)
  starting transfers between devices  51.2 us (31%)
  waiting for transfers between devices  33.8 us (20%)
  local copies, waits for them, and re-layouts  8.06 us (5%)
  matrix products  1.92 us (1%)
    all_to_all x6, starting transfers between devices, exchange(): return lax.all_to_all(value, axes, 0, 0, tiled=True)  28.8 us
    ppermute x17, waiting for transfers between devices, swap(): lax.ppermute(value, axis, [(i, i ^ offset) for i in range(lax.axis_size(a...  24.2 us
    ppermute x17, starting transfers between devices, swap(): lax.ppermute(value, axis, [(i, i ^ offset) for i in range(lax.axis_size(a...  22.4 us
    pallas_call x2, Pallas kernels, square_of(): call(functools.partial(square_kernel, last), 4 * count * block * width *...  15 us
    pallas_call x1, Pallas kernels, carry_rows(): call(functools.partial(carry_kernel, halves, share), 8 * flat_two.size *...  10.6 us
    pallas_call x1, Pallas kernels, sketch(): call(sketch_kernel, 2 * core_two.size * columns * 4, 4 * (core_two.size +...  10.3 us
    all_to_all x6, waiting for transfers between devices, exchange(): return lax.all_to_all(value, axes, 0, 0, tiled=True)  9.55 us
    pallas_call x1, Pallas kernels, first_factor(): call(functools.partial(first_kernel, scale, band), 8 * raw.size * columns...  9.18 us
  transfers between devices with their start and end apart: 23, of which 8 were waited for; matrix products, arithmetic and copies ran while one was open for 3% of the time, Pallas kernels for 26%

profile of v9, /device:TPU:0, one launch (start us, length us, event | category | flops | bytes accessed | tf_op | source)
XLA Modules:
  0.0 165.7 jit_solution(2186807789157405654)
XLA Ops:
  0.6 10.3 %shard_map.67 = (f32[40,128,128]{2,1,0:T(8,128)}, f32[128,128]{1,0:T(8,128)}) custom-call(f32[128,40,512]{2,1,0:T(8,128)} %refs_3_.1, f32[128,40,512]{2,1,0:T(8,128)} %refs_3_.1, f32[128,40,512]{2,1,0:T(8,128)} %refs_3_.1, f32[128,40,512]{2,1,0:T(8,128)} %refs_3_.1, f32[512,128]{1,0:T(8,128)} %refs_4_.1, f32[128,40,128]{2,1,0:T(8,128)} %refs_5_.1), custom_call_target="tpu_custom_call" | custom-call | flops 2684354560 | bytes 15728640 | tf_op jit(solution)/shard_map/pallas_call | solution.py:102
  10.9 6.3 %all-to-all-start = ((f32[8,16,128]{2,1,0:T(8,128)}), f32[8,16,128]{2,1,0:T(8,128)S(1)}, u32[]{:S(2)}, u32[]{:S(2)}) async-start(f32[8,16,128]{2,1,0:T(8,128)} %bitcast.28), calls=%async_computation | async-start | bytes 131072 | tf_op jit(solution)/shard_map/all_to_all | solution.py:399
  17.3 6.5 %shard_map.68.refs_0_ = f32[512,1024]{1,0:T(8,128)} custom-call(f32[5120,512]{1,0:T(8,128)} %bitcast.17), custom_call_target="tpu_custom_call" | custom-call | flops 2147483648 | bytes 4194304 | tf_op jit(solution)/shard_map/pallas_call | solution.py:153
  23.8 0.0 all-to-all-done
  23.8 0.7 broadcast_in_dim.6
  24.5 6.0 %all-to-all-start.1 = ((f32[32,16,128]{2,1,0:T(8,128)}), f32[32,16,128]{2,1,0:T(8,128)S(1)}, u32[]{:S(2)}, u32[]{:S(2)}) async-start(f32[32,16,128]{2,1,0:T(8,128)} %broadcast_in_dim.6), calls=%async_computation.1 | async-start | bytes 524288 | tf_op jit(solution)/shard_map/all_to_all | solution.py:399
  30.6 1.1 constant_dynamic-slice_fusion.3
  31.8 1.8 %collective-permute-start = (f32[10,128,128]{2,1,0:T(8,128)}, f32[10,128,128]{2,1,0:T(8,128)S(1)}, u32[]{:S(2)}, u32[]{:S(2)}) collective-permute-start(f32[10,128,128]{2,1,0:T(8,128)} %get-tuple-element.80), channel_id=1, source_target_pairs={{0,1},{1,0},{2,3},{3,2},{4,5},{5,4},{6,7},{7,6},{8,9},{9,8},{10,11... | collective-permute-start | bytes 1966088 | tf_op jit(solution)/shard_map/ppermute | solution.py:395
  33.5 1.5 collective-permute-start.1
  35.0 8.5 %shard_map.69.square_ref = bf16[512,1024]{1,0:T(8,128)(2,1)} custom-call(f32[5120,512]{1,0:T(8,128)} %bitcast.18, f32[512,1024]{1,0:T(8,128)} %shard_map.68.refs_0_), custom_call_target="tpu_custom_call" | custom-call | flops 3221225472 | bytes 6291456 | tf_op jit(solution)/shard_map/pallas_call | solution.py:153
  43.5 0.0 all-to-all-done.1
  43.5 0.7 copy-done.2
  44.2 2.4 %shard_map.70 = f32[512,128]{1,0:T(8,128)} custom-call(bf16[512,1024]{1,0:T(8,128)(2,1)} %shard_map.69.square_ref, f32[512,128]{1,0:T(8,128)} %bitcast.23), custom_call_target="tpu_custom_call" | custom-call | flops 268435456 | bytes 1572864 | tf_op jit(solution)/shard_map/pallas_call | solution.py:171
  46.6 3.7 %all-to-all-start.2 = ((f32[32,16,128]{2,1,0:T(8,128)}), f32[32,16,128]{2,1,0:T(8,128)S(1)}, u32[]{:S(2)}, u32[]{:S(2)}) async-start(f32[32,16,128]{2,1,0:T(8,128)} %bitcast.26), calls=%async_computation.2 | async-start | bytes 524288 | tf_op jit(solution)/shard_map/all_to_all | solution.py:399
  50.3 0.8 constant_dynamic-slice_fusion.2
  51.1 2.7 %collective-permute-start.2 = (f32[5,128,128]{2,1,0:T(8,128)}, f32[5,128,128]{2,1,0:T(8,128)}, u32[]{:S(2)}, u32[]{:S(2)}) collective-permute-start(f32[5,128,128]{2,1,0:T(8,128)} %constant_dynamic-slice_fusion.2), channel_id=1, source_target_pairs={{0,3},{1,2},{2,1},{3,0},{4,7},{5,6},{6,5},{7,4},{8,11},{9,10},{10,... | collective-permute-start | bytes 983048 | tf_op jit(solution)/shard_map/ppermute | solution.py:395
  53.8 7.6 %all-to-all-done.2 = f32[32,16,128]{2,1,0:T(8,128)S(1)} async-done(((f32[32,16,128]{2,1,0:T(8,128)}), f32[32,16,128]{2,1,0:T(8,128)S(1)}, u32[]{:S(2)}, u32[]{:S(2)}) %all-to-all-start.2) | async-done | bytes 262176 | tf_op jit(solution)/shard_map/all_to_all | solution.py:399
  61.4 2.9 %collective-permute-done.2.refs_3_ = f32[5,128,128]{2,1,0:T(8,128)} collective-permute-done((f32[5,128,128]{2,1,0:T(8,128)}, f32[5,128,128]{2,1,0:T(8,128)}, u32[]{:S(2)}, u32[]{:S(2)}) %collective-permute-start.2) | collective-permute-done | bytes 327712 | tf_op jit(solution)/shard_map/ppermute | solution.py:395
  64.3 0.0 collective-permute-done.refs_1_
  64.3 0.0 collective-permute-done.1.refs_2_
  64.3 0.8 broadcast_in_dim.7
  65.1 4.5 %all-to-all-start.3 = ((f32[32,16,128]{2,1,0:T(8,128)}), f32[32,16,128]{2,1,0:T(8,128)S(1)}, u32[]{:S(2)}, u32[]{:S(2)}) async-start(f32[32,16,128]{2,1,0:T(8,128)} %broadcast_in_dim.7), calls=%async_computation.3 | async-start | bytes 524288 | tf_op jit(solution)/shard_map/all_to_all | solution.py:399
  69.6 0.8 constant_dynamic-slice_fusion
  70.4 2.5 %collective-permute-start.3 = (f32[5,128,128]{2,1,0:T(8,128)}, f32[5,128,128]{2,1,0:T(8,128)}, u32[]{:S(2)}, u32[]{:S(2)}) collective-permute-start(f32[5,128,128]{2,1,0:T(8,128)} %constant_dynamic-slice_fusion), channel_id=1, source_target_pairs={{0,3},{1,2},{2,1},{3,0},{4,7},{5,6},{6,5},{7,4},{8,11},{9,10},{10,... | collective-permute-start | bytes 983048 | tf_op jit(solution)/shard_map/ppermute | solution.py:395
  72.9 0.9 constant_dynamic-slice_fusion.1.refs_0_
  73.8 9.6 %collective-permute-done.3.refs_4_ = f32[5,128,128]{2,1,0:T(8,128)} collective-permute-done((f32[5,128,128]{2,1,0:T(8,128)}, f32[5,128,128]{2,1,0:T(8,128)}, u32[]{:S(2)}, u32[]{:S(2)}) %collective-permute-start.3) | collective-permute-done | bytes 327712 | tf_op jit(solution)/shard_map/ppermute | solution.py:395
  83.4 0.0 all-to-all-done.3
  83.4 0.7 copy-done.1
  84.1 3.5 %shard_map.71 = (f32[5,128,128]{2,1,0:T(8,128)}, f32[5,128,128]{2,1,0:T(8,128)}) custom-call(s32[1]{0:T(128)} %bitcast.1.rank_ref, f32[512,128]{1,0:T(8,128)} %bitcast.21, f32[10,128,128]{2,1,0:T(8,128)} %constant_dynamic-slice_fusion.1.refs_0_, f32[10,128,128]{2,1,0:T(8,128)} %copy-done.3, f32[10,128,128]{2,1,0:T(8,128)} %collective-permute-done.1.refs_2_, ...), custom_call_target="tpu_custom_call" | custom-call | flops 671088640 | bytes 2883584 | tf_op jit(solution)/shard_map/pallas_call | solution.py:200
  87.6 1.1 collective-permute-start.5
  88.7 1.0 collective-permute-start.4
  89.7 1.1 collective-permute-start.6
  90.8 0.9 collective-permute-start.8
  91.7 9.2 %shard_map.72 = (f32[160,128]{1,0:T(8,128)}, f32[512,128]{1,0:T(8,128)}) custom-call(s32[1]{0:T(128)} %bitcast.1.rank_ref, f32[512,128]{1,0:T(8,128)} %bitcast.24, f32[512,128]{1,0:T(8,128)} %bitcast.22), custom_call_target="tpu_custom_call" | custom-call | flops 67108864 | bytes 1048576 | tf_op jit(solution)/shard_map/pallas_call | solution.py:365
  100.9 0.0 collective-permute-done.5.refs_5_
  100.9 1.1 collective-permute-start.7
  102.0 1.1 collective-permute-start.9
  103.0 3.6 %collective-permute-done.6.refs_6_ = f32[5,128,128]{2,1,0:T(8,128)S(1)} collective-permute-done((f32[5,128,128]{2,1,0:T(8,128)}, f32[5,128,128]{2,1,0:T(8,128)S(1)}, u32[]{:S(2)}, u32[]{:S(2)}) %collective-permute-start.6) | collective-permute-done | bytes 327712 | tf_op jit(solution)/shard_map/ppermute | solution.py:395
  106.6 0.0 collective-permute-done.8.refs_9_
  106.6 5.3 %collective-permute-done.7.refs_7_ = f32[5,128,128]{2,1,0:T(8,128)S(1)} collective-permute-done((f32[5,128,128]{2,1,0:T(8,128)S(1)}, f32[5,128,128]{2,1,0:T(8,128)S(1)}, u32[]{:S(2)}, u32[]{:S(2)}) %collective-permute-start.7) | collective-permute-done | bytes 327712 | tf_op jit(solution)/shard_map/ppermute | solution.py:395
  112.0 0.7 copy-done.8
  112.7 0.2 copy-done.9
  112.9 10.6 %shard_map.73 = (f32[512,128]{1,0:T(8,128)}, f32[128,128]{1,0:T(8,128)}, f32[1280,128]{1,0:T(8,128)}) custom-call(s32[1]{0:T(128)} %bitcast.1.rank_ref, f32[160,128]{1,0:T(8,128)} %get-tuple-element.65.weight_ref, f32[5120,512]{1,0:T(8,128)} %bitcast.13, f32[5120,512]{1,0:T(8,128)} %bitcast.14, f32[5120,512]{1,0:T(8,128)} %bitcast.15, f32[5120,512]{1,0:T(8,128)} %bitcast.16, ...), custom_call_target="tpu_custom_call" | custom-call | flops 2684354560 | bytes 13107200 | tf_op jit(solution)/shard_map/pallas_call | solution.py:253
  123.5 0.0 collective-permute-start.10
  123.5 1.5 collective-permute-done.10
  124.9 0.9 add.47
  125.8 1.0 collective-permute-start.12
  126.8 1.5 collective-permute-start.13
  128.3 1.1 collective-permute-start.11
  129.3 4.1 %all-to-all-start.4 = ((f32[32,16,128]{2,1,0:T(8,128)}), f32[32,16,128]{2,1,0:T(8,128)S(1)}, u32[]{:S(2)}, u32[]{:S(2)}) async-start(f32[32,16,128]{2,1,0:T(8,128)} %bitcast.27), calls=%async_computation.4 | async-start | bytes 524288 | tf_op jit(solution)/shard_map/all_to_all | solution.py:399
  133.4 0.0 collective-permute-done.12
  133.4 0.0 collective-permute-done.11
  133.4 2.7 %collective-permute-start.15 = (f32[128,128]{1,0:T(8,128)S(1)}, f32[128,128]{1,0:T(8,128)S(1)}, u32[]{:S(2)}, u32[]{:S(2)}) collective-permute-start(f32[128,128]{1,0:T(8,128)S(1)} %add_add_fusion.1), channel_id=1, source_target_pairs={{0,16},{4,20},{8,24},{12,28},{16,0},{20,4},{24,8},{28,12},{1,17},{... | collective-permute-start | bytes 196616 | tf_op jit(solution)/shard_map/ppermute | solution.py:395
  136.2 1.5 collective-permute-start.16
  137.6 0.1 collective-permute-start.14
  137.7 8.5 %shard_map.74 = f32[5120,128]{1,0:T(8,128)} custom-call(f32[5120,512]{1,0:T(8,128)} %bitcast.19, f32[512,128]{1,0:T(8,128)} %get-tuple-element.72.weight_ref), custom_call_target="tpu_custom_call" | custom-call | flops 2684354560 | bytes 13107200 | tf_op jit(solution)/shard_map/pallas_call | solution.py:283
  146.2 1.3 collective-permute-done.15
  147.5 0.6 add_add_fusion.gram_ref
  148.1 0.0 all-to-all-done.4
  148.1 0.7 broadcast_in_dim.8
  148.9 4.1 %all-to-all-start.5 = ((f32[32,16,128]{2,1,0:T(8,128)}), f32[32,16,128]{2,1,0:T(8,128)S(1)}, u32[]{:S(2)}, u32[]{:S(2)}) async-start(f32[32,16,128]{2,1,0:T(8,128)} %broadcast_in_dim.8), calls=%async_computation.5 | async-start | bytes 524288 | tf_op jit(solution)/shard_map/all_to_all | solution.py:399
  153.0 8.8 %shard_map.75 = (f32[128,128]{1,0:T(8,128)}, f32[1280,128]{1,0:T(8,128)}) custom-call(f32[128,128]{1,0:T(8,128)} %add_add_fusion.gram_ref, f32[1280,128]{1,0:T(8,128)} %get-tuple-element.75.middle_ref), custom_call_target="tpu_custom_call" | custom-call | flops 167772160 | bytes 1310720 | tf_op jit(solution)/shard_map/pallas_call | solution.py:384
  161.8 1.9 %all-to-all-done.5 = f32[32,16,128]{2,1,0:T(8,128)S(1)} async-done(((f32[32,16,128]{2,1,0:T(8,128)}), f32[32,16,128]{2,1,0:T(8,128)S(1)}, u32[]{:S(2)}, u32[]{:S(2)}) %all-to-all-start.5) | async-done | bytes 262176 | tf_op jit(solution)/shard_map/all_to_all | solution.py:399
  163.7 1.9 %fusion = f32[128,512]{1,0:T(8,128)} fusion(f32[128,128]{1,0:T(8,128)} %get-tuple-element.77, f32[512,128]{1,0:T(8,128)S(1)} %bitcast.25), kind=kOutput, calls=%fused_computation.7 | convolution fusion | flops 100663296 | bytes 589824 | tf_op jit(solution)/shard_map/dot_general | solution.py:53
  (25 shorter events, 0.1 us)
Async XLA Ops:
  10.9 12.9 %all-to-all-start = ((f32[8,16,128]{2,1,0:T(8,128)}), f32[8,16,128]{2,1,0:T(8,128)S(1)}, u32[]{:S(2)}, u32[]{:S(2)}) async-start(f32[8,16,128]{2,1,0:T(8,128)} %bitcast.28), calls=%async_computation | async-start | bytes 131072 | tf_op jit(solution)/shard_map/all_to_all | solution.py:399
  17.3 13.4 %copy-start = (f32[40,128,128]{2,1,0:T(8,128)S(1)}, f32[40,128,128]{2,1,0:T(8,128)}, u32[]{:S(2)}) copy-start(f32[40,128,128]{2,1,0:T(8,128)} %get-tuple-element.56) | copy-start | bytes 7864324
  24.5 18.9 %all-to-all-start.1 = ((f32[32,16,128]{2,1,0:T(8,128)}), f32[32,16,128]{2,1,0:T(8,128)S(1)}, u32[]{:S(2)}, u32[]{:S(2)}) async-start(f32[32,16,128]{2,1,0:T(8,128)} %broadcast_in_dim.6), calls=%async_computation.1 | async-start | bytes 524288 | tf_op jit(solution)/shard_map/all_to_all | solution.py:399
  31.8 32.5 %collective-permute-start = (f32[10,128,128]{2,1,0:T(8,128)}, f32[10,128,128]{2,1,0:T(8,128)S(1)}, u32[]{:S(2)}, u32[]{:S(2)}) collective-permute-start(f32[10,128,128]{2,1,0:T(8,128)} %get-tuple-element.80), channel_id=1, source_target_pairs={{0,1},{1,0},{2,3},{3,2},{4,5},{5,4},{6,7},{7,6},{8,9},{9,8},{10,11... | collective-permute-start | bytes 1966088 | tf_op jit(solution)/shard_map/ppermute | solution.py:395
  33.5 30.8 %collective-permute-start.1 = (f32[10,128,128]{2,1,0:T(8,128)}, f32[10,128,128]{2,1,0:T(8,128)}, u32[]{:S(2)}, u32[]{:S(2)}) collective-permute-start(f32[10,128,128]{2,1,0:T(8,128)} %get-tuple-element.79), channel_id=1, source_target_pairs={{0,2},{1,3},{2,0},{3,1},{4,6},{5,7},{6,4},{7,5},{8,10},{9,11},{10,... | collective-permute-start | bytes 1966088 | tf_op jit(solution)/shard_map/ppermute | solution.py:395
  43.5 0.7 copy-start.2
  46.6 14.8 %all-to-all-start.2 = ((f32[32,16,128]{2,1,0:T(8,128)}), f32[32,16,128]{2,1,0:T(8,128)S(1)}, u32[]{:S(2)}, u32[]{:S(2)}) async-start(f32[32,16,128]{2,1,0:T(8,128)} %bitcast.26), calls=%async_computation.2 | async-start | bytes 524288 | tf_op jit(solution)/shard_map/all_to_all | solution.py:399
  51.1 13.2 %collective-permute-start.2 = (f32[5,128,128]{2,1,0:T(8,128)}, f32[5,128,128]{2,1,0:T(8,128)}, u32[]{:S(2)}, u32[]{:S(2)}) collective-permute-start(f32[5,128,128]{2,1,0:T(8,128)} %constant_dynamic-slice_fusion.2), channel_id=1, source_target_pairs={{0,3},{1,2},{2,1},{3,0},{4,7},{5,6},{6,5},{7,4},{8,11},{9,10},{10,... | collective-permute-start | bytes 983048 | tf_op jit(solution)/shard_map/ppermute | solution.py:395
  64.3 19.1 %copy-start.3 = (f32[10,128,128]{2,1,0:T(8,128)}, f32[10,128,128]{2,1,0:T(8,128)S(1)}, u32[]{:S(2)}) copy-start(f32[10,128,128]{2,1,0:T(8,128)S(1)} %collective-permute-done.refs_1_) | copy-start | bytes 1966084
  65.1 18.3 %all-to-all-start.3 = ((f32[32,16,128]{2,1,0:T(8,128)}), f32[32,16,128]{2,1,0:T(8,128)S(1)}, u32[]{:S(2)}, u32[]{:S(2)}) async-start(f32[32,16,128]{2,1,0:T(8,128)} %broadcast_in_dim.7), calls=%async_computation.3 | async-start | bytes 524288 | tf_op jit(solution)/shard_map/all_to_all | solution.py:399
  70.4 13.0 %collective-permute-start.3 = (f32[5,128,128]{2,1,0:T(8,128)}, f32[5,128,128]{2,1,0:T(8,128)}, u32[]{:S(2)}, u32[]{:S(2)}) collective-permute-start(f32[5,128,128]{2,1,0:T(8,128)} %constant_dynamic-slice_fusion), channel_id=1, source_target_pairs={{0,3},{1,2},{2,1},{3,0},{4,7},{5,6},{6,5},{7,4},{8,11},{9,10},{10,... | collective-permute-start | bytes 983048 | tf_op jit(solution)/shard_map/ppermute | solution.py:395
  83.4 0.7 copy-start.1
  87.6 13.2 %collective-permute-start.5 = (f32[5,128,128]{2,1,0:T(8,128)}, f32[5,128,128]{2,1,0:T(8,128)S(1)}, u32[]{:S(2)}, u32[]{:S(2)}) collective-permute-start(f32[5,128,128]{2,1,0:T(8,128)} %get-tuple-element.60.refs_4_), channel_id=1, source_target_pairs={{0,1},{1,0},{2,3},{3,2},{4,5},{5,4},{6,7},{7,6},{8,9},{9,8},{10,11... | collective-permute-start | bytes 983048 | tf_op jit(solution)/shard_map/ppermute | solution.py:395
  88.7 12.1 %collective-permute-start.4 = (f32[5,128,128]{2,1,0:T(8,128)}, f32[5,128,128]{2,1,0:T(8,128)S(1)}, u32[]{:S(2)}, u32[]{:S(2)}) collective-permute-start(f32[5,128,128]{2,1,0:T(8,128)} %get-tuple-element.59.refs_8_), channel_id=1, source_target_pairs={{0,2},{1,3},{2,0},{3,1},{4,6},{5,7},{6,4},{7,5},{8,10},{9,11},{10,... | collective-permute-start | bytes 983048 | tf_op jit(solution)/shard_map/ppermute | solution.py:395
  89.7 16.9 %collective-permute-start.6 = (f32[5,128,128]{2,1,0:T(8,128)}, f32[5,128,128]{2,1,0:T(8,128)S(1)}, u32[]{:S(2)}, u32[]{:S(2)}) collective-permute-start(f32[5,128,128]{2,1,0:T(8,128)} %get-tuple-element.60.refs_4_), channel_id=1, source_target_pairs={{0,2},{1,3},{2,0},{3,1},{4,6},{5,7},{6,4},{7,5},{8,10},{9,11},{10,... | collective-permute-start | bytes 983048 | tf_op jit(solution)/shard_map/ppermute | solution.py:395
  90.8 15.9 %collective-permute-start.8 = (f32[5,128,128]{2,1,0:T(8,128)}, f32[5,128,128]{2,1,0:T(8,128)S(1)}, u32[]{:S(2)}, u32[]{:S(2)}) collective-permute-start(f32[5,128,128]{2,1,0:T(8,128)} %get-tuple-element.59.refs_8_), channel_id=1, source_target_pairs={{0,1},{1,0},{2,3},{3,2},{4,5},{5,4},{6,7},{7,6},{8,9},{9,8},{10,11... | collective-permute-start | bytes 983048 | tf_op jit(solution)/shard_map/ppermute | solution.py:395
  100.9 11.1 %copy-start.4 = (f32[5,128,128]{2,1,0:T(8,128)}, f32[5,128,128]{2,1,0:T(8,128)S(1)}, u32[]{:S(2)}) copy-start(f32[5,128,128]{2,1,0:T(8,128)S(1)} %collective-permute-done.5.refs_5_) | copy-start | bytes 983044
  100.9 11.1 %copy-start.5 = (f32[5,128,128]{2,1,0:T(8,128)}, f32[5,128,128]{2,1,0:T(8,128)S(1)}, u32[]{:S(2)}) copy-start(f32[5,128,128]{2,1,0:T(8,128)S(1)} %collective-permute-done.4.refs_10_) | copy-start | bytes 983044
  100.9 11.1 %collective-permute-start.7 = (f32[5,128,128]{2,1,0:T(8,128)S(1)}, f32[5,128,128]{2,1,0:T(8,128)S(1)}, u32[]{:S(2)}, u32[]{:S(2)}) collective-permute-start(f32[5,128,128]{2,1,0:T(8,128)S(1)} %collective-permute-done.5.refs_5_), channel_id=1, source_target_pairs={{0,2},{1,3},{2,0},{3,1},{4,6},{5,7},{6,4},{7,5},{8,10},{9,11},{10,... | collective-permute-start | bytes 983048 | tf_op jit(solution)/shard_map/ppermute | solution.py:395
  102.0 10.0 %collective-permute-start.9 = (f32[5,128,128]{2,1,0:T(8,128)S(1)}, f32[5,128,128]{2,1,0:T(8,128)S(1)}, u32[]{:S(2)}, u32[]{:S(2)}) collective-permute-start(f32[5,128,128]{2,1,0:T(8,128)S(1)} %collective-permute-done.4.refs_10_), channel_id=1, source_target_pairs={{0,1},{1,0},{2,3},{3,2},{4,5},{5,4},{6,7},{7,6},{8,9},{9,8},{10,11... | collective-permute-start | bytes 983048 | tf_op jit(solution)/shard_map/ppermute | solution.py:395
  106.6 5.4 %copy-start.6 = (f32[5,128,128]{2,1,0:T(8,128)}, f32[5,128,128]{2,1,0:T(8,128)S(1)}, u32[]{:S(2)}) copy-start(f32[5,128,128]{2,1,0:T(8,128)S(1)} %collective-permute-done.6.refs_6_) | copy-start | bytes 983044
  106.6 5.4 %copy-start.7 = (f32[5,128,128]{2,1,0:T(8,128)}, f32[5,128,128]{2,1,0:T(8,128)S(1)}, u32[]{:S(2)}) copy-start(f32[5,128,128]{2,1,0:T(8,128)S(1)} %collective-permute-done.8.refs_9_) | copy-start | bytes 983044
  112.0 0.7 copy-start.8
  112.0 0.9 copy-start.9
  123.5 1.5 collective-permute-start.10
  125.8 7.6 %collective-permute-start.12 = (f32[128,128]{1,0:T(8,128)S(1)}, f32[128,128]{1,0:T(8,128)S(1)}, u32[]{:S(2)}, u32[]{:S(2)}) collective-permute-start(f32[128,128]{1,0:T(8,128)S(1)} %add.47), channel_id=1, source_target_pairs={{0,2},{1,3},{2,0},{3,1},{4,6},{5,7},{6,4},{7,5},{8,10},{9,11},{10,... | collective-permute-start | bytes 196616 | tf_op jit(solution)/shard_map/ppermute | solution.py:395
  126.8 6.6 %collective-permute-start.13 = (f32[128,128]{1,0:T(8,128)S(1)}, f32[128,128]{1,0:T(8,128)S(1)}, u32[]{:S(2)}, u32[]{:S(2)}) collective-permute-start(f32[128,128]{1,0:T(8,128)S(1)} %add.47), channel_id=1, source_target_pairs={{0,3},{1,2},{2,1},{3,0},{4,7},{5,6},{6,5},{7,4},{8,11},{9,10},{10,... | collective-permute-start | bytes 196616 | tf_op jit(solution)/shard_map/ppermute | solution.py:395
  128.3 5.1 %collective-permute-start.11 = (f32[128,128]{1,0:T(8,128)S(1)}, f32[128,128]{1,0:T(8,128)S(1)}, u32[]{:S(2)}, u32[]{:S(2)}) collective-permute-start(f32[128,128]{1,0:T(8,128)S(1)} %add.47), channel_id=1, source_target_pairs={{0,1},{1,0},{2,3},{3,2},{4,5},{5,4},{6,7},{7,6},{8,9},{9,8},{10,11... | collective-permute-start | bytes 196616 | tf_op jit(solution)/shard_map/ppermute | solution.py:395
  129.3 18.8 %all-to-all-start.4 = ((f32[32,16,128]{2,1,0:T(8,128)}), f32[32,16,128]{2,1,0:T(8,128)S(1)}, u32[]{:S(2)}, u32[]{:S(2)}) async-start(f32[32,16,128]{2,1,0:T(8,128)} %bitcast.27), calls=%async_computation.4 | async-start | bytes 524288 | tf_op jit(solution)/shard_map/all_to_all | solution.py:399
  133.4 14.0 %collective-permute-start.15 = (f32[128,128]{1,0:T(8,128)S(1)}, f32[128,128]{1,0:T(8,128)S(1)}, u32[]{:S(2)}, u32[]{:S(2)}) collective-permute-start(f32[128,128]{1,0:T(8,128)S(1)} %add_add_fusion.1), channel_id=1, source_target_pairs={{0,16},{4,20},{8,24},{12,28},{16,0},{20,4},{24,8},{28,12},{1,17},{... | collective-permute-start | bytes 196616 | tf_op jit(solution)/shard_map/ppermute | solution.py:395
  136.2 11.3 %collective-permute-start.16 = (f32[128,128]{1,0:T(8,128)S(1)}, f32[128,128]{1,0:T(8,128)S(1)}, u32[]{:S(2)}, u32[]{:S(2)}) collective-permute-start(f32[128,128]{1,0:T(8,128)S(1)} %add_add_fusion.1), channel_id=1, source_target_pairs={{0,24},{4,28},{8,16},{12,20},{16,8},{20,12},{24,0},{28,4},{1,25},{... | collective-permute-start | bytes 196616 | tf_op jit(solution)/shard_map/ppermute | solution.py:395
  137.6 9.8 %collective-permute-start.14 = (f32[128,128]{1,0:T(8,128)S(1)}, f32[128,128]{1,0:T(8,128)S(1)}, u32[]{:S(2)}, u32[]{:S(2)}) collective-permute-start(f32[128,128]{1,0:T(8,128)S(1)} %add_add_fusion.1), channel_id=1, source_target_pairs={{0,8},{4,12},{8,0},{12,4},{16,24},{20,28},{24,16},{28,20},{1,9},{5... | collective-permute-start | bytes 196616 | tf_op jit(solution)/shard_map/ppermute | solution.py:395
  148.9 14.9 %all-to-all-start.5 = ((f32[32,16,128]{2,1,0:T(8,128)}), f32[32,16,128]{2,1,0:T(8,128)S(1)}, u32[]{:S(2)}, u32[]{:S(2)}) async-start(f32[32,16,128]{2,1,0:T(8,128)} %broadcast_in_dim.8), calls=%async_computation.5 | async-start | bytes 524288 | tf_op jit(solution)/shard_map/all_to_all | solution.py:399

commit v10 on v9

--- a/solution.py
+++ b/solution.py
@@ -176,29 +176,30 @@
     )(square, bridge)
 
 
-def loose_kernel(plan, rank_ref, raw_ref, *refs):
+def loose_kernel(rank_ref, raw_ref, *refs):
     piece_refs, out_refs = refs[:-2], refs[-2:]
-    ranks = len(plan[0])
     local_rows, columns = piece_refs[0].shape[1:]
     rows = []
-    for offset in range(ranks):
+    for offset in range(len(piece_refs)):
         start = pl.multiple_of((rank_ref[0] ^ offset) * local_rows, local_rows)
         rows.append(raw_ref[pl.ds(start, local_rows), :])
     raw = twice(both_parts(jnp.concatenate(rows, axis=0), 1).T, 1)
-    for places, out_ref in zip(plan, out_refs):
+    first = 0
+    for out_ref in out_refs:
         count = out_ref.shape[0]
-        value = [jnp.concatenate([piece_refs[ref][first + n] for n in range(count)], axis=1) for ref, first in places]
+        value = [jnp.concatenate([ref[first + n] for n in range(count)], axis=1) for ref in piece_refs]
         product = fold(mxu(raw, both_parts(jnp.concatenate(value, axis=0), 0), NN), 0)
         for n in range(count):
             out_ref[n] = product[:, n * columns:(n + 1) * columns]
-
-
-def loosen(rank_index, raw, pieces, plan, halves):
+        first += count
+
+
+def loosen(rank_index, raw, pieces, halves):
     columns = raw.shape[1]
     size = sum(piece.size for piece in pieces)
     whole = pl.BlockSpec(memory_space=pltpu.VMEM)
     return call(
-        functools.partial(loose_kernel, plan),
+        loose_kernel,
         8 * size * columns,
         4 * raw.size + 4 * size,
         in_specs=[pl.BlockSpec(memory_space=pltpu.SMEM)] + [whole] * (len(pieces) + 1),
@@ -207,9 +208,31 @@
     )(rank_index, raw, *pieces)
 
 
+def gram_kernel(inverse_ref, *refs):
+    loose_refs, gram_ref = refs[:-1], refs[-1]
+    columns = inverse_ref.shape[0]
+    inverse = twice(both_parts(inverse_ref[...], 0), 1)
+    value = jnp.concatenate([ref[n] for ref in loose_refs for n in range(ref.shape[0])], axis=1)
+    rows = fold(mxu(inverse, both_parts(value, 0), NN), 0)
+    count = rows.shape[1] // columns
+    rows = jnp.concatenate([rows[:, n * columns:(n + 1) * columns] for n in range(count)], axis=0)
+    rows = both_parts(rows, 1)
+    gram_ref[...] = fold(fold(mxu(rows, rows, TN), 0), 1)
+
+
+def gram_of(inverse, loose):
+    size = sum(value.size for value in loose)
+    return call(
+        gram_kernel,
+        16 * size * inverse.shape[0],
+        4 * size,
+        out_shape=shape(*inverse.shape),
+    )(inverse, *loose)
+
+
 def carry_kernel(halves, share, rank_ref, weight_ref, *refs):
-    core_refs, piece_refs = refs[:PARTS], refs[PARTS:-5]
-    raw_ref, gram_ref, middle_ref, rows_ref, sum_ref = refs[-5:]
+    core_refs, piece_refs = refs[:PARTS], refs[PARTS:-4]
+    raw_ref, middle_ref, rows_ref, sum_ref = refs[-4:]
     step = pl.program_id(0)
     block, width = core_refs[0].shape[0] * PARTS, core_refs[0].shape[1]
     columns = weight_ref.shape[1]
@@ -240,8 +263,6 @@
     @pl.when(step == pl.num_programs(0) - 1)
     def _():
         raw_ref[...] = sum_ref[...].T
-        middle = both_parts(middle_ref[...], 1)
-        gram_ref[...] = fold(fold(mxu(middle, middle, TN), 0), 1)
 
 
 def carry_rows(rank_index, weight, flat_two, pieces, halves, share, band):
@@ -263,10 +284,9 @@
         + [pl.BlockSpec(piece.shape, lambda i: (0, 0, 0)) for piece in pieces],
         out_specs=[
             pl.BlockSpec((width, columns), lambda i: (0, 0)),
-            pl.BlockSpec((columns, columns), lambda i: (0, 0)),
             pl.BlockSpec((band * share * ranks, columns), lambda i: (0, 0)),
         ],
-        out_shape=[shape(width, columns), shape(columns, columns), shape(band * share * ranks, columns)],
+        out_shape=[shape(width, columns), shape(band * share * ranks, columns)],
         scratch_shapes=[pltpu.VMEM((rows, columns), jnp.float32), pltpu.VMEM((columns, width), jnp.float32)],
     )(rank_index, weight, *[flat_two] * PARTS, *pieces)
 
@@ -367,9 +387,8 @@
         8 * raw.size * columns,
         16 * raw.size,
         in_specs=[pl.BlockSpec(memory_space=pltpu.SMEM), whole, whole],
-        out_specs=[whole, whole],
-        out_shape=[shape(local_rows + band, columns), shape(*raw.shape)],
-        scratch_shapes=[pltpu.VMEM((columns, columns), jnp.float32)],
+        out_specs=[whole] * 3,
+        out_shape=[shape(local_rows + band, columns), shape(*raw.shape), shape(columns, columns)],
     )(rank_index, bridge, raw)
 
 
@@ -406,6 +425,15 @@
 
 def pairs_of(axis, bits):
     return [(axis, bits[start:start + 2]) for start in range(0, len(bits), 2)]
+
+
+def total_over(value, steps):
+    for axis, pair in steps:
+        other = value + swap(value, axis, pair[0])
+        if len(pair) > 1:
+            other = other + (swap(value, axis, pair[1]) + swap(value, axis, pair[0] ^ pair[1]))
+        value = other
+    return value
 
 
 def after(value, others):
@@ -431,9 +459,8 @@
 
     sketched, part = sketch(core_two, right_sketch, sketch_core)
 
-    def part_for(offset, source, half=None):
-        start = (rank ^ offset) * share + (halves[0] if half else 0)
-        return lax.dynamic_slice_in_dim(source, start, share if half is None else halves[half], 0)
+    def part_for(offset, source):
+        return lax.dynamic_slice_in_dim(source, (rank ^ offset) * share, share, 0)
 
     cut_bits = [1 << bit for bit in range((cuts - 1).bit_length())]
     bits = [1 << bit for bit in range((ranks - 1).bit_length())]
@@ -443,10 +470,10 @@
     bridge_rows = jnp.sum(exchange(part.reshape(cuts, local_rows // cuts, columns), "cuts"), axis=0)
     flat_late, part = after(flat_one, part)
     square = [square_of(flat_late, 0, early, [], False)] if early else []
-    flat_late, (bridge_rows, square) = after(flat_one, (bridge_rows, square))
+    moved = [swap(part_for(offset, sketched), "rank", offset) for offset in range(1, far)]
+    flat_late, (bridge_rows, square, moved) = after(flat_one, (bridge_rows, square, moved))
     sketched, bridge_rows = after(sketched, bridge_rows)
-    moved = [swap(part_for(offset, sketched), "rank", offset) for offset in range(1, far)]
-    moved.append(swap(part_for(far, sketched, 0), "rank", far))
+    moved.append(swap(part_for(far, sketched), "rank", far))
     bridge = gather_all(bridge_rows, ("rank", "cuts")).reshape(width, columns)
     square = square_of(flat_late, early, blocks - early, square, True)
 
@@ -455,36 +482,32 @@
     own = part_for(0, sketched)
     raw = jnp.sum(exchange(raw.reshape(parts, -1, columns), both), axis=0)
     raw, moved = after(raw, moved)
-    sketched, raw = after(sketched, raw)
-    pieces = [own] + moved + [swap(part_for(far, sketched, 1), "rank", far)]
     raw = gather_all(raw, both).reshape(width, columns)
 
-    near = list(range(far))
-    plan = [[(ref, 0) for ref in near + [far]], [(ref, halves[0]) for ref in near] + [(ranks, 0)]]
-    loose = loosen(rank_index, raw, pieces, plan, halves)
+    loose = loosen(rank_index, raw, [own] + moved, halves)
     loose, (bridge, raw) = after(loose, (bridge, raw))
     scale = math.sqrt(local_rows * ranks * slices * cuts)
-    weight, solve = first_factor(rank_index, bridge, raw, scale, local_rows, band)
-    everyone = []
+    weight, solve, inverse = first_factor(rank_index, bridge, raw, scale, local_rows, band)
+    everyone, sent = [], []
     for half, order in enumerate((bits, bits[::-1])):
         found = {0: loose[half]}
         for bit in order:
             moved = {bit: swap(found[0], "rank", bit)}
+            sent.append(moved[bit])
             if len(found) > 1:
                 late, weight = after({offset: found[offset] for offset in found if offset}, weight)
                 moved.update({offset ^ bit: swap(held, "rank", bit) for offset, held in late.items()})
             found.update(moved)
         everyone += [found[offset] for offset in range(ranks)]
 
-    raw, gram, middle = carry_rows(rank_index, weight, flat_two, everyone, halves, share, band)
-    flat_late, raw = after(flat_one, raw)
+    inverse, sent = after(inverse, sent)
+    gram = total_over(gram_of(inverse, loose), [("cuts", [1])])
+    weight, gram = after(weight, gram)
+    raw, middle = carry_rows(rank_index, weight, flat_two, everyone, halves, share, band)
+    (flat_late, gram), raw = after((flat_one, gram), raw)
     left_core = apply_to(flat_late, solve)
     raw = jnp.sum(exchange(raw.reshape(parts, -1, columns), both), axis=0)
-    for axis, pair in [("cuts", [1])] + pairs_of("rank", bits) + pairs_of("cuts", cut_bits[1:]):
-        other = gram + swap(gram, axis, pair[0])
-        if len(pair) > 1:
-            other = other + (swap(gram, axis, pair[1]) + swap(gram, axis, pair[0] ^ pair[1]))
-        gram = other
+    gram = total_over(gram, pairs_of("rank", bits) + pairs_of("cuts", cut_bits[1:]))
     raw, (gram, left_core) = after(raw, (gram, left_core))
     left_core = left_core.reshape(local_rows, slices, columns)
     raw = gather_all(raw, both).reshape(width, columns)

time: 167 us -> 162 us (0.970)
  blocking collectives: 0 us -> 14.7 us
  waiting for transfers between devices: 33.8 us -> 22.1 us
  starting transfers between devices: 51.2 us -> 40.9 us
  Pallas kernels: 68.3 us -> 70.7 us
    all_to_all x0 -> x1, blocking collectives: none -> 14.7 us  [exchange(): return lax.all_to_all(value, axes, 0, 0, tiled=True)]
    ppermute x17 -> x16, waiting for transfers between devices: 24.2 us -> 10.3 us  [swap(): lax.ppermute(value, axis, [(i, i ^ offset) for i in range(lax.axis_size(a...]
    all_to_all x6 -> x5, starting transfers between devices: 28.8 us -> 20.4 us  [exchange(): return lax.all_to_all(value, axes, 0, 0, tiled=True)]
    pallas_call x1 -> x2, Pallas kernels: 3.49 us -> 6.15 us  [the longest x1 3.53 us: loosen(): call(loose_kernel, 8 * size * columns, 4 * raw.size + 4 * size, in_specs=...]
    all_to_all x6 -> x5, waiting for transfers between devices: 9.55 us -> 11.8 us  [exchange(): return lax.all_to_all(value, axes, 0, 0, tiled=True)]
    ppermute x17 -> x16, starting transfers between devices: 22.4 us -> 20.6 us  [swap(): lax.ppermute(value, axis, [(i, i ^ offset) for i in range(lax.axis_size(a...]
    dynamic_slice x4 -> x3, local copies, waits for them, and re-layouts: 3.56 us -> 4.23 us  [part_for(): return lax.dynamic_slice_in_dim(source, (rank ^ offset) * share, share, 0)]
  transfers between devices with their start and end apart: 23 -> 21, of which waited for: 8 -> 10; matrix products, arithmetic and copies ran while one was open for 3% -> 2% of each run, Pallas kernels for 26% -> 29%
where the time goes in v10:
time: 162 us; the launch traced here: 161 us
  Pallas kernels  70.7 us (44%)
  starting transfers between devices  40.9 us (25%)
  waiting for transfers between devices  22.1 us (14%)
  blocking collectives  14.7 us (9%)
  local copies, waits for them, and re-layouts  8.5 us (5%)
  matrix products  1.92 us (1%)
    ppermute x16, starting transfers between devices, swap(): lax.ppermute(value, axis, [(i, i ^ offset) for i in range(lax.axis_size(a...  20.6 us
    all_to_all x5, starting transfers between devices, exchange(): return lax.all_to_all(value, axes, 0, 0, tiled=True)  20.4 us
    pallas_call x2, Pallas kernels, square_of(): call(functools.partial(square_kernel, last), 4 * count * block * width *...  15 us
    all_to_all x1, blocking collectives, exchange(): return lax.all_to_all(value, axes, 0, 0, tiled=True)  14.7 us
    all_to_all x5, waiting for transfers between devices, exchange(): return lax.all_to_all(value, axes, 0, 0, tiled=True)  11.8 us
    ppermute x16, waiting for transfers between devices, swap(): lax.ppermute(value, axis, [(i, i ^ offset) for i in range(lax.axis_size(a...  10.3 us
    pallas_call x1, Pallas kernels, carry_rows(): call(functools.partial(carry_kernel, halves, share), 8 * flat_two.size *...  10.3 us
    pallas_call x1, Pallas kernels, sketch(): call(sketch_kernel, 2 * core_two.size * columns * 4, 4 * (core_two.size +...  10.3 us
  transfers between devices with their start and end apart: 21, of which 10 were waited for; matrix products, arithmetic and copies ran while one was open for 2% of the time, Pallas kernels for 29%

profile of v10, /device:TPU:0, one launch (start us, length us, event | category | flops | bytes accessed | tf_op | source)
XLA Modules:
  0.0 161.3 jit_solution(13262735589234062550)
XLA Ops:
  0.6 10.3 %shard_map.67 = (f32[40,128,128]{2,1,0:T(8,128)}, f32[128,128]{1,0:T(8,128)}) custom-call(f32[128,40,512]{2,1,0:T(8,128)} %refs_3_.1, f32[128,40,512]{2,1,0:T(8,128)} %refs_3_.1, f32[128,40,512]{2,1,0:T(8,128)} %refs_3_.1, f32[128,40,512]{2,1,0:T(8,128)} %refs_3_.1, f32[512,128]{1,0:T(8,128)} %refs_4_.1, f32[128,40,128]{2,1,0:T(8,128)} %refs_5_.1), custom_call_target="tpu_custom_call" | custom-call | flops 2684354560 | bytes 15728640 | tf_op jit(solution)/shard_map/pallas_call | solution.py:102
  10.9 2.5 %constant_dynamic-slice_fusion.2 = (f32[10,128,128]{2,1,0:T(8,128)}, f32[10,128,128]{2,1,0:T(8,128)}) fusion(f32[40,128,128]{2,1,0:T(8,128)} %get-tuple-element.57, s32[]{:T(128)S(6)} %select_n.13, s32[]{:T(128)S(6)} %select_n.12), kind=kLoop, calls=%fused_computation.4 | loop fusion | bytes 2621448 | tf_op jit(solution)/shard_map/dynamic_slice | solution.py:463
  13.4 2.9 %collective-permute-start = (f32[10,128,128]{2,1,0:T(8,128)}, f32[10,128,128]{2,1,0:T(8,128)S(1)}, u32[]{:S(2)}, u32[]{:S(2)}) collective-permute-start(f32[10,128,128]{2,1,0:T(8,128)} %get-tuple-element.88), channel_id=1, source_target_pairs={{0,1},{1,0},{2,3},{3,2},{4,5},{5,4},{6,7},{7,6},{8,9},{9,8},{10,11... | collective-permute-start | bytes 1966088 | tf_op jit(solution)/shard_map/ppermute | solution.py:414
  16.3 1.5 collective-permute-start.1
  17.9 4.9 %all-to-all-start = ((f32[8,16,128]{2,1,0:T(8,128)}), f32[8,16,128]{2,1,0:T(8,128)S(1)}, u32[]{:S(2)}, u32[]{:S(2)}) async-start(f32[8,16,128]{2,1,0:T(8,128)} %bitcast.2), calls=%async_computation | async-start | bytes 131072 | tf_op jit(solution)/shard_map/all_to_all | solution.py:418
  22.7 6.6 %shard_map.68.refs_0_ = f32[512,1024]{1,0:T(8,128)} custom-call(f32[5120,512]{1,0:T(8,128)} %bitcast.17), custom_call_target="tpu_custom_call" | custom-call | flops 2147483648 | bytes 4194304 | tf_op jit(solution)/shard_map/pallas_call | solution.py:153
  29.3 0.0 all-to-all-done
  29.3 2.0 %collective-permute-done.refs_1_ = f32[10,128,128]{2,1,0:T(8,128)S(1)} collective-permute-done((f32[10,128,128]{2,1,0:T(8,128)}, f32[10,128,128]{2,1,0:T(8,128)S(1)}, u32[]{:S(2)}, u32[]{:S(2)}) %collective-permute-start) | collective-permute-done | bytes 655392 | tf_op jit(solution)/shard_map/ppermute | solution.py:414
  31.3 1.6 collective-permute-done.1.refs_2_
  32.8 0.7 broadcast_in_dim.6
  33.6 4.9 %all-to-all-start.1 = ((f32[32,16,128]{2,1,0:T(8,128)}), f32[32,16,128]{2,1,0:T(8,128)S(1)}, u32[]{:S(2)}, u32[]{:S(2)}) async-start(f32[32,16,128]{2,1,0:T(8,128)} %broadcast_in_dim.6), calls=%async_computation.1 | async-start | bytes 524288 | tf_op jit(solution)/shard_map/all_to_all | solution.py:418
  38.5 0.9 constant_dynamic-slice_fusion.1
  39.4 2.7 %collective-permute-start.2 = (f32[10,128,128]{2,1,0:T(8,128)}, f32[10,128,128]{2,1,0:T(8,128)}, u32[]{:S(2)}, u32[]{:S(2)}) collective-permute-start(f32[10,128,128]{2,1,0:T(8,128)} %constant_dynamic-slice_fusion.1), channel_id=1, source_target_pairs={{0,3},{1,2},{2,1},{3,0},{4,7},{5,6},{6,5},{7,4},{8,11},{9,10},{10,... | collective-permute-start | bytes 1966088 | tf_op jit(solution)/shard_map/ppermute | solution.py:414
  42.1 8.5 %shard_map.69.square_ref = bf16[512,1024]{1,0:T(8,128)(2,1)} custom-call(f32[5120,512]{1,0:T(8,128)} %bitcast.18, f32[512,1024]{1,0:T(8,128)} %shard_map.68.refs_0_), custom_call_target="tpu_custom_call" | custom-call | flops 3221225472 | bytes 6291456 | tf_op jit(solution)/shard_map/pallas_call | solution.py:153
  50.6 0.0 all-to-all-done.1
  50.6 0.7 copy-done.2
  51.3 2.4 %shard_map.70 = f32[512,128]{1,0:T(8,128)} custom-call(bf16[512,1024]{1,0:T(8,128)(2,1)} %shard_map.69.square_ref, f32[512,128]{1,0:T(8,128)} %bitcast.23), custom_call_target="tpu_custom_call" | custom-call | flops 268435456 | bytes 1572864 | tf_op jit(solution)/shard_map/pallas_call | solution.py:171
  53.7 14.7 %all_to_all.30 = f32[32,16,128]{2,1,0:T(8,128)S(1)} all-to-all(f32[32,16,128]{2,1,0:T(8,128)} %bitcast.26), channel_id=1, replica_groups=mesh['cuts'=8,'rank'=4] {'cuts','rank'}, dimensions={0} | all-to-all | bytes 524288 | tf_op jit(solution)/shard_map/all_to_all | solution.py:418
  68.4 0.0 collective-permute-done.2.refs_3_
  68.4 0.7 broadcast_in_dim.7
  69.1 2.8 %all-to-all-start.3 = ((f32[32,16,128]{2,1,0:T(8,128)}), f32[32,16,128]{2,1,0:T(8,128)S(1)}, u32[]{:S(2)}, u32[]{:S(2)}) async-start(f32[32,16,128]{2,1,0:T(8,128)} %broadcast_in_dim.7), calls=%async_computation.3 | async-start | bytes 524288 | tf_op jit(solution)/shard_map/all_to_all | solution.py:418
  71.9 0.9 constant_dynamic-slice_fusion.refs_0_
  72.8 9.9 %all-to-all-done.3 = f32[32,16,128]{2,1,0:T(8,128)S(1)} async-done(((f32[32,16,128]{2,1,0:T(8,128)}), f32[32,16,128]{2,1,0:T(8,128)S(1)}, u32[]{:S(2)}, u32[]{:S(2)}) %all-to-all-start.3) | async-done | bytes 262176 | tf_op jit(solution)/shard_map/all_to_all | solution.py:418
  82.7 0.7 copy-done.1
  83.3 3.5 %shard_map.71 = (f32[5,128,128]{2,1,0:T(8,128)}, f32[5,128,128]{2,1,0:T(8,128)}) custom-call(s32[1]{0:T(128)} %bitcast.1.rank_ref, f32[512,128]{1,0:T(8,128)} %bitcast.21, f32[10,128,128]{2,1,0:T(8,128)} %constant_dynamic-slice_fusion.refs_0_, f32[10,128,128]{2,1,0:T(8,128)} %copy-done.3, f32[10,128,128]{2,1,0:T(8,128)} %collective-permute-done.1.refs_2_, ...), custom_call_target="tpu_custom_call" | custom-call | flops 671088640 | bytes 2883584 | tf_op jit(solution)/shard_map/pallas_call | solution.py:201
  86.9 0.0 collective-permute-start.4
  86.9 1.4 collective-permute-start.3
  88.3 0.6 collective-permute-start.5
  88.9 2.0 %collective-permute-start.6 = (f32[5,128,128]{2,1,0:T(8,128)}, f32[5,128,128]{2,1,0:T(8,128)S(1)}, u32[]{:S(2)}, u32[]{:S(2)}) collective-permute-start(f32[5,128,128]{2,1,0:T(8,128)} %get-tuple-element.63.refs_1_.refs_8_), channel_id=1, source_target_pairs={{0,1},{1,0},{2,3},{3,2},{4,5},{5,4},{6,7},{7,6},{8,9},{9,8},{10,11... | collective-permute-start | bytes 983048 | tf_op jit(solution)/shard_map/ppermute | solution.py:414
  90.9 9.2 %shard_map.72 = (f32[160,128]{1,0:T(8,128)}, f32[512,128]{1,0:T(8,128)}, f32[128,128]{1,0:T(8,128)}) custom-call(s32[1]{0:T(128)} %bitcast.1.rank_ref, f32[512,128]{1,0:T(8,128)} %bitcast.24, f32[512,128]{1,0:T(8,128)} %bitcast.22), custom_call_target="tpu_custom_call" | custom-call | flops 67108864 | bytes 1048576 | tf_op jit(solution)/shard_map/pallas_call | solution.py:385
  100.1 0.0 collective-permute-done.4.refs_5_
  100.1 0.0 collective-permute-done.3.refs_10_
  100.1 0.1 collective-permute-start.9
  100.2 1.4 collective-permute-start.8
  101.6 3.1 %collective-permute-done.5.refs_6_ = f32[5,128,128]{2,1,0:T(8,128)S(1)} collective-permute-done((f32[5,128,128]{2,1,0:T(8,128)}, f32[5,128,128]{2,1,0:T(8,128)S(1)}, u32[]{:S(2)}, u32[]{:S(2)}) %collective-permute-start.5) | collective-permute-done | bytes 327712 | tf_op jit(solution)/shard_map/ppermute | solution.py:414
  104.7 0.1 collective-permute-done.6.refs_9_
  104.7 2.6 %shard_map.73 = f32[128,128]{1,0:T(8,128)} custom-call(f32[128,128]{1,0:T(8,128)} %get-tuple-element.71.inverse_ref, f32[5,128,128]{2,1,0:T(8,128)} %get-tuple-element.64.refs_0_.refs_4_, f32[5,128,128]{2,1,0:T(8,128)} %get-tuple-element.63.refs_1_.refs_8_), custom_call_target="tpu_custom_call" | custom-call | flops 335544320 | bytes 655360 | tf_op jit(solution)/shard_map/pallas_call | solution.py:225
  107.4 0.0 collective-permute-start.7
  107.4 1.5 collective-permute-done.7
  108.8 0.8 add.37
  109.7 0.3 collective-permute-done.9.refs_11_
  109.9 0.8 collective-permute-done.8.refs_7_
  110.8 0.7 copy-done.9
  111.5 10.3 %shard_map.74 = (f32[512,128]{1,0:T(8,128)}, f32[1280,128]{1,0:T(8,128)}) custom-call(s32[1]{0:T(128)} %bitcast.1.rank_ref, f32[160,128]{1,0:T(8,128)} %get-tuple-element.73.weight_ref, f32[5120,512]{1,0:T(8,128)} %bitcast.13, f32[5120,512]{1,0:T(8,128)} %bitcast.14, f32[5120,512]{1,0:T(8,128)} %bitcast.15, f32[5120,512]{1,0:T(8,128)} %bitcast.16, ...), custom_call_target="tpu_custom_call" | custom-call | flops 2684354560 | bytes 13107200 | tf_op jit(solution)/shard_map/pallas_call | solution.py:274
  121.8 1.0 collective-permute-start.10
  122.8 1.3 collective-permute-start.11
  124.0 1.3 collective-permute-start.12
  125.3 2.8 %all-to-all-start.4 = ((f32[32,16,128]{2,1,0:T(8,128)}), f32[32,16,128]{2,1,0:T(8,128)S(1)}, u32[]{:S(2)}, u32[]{:S(2)}) async-start(f32[32,16,128]{2,1,0:T(8,128)} %bitcast.27), calls=%async_computation.4 | async-start | bytes 524288 | tf_op jit(solution)/shard_map/all_to_all | solution.py:418
  128.1 0.0 collective-permute-done.10
  128.1 0.0 collective-permute-done.11
  128.1 1.1 collective-permute-done.12
  129.2 0.8 collective-permute-start.13
  130.0 2.4 %collective-permute-start.14 = (f32[128,128]{1,0:T(8,128)S(1)}, f32[128,128]{1,0:T(8,128)S(1)}, u32[]{:S(2)}, u32[]{:S(2)}) collective-permute-start(f32[128,128]{1,0:T(8,128)S(1)} %add_add_fusion.1), channel_id=1, source_target_pairs={{0,16},{4,20},{8,24},{12,28},{16,0},{20,4},{24,8},{28,12},{1,17},{... | collective-permute-start | bytes 196616 | tf_op jit(solution)/shard_map/ppermute | solution.py:414
  132.4 1.3 collective-permute-start.15
  133.7 8.5 %shard_map.75 = f32[5120,128]{1,0:T(8,128)} custom-call(f32[5120,512]{1,0:T(8,128)} %bitcast.19, f32[512,128]{1,0:T(8,128)} %get-tuple-element.80.weight_ref), custom_call_target="tpu_custom_call" | custom-call | flops 2684354560 | bytes 13107200 | tf_op jit(solution)/shard_map/pallas_call | solution.py:303
  142.2 0.0 collective-permute-done.13
  142.2 0.0 collective-permute-done.14
  142.2 0.6 add_add_fusion.gram_ref
  142.8 0.0 all-to-all-done.4
  142.9 0.7 broadcast_in_dim.8
  143.6 5.0 %all-to-all-start.5 = ((f32[32,16,128]{2,1,0:T(8,128)}), f32[32,16,128]{2,1,0:T(8,128)S(1)}, u32[]{:S(2)}, u32[]{:S(2)}) async-start(f32[32,16,128]{2,1,0:T(8,128)} %broadcast_in_dim.8), calls=%async_computation.5 | async-start | bytes 524288 | tf_op jit(solution)/shard_map/all_to_all | solution.py:418
  148.6 8.8 %shard_map.76 = (f32[128,128]{1,0:T(8,128)}, f32[1280,128]{1,0:T(8,128)}) custom-call(f32[128,128]{1,0:T(8,128)} %add_add_fusion.gram_ref, f32[1280,128]{1,0:T(8,128)} %get-tuple-element.83.middle_ref), custom_call_target="tpu_custom_call" | custom-call | flops 167772160 | bytes 1310720 | tf_op jit(solution)/shard_map/pallas_call | solution.py:403
  157.4 1.9 %all-to-all-done.5 = f32[32,16,128]{2,1,0:T(8,128)S(1)} async-done(((f32[32,16,128]{2,1,0:T(8,128)}), f32[32,16,128]{2,1,0:T(8,128)S(1)}, u32[]{:S(2)}, u32[]{:S(2)}) %all-to-all-start.5) | async-done | bytes 262176 | tf_op jit(solution)/shard_map/all_to_all | solution.py:418
  159.3 1.9 %fusion = f32[128,512]{1,0:T(8,128)} fusion(f32[128,128]{1,0:T(8,128)} %get-tuple-element.85, f32[512,128]{1,0:T(8,128)S(1)} %bitcast.25), kind=kOutput, calls=%fused_computation.6 | convolution fusion | flops 100663296 | bytes 589824 | tf_op jit(solution)/shard_map/dot_general | solution.py:53
  (22 shorter events, 0.1 us)
Async XLA Ops:
  13.4 17.9 %collective-permute-start = (f32[10,128,128]{2,1,0:T(8,128)}, f32[10,128,128]{2,1,0:T(8,128)S(1)}, u32[]{:S(2)}, u32[]{:S(2)}) collective-permute-start(f32[10,128,128]{2,1,0:T(8,128)} %get-tuple-element.88), channel_id=1, source_target_pairs={{0,1},{1,0},{2,3},{3,2},{4,5},{5,4},{6,7},{7,6},{8,9},{9,8},{10,11... | collective-permute-start | bytes 1966088 | tf_op jit(solution)/shard_map/ppermute | solution.py:414
  16.3 16.5 %collective-permute-start.1 = (f32[10,128,128]{2,1,0:T(8,128)}, f32[10,128,128]{2,1,0:T(8,128)}, u32[]{:S(2)}, u32[]{:S(2)}) collective-permute-start(f32[10,128,128]{2,1,0:T(8,128)} %get-tuple-element.87), channel_id=1, source_target_pairs={{0,2},{1,3},{2,0},{3,1},{4,6},{5,7},{6,4},{7,5},{8,10},{9,11},{10,... | collective-permute-start | bytes 1966088 | tf_op jit(solution)/shard_map/ppermute | solution.py:414
  17.9 11.4 %all-to-all-start = ((f32[8,16,128]{2,1,0:T(8,128)}), f32[8,16,128]{2,1,0:T(8,128)S(1)}, u32[]{:S(2)}, u32[]{:S(2)}) async-start(f32[8,16,128]{2,1,0:T(8,128)} %bitcast.2), calls=%async_computation | async-start | bytes 131072 | tf_op jit(solution)/shard_map/all_to_all | solution.py:418
  22.7 15.8 %copy-start = (f32[40,128,128]{2,1,0:T(8,128)S(1)}, f32[40,128,128]{2,1,0:T(8,128)}, u32[]{:S(2)}) copy-start(f32[40,128,128]{2,1,0:T(8,128)} %get-tuple-element.57) | copy-start | bytes 7864324
  31.3 2.3 %copy-start.3 = (f32[10,128,128]{2,1,0:T(8,128)}, f32[10,128,128]{2,1,0:T(8,128)S(1)}, u32[]{:S(2)}) copy-start(f32[10,128,128]{2,1,0:T(8,128)S(1)} %collective-permute-done.refs_1_) | copy-start | bytes 1966084
  33.6 17.0 %all-to-all-start.1 = ((f32[32,16,128]{2,1,0:T(8,128)}), f32[32,16,128]{2,1,0:T(8,128)S(1)}, u32[]{:S(2)}, u32[]{:S(2)}) async-start(f32[32,16,128]{2,1,0:T(8,128)} %broadcast_in_dim.6), calls=%async_computation.1 | async-start | bytes 524288 | tf_op jit(solution)/shard_map/all_to_all | solution.py:418
  39.4 29.0 %collective-permute-start.2 = (f32[10,128,128]{2,1,0:T(8,128)}, f32[10,128,128]{2,1,0:T(8,128)}, u32[]{:S(2)}, u32[]{:S(2)}) collective-permute-start(f32[10,128,128]{2,1,0:T(8,128)} %constant_dynamic-slice_fusion.1), channel_id=1, source_target_pairs={{0,3},{1,2},{2,1},{3,0},{4,7},{5,6},{6,5},{7,4},{8,11},{9,10},{10,... | collective-permute-start | bytes 1966088 | tf_op jit(solution)/shard_map/ppermute | solution.py:414
  50.6 0.7 copy-start.2
  69.1 13.5 %all-to-all-start.3 = ((f32[32,16,128]{2,1,0:T(8,128)}), f32[32,16,128]{2,1,0:T(8,128)S(1)}, u32[]{:S(2)}, u32[]{:S(2)}) async-start(f32[32,16,128]{2,1,0:T(8,128)} %broadcast_in_dim.7), calls=%async_computation.3 | async-start | bytes 524288 | tf_op jit(solution)/shard_map/all_to_all | solution.py:418
  82.7 0.7 copy-start.1
  86.9 13.2 %collective-permute-start.4 = (f32[5,128,128]{2,1,0:T(8,128)}, f32[5,128,128]{2,1,0:T(8,128)S(1)}, u32[]{:S(2)}, u32[]{:S(2)}) collective-permute-start(f32[5,128,128]{2,1,0:T(8,128)} %get-tuple-element.64.refs_0_.refs_4_), channel_id=1, source_target_pairs={{0,1},{1,0},{2,3},{3,2},{4,5},{5,4},{6,7},{7,6},{8,9},{9,8},{10,11... | collective-permute-start | bytes 983048 | tf_op jit(solution)/shard_map/ppermute | solution.py:414
  86.9 13.2 %collective-permute-start.3 = (f32[5,128,128]{2,1,0:T(8,128)}, f32[5,128,128]{2,1,0:T(8,128)S(1)}, u32[]{:S(2)}, u32[]{:S(2)}) collective-permute-start(f32[5,128,128]{2,1,0:T(8,128)} %get-tuple-element.63.refs_1_.refs_8_), channel_id=1, source_target_pairs={{0,2},{1,3},{2,0},{3,1},{4,6},{5,7},{6,4},{7,5},{8,10},{9,11},{10,... | collective-permute-start | bytes 983048 | tf_op jit(solution)/shard_map/ppermute | solution.py:414
  88.3 16.4 %collective-permute-start.5 = (f32[5,128,128]{2,1,0:T(8,128)}, f32[5,128,128]{2,1,0:T(8,128)S(1)}, u32[]{:S(2)}, u32[]{:S(2)}) collective-permute-start(f32[5,128,128]{2,1,0:T(8,128)} %get-tuple-element.64.refs_0_.refs_4_), channel_id=1, source_target_pairs={{0,2},{1,3},{2,0},{3,1},{4,6},{5,7},{6,4},{7,5},{8,10},{9,11},{10,... | collective-permute-start | bytes 983048 | tf_op jit(solution)/shard_map/ppermute | solution.py:414
  88.9 15.8 %collective-permute-start.6 = (f32[5,128,128]{2,1,0:T(8,128)}, f32[5,128,128]{2,1,0:T(8,128)S(1)}, u32[]{:S(2)}, u32[]{:S(2)}) collective-permute-start(f32[5,128,128]{2,1,0:T(8,128)} %get-tuple-element.63.refs_1_.refs_8_), channel_id=1, source_target_pairs={{0,1},{1,0},{2,3},{3,2},{4,5},{5,4},{6,7},{7,6},{8,9},{9,8},{10,11... | collective-permute-start | bytes 983048 | tf_op jit(solution)/shard_map/ppermute | solution.py:414
  100.1 10.7 %copy-start.4 = (f32[5,128,128]{2,1,0:T(8,128)}, f32[5,128,128]{2,1,0:T(8,128)S(1)}, u32[]{:S(2)}) copy-start(f32[5,128,128]{2,1,0:T(8,128)S(1)} %collective-permute-done.4.refs_5_) | copy-start | bytes 983044
  100.1 10.7 %copy-start.5 = (f32[5,128,128]{2,1,0:T(8,128)}, f32[5,128,128]{2,1,0:T(8,128)S(1)}, u32[]{:S(2)}) copy-start(f32[5,128,128]{2,1,0:T(8,128)S(1)} %collective-permute-done.3.refs_10_) | copy-start | bytes 983044
  100.1 9.8 %collective-permute-start.9 = (f32[5,128,128]{2,1,0:T(8,128)S(1)}, f32[5,128,128]{2,1,0:T(8,128)S(1)}, u32[]{:S(2)}, u32[]{:S(2)}) collective-permute-start(f32[5,128,128]{2,1,0:T(8,128)S(1)} %collective-permute-done.3.refs_10_), channel_id=1, source_target_pairs={{0,1},{1,0},{2,3},{3,2},{4,5},{5,4},{6,7},{7,6},{8,9},{9,8},{10,11... | collective-permute-start | bytes 983048 | tf_op jit(solution)/shard_map/ppermute | solution.py:414
  100.2 10.6 %collective-permute-start.8 = (f32[5,128,128]{2,1,0:T(8,128)S(1)}, f32[5,128,128]{2,1,0:T(8,128)S(1)}, u32[]{:S(2)}, u32[]{:S(2)}) collective-permute-start(f32[5,128,128]{2,1,0:T(8,128)S(1)} %collective-permute-done.4.refs_5_), channel_id=1, source_target_pairs={{0,2},{1,3},{2,0},{3,1},{4,6},{5,7},{6,4},{7,5},{8,10},{9,11},{10,... | collective-permute-start | bytes 983048 | tf_op jit(solution)/shard_map/ppermute | solution.py:414
  104.7 6.1 %copy-start.6 = (f32[5,128,128]{2,1,0:T(8,128)}, f32[5,128,128]{2,1,0:T(8,128)S(1)}, u32[]{:S(2)}) copy-start(f32[5,128,128]{2,1,0:T(8,128)S(1)} %collective-permute-done.5.refs_6_) | copy-start | bytes 983044
  104.7 6.0 %copy-start.7 = (f32[5,128,128]{2,1,0:T(8,128)}, f32[5,128,128]{2,1,0:T(8,128)S(1)}, u32[]{:S(2)}) copy-start(f32[5,128,128]{2,1,0:T(8,128)S(1)} %collective-permute-done.6.refs_9_) | copy-start | bytes 983044
  107.4 1.5 collective-permute-start.7
  109.9 0.9 copy-start.8
  110.8 0.7 copy-start.9
  121.8 6.3 %collective-permute-start.10 = (f32[128,128]{1,0:T(8,128)S(1)}, f32[128,128]{1,0:T(8,128)S(1)}, u32[]{:S(2)}, u32[]{:S(2)}) collective-permute-start(f32[128,128]{1,0:T(8,128)S(1)} %add.37), channel_id=1, source_target_pairs={{0,1},{1,0},{2,3},{3,2},{4,5},{5,4},{6,7},{7,6},{8,9},{9,8},{10,11... | collective-permute-start | bytes 196616 | tf_op jit(solution)/shard_map/ppermute | solution.py:414
  122.8 5.3 %collective-permute-start.11 = (f32[128,128]{1,0:T(8,128)S(1)}, f32[128,128]{1,0:T(8,128)S(1)}, u32[]{:S(2)}, u32[]{:S(2)}) collective-permute-start(f32[128,128]{1,0:T(8,128)S(1)} %add.37), channel_id=1, source_target_pairs={{0,2},{1,3},{2,0},{3,1},{4,6},{5,7},{6,4},{7,5},{8,10},{9,11},{10,... | collective-permute-start | bytes 196616 | tf_op jit(solution)/shard_map/ppermute | solution.py:414
  124.0 5.2 %collective-permute-start.12 = (f32[128,128]{1,0:T(8,128)S(1)}, f32[128,128]{1,0:T(8,128)S(1)}, u32[]{:S(2)}, u32[]{:S(2)}) collective-permute-start(f32[128,128]{1,0:T(8,128)S(1)} %add.37), channel_id=1, source_target_pairs={{0,3},{1,2},{2,1},{3,0},{4,7},{5,6},{6,5},{7,4},{8,11},{9,10},{10,... | collective-permute-start | bytes 196616 | tf_op jit(solution)/shard_map/ppermute | solution.py:414
  125.3 17.6 %all-to-all-start.4 = ((f32[32,16,128]{2,1,0:T(8,128)}), f32[32,16,128]{2,1,0:T(8,128)S(1)}, u32[]{:S(2)}, u32[]{:S(2)}) async-start(f32[32,16,128]{2,1,0:T(8,128)} %bitcast.27), calls=%async_computation.4 | async-start | bytes 524288 | tf_op jit(solution)/shard_map/all_to_all | solution.py:418
  129.2 13.0 %collective-permute-start.13 = (f32[128,128]{1,0:T(8,128)S(1)}, f32[128,128]{1,0:T(8,128)S(1)}, u32[]{:S(2)}, u32[]{:S(2)}) collective-permute-start(f32[128,128]{1,0:T(8,128)S(1)} %add_add_fusion.1), channel_id=1, source_target_pairs={{0,8},{4,12},{8,0},{12,4},{16,24},{20,28},{24,16},{28,20},{1,9},{5... | collective-permute-start | bytes 196616 | tf_op jit(solution)/shard_map/ppermute | solution.py:414
  130.0 12.2 %collective-permute-start.14 = (f32[128,128]{1,0:T(8,128)S(1)}, f32[128,128]{1,0:T(8,128)S(1)}, u32[]{:S(2)}, u32[]{:S(2)}) collective-permute-start(f32[128,128]{1,0:T(8,128)S(1)} %add_add_fusion.1), channel_id=1, source_target_pairs={{0,16},{4,20},{8,24},{12,28},{16,0},{20,4},{24,8},{28,12},{1,17},{... | collective-permute-start | bytes 196616 | tf_op jit(solution)/shard_map/ppermute | solution.py:414
  132.4 9.8 %collective-permute-start.15 = (f32[128,128]{1,0:T(8,128)S(1)}, f32[128,128]{1,0:T(8,128)S(1)}, u32[]{:S(2)}, u32[]{:S(2)}) collective-permute-start(f32[128,128]{1,0:T(8,128)S(1)} %add_add_fusion.1), channel_id=1, source_target_pairs={{0,24},{4,28},{8,16},{12,20},{16,8},{20,12},{24,0},{28,4},{1,25},{... | collective-permute-start | bytes 196616 | tf_op jit(solution)/shard_map/ppermute | solution.py:414
  143.6 15.7 %all-to-all-start.5 = ((f32[32,16,128]{2,1,0:T(8,128)}), f32[32,16,128]{2,1,0:T(8,128)S(1)}, u32[]{:S(2)}, u32[]{:S(2)}) async-start(f32[32,16,128]{2,1,0:T(8,128)} %broadcast_in_dim.8), calls=%async_computation.5 | async-start | bytes 524288 | tf_op jit(solution)/shard_map/all_to_all | solution.py:418

commit v11 on v10

--- a/solution.py
+++ b/solution.py
@@ -15,7 +15,7 @@
 BLOCK = 8
 
 
-PARTS = 4
+PARTS = 1
 
 
 def tiles(block, width):
@@ -118,8 +118,7 @@
     )(*[core_two] * PARTS, right_sketch, sketch_core)
 
 
-def block_of(rows):
-    block = 1024
+def block_of(rows, block=1024):
     while rows % block:
         block //= 2
     return block
@@ -268,7 +267,7 @@
 def carry_rows(rank_index, weight, flat_two, pieces, halves, share, band):
     rows, width = flat_two.shape
     columns = weight.shape[1]
-    block = block_of(rows)
+    block = block_of(rows, 512)
     ranks = len(pieces) // len(halves)
     whole = pl.BlockSpec(memory_space=pltpu.VMEM)
     return call(
@@ -299,7 +298,7 @@
 def apply_to(rows, weight):
     count, width = rows.shape
     columns = weight.shape[1]
-    block = block_of(count)
+    block = block_of(count, 512)
     return call(
         apply_kernel,
         8 * rows.size * columns,
@@ -466,7 +465,7 @@
     bits = [1 << bit for bit in range((ranks - 1).bit_length())]
     far = ranks - 1
     blocks = flat_one.shape[0] // block_of(flat_one.shape[0])
-    early = 2 * blocks // 5
+    early = 3 * blocks // 5
     bridge_rows = jnp.sum(exchange(part.reshape(cuts, local_rows // cuts, columns), "cuts"), axis=0)
     flat_late, part = after(flat_one, part)
     square = [square_of(flat_late, 0, early, [], False)] if early else []

time: 162 us -> 165 us (1.019)
  Pallas kernels: 70.7 us -> 74.5 us
    pallas_call x1, Pallas kernels: 10.3 us -> 12.6 us  [carry_rows(): call(functools.partial(carry_kernel, halves, share), 8 * flat_two.size *...]
    pallas_call x1, Pallas kernels: 8.51 us -> 10.5 us  [apply_to(): call(apply_kernel, 8 * rows.size * columns, 4 * (rows.size + count * colu...]
  transfers between devices with their start and end apart: 21 -> 21, of which waited for: 10 -> 10; matrix products, arithmetic and copies ran while one was open for 2% -> 2% of each run, Pallas kernels for 29% -> 30%
where the time goes in v11:
time: 165 us; the launch traced here: 163 us
  Pallas kernels  74.5 us (45%)
  starting transfers between devices  40.9 us (25%)
  waiting for transfers between devices  20.5 us (12%)
  blocking collectives  14.7 us (9%)
  local copies, waits for them, and re-layouts  8.5 us (5%)
  matrix products  1.92 us (1%)
    ppermute x16, starting transfers between devices, swap(): lax.ppermute(value, axis, [(i, i ^ offset) for i in range(lax.axis_size(a...  20.6 us
    all_to_all x5, starting transfers between devices, exchange(): return lax.all_to_all(value, axes, 0, 0, tiled=True)  20.3 us
    pallas_call x2, Pallas kernels, square_of(): call(functools.partial(square_kernel, last), 4 * count * block * width *...  15 us
    all_to_all x1, blocking collectives, exchange(): return lax.all_to_all(value, axes, 0, 0, tiled=True)  14.7 us
    pallas_call x1, Pallas kernels, carry_rows(): call(functools.partial(carry_kernel, halves, share), 8 * flat_two.size *...  12.6 us
    all_to_all x5, waiting for transfers between devices, exchange(): return lax.all_to_all(value, axes, 0, 0, tiled=True)  11.8 us
    pallas_call x1, Pallas kernels, apply_to(): call(apply_kernel, 8 * rows.size * columns, 4 * (rows.size + count * colu...  10.5 us
    pallas_call x1, Pallas kernels, sketch(): call(sketch_kernel, 2 * core_two.size * columns * 4, 4 * (core_two.size +...  9.8 us
  transfers between devices with their start and end apart: 21, of which 10 were waited for; matrix products, arithmetic and copies ran while one was open for 2% of the time, Pallas kernels for 30%

profile of v11, /device:TPU:0, one launch (start us, length us, event | category | flops | bytes accessed | tf_op | source)
XLA Modules:
  0.0 163.4 jit_solution(14247810247252583310)
XLA Ops:
  0.6 9.8 %shard_map.67 = (f32[40,128,128]{2,1,0:T(8,128)}, f32[128,128]{1,0:T(8,128)}) custom-call(f32[128,40,512]{2,1,0:T(8,128)} %refs_0_.1, f32[512,128]{1,0:T(8,128)} %refs_1_.1, f32[128,40,128]{2,1,0:T(8,128)} %refs_2_.1), custom_call_target="tpu_custom_call" | custom-call | flops 2684354560 | bytes 15728640 | tf_op jit(solution)/shard_map/pallas_call | solution.py:102
  10.4 2.5 %constant_dynamic-slice_fusion.2 = (f32[10,128,128]{2,1,0:T(8,128)}, f32[10,128,128]{2,1,0:T(8,128)}) fusion(f32[40,128,128]{2,1,0:T(8,128)} %get-tuple-element.57, s32[]{:T(128)S(6)} %select_n.13, s32[]{:T(128)S(6)} %select_n.12), kind=kLoop, calls=%fused_computation.4 | loop fusion | bytes 2621448 | tf_op jit(solution)/shard_map/dynamic_slice | solution.py:462
  12.9 2.9 %collective-permute-start = (f32[10,128,128]{2,1,0:T(8,128)}, f32[10,128,128]{2,1,0:T(8,128)S(1)}, u32[]{:S(2)}, u32[]{:S(2)}) collective-permute-start(f32[10,128,128]{2,1,0:T(8,128)} %get-tuple-element.88), channel_id=1, source_target_pairs={{0,1},{1,0},{2,3},{3,2},{4,5},{5,4},{6,7},{7,6},{8,9},{9,8},{10,11... | collective-permute-start | bytes 1966088 | tf_op jit(solution)/shard_map/ppermute | solution.py:413
  15.8 1.5 collective-permute-start.1
  17.4 4.9 %all-to-all-start = ((f32[8,16,128]{2,1,0:T(8,128)}), f32[8,16,128]{2,1,0:T(8,128)S(1)}, u32[]{:S(2)}, u32[]{:S(2)}) async-start(f32[8,16,128]{2,1,0:T(8,128)} %bitcast.2), calls=%async_computation | async-start | bytes 131072 | tf_op jit(solution)/shard_map/all_to_all | solution.py:417
  22.2 8.2 %shard_map.68.refs_0_ = f32[512,1024]{1,0:T(8,128)} custom-call(f32[5120,512]{1,0:T(8,128)} %bitcast.13), custom_call_target="tpu_custom_call" | custom-call | flops 3221225472 | bytes 6291456 | tf_op jit(solution)/shard_map/pallas_call | solution.py:152
  30.4 0.0 all-to-all-done
  30.4 0.4 collective-permute-done.refs_1_
  30.8 1.6 collective-permute-done.1.refs_2_
  32.4 0.7 broadcast_in_dim.6
  33.1 4.9 %all-to-all-start.1 = ((f32[32,16,128]{2,1,0:T(8,128)}), f32[32,16,128]{2,1,0:T(8,128)S(1)}, u32[]{:S(2)}, u32[]{:S(2)}) async-start(f32[32,16,128]{2,1,0:T(8,128)} %broadcast_in_dim.6), calls=%async_computation.1 | async-start | bytes 524288 | tf_op jit(solution)/shard_map/all_to_all | solution.py:417
  38.0 0.9 constant_dynamic-slice_fusion.1
  38.9 2.7 %collective-permute-start.2 = (f32[10,128,128]{2,1,0:T(8,128)}, f32[10,128,128]{2,1,0:T(8,128)}, u32[]{:S(2)}, u32[]{:S(2)}) collective-permute-start(f32[10,128,128]{2,1,0:T(8,128)} %constant_dynamic-slice_fusion.1), channel_id=1, source_target_pairs={{0,3},{1,2},{2,1},{3,0},{4,7},{5,6},{6,5},{7,4},{8,11},{9,10},{10,... | collective-permute-start | bytes 1966088 | tf_op jit(solution)/shard_map/ppermute | solution.py:413
  41.6 6.9 %shard_map.69.square_ref = bf16[512,1024]{1,0:T(8,128)(2,1)} custom-call(f32[5120,512]{1,0:T(8,128)} %bitcast.14, f32[512,1024]{1,0:T(8,128)} %shard_map.68.refs_0_), custom_call_target="tpu_custom_call" | custom-call | flops 2147483648 | bytes 4194304 | tf_op jit(solution)/shard_map/pallas_call | solution.py:152
  48.5 0.0 all-to-all-done.1
  48.5 0.7 copy-done.2
  49.2 2.4 %shard_map.70 = f32[512,128]{1,0:T(8,128)} custom-call(bf16[512,1024]{1,0:T(8,128)(2,1)} %shard_map.69.square_ref, f32[512,128]{1,0:T(8,128)} %bitcast.20), custom_call_target="tpu_custom_call" | custom-call | flops 268435456 | bytes 1572864 | tf_op jit(solution)/shard_map/pallas_call | solution.py:170
  51.6 14.7 %all_to_all.30 = f32[32,16,128]{2,1,0:T(8,128)S(1)} all-to-all(f32[32,16,128]{2,1,0:T(8,128)} %bitcast.23), channel_id=1, replica_groups=mesh['cuts'=8,'rank'=4] {'cuts','rank'}, dimensions={0} | all-to-all | bytes 524288 | tf_op jit(solution)/shard_map/all_to_all | solution.py:417
  66.3 0.0 collective-permute-done.2.refs_3_
  66.3 0.7 broadcast_in_dim.7
  67.0 2.8 %all-to-all-start.3 = ((f32[32,16,128]{2,1,0:T(8,128)}), f32[32,16,128]{2,1,0:T(8,128)S(1)}, u32[]{:S(2)}, u32[]{:S(2)}) async-start(f32[32,16,128]{2,1,0:T(8,128)} %broadcast_in_dim.7), calls=%async_computation.3 | async-start | bytes 524288 | tf_op jit(solution)/shard_map/all_to_all | solution.py:417
  69.8 0.9 constant_dynamic-slice_fusion.refs_0_
  70.7 9.9 %all-to-all-done.3 = f32[32,16,128]{2,1,0:T(8,128)S(1)} async-done(((f32[32,16,128]{2,1,0:T(8,128)}), f32[32,16,128]{2,1,0:T(8,128)S(1)}, u32[]{:S(2)}, u32[]{:S(2)}) %all-to-all-start.3) | async-done | bytes 262176 | tf_op jit(solution)/shard_map/all_to_all | solution.py:417
  80.6 0.7 copy-done.1
  81.3 3.5 %shard_map.71 = (f32[5,128,128]{2,1,0:T(8,128)}, f32[5,128,128]{2,1,0:T(8,128)}) custom-call(s32[1]{0:T(128)} %bitcast.1.rank_ref, f32[512,128]{1,0:T(8,128)} %bitcast.18, f32[10,128,128]{2,1,0:T(8,128)} %constant_dynamic-slice_fusion.refs_0_, f32[10,128,128]{2,1,0:T(8,128)} %copy-done.3, f32[10,128,128]{2,1,0:T(8,128)} %collective-permute-done.1.refs_2_, ...), custom_call_target="tpu_custom_call" | custom-call | flops 671088640 | bytes 2883584 | tf_op jit(solution)/shard_map/pallas_call | solution.py:200
  84.8 0.0 collective-permute-start.4
  84.8 1.4 collective-permute-start.3
  86.2 0.6 collective-permute-start.5
  86.8 2.0 %collective-permute-start.6 = (f32[5,128,128]{2,1,0:T(8,128)}, f32[5,128,128]{2,1,0:T(8,128)S(1)}, u32[]{:S(2)}, u32[]{:S(2)}) collective-permute-start(f32[5,128,128]{2,1,0:T(8,128)} %get-tuple-element.63.refs_1_.refs_5_), channel_id=1, source_target_pairs={{0,1},{1,0},{2,3},{3,2},{4,5},{5,4},{6,7},{7,6},{8,9},{9,8},{10,11... | collective-permute-start | bytes 983048 | tf_op jit(solution)/shard_map/ppermute | solution.py:413
  88.8 9.2 %shard_map.72 = (f32[160,128]{1,0:T(8,128)}, f32[512,128]{1,0:T(8,128)}, f32[128,128]{1,0:T(8,128)}) custom-call(s32[1]{0:T(128)} %bitcast.1.rank_ref, f32[512,128]{1,0:T(8,128)} %bitcast.21, f32[512,128]{1,0:T(8,128)} %bitcast.19), custom_call_target="tpu_custom_call" | custom-call | flops 67108864 | bytes 1048576 | tf_op jit(solution)/shard_map/pallas_call | solution.py:384
  98.0 0.0 collective-permute-done.4.refs_2_
  98.0 0.0 collective-permute-done.3.refs_7_
  98.1 0.1 collective-permute-start.9
  98.1 1.4 collective-permute-start.8
  99.5 3.1 %collective-permute-done.5.refs_3_ = f32[5,128,128]{2,1,0:T(8,128)S(1)} collective-permute-done((f32[5,128,128]{2,1,0:T(8,128)}, f32[5,128,128]{2,1,0:T(8,128)S(1)}, u32[]{:S(2)}, u32[]{:S(2)}) %collective-permute-start.5) | collective-permute-done | bytes 327712 | tf_op jit(solution)/shard_map/ppermute | solution.py:413
  102.6 0.1 collective-permute-done.6.refs_6_
  102.7 2.6 %shard_map.73 = f32[128,128]{1,0:T(8,128)} custom-call(f32[128,128]{1,0:T(8,128)} %get-tuple-element.71.inverse_ref, f32[5,128,128]{2,1,0:T(8,128)} %get-tuple-element.64.refs_0_.refs_1_, f32[5,128,128]{2,1,0:T(8,128)} %get-tuple-element.63.refs_1_.refs_5_), custom_call_target="tpu_custom_call" | custom-call | flops 335544320 | bytes 655360 | tf_op jit(solution)/shard_map/pallas_call | solution.py:224
  105.3 0.0 collective-permute-start.7
  105.3 1.5 collective-permute-done.7
  106.8 0.8 add.37
  107.6 0.2 collective-permute-done.9.refs_8_
  107.9 0.8 collective-permute-done.8.refs_4_
  108.7 0.7 copy-done.9
  109.4 12.6 %shard_map.74 = (f32[512,128]{1,0:T(8,128)}, f32[1280,128]{1,0:T(8,128)}) custom-call(s32[1]{0:T(128)} %bitcast.1.rank_ref, f32[160,128]{1,0:T(8,128)} %get-tuple-element.73.weight_ref, f32[5120,512]{1,0:T(8,128)} %bitcast.16, f32[5,128,128]{2,1,0:T(8,128)} %get-tuple-element.64.refs_0_.refs_1_, f32[5,128,128]{2,1,0:T(8,128)} %copy-done.4, ...), custom_call_target="tpu_custom_call" | custom-call | flops 2684354560 | bytes 13107200 | tf_op jit(solution)/shard_map/pallas_call | solution.py:273
  122.0 1.0 collective-permute-start.10
  123.0 1.2 collective-permute-start.11
  124.3 1.3 collective-permute-start.12
  125.5 2.8 %all-to-all-start.4 = ((f32[32,16,128]{2,1,0:T(8,128)}), f32[32,16,128]{2,1,0:T(8,128)S(1)}, u32[]{:S(2)}, u32[]{:S(2)}) async-start(f32[32,16,128]{2,1,0:T(8,128)} %bitcast.24), calls=%async_computation.4 | async-start | bytes 524288 | tf_op jit(solution)/shard_map/all_to_all | solution.py:417
  128.3 0.0 collective-permute-done.10
  128.3 0.0 collective-permute-done.11
  128.3 1.1 collective-permute-done.12
  129.4 0.8 collective-permute-start.13
  130.2 2.4 %collective-permute-start.14 = (f32[128,128]{1,0:T(8,128)S(1)}, f32[128,128]{1,0:T(8,128)S(1)}, u32[]{:S(2)}, u32[]{:S(2)}) collective-permute-start(f32[128,128]{1,0:T(8,128)S(1)} %add_add_fusion.1), channel_id=1, source_target_pairs={{0,16},{4,20},{8,24},{12,28},{16,0},{20,4},{24,8},{28,12},{1,17},{... | collective-permute-start | bytes 196616 | tf_op jit(solution)/shard_map/ppermute | solution.py:413
  132.6 1.3 collective-permute-start.15
  133.9 10.5 %shard_map.75 = f32[5120,128]{1,0:T(8,128)} custom-call(f32[5120,512]{1,0:T(8,128)} %bitcast.15, f32[512,128]{1,0:T(8,128)} %get-tuple-element.80.weight_ref), custom_call_target="tpu_custom_call" | custom-call | flops 2684354560 | bytes 13107200 | tf_op jit(solution)/shard_map/pallas_call | solution.py:302
  144.4 0.0 collective-permute-done.13
  144.4 0.0 collective-permute-done.15
  144.4 0.6 add_add_fusion.gram_ref
  145.0 0.0 all-to-all-done.4
  145.1 0.7 broadcast_in_dim.8
  145.8 5.0 %all-to-all-start.5 = ((f32[32,16,128]{2,1,0:T(8,128)}), f32[32,16,128]{2,1,0:T(8,128)S(1)}, u32[]{:S(2)}, u32[]{:S(2)}) async-start(f32[32,16,128]{2,1,0:T(8,128)} %broadcast_in_dim.8), calls=%async_computation.5 | async-start | bytes 524288 | tf_op jit(solution)/shard_map/all_to_all | solution.py:417
  150.8 8.8 %shard_map.76 = (f32[128,128]{1,0:T(8,128)}, f32[1280,128]{1,0:T(8,128)}) custom-call(f32[128,128]{1,0:T(8,128)} %add_add_fusion.gram_ref, f32[1280,128]{1,0:T(8,128)} %get-tuple-element.83.middle_ref), custom_call_target="tpu_custom_call" | custom-call | flops 167772160 | bytes 1310720 | tf_op jit(solution)/shard_map/pallas_call | solution.py:402
  159.6 1.9 %all-to-all-done.5 = f32[32,16,128]{2,1,0:T(8,128)S(1)} async-done(((f32[32,16,128]{2,1,0:T(8,128)}), f32[32,16,128]{2,1,0:T(8,128)S(1)}, u32[]{:S(2)}, u32[]{:S(2)}) %all-to-all-start.5) | async-done | bytes 262176 | tf_op jit(solution)/shard_map/all_to_all | solution.py:417
  161.5 1.9 %fusion = f32[128,512]{1,0:T(8,128)} fusion(f32[128,128]{1,0:T(8,128)} %get-tuple-element.85, f32[512,128]{1,0:T(8,128)S(1)} %bitcast.22), kind=kOutput, calls=%fused_computation.6 | convolution fusion | flops 100663296 | bytes 589824 | tf_op jit(solution)/shard_map/dot_general | solution.py:53
  (22 shorter events, 0.1 us)
Async XLA Ops:
  12.9 17.9 %collective-permute-start = (f32[10,128,128]{2,1,0:T(8,128)}, f32[10,128,128]{2,1,0:T(8,128)S(1)}, u32[]{:S(2)}, u32[]{:S(2)}) collective-permute-start(f32[10,128,128]{2,1,0:T(8,128)} %get-tuple-element.88), channel_id=1, source_target_pairs={{0,1},{1,0},{2,3},{3,2},{4,5},{5,4},{6,7},{7,6},{8,9},{9,8},{10,11... | collective-permute-start | bytes 1966088 | tf_op jit(solution)/shard_map/ppermute | solution.py:413
  15.8 16.5 %collective-permute-start.1 = (f32[10,128,128]{2,1,0:T(8,128)}, f32[10,128,128]{2,1,0:T(8,128)}, u32[]{:S(2)}, u32[]{:S(2)}) collective-permute-start(f32[10,128,128]{2,1,0:T(8,128)} %get-tuple-element.87), channel_id=1, source_target_pairs={{0,2},{1,3},{2,0},{3,1},{4,6},{5,7},{6,4},{7,5},{8,10},{9,11},{10,... | collective-permute-start | bytes 1966088 | tf_op jit(solution)/shard_map/ppermute | solution.py:413
  17.4 13.0 %all-to-all-start = ((f32[8,16,128]{2,1,0:T(8,128)}), f32[8,16,128]{2,1,0:T(8,128)S(1)}, u32[]{:S(2)}, u32[]{:S(2)}) async-start(f32[8,16,128]{2,1,0:T(8,128)} %bitcast.2), calls=%async_computation | async-start | bytes 131072 | tf_op jit(solution)/shard_map/all_to_all | solution.py:417
  22.2 15.8 %copy-start = (f32[40,128,128]{2,1,0:T(8,128)S(1)}, f32[40,128,128]{2,1,0:T(8,128)}, u32[]{:S(2)}) copy-start(f32[40,128,128]{2,1,0:T(8,128)} %get-tuple-element.57) | copy-start | bytes 7864324
  30.8 2.3 %copy-start.3 = (f32[10,128,128]{2,1,0:T(8,128)}, f32[10,128,128]{2,1,0:T(8,128)S(1)}, u32[]{:S(2)}) copy-start(f32[10,128,128]{2,1,0:T(8,128)S(1)} %collective-permute-done.refs_1_) | copy-start | bytes 1966084
  33.1 15.4 %all-to-all-start.1 = ((f32[32,16,128]{2,1,0:T(8,128)}), f32[32,16,128]{2,1,0:T(8,128)S(1)}, u32[]{:S(2)}, u32[]{:S(2)}) async-start(f32[32,16,128]{2,1,0:T(8,128)} %broadcast_in_dim.6), calls=%async_computation.1 | async-start | bytes 524288 | tf_op jit(solution)/shard_map/all_to_all | solution.py:417
  38.9 27.4 %collective-permute-start.2 = (f32[10,128,128]{2,1,0:T(8,128)}, f32[10,128,128]{2,1,0:T(8,128)}, u32[]{:S(2)}, u32[]{:S(2)}) collective-permute-start(f32[10,128,128]{2,1,0:T(8,128)} %constant_dynamic-slice_fusion.1), channel_id=1, source_target_pairs={{0,3},{1,2},{2,1},{3,0},{4,7},{5,6},{6,5},{7,4},{8,11},{9,10},{10,... | collective-permute-start | bytes 1966088 | tf_op jit(solution)/shard_map/ppermute | solution.py:413
  48.5 0.7 copy-start.2
  67.0 13.5 %all-to-all-start.3 = ((f32[32,16,128]{2,1,0:T(8,128)}), f32[32,16,128]{2,1,0:T(8,128)S(1)}, u32[]{:S(2)}, u32[]{:S(2)}) async-start(f32[32,16,128]{2,1,0:T(8,128)} %broadcast_in_dim.7), calls=%async_computation.3 | async-start | bytes 524288 | tf_op jit(solution)/shard_map/all_to_all | solution.py:417
  80.6 0.7 copy-start.1
  84.8 13.2 %collective-permute-start.4 = (f32[5,128,128]{2,1,0:T(8,128)}, f32[5,128,128]{2,1,0:T(8,128)S(1)}, u32[]{:S(2)}, u32[]{:S(2)}) collective-permute-start(f32[5,128,128]{2,1,0:T(8,128)} %get-tuple-element.64.refs_0_.refs_1_), channel_id=1, source_target_pairs={{0,1},{1,0},{2,3},{3,2},{4,5},{5,4},{6,7},{7,6},{8,9},{9,8},{10,11... | collective-permute-start | bytes 983048 | tf_op jit(solution)/shard_map/ppermute | solution.py:413
  84.8 13.2 %collective-permute-start.3 = (f32[5,128,128]{2,1,0:T(8,128)}, f32[5,128,128]{2,1,0:T(8,128)S(1)}, u32[]{:S(2)}, u32[]{:S(2)}) collective-permute-start(f32[5,128,128]{2,1,0:T(8,128)} %get-tuple-element.63.refs_1_.refs_5_), channel_id=1, source_target_pairs={{0,2},{1,3},{2,0},{3,1},{4,6},{5,7},{6,4},{7,5},{8,10},{9,11},{10,... | collective-permute-start | bytes 983048 | tf_op jit(solution)/shard_map/ppermute | solution.py:413
  86.2 16.4 %collective-permute-start.5 = (f32[5,128,128]{2,1,0:T(8,128)}, f32[5,128,128]{2,1,0:T(8,128)S(1)}, u32[]{:S(2)}, u32[]{:S(2)}) collective-permute-start(f32[5,128,128]{2,1,0:T(8,128)} %get-tuple-element.64.refs_0_.refs_1_), channel_id=1, source_target_pairs={{0,2},{1,3},{2,0},{3,1},{4,6},{5,7},{6,4},{7,5},{8,10},{9,11},{10,... | collective-permute-start | bytes 983048 | tf_op jit(solution)/shard_map/ppermute | solution.py:413
  86.8 15.9 %collective-permute-start.6 = (f32[5,128,128]{2,1,0:T(8,128)}, f32[5,128,128]{2,1,0:T(8,128)S(1)}, u32[]{:S(2)}, u32[]{:S(2)}) collective-permute-start(f32[5,128,128]{2,1,0:T(8,128)} %get-tuple-element.63.refs_1_.refs_5_), channel_id=1, source_target_pairs={{0,1},{1,0},{2,3},{3,2},{4,5},{5,4},{6,7},{7,6},{8,9},{9,8},{10,11... | collective-permute-start | bytes 983048 | tf_op jit(solution)/shard_map/ppermute | solution.py:413
  98.0 10.7 %copy-start.4 = (f32[5,128,128]{2,1,0:T(8,128)}, f32[5,128,128]{2,1,0:T(8,128)S(1)}, u32[]{:S(2)}) copy-start(f32[5,128,128]{2,1,0:T(8,128)S(1)} %collective-permute-done.4.refs_2_) | copy-start | bytes 983044
  98.0 10.7 %copy-start.5 = (f32[5,128,128]{2,1,0:T(8,128)}, f32[5,128,128]{2,1,0:T(8,128)S(1)}, u32[]{:S(2)}) copy-start(f32[5,128,128]{2,1,0:T(8,128)S(1)} %collective-permute-done.3.refs_7_) | copy-start | bytes 983044
  98.1 9.8 %collective-permute-start.9 = (f32[5,128,128]{2,1,0:T(8,128)S(1)}, f32[5,128,128]{2,1,0:T(8,128)S(1)}, u32[]{:S(2)}, u32[]{:S(2)}) collective-permute-start(f32[5,128,128]{2,1,0:T(8,128)S(1)} %collective-permute-done.3.refs_7_), channel_id=1, source_target_pairs={{0,1},{1,0},{2,3},{3,2},{4,5},{5,4},{6,7},{7,6},{8,9},{9,8},{10,11... | collective-permute-start | bytes 983048 | tf_op jit(solution)/shard_map/ppermute | solution.py:413
  98.1 10.6 %collective-permute-start.8 = (f32[5,128,128]{2,1,0:T(8,128)S(1)}, f32[5,128,128]{2,1,0:T(8,128)S(1)}, u32[]{:S(2)}, u32[]{:S(2)}) collective-permute-start(f32[5,128,128]{2,1,0:T(8,128)S(1)} %collective-permute-done.4.refs_2_), channel_id=1, source_target_pairs={{0,2},{1,3},{2,0},{3,1},{4,6},{5,7},{6,4},{7,5},{8,10},{9,11},{10,... | collective-permute-start | bytes 983048 | tf_op jit(solution)/shard_map/ppermute | solution.py:413
  102.6 6.1 %copy-start.6 = (f32[5,128,128]{2,1,0:T(8,128)}, f32[5,128,128]{2,1,0:T(8,128)S(1)}, u32[]{:S(2)}) copy-start(f32[5,128,128]{2,1,0:T(8,128)S(1)} %collective-permute-done.5.refs_3_) | copy-start | bytes 983044
  102.7 6.0 %copy-start.7 = (f32[5,128,128]{2,1,0:T(8,128)}, f32[5,128,128]{2,1,0:T(8,128)S(1)}, u32[]{:S(2)}) copy-start(f32[5,128,128]{2,1,0:T(8,128)S(1)} %collective-permute-done.6.refs_6_) | copy-start | bytes 983044
  105.3 1.5 collective-permute-start.7
  107.9 0.9 copy-start.8
  108.7 0.7 copy-start.9
  122.0 6.3 %collective-permute-start.10 = (f32[128,128]{1,0:T(8,128)S(1)}, f32[128,128]{1,0:T(8,128)S(1)}, u32[]{:S(2)}, u32[]{:S(2)}) collective-permute-start(f32[128,128]{1,0:T(8,128)S(1)} %add.37), channel_id=1, source_target_pairs={{0,1},{1,0},{2,3},{3,2},{4,5},{5,4},{6,7},{7,6},{8,9},{9,8},{10,11... | collective-permute-start | bytes 196616 | tf_op jit(solution)/shard_map/ppermute | solution.py:413
  123.0 5.3 %collective-permute-start.11 = (f32[128,128]{1,0:T(8,128)S(1)}, f32[128,128]{1,0:T(8,128)S(1)}, u32[]{:S(2)}, u32[]{:S(2)}) collective-permute-start(f32[128,128]{1,0:T(8,128)S(1)} %add.37), channel_id=1, source_target_pairs={{0,2},{1,3},{2,0},{3,1},{4,6},{5,7},{6,4},{7,5},{8,10},{9,11},{10,... | collective-permute-start | bytes 196616 | tf_op jit(solution)/shard_map/ppermute | solution.py:413
  124.3 5.2 %collective-permute-start.12 = (f32[128,128]{1,0:T(8,128)S(1)}, f32[128,128]{1,0:T(8,128)S(1)}, u32[]{:S(2)}, u32[]{:S(2)}) collective-permute-start(f32[128,128]{1,0:T(8,128)S(1)} %add.37), channel_id=1, source_target_pairs={{0,3},{1,2},{2,1},{3,0},{4,7},{5,6},{6,5},{7,4},{8,11},{9,10},{10,... | collective-permute-start | bytes 196616 | tf_op jit(solution)/shard_map/ppermute | solution.py:413
  125.5 19.5 %all-to-all-start.4 = ((f32[32,16,128]{2,1,0:T(8,128)}), f32[32,16,128]{2,1,0:T(8,128)S(1)}, u32[]{:S(2)}, u32[]{:S(2)}) async-start(f32[32,16,128]{2,1,0:T(8,128)} %bitcast.24), calls=%async_computation.4 | async-start | bytes 524288 | tf_op jit(solution)/shard_map/all_to_all | solution.py:417
  129.4 14.9 %collective-permute-start.13 = (f32[128,128]{1,0:T(8,128)S(1)}, f32[128,128]{1,0:T(8,128)S(1)}, u32[]{:S(2)}, u32[]{:S(2)}) collective-permute-start(f32[128,128]{1,0:T(8,128)S(1)} %add_add_fusion.1), channel_id=1, source_target_pairs={{0,8},{4,12},{8,0},{12,4},{16,24},{20,28},{24,16},{28,20},{1,9},{5... | collective-permute-start | bytes 196616 | tf_op jit(solution)/shard_map/ppermute | solution.py:413
  130.2 14.2 %collective-permute-start.14 = (f32[128,128]{1,0:T(8,128)S(1)}, f32[128,128]{1,0:T(8,128)S(1)}, u32[]{:S(2)}, u32[]{:S(2)}) collective-permute-start(f32[128,128]{1,0:T(8,128)S(1)} %add_add_fusion.1), channel_id=1, source_target_pairs={{0,16},{4,20},{8,24},{12,28},{16,0},{20,4},{24,8},{28,12},{1,17},{... | collective-permute-start | bytes 196616 | tf_op jit(solution)/shard_map/ppermute | solution.py:413
  132.6 11.8 %collective-permute-start.15 = (f32[128,128]{1,0:T(8,128)S(1)}, f32[128,128]{1,0:T(8,128)S(1)}, u32[]{:S(2)}, u32[]{:S(2)}) collective-permute-start(f32[128,128]{1,0:T(8,128)S(1)} %add_add_fusion.1), channel_id=1, source_target_pairs={{0,24},{4,28},{8,16},{12,20},{16,8},{20,12},{24,0},{28,4},{1,25},{... | collective-permute-start | bytes 196616 | tf_op jit(solution)/shard_map/ppermute | solution.py:413
  145.8 15.7 %all-to-all-start.5 = ((f32[32,16,128]{2,1,0:T(8,128)}), f32[32,16,128]{2,1,0:T(8,128)S(1)}, u32[]{:S(2)}, u32[]{:S(2)}) async-start(f32[32,16,128]{2,1,0:T(8,128)} %broadcast_in_dim.8), calls=%async_computation.5 | async-start | bytes 524288 | tf_op jit(solution)/shard_map/all_to_all | solution.py:417

commit v12 on v10

--- a/solution.py
+++ b/solution.py
@@ -15,7 +15,7 @@
 BLOCK = 8
 
 
-PARTS = 4
+PARTS = 1
 
 
 def tiles(block, width):
@@ -466,7 +466,7 @@
     bits = [1 << bit for bit in range((ranks - 1).bit_length())]
     far = ranks - 1
     blocks = flat_one.shape[0] // block_of(flat_one.shape[0])
-    early = 2 * blocks // 5
+    early = 4 * blocks // 5
     bridge_rows = jnp.sum(exchange(part.reshape(cuts, local_rows // cuts, columns), "cuts"), axis=0)
     flat_late, part = after(flat_one, part)
     square = [square_of(flat_late, 0, early, [], False)] if early else []

time: 162 us -> 159 us (0.981)
    ppermute x16, waiting for transfers between devices: 10.3 us -> 7.14 us  [swap(): lax.ppermute(value, axis, [(i, i ^ offset) for i in range(lax.axis_size(a...]
    all_to_all x5, waiting for transfers between devices: 11.8 us -> 13.9 us  [exchange(): return lax.all_to_all(value, axes, 0, 0, tiled=True)]
where the time goes in v12:
time: 159 us; the launch traced here: 158 us
  Pallas kernels  69.6 us (44%)
  starting transfers between devices  41 us (26%)
  waiting for transfers between devices  21 us (13%)
  blocking collectives  13.5 us (8%)
  local copies, waits for them, and re-layouts  8.5 us (5%)
  matrix products  1.92 us (1%)
    ppermute x16, starting transfers between devices, swap(): lax.ppermute(value, axis, [(i, i ^ offset) for i in range(lax.axis_size(a...  20.6 us
    all_to_all x5, starting transfers between devices, exchange(): return lax.all_to_all(value, axes, 0, 0, tiled=True)  20.4 us
    pallas_call x2, Pallas kernels, square_of(): call(functools.partial(square_kernel, last), 4 * count * block * width *...  14.5 us
    all_to_all x5, waiting for transfers between devices, exchange(): return lax.all_to_all(value, axes, 0, 0, tiled=True)  13.9 us
    all_to_all x1, blocking collectives, exchange(): return lax.all_to_all(value, axes, 0, 0, tiled=True)  13.5 us
    pallas_call x1, Pallas kernels, carry_rows(): call(functools.partial(carry_kernel, halves, share), 8 * flat_two.size *...  10.3 us
    pallas_call x1, Pallas kernels, sketch(): call(sketch_kernel, 2 * core_two.size * columns * 4, 4 * (core_two.size +...  9.8 us
    pallas_call x1, Pallas kernels, first_factor(): call(functools.partial(first_kernel, scale, band), 8 * raw.size * columns...  9.19 us
  transfers between devices with their start and end apart: 21, of which 10 were waited for; matrix products, arithmetic and copies ran while one was open for 2% of the time, Pallas kernels for 29%

profile of v12, /device:TPU:0, one launch (start us, length us, event | category | flops | bytes accessed | tf_op | source)
XLA Modules:
  0.0 157.9 jit_solution(11152160819438032370)
XLA Ops:
  0.6 9.8 %shard_map.67 = (f32[40,128,128]{2,1,0:T(8,128)}, f32[128,128]{1,0:T(8,128)}) custom-call(f32[128,40,512]{2,1,0:T(8,128)} %refs_0_.1, f32[512,128]{1,0:T(8,128)} %refs_1_.1, f32[128,40,128]{2,1,0:T(8,128)} %refs_2_.1), custom_call_target="tpu_custom_call" | custom-call | flops 2684354560 | bytes 15728640 | tf_op jit(solution)/shard_map/pallas_call | solution.py:102
  10.4 2.5 %constant_dynamic-slice_fusion.2 = (f32[10,128,128]{2,1,0:T(8,128)}, f32[10,128,128]{2,1,0:T(8,128)}) fusion(f32[40,128,128]{2,1,0:T(8,128)} %get-tuple-element.57, s32[]{:T(128)S(6)} %select_n.13, s32[]{:T(128)S(6)} %select_n.12), kind=kLoop, calls=%fused_computation.4 | loop fusion | bytes 2621448 | tf_op jit(solution)/shard_map/dynamic_slice | solution.py:463
  12.9 2.9 %collective-permute-start = (f32[10,128,128]{2,1,0:T(8,128)}, f32[10,128,128]{2,1,0:T(8,128)S(1)}, u32[]{:S(2)}, u32[]{:S(2)}) collective-permute-start(f32[10,128,128]{2,1,0:T(8,128)} %get-tuple-element.88), channel_id=1, source_target_pairs={{0,1},{1,0},{2,3},{3,2},{4,5},{5,4},{6,7},{7,6},{8,9},{9,8},{10,11... | collective-permute-start | bytes 1966088 | tf_op jit(solution)/shard_map/ppermute | solution.py:414
  15.8 1.5 collective-permute-start.1
  17.4 4.9 %all-to-all-start = ((f32[8,16,128]{2,1,0:T(8,128)}), f32[8,16,128]{2,1,0:T(8,128)S(1)}, u32[]{:S(2)}, u32[]{:S(2)}) async-start(f32[8,16,128]{2,1,0:T(8,128)} %bitcast.2), calls=%async_computation | async-start | bytes 131072 | tf_op jit(solution)/shard_map/all_to_all | solution.py:418
  22.2 9.8 %shard_map.68.refs_0_ = f32[512,1024]{1,0:T(8,128)} custom-call(f32[5120,512]{1,0:T(8,128)} %bitcast.14), custom_call_target="tpu_custom_call" | custom-call | flops 4294967296 | bytes 8388608 | tf_op jit(solution)/shard_map/pallas_call | solution.py:153
  32.0 0.0 all-to-all-done
  32.0 0.0 collective-permute-done.refs_1_
  32.1 0.3 collective-permute-done.1.refs_2_
  32.4 0.7 broadcast_in_dim.6
  33.1 4.9 %all-to-all-start.1 = ((f32[32,16,128]{2,1,0:T(8,128)}), f32[32,16,128]{2,1,0:T(8,128)S(1)}, u32[]{:S(2)}, u32[]{:S(2)}) async-start(f32[32,16,128]{2,1,0:T(8,128)} %broadcast_in_dim.6), calls=%async_computation.1 | async-start | bytes 524288 | tf_op jit(solution)/shard_map/all_to_all | solution.py:418
  38.0 0.9 constant_dynamic-slice_fusion.1
  38.9 2.7 %collective-permute-start.2 = (f32[10,128,128]{2,1,0:T(8,128)}, f32[10,128,128]{2,1,0:T(8,128)}, u32[]{:S(2)}, u32[]{:S(2)}) collective-permute-start(f32[10,128,128]{2,1,0:T(8,128)} %constant_dynamic-slice_fusion.1), channel_id=1, source_target_pairs={{0,3},{1,2},{2,1},{3,0},{4,7},{5,6},{6,5},{7,4},{8,11},{9,10},{10,... | collective-permute-start | bytes 1966088 | tf_op jit(solution)/shard_map/ppermute | solution.py:414
  41.6 4.7 %shard_map.69.square_ref = bf16[512,1024]{1,0:T(8,128)(2,1)} custom-call(f32[5120,512]{1,0:T(8,128)} %bitcast.15, f32[512,1024]{1,0:T(8,128)} %shard_map.68.refs_0_), custom_call_target="tpu_custom_call" | custom-call | flops 1073741824 | bytes 2097152 | tf_op jit(solution)/shard_map/pallas_call | solution.py:153
  46.3 2.1 %all-to-all-done.1 = f32[32,16,128]{2,1,0:T(8,128)S(1)} async-done(((f32[32,16,128]{2,1,0:T(8,128)}), f32[32,16,128]{2,1,0:T(8,128)S(1)}, u32[]{:S(2)}, u32[]{:S(2)}) %all-to-all-start.1) | async-done | bytes 262176 | tf_op jit(solution)/shard_map/all_to_all | solution.py:418
  48.4 0.7 copy-done.2
  49.1 2.4 %shard_map.70 = f32[512,128]{1,0:T(8,128)} custom-call(bf16[512,1024]{1,0:T(8,128)(2,1)} %shard_map.69.square_ref, f32[512,128]{1,0:T(8,128)} %bitcast.20), custom_call_target="tpu_custom_call" | custom-call | flops 268435456 | bytes 1572864 | tf_op jit(solution)/shard_map/pallas_call | solution.py:171
  51.5 13.5 %all_to_all.30 = f32[32,16,128]{2,1,0:T(8,128)S(1)} all-to-all(f32[32,16,128]{2,1,0:T(8,128)} %bitcast.23), channel_id=1, replica_groups=mesh['cuts'=8,'rank'=4] {'cuts','rank'}, dimensions={0} | all-to-all | bytes 524288 | tf_op jit(solution)/shard_map/all_to_all | solution.py:418
  65.1 0.0 collective-permute-done.2.refs_3_
  65.1 0.7 broadcast_in_dim.7
  65.8 2.8 %all-to-all-start.3 = ((f32[32,16,128]{2,1,0:T(8,128)}), f32[32,16,128]{2,1,0:T(8,128)S(1)}, u32[]{:S(2)}, u32[]{:S(2)}) async-start(f32[32,16,128]{2,1,0:T(8,128)} %broadcast_in_dim.7), calls=%async_computation.3 | async-start | bytes 524288 | tf_op jit(solution)/shard_map/all_to_all | solution.py:418
  68.6 0.9 constant_dynamic-slice_fusion.refs_0_
  69.5 9.9 %all-to-all-done.3 = f32[32,16,128]{2,1,0:T(8,128)S(1)} async-done(((f32[32,16,128]{2,1,0:T(8,128)}), f32[32,16,128]{2,1,0:T(8,128)S(1)}, u32[]{:S(2)}, u32[]{:S(2)}) %all-to-all-start.3) | async-done | bytes 262176 | tf_op jit(solution)/shard_map/all_to_all | solution.py:418
  79.3 0.7 copy-done.1
  80.0 3.5 %shard_map.71 = (f32[5,128,128]{2,1,0:T(8,128)}, f32[5,128,128]{2,1,0:T(8,128)}) custom-call(s32[1]{0:T(128)} %bitcast.1.rank_ref, f32[512,128]{1,0:T(8,128)} %bitcast.18, f32[10,128,128]{2,1,0:T(8,128)} %constant_dynamic-slice_fusion.refs_0_, f32[10,128,128]{2,1,0:T(8,128)} %copy-done.3, f32[10,128,128]{2,1,0:T(8,128)} %collective-permute-done.1.refs_2_, ...), custom_call_target="tpu_custom_call" | custom-call | flops 671088640 | bytes 2883584 | tf_op jit(solution)/shard_map/pallas_call | solution.py:201
  83.6 0.0 collective-permute-start.4
  83.6 1.4 collective-permute-start.3
  84.9 0.6 collective-permute-start.5
  85.6 2.0 %collective-permute-start.6 = (f32[5,128,128]{2,1,0:T(8,128)}, f32[5,128,128]{2,1,0:T(8,128)S(1)}, u32[]{:S(2)}, u32[]{:S(2)}) collective-permute-start(f32[5,128,128]{2,1,0:T(8,128)} %get-tuple-element.63.refs_1_.refs_5_), channel_id=1, source_target_pairs={{0,1},{1,0},{2,3},{3,2},{4,5},{5,4},{6,7},{7,6},{8,9},{9,8},{10,11... | collective-permute-start | bytes 983048 | tf_op jit(solution)/shard_map/ppermute | solution.py:414
  87.6 9.2 %shard_map.72 = (f32[160,128]{1,0:T(8,128)}, f32[512,128]{1,0:T(8,128)}, f32[128,128]{1,0:T(8,128)}) custom-call(s32[1]{0:T(128)} %bitcast.1.rank_ref, f32[512,128]{1,0:T(8,128)} %bitcast.21, f32[512,128]{1,0:T(8,128)} %bitcast.19), custom_call_target="tpu_custom_call" | custom-call | flops 67108864 | bytes 1048576 | tf_op jit(solution)/shard_map/pallas_call | solution.py:385
  96.8 0.0 collective-permute-done.4.refs_2_
  96.8 0.0 collective-permute-done.3.refs_7_
  96.8 0.1 collective-permute-start.9
  96.9 1.4 collective-permute-start.8
  98.3 3.1 %collective-permute-done.5.refs_3_ = f32[5,128,128]{2,1,0:T(8,128)S(1)} collective-permute-done((f32[5,128,128]{2,1,0:T(8,128)}, f32[5,128,128]{2,1,0:T(8,128)S(1)}, u32[]{:S(2)}, u32[]{:S(2)}) %collective-permute-start.5) | collective-permute-done | bytes 327712 | tf_op jit(solution)/shard_map/ppermute | solution.py:414
  101.4 0.1 collective-permute-done.6.refs_6_
  101.4 2.6 %shard_map.73 = f32[128,128]{1,0:T(8,128)} custom-call(f32[128,128]{1,0:T(8,128)} %get-tuple-element.71.inverse_ref, f32[5,128,128]{2,1,0:T(8,128)} %get-tuple-element.64.refs_0_.refs_1_, f32[5,128,128]{2,1,0:T(8,128)} %get-tuple-element.63.refs_1_.refs_5_), custom_call_target="tpu_custom_call" | custom-call | flops 335544320 | bytes 655360 | tf_op jit(solution)/shard_map/pallas_call | solution.py:225
  104.1 0.0 collective-permute-start.7
  104.1 1.5 collective-permute-done.7
  105.5 0.8 add.37
  106.4 0.3 collective-permute-done.9.refs_8_
  106.6 0.8 collective-permute-done.8.refs_4_
  107.5 0.7 copy-done.9
  108.2 10.3 %shard_map.74 = (f32[512,128]{1,0:T(8,128)}, f32[1280,128]{1,0:T(8,128)}) custom-call(s32[1]{0:T(128)} %bitcast.1.rank_ref, f32[160,128]{1,0:T(8,128)} %get-tuple-element.73.weight_ref, f32[5120,512]{1,0:T(8,128)} %bitcast.13, f32[5,128,128]{2,1,0:T(8,128)} %get-tuple-element.64.refs_0_.refs_1_, f32[5,128,128]{2,1,0:T(8,128)} %copy-done.4, ...), custom_call_target="tpu_custom_call" | custom-call | flops 2684354560 | bytes 13107200 | tf_op jit(solution)/shard_map/pallas_call | solution.py:274
  118.5 1.0 collective-permute-start.10
  119.5 1.2 collective-permute-start.11
  120.7 1.3 collective-permute-start.12
  122.0 2.8 %all-to-all-start.4 = ((f32[32,16,128]{2,1,0:T(8,128)}), f32[32,16,128]{2,1,0:T(8,128)S(1)}, u32[]{:S(2)}, u32[]{:S(2)}) async-start(f32[32,16,128]{2,1,0:T(8,128)} %bitcast.24), calls=%async_computation.4 | async-start | bytes 524288 | tf_op jit(solution)/shard_map/all_to_all | solution.py:418
  124.8 0.0 collective-permute-done.10
  124.8 0.0 collective-permute-done.11
  124.8 1.1 collective-permute-done.12
  125.9 0.8 collective-permute-start.13
  126.7 2.4 %collective-permute-start.14 = (f32[128,128]{1,0:T(8,128)S(1)}, f32[128,128]{1,0:T(8,128)S(1)}, u32[]{:S(2)}, u32[]{:S(2)}) collective-permute-start(f32[128,128]{1,0:T(8,128)S(1)} %add_add_fusion.1), channel_id=1, source_target_pairs={{0,16},{4,20},{8,24},{12,28},{16,0},{20,4},{24,8},{28,12},{1,17},{... | collective-permute-start | bytes 196616 | tf_op jit(solution)/shard_map/ppermute | solution.py:414
  129.1 1.3 collective-permute-start.15
  130.3 8.5 %shard_map.75 = f32[5120,128]{1,0:T(8,128)} custom-call(f32[5120,512]{1,0:T(8,128)} %bitcast.16, f32[512,128]{1,0:T(8,128)} %get-tuple-element.80.weight_ref), custom_call_target="tpu_custom_call" | custom-call | flops 2684354560 | bytes 13107200 | tf_op jit(solution)/shard_map/pallas_call | solution.py:303
  138.8 0.0 collective-permute-done.14
  138.8 0.0 collective-permute-done.15
  138.8 0.6 add_add_fusion.gram_ref
  139.5 0.0 all-to-all-done.4
  139.5 0.7 broadcast_in_dim.8
  140.2 5.0 %all-to-all-start.5 = ((f32[32,16,128]{2,1,0:T(8,128)}), f32[32,16,128]{2,1,0:T(8,128)S(1)}, u32[]{:S(2)}, u32[]{:S(2)}) async-start(f32[32,16,128]{2,1,0:T(8,128)} %broadcast_in_dim.8), calls=%async_computation.5 | async-start | bytes 524288 | tf_op jit(solution)/shard_map/all_to_all | solution.py:418
  145.3 8.8 %shard_map.76 = (f32[128,128]{1,0:T(8,128)}, f32[1280,128]{1,0:T(8,128)}) custom-call(f32[128,128]{1,0:T(8,128)} %add_add_fusion.gram_ref, f32[1280,128]{1,0:T(8,128)} %get-tuple-element.83.middle_ref), custom_call_target="tpu_custom_call" | custom-call | flops 167772160 | bytes 1310720 | tf_op jit(solution)/shard_map/pallas_call | solution.py:403
  154.1 1.9 %all-to-all-done.5 = f32[32,16,128]{2,1,0:T(8,128)S(1)} async-done(((f32[32,16,128]{2,1,0:T(8,128)}), f32[32,16,128]{2,1,0:T(8,128)S(1)}, u32[]{:S(2)}, u32[]{:S(2)}) %all-to-all-start.5) | async-done | bytes 262176 | tf_op jit(solution)/shard_map/all_to_all | solution.py:418
  156.0 1.9 %fusion = f32[128,512]{1,0:T(8,128)} fusion(f32[128,128]{1,0:T(8,128)} %get-tuple-element.85, f32[512,128]{1,0:T(8,128)S(1)} %bitcast.22), kind=kOutput, calls=%fused_computation.6 | convolution fusion | flops 100663296 | bytes 589824 | tf_op jit(solution)/shard_map/dot_general | solution.py:53
  (22 shorter events, 0.1 us)
Async XLA Ops:
  12.9 19.1 %collective-permute-start = (f32[10,128,128]{2,1,0:T(8,128)}, f32[10,128,128]{2,1,0:T(8,128)S(1)}, u32[]{:S(2)}, u32[]{:S(2)}) collective-permute-start(f32[10,128,128]{2,1,0:T(8,128)} %get-tuple-element.88), channel_id=1, source_target_pairs={{0,1},{1,0},{2,3},{3,2},{4,5},{5,4},{6,7},{7,6},{8,9},{9,8},{10,11... | collective-permute-start | bytes 1966088 | tf_op jit(solution)/shard_map/ppermute | solution.py:414
  15.8 16.5 %collective-permute-start.1 = (f32[10,128,128]{2,1,0:T(8,128)}, f32[10,128,128]{2,1,0:T(8,128)}, u32[]{:S(2)}, u32[]{:S(2)}) collective-permute-start(f32[10,128,128]{2,1,0:T(8,128)} %get-tuple-element.87), channel_id=1, source_target_pairs={{0,2},{1,3},{2,0},{3,1},{4,6},{5,7},{6,4},{7,5},{8,10},{9,11},{10,... | collective-permute-start | bytes 1966088 | tf_op jit(solution)/shard_map/ppermute | solution.py:414
  17.4 14.7 %all-to-all-start = ((f32[8,16,128]{2,1,0:T(8,128)}), f32[8,16,128]{2,1,0:T(8,128)S(1)}, u32[]{:S(2)}, u32[]{:S(2)}) async-start(f32[8,16,128]{2,1,0:T(8,128)} %bitcast.2), calls=%async_computation | async-start | bytes 131072 | tf_op jit(solution)/shard_map/all_to_all | solution.py:418
  22.2 15.8 %copy-start = (f32[40,128,128]{2,1,0:T(8,128)S(1)}, f32[40,128,128]{2,1,0:T(8,128)}, u32[]{:S(2)}) copy-start(f32[40,128,128]{2,1,0:T(8,128)} %get-tuple-element.57) | copy-start | bytes 7864324
  32.0 1.0 copy-start.3
  33.1 15.3 %all-to-all-start.1 = ((f32[32,16,128]{2,1,0:T(8,128)}), f32[32,16,128]{2,1,0:T(8,128)S(1)}, u32[]{:S(2)}, u32[]{:S(2)}) async-start(f32[32,16,128]{2,1,0:T(8,128)} %broadcast_in_dim.6), calls=%async_computation.1 | async-start | bytes 524288 | tf_op jit(solution)/shard_map/all_to_all | solution.py:418
  38.9 26.1 %collective-permute-start.2 = (f32[10,128,128]{2,1,0:T(8,128)}, f32[10,128,128]{2,1,0:T(8,128)}, u32[]{:S(2)}, u32[]{:S(2)}) collective-permute-start(f32[10,128,128]{2,1,0:T(8,128)} %constant_dynamic-slice_fusion.1), channel_id=1, source_target_pairs={{0,3},{1,2},{2,1},{3,0},{4,7},{5,6},{6,5},{7,4},{8,11},{9,10},{10,... | collective-permute-start | bytes 1966088 | tf_op jit(solution)/shard_map/ppermute | solution.py:414
  48.4 0.7 copy-start.2
  65.8 13.5 %all-to-all-start.3 = ((f32[32,16,128]{2,1,0:T(8,128)}), f32[32,16,128]{2,1,0:T(8,128)S(1)}, u32[]{:S(2)}, u32[]{:S(2)}) async-start(f32[32,16,128]{2,1,0:T(8,128)} %broadcast_in_dim.7), calls=%async_computation.3 | async-start | bytes 524288 | tf_op jit(solution)/shard_map/all_to_all | solution.py:418
  79.3 0.7 copy-start.1
  83.6 13.2 %collective-permute-start.4 = (f32[5,128,128]{2,1,0:T(8,128)}, f32[5,128,128]{2,1,0:T(8,128)S(1)}, u32[]{:S(2)}, u32[]{:S(2)}) collective-permute-start(f32[5,128,128]{2,1,0:T(8,128)} %get-tuple-element.64.refs_0_.refs_1_), channel_id=1, source_target_pairs={{0,1},{1,0},{2,3},{3,2},{4,5},{5,4},{6,7},{7,6},{8,9},{9,8},{10,11... | collective-permute-start | bytes 983048 | tf_op jit(solution)/shard_map/ppermute | solution.py:414
  83.6 13.2 %collective-permute-start.3 = (f32[5,128,128]{2,1,0:T(8,128)}, f32[5,128,128]{2,1,0:T(8,128)S(1)}, u32[]{:S(2)}, u32[]{:S(2)}) collective-permute-start(f32[5,128,128]{2,1,0:T(8,128)} %get-tuple-element.63.refs_1_.refs_5_), channel_id=1, source_target_pairs={{0,2},{1,3},{2,0},{3,1},{4,6},{5,7},{6,4},{7,5},{8,10},{9,11},{10,... | collective-permute-start | bytes 983048 | tf_op jit(solution)/shard_map/ppermute | solution.py:414
  84.9 16.4 %collective-permute-start.5 = (f32[5,128,128]{2,1,0:T(8,128)}, f32[5,128,128]{2,1,0:T(8,128)S(1)}, u32[]{:S(2)}, u32[]{:S(2)}) collective-permute-start(f32[5,128,128]{2,1,0:T(8,128)} %get-tuple-element.64.refs_0_.refs_1_), channel_id=1, source_target_pairs={{0,2},{1,3},{2,0},{3,1},{4,6},{5,7},{6,4},{7,5},{8,10},{9,11},{10,... | collective-permute-start | bytes 983048 | tf_op jit(solution)/shard_map/ppermute | solution.py:414
  85.6 15.9 %collective-permute-start.6 = (f32[5,128,128]{2,1,0:T(8,128)}, f32[5,128,128]{2,1,0:T(8,128)S(1)}, u32[]{:S(2)}, u32[]{:S(2)}) collective-permute-start(f32[5,128,128]{2,1,0:T(8,128)} %get-tuple-element.63.refs_1_.refs_5_), channel_id=1, source_target_pairs={{0,1},{1,0},{2,3},{3,2},{4,5},{5,4},{6,7},{7,6},{8,9},{9,8},{10,11... | collective-permute-start | bytes 983048 | tf_op jit(solution)/shard_map/ppermute | solution.py:414
  96.8 10.7 %copy-start.4 = (f32[5,128,128]{2,1,0:T(8,128)}, f32[5,128,128]{2,1,0:T(8,128)S(1)}, u32[]{:S(2)}) copy-start(f32[5,128,128]{2,1,0:T(8,128)S(1)} %collective-permute-done.4.refs_2_) | copy-start | bytes 983044
  96.8 10.7 %copy-start.5 = (f32[5,128,128]{2,1,0:T(8,128)}, f32[5,128,128]{2,1,0:T(8,128)S(1)}, u32[]{:S(2)}) copy-start(f32[5,128,128]{2,1,0:T(8,128)S(1)} %collective-permute-done.3.refs_7_) | copy-start | bytes 983044
  96.8 9.8 %collective-permute-start.9 = (f32[5,128,128]{2,1,0:T(8,128)S(1)}, f32[5,128,128]{2,1,0:T(8,128)S(1)}, u32[]{:S(2)}, u32[]{:S(2)}) collective-permute-start(f32[5,128,128]{2,1,0:T(8,128)S(1)} %collective-permute-done.3.refs_7_), channel_id=1, source_target_pairs={{0,1},{1,0},{2,3},{3,2},{4,5},{5,4},{6,7},{7,6},{8,9},{9,8},{10,11... | collective-permute-start | bytes 983048 | tf_op jit(solution)/shard_map/ppermute | solution.py:414
  96.9 10.6 %collective-permute-start.8 = (f32[5,128,128]{2,1,0:T(8,128)S(1)}, f32[5,128,128]{2,1,0:T(8,128)S(1)}, u32[]{:S(2)}, u32[]{:S(2)}) collective-permute-start(f32[5,128,128]{2,1,0:T(8,128)S(1)} %collective-permute-done.4.refs_2_), channel_id=1, source_target_pairs={{0,2},{1,3},{2,0},{3,1},{4,6},{5,7},{6,4},{7,5},{8,10},{9,11},{10,... | collective-permute-start | bytes 983048 | tf_op jit(solution)/shard_map/ppermute | solution.py:414
  101.4 6.1 %copy-start.6 = (f32[5,128,128]{2,1,0:T(8,128)}, f32[5,128,128]{2,1,0:T(8,128)S(1)}, u32[]{:S(2)}) copy-start(f32[5,128,128]{2,1,0:T(8,128)S(1)} %collective-permute-done.5.refs_3_) | copy-start | bytes 983044
  101.4 6.1 %copy-start.7 = (f32[5,128,128]{2,1,0:T(8,128)}, f32[5,128,128]{2,1,0:T(8,128)S(1)}, u32[]{:S(2)}) copy-start(f32[5,128,128]{2,1,0:T(8,128)S(1)} %collective-permute-done.6.refs_6_) | copy-start | bytes 983044
  104.1 1.5 collective-permute-start.7
  106.6 0.9 copy-start.8
  107.5 0.7 copy-start.9
  118.5 6.3 %collective-permute-start.10 = (f32[128,128]{1,0:T(8,128)S(1)}, f32[128,128]{1,0:T(8,128)S(1)}, u32[]{:S(2)}, u32[]{:S(2)}) collective-permute-start(f32[128,128]{1,0:T(8,128)S(1)} %add.37), channel_id=1, source_target_pairs={{0,1},{1,0},{2,3},{3,2},{4,5},{5,4},{6,7},{7,6},{8,9},{9,8},{10,11... | collective-permute-start | bytes 196616 | tf_op jit(solution)/shard_map/ppermute | solution.py:414
  119.5 5.3 %collective-permute-start.11 = (f32[128,128]{1,0:T(8,128)S(1)}, f32[128,128]{1,0:T(8,128)S(1)}, u32[]{:S(2)}, u32[]{:S(2)}) collective-permute-start(f32[128,128]{1,0:T(8,128)S(1)} %add.37), channel_id=1, source_target_pairs={{0,2},{1,3},{2,0},{3,1},{4,6},{5,7},{6,4},{7,5},{8,10},{9,11},{10,... | collective-permute-start | bytes 196616 | tf_op jit(solution)/shard_map/ppermute | solution.py:414
  120.7 5.2 %collective-permute-start.12 = (f32[128,128]{1,0:T(8,128)S(1)}, f32[128,128]{1,0:T(8,128)S(1)}, u32[]{:S(2)}, u32[]{:S(2)}) collective-permute-start(f32[128,128]{1,0:T(8,128)S(1)} %add.37), channel_id=1, source_target_pairs={{0,3},{1,2},{2,1},{3,0},{4,7},{5,6},{6,5},{7,4},{8,11},{9,10},{10,... | collective-permute-start | bytes 196616 | tf_op jit(solution)/shard_map/ppermute | solution.py:414
  122.0 17.5 %all-to-all-start.4 = ((f32[32,16,128]{2,1,0:T(8,128)}), f32[32,16,128]{2,1,0:T(8,128)S(1)}, u32[]{:S(2)}, u32[]{:S(2)}) async-start(f32[32,16,128]{2,1,0:T(8,128)} %bitcast.24), calls=%async_computation.4 | async-start | bytes 524288 | tf_op jit(solution)/shard_map/all_to_all | solution.py:418
  125.9 12.9 %collective-permute-start.13 = (f32[128,128]{1,0:T(8,128)S(1)}, f32[128,128]{1,0:T(8,128)S(1)}, u32[]{:S(2)}, u32[]{:S(2)}) collective-permute-start(f32[128,128]{1,0:T(8,128)S(1)} %add_add_fusion.1), channel_id=1, source_target_pairs={{0,8},{4,12},{8,0},{12,4},{16,24},{20,28},{24,16},{28,20},{1,9},{5... | collective-permute-start | bytes 196616 | tf_op jit(solution)/shard_map/ppermute | solution.py:414
  126.7 12.2 %collective-permute-start.14 = (f32[128,128]{1,0:T(8,128)S(1)}, f32[128,128]{1,0:T(8,128)S(1)}, u32[]{:S(2)}, u32[]{:S(2)}) collective-permute-start(f32[128,128]{1,0:T(8,128)S(1)} %add_add_fusion.1), channel_id=1, source_target_pairs={{0,16},{4,20},{8,24},{12,28},{16,0},{20,4},{24,8},{28,12},{1,17},{... | collective-permute-start | bytes 196616 | tf_op jit(solution)/shard_map/ppermute | solution.py:414
  129.1 9.8 %collective-permute-start.15 = (f32[128,128]{1,0:T(8,128)S(1)}, f32[128,128]{1,0:T(8,128)S(1)}, u32[]{:S(2)}, u32[]{:S(2)}) collective-permute-start(f32[128,128]{1,0:T(8,128)S(1)} %add_add_fusion.1), channel_id=1, source_target_pairs={{0,24},{4,28},{8,16},{12,20},{16,8},{20,12},{24,0},{28,4},{1,25},{... | collective-permute-start | bytes 196616 | tf_op jit(solution)/shard_map/ppermute | solution.py:414
  140.2 15.7 %all-to-all-start.5 = ((f32[32,16,128]{2,1,0:T(8,128)}), f32[32,16,128]{2,1,0:T(8,128)S(1)}, u32[]{:S(2)}, u32[]{:S(2)}) async-start(f32[32,16,128]{2,1,0:T(8,128)} %broadcast_in_dim.8), calls=%async_computation.5 | async-start | bytes 524288 | tf_op jit(solution)/shard_map/all_to_all | solution.py:418

commit v13 on v12

--- a/solution.py
+++ b/solution.py
@@ -466,13 +466,13 @@
     bits = [1 << bit for bit in range((ranks - 1).bit_length())]
     far = ranks - 1
     blocks = flat_one.shape[0] // block_of(flat_one.shape[0])
-    early = 4 * blocks // 5
+    early = 2 * blocks // 5
     bridge_rows = jnp.sum(exchange(part.reshape(cuts, local_rows // cuts, columns), "cuts"), axis=0)
     flat_late, part = after(flat_one, part)
     square = [square_of(flat_late, 0, early, [], False)] if early else []
     moved = [swap(part_for(offset, sketched), "rank", offset) for offset in range(1, far)]
-    flat_late, (bridge_rows, square, moved) = after(flat_one, (bridge_rows, square, moved))
-    sketched, bridge_rows = after(sketched, bridge_rows)
+    flat_late, (bridge_rows, square) = after(flat_one, (bridge_rows, square))
+    sketched, (_, moved) = after(sketched, (bridge_rows, moved))
     moved.append(swap(part_for(far, sketched), "rank", far))
     bridge = gather_all(bridge_rows, ("rank", "cuts")).reshape(width, columns)
     square = square_of(flat_late, early, blocks - early, square, True)

time: 159 us -> 158 us (level)
  waiting for transfers between devices: 21 us -> 18.6 us
    all_to_all x5, waiting for transfers between devices: 13.9 us -> 11.8 us  [exchange(): return lax.all_to_all(value, axes, 0, 0, tiled=True)]
  transfers between devices with their start and end apart: 21 -> 21, of which waited for: 10 -> 8; matrix products, arithmetic and copies ran while one was open for 2% -> 3% of each run, Pallas kernels for 29% -> 30%
where the time goes in v13:
time: 158 us; the launch traced here: 157 us
  Pallas kernels  70.2 us (44%)
  starting transfers between devices  40.2 us (25%)
  waiting for transfers between devices  18.6 us (12%)
  blocking collectives  14.7 us (9%)
  local copies, waits for them, and re-layouts  8.5 us (5%)
  matrix products  1.92 us (1%)
  other arithmetic  1.59 us (1%)
    ppermute x16, starting transfers between devices, swap(): lax.ppermute(value, axis, [(i, i ^ offset) for i in range(lax.axis_size(a...  20.6 us
    all_to_all x5, starting transfers between devices, exchange(): return lax.all_to_all(value, axes, 0, 0, tiled=True)  19.6 us
    pallas_call x2, Pallas kernels, square_of(): call(functools.partial(square_kernel, last), 4 * count * block * width *...  15.1 us
    all_to_all x1, blocking collectives, exchange(): return lax.all_to_all(value, axes, 0, 0, tiled=True)  14.7 us
    all_to_all x5, waiting for transfers between devices, exchange(): return lax.all_to_all(value, axes, 0, 0, tiled=True)  11.8 us
    pallas_call x1, Pallas kernels, carry_rows(): call(functools.partial(carry_kernel, halves, share), 8 * flat_two.size *...  10.3 us
    pallas_call x1, Pallas kernels, sketch(): call(sketch_kernel, 2 * core_two.size * columns * 4, 4 * (core_two.size +...  9.8 us
    pallas_call x1, Pallas kernels, first_factor(): call(functools.partial(first_kernel, scale, band), 8 * raw.size * columns...  9.19 us
  transfers between devices with their start and end apart: 21, of which 8 were waited for; matrix products, arithmetic and copies ran while one was open for 3% of the time, Pallas kernels for 30%

profile of v13, /device:TPU:0, one launch (start us, length us, event | category | flops | bytes accessed | tf_op | source)
XLA Modules:
  0.0 156.5 jit_solution(2067568932934077495)
XLA Ops:
  0.6 9.8 %shard_map.67 = (f32[40,128,128]{2,1,0:T(8,128)}, f32[128,128]{1,0:T(8,128)}) custom-call(f32[128,40,512]{2,1,0:T(8,128)} %refs_0_.1, f32[512,128]{1,0:T(8,128)} %refs_1_.1, f32[128,40,128]{2,1,0:T(8,128)} %refs_2_.1), custom_call_target="tpu_custom_call" | custom-call | flops 2684354560 | bytes 15728640 | tf_op jit(solution)/shard_map/pallas_call | solution.py:102
  10.4 2.5 %constant_dynamic-slice_fusion.2 = (f32[10,128,128]{2,1,0:T(8,128)}, f32[10,128,128]{2,1,0:T(8,128)}) fusion(f32[40,128,128]{2,1,0:T(8,128)} %get-tuple-element.55, s32[]{:T(128)S(6)} %select_n.13, s32[]{:T(128)S(6)} %select_n.12), kind=kLoop, calls=%fused_computation.4 | loop fusion | bytes 2621448 | tf_op jit(solution)/shard_map/dynamic_slice | solution.py:463
  12.9 2.9 %collective-permute-start = (f32[10,128,128]{2,1,0:T(8,128)}, f32[10,128,128]{2,1,0:T(8,128)}, u32[]{:S(2)}, u32[]{:S(2)}) collective-permute-start(f32[10,128,128]{2,1,0:T(8,128)} %get-tuple-element.86), channel_id=1, source_target_pairs={{0,1},{1,0},{2,3},{3,2},{4,5},{5,4},{6,7},{7,6},{8,9},{9,8},{10,11... | collective-permute-start | bytes 1966088 | tf_op jit(solution)/shard_map/ppermute | solution.py:414
  15.8 1.5 collective-permute-start.1
  17.4 4.9 %all-to-all-start = ((f32[8,16,128]{2,1,0:T(8,128)}), f32[8,16,128]{2,1,0:T(8,128)S(1)}, u32[]{:S(2)}, u32[]{:S(2)}) async-start(f32[8,16,128]{2,1,0:T(8,128)} %bitcast.2), calls=%async_computation | async-start | bytes 131072 | tf_op jit(solution)/shard_map/all_to_all | solution.py:418
  22.2 6.6 %shard_map.68.refs_0_ = f32[512,1024]{1,0:T(8,128)} custom-call(f32[5120,512]{1,0:T(8,128)} %bitcast.13), custom_call_target="tpu_custom_call" | custom-call | flops 2147483648 | bytes 4194304 | tf_op jit(solution)/shard_map/pallas_call | solution.py:153
  28.8 0.0 all-to-all-done
  28.8 0.7 broadcast_in_dim.6
  29.6 4.2 %all-to-all-start.1 = ((f32[32,16,128]{2,1,0:T(8,128)}), f32[32,16,128]{2,1,0:T(8,128)S(1)}, u32[]{:S(2)}, u32[]{:S(2)}) async-start(f32[32,16,128]{2,1,0:T(8,128)} %broadcast_in_dim.6), calls=%async_computation.1 | async-start | bytes 524288 | tf_op jit(solution)/shard_map/all_to_all | solution.py:418
  33.7 0.0 collective-permute-done.refs_1_
  33.8 0.0 collective-permute-done.1.refs_2_
  33.8 0.9 constant_dynamic-slice_fusion.1
  34.7 2.7 %collective-permute-start.2 = (f32[10,128,128]{2,1,0:T(8,128)}, f32[10,128,128]{2,1,0:T(8,128)}, u32[]{:S(2)}, u32[]{:S(2)}) collective-permute-start(f32[10,128,128]{2,1,0:T(8,128)} %constant_dynamic-slice_fusion.1), channel_id=1, source_target_pairs={{0,3},{1,2},{2,1},{3,0},{4,7},{5,6},{6,5},{7,4},{8,11},{9,10},{10,... | collective-permute-start | bytes 1966088 | tf_op jit(solution)/shard_map/ppermute | solution.py:414
  37.3 8.5 %shard_map.69.square_ref = bf16[512,1024]{1,0:T(8,128)(2,1)} custom-call(f32[5120,512]{1,0:T(8,128)} %bitcast.14, f32[512,1024]{1,0:T(8,128)} %shard_map.68.refs_0_), custom_call_target="tpu_custom_call" | custom-call | flops 3221225472 | bytes 6291456 | tf_op jit(solution)/shard_map/pallas_call | solution.py:153
  45.8 0.0 all-to-all-done.1
  45.8 0.7 copy-done.2
  46.5 2.4 %shard_map.70 = f32[512,128]{1,0:T(8,128)} custom-call(bf16[512,1024]{1,0:T(8,128)(2,1)} %shard_map.69.square_ref, f32[512,128]{1,0:T(8,128)} %bitcast.20), custom_call_target="tpu_custom_call" | custom-call | flops 268435456 | bytes 1572864 | tf_op jit(solution)/shard_map/pallas_call | solution.py:171
  48.9 14.7 %all_to_all.30 = f32[32,16,128]{2,1,0:T(8,128)S(1)} all-to-all(f32[32,16,128]{2,1,0:T(8,128)} %bitcast.23), channel_id=1, replica_groups=mesh['cuts'=8,'rank'=4] {'cuts','rank'}, dimensions={0} | all-to-all | bytes 524288 | tf_op jit(solution)/shard_map/all_to_all | solution.py:418
  63.7 0.0 collective-permute-done.2.refs_3_
  63.7 0.7 broadcast_in_dim.7
  64.4 2.8 %all-to-all-start.3 = ((f32[32,16,128]{2,1,0:T(8,128)}), f32[32,16,128]{2,1,0:T(8,128)S(1)}, u32[]{:S(2)}, u32[]{:S(2)}) async-start(f32[32,16,128]{2,1,0:T(8,128)} %broadcast_in_dim.7), calls=%async_computation.3 | async-start | bytes 524288 | tf_op jit(solution)/shard_map/all_to_all | solution.py:418
  67.2 0.9 constant_dynamic-slice_fusion.refs_0_
  68.1 9.9 %all-to-all-done.3 = f32[32,16,128]{2,1,0:T(8,128)S(1)} async-done(((f32[32,16,128]{2,1,0:T(8,128)}), f32[32,16,128]{2,1,0:T(8,128)S(1)}, u32[]{:S(2)}, u32[]{:S(2)}) %all-to-all-start.3) | async-done | bytes 262176 | tf_op jit(solution)/shard_map/all_to_all | solution.py:418
  77.9 0.7 copy-done.1
  78.6 3.5 %shard_map.71 = (f32[5,128,128]{2,1,0:T(8,128)}, f32[5,128,128]{2,1,0:T(8,128)}) custom-call(s32[1]{0:T(128)} %bitcast.1.rank_ref, f32[512,128]{1,0:T(8,128)} %bitcast.18, f32[10,128,128]{2,1,0:T(8,128)} %constant_dynamic-slice_fusion.refs_0_, f32[10,128,128]{2,1,0:T(8,128)} %collective-permute-done.refs_1_, f32[10,128,128]{2,1,0:T(8,128)} %collective-permute-done.1.refs_2_, ...), custom_call_target="tpu_custom_call" | custom-call | flops 671088640 | bytes 2883584 | tf_op jit(solution)/shard_map/pallas_call | solution.py:201
  82.2 0.0 collective-permute-start.4
  82.2 1.4 collective-permute-start.3
  83.6 0.6 collective-permute-start.5
  84.2 2.0 %collective-permute-start.6 = (f32[5,128,128]{2,1,0:T(8,128)}, f32[5,128,128]{2,1,0:T(8,128)S(1)}, u32[]{:S(2)}, u32[]{:S(2)}) collective-permute-start(f32[5,128,128]{2,1,0:T(8,128)} %get-tuple-element.61.refs_1_.refs_5_), channel_id=1, source_target_pairs={{0,1},{1,0},{2,3},{3,2},{4,5},{5,4},{6,7},{7,6},{8,9},{9,8},{10,11... | collective-permute-start | bytes 983048 | tf_op jit(solution)/shard_map/ppermute | solution.py:414
  86.2 9.2 %shard_map.72 = (f32[160,128]{1,0:T(8,128)}, f32[512,128]{1,0:T(8,128)}, f32[128,128]{1,0:T(8,128)}) custom-call(s32[1]{0:T(128)} %bitcast.1.rank_ref, f32[512,128]{1,0:T(8,128)} %bitcast.21, f32[512,128]{1,0:T(8,128)} %bitcast.19), custom_call_target="tpu_custom_call" | custom-call | flops 67108864 | bytes 1048576 | tf_op jit(solution)/shard_map/pallas_call | solution.py:385
  95.4 0.0 collective-permute-done.4.refs_2_
  95.4 0.0 collective-permute-done.3.refs_7_
  95.4 0.1 collective-permute-start.9
  95.5 1.4 collective-permute-start.8
  96.9 3.1 %collective-permute-done.5.refs_3_ = f32[5,128,128]{2,1,0:T(8,128)S(1)} collective-permute-done((f32[5,128,128]{2,1,0:T(8,128)}, f32[5,128,128]{2,1,0:T(8,128)S(1)}, u32[]{:S(2)}, u32[]{:S(2)}) %collective-permute-start.5) | collective-permute-done | bytes 327712 | tf_op jit(solution)/shard_map/ppermute | solution.py:414
  100.0 0.1 collective-permute-done.6.refs_6_
  100.1 2.6 %shard_map.73 = f32[128,128]{1,0:T(8,128)} custom-call(f32[128,128]{1,0:T(8,128)} %get-tuple-element.69.inverse_ref, f32[5,128,128]{2,1,0:T(8,128)} %get-tuple-element.62.refs_0_.refs_1_, f32[5,128,128]{2,1,0:T(8,128)} %get-tuple-element.61.refs_1_.refs_5_), custom_call_target="tpu_custom_call" | custom-call | flops 335544320 | bytes 655360 | tf_op jit(solution)/shard_map/pallas_call | solution.py:225
  102.7 0.0 collective-permute-start.7
  102.7 1.5 collective-permute-done.7
  104.1 0.8 add.37
  105.0 0.2 collective-permute-done.9.refs_8_
  105.2 0.8 collective-permute-done.8.refs_4_
  106.1 0.7 copy-done.8
  106.8 10.3 %shard_map.74 = (f32[512,128]{1,0:T(8,128)}, f32[1280,128]{1,0:T(8,128)}) custom-call(s32[1]{0:T(128)} %bitcast.1.rank_ref, f32[160,128]{1,0:T(8,128)} %get-tuple-element.71.weight_ref, f32[5120,512]{1,0:T(8,128)} %bitcast.16, f32[5,128,128]{2,1,0:T(8,128)} %get-tuple-element.62.refs_0_.refs_1_, f32[5,128,128]{2,1,0:T(8,128)} %copy-done.3, ...), custom_call_target="tpu_custom_call" | custom-call | flops 2684354560 | bytes 13107200 | tf_op jit(solution)/shard_map/pallas_call | solution.py:274
  117.1 1.0 collective-permute-start.10
  118.1 1.2 collective-permute-start.11
  119.3 1.3 collective-permute-start.12
  120.6 2.8 %all-to-all-start.4 = ((f32[32,16,128]{2,1,0:T(8,128)}), f32[32,16,128]{2,1,0:T(8,128)S(1)}, u32[]{:S(2)}, u32[]{:S(2)}) async-start(f32[32,16,128]{2,1,0:T(8,128)} %bitcast.24), calls=%async_computation.4 | async-start | bytes 524288 | tf_op jit(solution)/shard_map/all_to_all | solution.py:418
  123.4 0.0 collective-permute-done.10
  123.4 0.0 collective-permute-done.11
  123.4 1.1 collective-permute-done.12
  124.5 0.8 collective-permute-start.13
  125.3 2.4 %collective-permute-start.14 = (f32[128,128]{1,0:T(8,128)S(1)}, f32[128,128]{1,0:T(8,128)S(1)}, u32[]{:S(2)}, u32[]{:S(2)}) collective-permute-start(f32[128,128]{1,0:T(8,128)S(1)} %add_add_fusion.1), channel_id=1, source_target_pairs={{0,16},{4,20},{8,24},{12,28},{16,0},{20,4},{24,8},{28,12},{1,17},{... | collective-permute-start | bytes 196616 | tf_op jit(solution)/shard_map/ppermute | solution.py:414
  127.7 1.3 collective-permute-start.15
  129.0 8.5 %shard_map.75 = f32[5120,128]{1,0:T(8,128)} custom-call(f32[5120,512]{1,0:T(8,128)} %bitcast.15, f32[512,128]{1,0:T(8,128)} %get-tuple-element.78.weight_ref), custom_call_target="tpu_custom_call" | custom-call | flops 2684354560 | bytes 13107200 | tf_op jit(solution)/shard_map/pallas_call | solution.py:303
  137.5 0.0 collective-permute-done.13
  137.5 0.0 collective-permute-done.14
  137.5 0.0 collective-permute-done.15
  137.5 0.6 add_add_fusion.gram_ref
  138.2 0.7 broadcast_in_dim.8
  138.9 5.0 %all-to-all-start.5 = ((f32[32,16,128]{2,1,0:T(8,128)}), f32[32,16,128]{2,1,0:T(8,128)S(1)}, u32[]{:S(2)}, u32[]{:S(2)}) async-start(f32[32,16,128]{2,1,0:T(8,128)} %broadcast_in_dim.8), calls=%async_computation.5 | async-start | bytes 524288 | tf_op jit(solution)/shard_map/all_to_all | solution.py:418
  143.9 8.8 %shard_map.76 = (f32[128,128]{1,0:T(8,128)}, f32[1280,128]{1,0:T(8,128)}) custom-call(f32[128,128]{1,0:T(8,128)} %add_add_fusion.gram_ref, f32[1280,128]{1,0:T(8,128)} %get-tuple-element.81.middle_ref), custom_call_target="tpu_custom_call" | custom-call | flops 167772160 | bytes 1310720 | tf_op jit(solution)/shard_map/pallas_call | solution.py:403
  152.7 1.9 %all-to-all-done.5 = f32[32,16,128]{2,1,0:T(8,128)S(1)} async-done(((f32[32,16,128]{2,1,0:T(8,128)}), f32[32,16,128]{2,1,0:T(8,128)S(1)}, u32[]{:S(2)}, u32[]{:S(2)}) %all-to-all-start.5) | async-done | bytes 262176 | tf_op jit(solution)/shard_map/all_to_all | solution.py:418
  154.6 1.9 %fusion = f32[128,512]{1,0:T(8,128)} fusion(f32[128,128]{1,0:T(8,128)} %get-tuple-element.83, f32[512,128]{1,0:T(8,128)S(1)} %bitcast.22), kind=kOutput, calls=%fused_computation.6 | convolution fusion | flops 100663296 | bytes 589824 | tf_op jit(solution)/shard_map/dot_general | solution.py:53
  (20 shorter events, 0.1 us)
Async XLA Ops:
  12.9 20.8 %collective-permute-start = (f32[10,128,128]{2,1,0:T(8,128)}, f32[10,128,128]{2,1,0:T(8,128)}, u32[]{:S(2)}, u32[]{:S(2)}) collective-permute-start(f32[10,128,128]{2,1,0:T(8,128)} %get-tuple-element.86), channel_id=1, source_target_pairs={{0,1},{1,0},{2,3},{3,2},{4,5},{5,4},{6,7},{7,6},{8,9},{9,8},{10,11... | collective-permute-start | bytes 1966088 | tf_op jit(solution)/shard_map/ppermute | solution.py:414
  15.8 17.9 %collective-permute-start.1 = (f32[10,128,128]{2,1,0:T(8,128)}, f32[10,128,128]{2,1,0:T(8,128)}, u32[]{:S(2)}, u32[]{:S(2)}) collective-permute-start(f32[10,128,128]{2,1,0:T(8,128)} %get-tuple-element.85), channel_id=1, source_target_pairs={{0,2},{1,3},{2,0},{3,1},{4,6},{5,7},{6,4},{7,5},{8,10},{9,11},{10,... | collective-permute-start | bytes 1966088 | tf_op jit(solution)/shard_map/ppermute | solution.py:414
  17.4 11.5 %all-to-all-start = ((f32[8,16,128]{2,1,0:T(8,128)}), f32[8,16,128]{2,1,0:T(8,128)S(1)}, u32[]{:S(2)}, u32[]{:S(2)}) async-start(f32[8,16,128]{2,1,0:T(8,128)} %bitcast.2), calls=%async_computation | async-start | bytes 131072 | tf_op jit(solution)/shard_map/all_to_all | solution.py:418
  22.2 11.5 %copy-start = (f32[40,128,128]{2,1,0:T(8,128)S(1)}, f32[40,128,128]{2,1,0:T(8,128)}, u32[]{:S(2)}) copy-start(f32[40,128,128]{2,1,0:T(8,128)} %get-tuple-element.55) | copy-start | bytes 7864324
  29.6 16.3 %all-to-all-start.1 = ((f32[32,16,128]{2,1,0:T(8,128)}), f32[32,16,128]{2,1,0:T(8,128)S(1)}, u32[]{:S(2)}, u32[]{:S(2)}) async-start(f32[32,16,128]{2,1,0:T(8,128)} %broadcast_in_dim.6), calls=%async_computation.1 | async-start | bytes 524288 | tf_op jit(solution)/shard_map/all_to_all | solution.py:418
  34.7 29.0 %collective-permute-start.2 = (f32[10,128,128]{2,1,0:T(8,128)}, f32[10,128,128]{2,1,0:T(8,128)}, u32[]{:S(2)}, u32[]{:S(2)}) collective-permute-start(f32[10,128,128]{2,1,0:T(8,128)} %constant_dynamic-slice_fusion.1), channel_id=1, source_target_pairs={{0,3},{1,2},{2,1},{3,0},{4,7},{5,6},{6,5},{7,4},{8,11},{9,10},{10,... | collective-permute-start | bytes 1966088 | tf_op jit(solution)/shard_map/ppermute | solution.py:414
  45.8 0.7 copy-start.2
  64.4 13.5 %all-to-all-start.3 = ((f32[32,16,128]{2,1,0:T(8,128)}), f32[32,16,128]{2,1,0:T(8,128)S(1)}, u32[]{:S(2)}, u32[]{:S(2)}) async-start(f32[32,16,128]{2,1,0:T(8,128)} %broadcast_in_dim.7), calls=%async_computation.3 | async-start | bytes 524288 | tf_op jit(solution)/shard_map/all_to_all | solution.py:418
  77.9 0.7 copy-start.1
  82.2 13.2 %collective-permute-start.4 = (f32[5,128,128]{2,1,0:T(8,128)}, f32[5,128,128]{2,1,0:T(8,128)S(1)}, u32[]{:S(2)}, u32[]{:S(2)}) collective-permute-start(f32[5,128,128]{2,1,0:T(8,128)} %get-tuple-element.62.refs_0_.refs_1_), channel_id=1, source_target_pairs={{0,1},{1,0},{2,3},{3,2},{4,5},{5,4},{6,7},{7,6},{8,9},{9,8},{10,11... | collective-permute-start | bytes 983048 | tf_op jit(solution)/shard_map/ppermute | solution.py:414
  82.2 13.2 %collective-permute-start.3 = (f32[5,128,128]{2,1,0:T(8,128)}, f32[5,128,128]{2,1,0:T(8,128)S(1)}, u32[]{:S(2)}, u32[]{:S(2)}) collective-permute-start(f32[5,128,128]{2,1,0:T(8,128)} %get-tuple-element.61.refs_1_.refs_5_), channel_id=1, source_target_pairs={{0,2},{1,3},{2,0},{3,1},{4,6},{5,7},{6,4},{7,5},{8,10},{9,11},{10,... | collective-permute-start | bytes 983048 | tf_op jit(solution)/shard_map/ppermute | solution.py:414
  83.6 16.4 %collective-permute-start.5 = (f32[5,128,128]{2,1,0:T(8,128)}, f32[5,128,128]{2,1,0:T(8,128)S(1)}, u32[]{:S(2)}, u32[]{:S(2)}) collective-permute-start(f32[5,128,128]{2,1,0:T(8,128)} %get-tuple-element.62.refs_0_.refs_1_), channel_id=1, source_target_pairs={{0,2},{1,3},{2,0},{3,1},{4,6},{5,7},{6,4},{7,5},{8,10},{9,11},{10,... | collective-permute-start | bytes 983048 | tf_op jit(solution)/shard_map/ppermute | solution.py:414
  84.2 15.9 %collective-permute-start.6 = (f32[5,128,128]{2,1,0:T(8,128)}, f32[5,128,128]{2,1,0:T(8,128)S(1)}, u32[]{:S(2)}, u32[]{:S(2)}) collective-permute-start(f32[5,128,128]{2,1,0:T(8,128)} %get-tuple-element.61.refs_1_.refs_5_), channel_id=1, source_target_pairs={{0,1},{1,0},{2,3},{3,2},{4,5},{5,4},{6,7},{7,6},{8,9},{9,8},{10,11... | collective-permute-start | bytes 983048 | tf_op jit(solution)/shard_map/ppermute | solution.py:414
  95.4 10.7 %copy-start.3 = (f32[5,128,128]{2,1,0:T(8,128)}, f32[5,128,128]{2,1,0:T(8,128)S(1)}, u32[]{:S(2)}) copy-start(f32[5,128,128]{2,1,0:T(8,128)S(1)} %collective-permute-done.4.refs_2_) | copy-start | bytes 983044
  95.4 10.7 %copy-start.4 = (f32[5,128,128]{2,1,0:T(8,128)}, f32[5,128,128]{2,1,0:T(8,128)S(1)}, u32[]{:S(2)}) copy-start(f32[5,128,128]{2,1,0:T(8,128)S(1)} %collective-permute-done.3.refs_7_) | copy-start | bytes 983044
  95.4 9.8 %collective-permute-start.9 = (f32[5,128,128]{2,1,0:T(8,128)S(1)}, f32[5,128,128]{2,1,0:T(8,128)S(1)}, u32[]{:S(2)}, u32[]{:S(2)}) collective-permute-start(f32[5,128,128]{2,1,0:T(8,128)S(1)} %collective-permute-done.3.refs_7_), channel_id=1, source_target_pairs={{0,1},{1,0},{2,3},{3,2},{4,5},{5,4},{6,7},{7,6},{8,9},{9,8},{10,11... | collective-permute-start | bytes 983048 | tf_op jit(solution)/shard_map/ppermute | solution.py:414
  95.5 10.6 %collective-permute-start.8 = (f32[5,128,128]{2,1,0:T(8,128)S(1)}, f32[5,128,128]{2,1,0:T(8,128)S(1)}, u32[]{:S(2)}, u32[]{:S(2)}) collective-permute-start(f32[5,128,128]{2,1,0:T(8,128)S(1)} %collective-permute-done.4.refs_2_), channel_id=1, source_target_pairs={{0,2},{1,3},{2,0},{3,1},{4,6},{5,7},{6,4},{7,5},{8,10},{9,11},{10,... | collective-permute-start | bytes 983048 | tf_op jit(solution)/shard_map/ppermute | solution.py:414
  100.0 6.1 %copy-start.5 = (f32[5,128,128]{2,1,0:T(8,128)}, f32[5,128,128]{2,1,0:T(8,128)S(1)}, u32[]{:S(2)}) copy-start(f32[5,128,128]{2,1,0:T(8,128)S(1)} %collective-permute-done.5.refs_3_) | copy-start | bytes 983044
  100.0 6.0 %copy-start.6 = (f32[5,128,128]{2,1,0:T(8,128)}, f32[5,128,128]{2,1,0:T(8,128)S(1)}, u32[]{:S(2)}) copy-start(f32[5,128,128]{2,1,0:T(8,128)S(1)} %collective-permute-done.6.refs_6_) | copy-start | bytes 983044
  102.7 1.5 collective-permute-start.7
  105.2 0.9 copy-start.7
  106.1 0.7 copy-start.8
  117.1 6.3 %collective-permute-start.10 = (f32[128,128]{1,0:T(8,128)S(1)}, f32[128,128]{1,0:T(8,128)S(1)}, u32[]{:S(2)}, u32[]{:S(2)}) collective-permute-start(f32[128,128]{1,0:T(8,128)S(1)} %add.37), channel_id=1, source_target_pairs={{0,1},{1,0},{2,3},{3,2},{4,5},{5,4},{6,7},{7,6},{8,9},{9,8},{10,11... | collective-permute-start | bytes 196616 | tf_op jit(solution)/shard_map/ppermute | solution.py:414
  118.1 5.3 %collective-permute-start.11 = (f32[128,128]{1,0:T(8,128)S(1)}, f32[128,128]{1,0:T(8,128)S(1)}, u32[]{:S(2)}, u32[]{:S(2)}) collective-permute-start(f32[128,128]{1,0:T(8,128)S(1)} %add.37), channel_id=1, source_target_pairs={{0,2},{1,3},{2,0},{3,1},{4,6},{5,7},{6,4},{7,5},{8,10},{9,11},{10,... | collective-permute-start | bytes 196616 | tf_op jit(solution)/shard_map/ppermute | solution.py:414
  119.3 5.2 %collective-permute-start.12 = (f32[128,128]{1,0:T(8,128)S(1)}, f32[128,128]{1,0:T(8,128)S(1)}, u32[]{:S(2)}, u32[]{:S(2)}) collective-permute-start(f32[128,128]{1,0:T(8,128)S(1)} %add.37), channel_id=1, source_target_pairs={{0,3},{1,2},{2,1},{3,0},{4,7},{5,6},{6,5},{7,4},{8,11},{9,10},{10,... | collective-permute-start | bytes 196616 | tf_op jit(solution)/shard_map/ppermute | solution.py:414
  120.6 17.5 %all-to-all-start.4 = ((f32[32,16,128]{2,1,0:T(8,128)}), f32[32,16,128]{2,1,0:T(8,128)S(1)}, u32[]{:S(2)}, u32[]{:S(2)}) async-start(f32[32,16,128]{2,1,0:T(8,128)} %bitcast.24), calls=%async_computation.4 | async-start | bytes 524288 | tf_op jit(solution)/shard_map/all_to_all | solution.py:418
  124.5 12.9 %collective-permute-start.13 = (f32[128,128]{1,0:T(8,128)S(1)}, f32[128,128]{1,0:T(8,128)S(1)}, u32[]{:S(2)}, u32[]{:S(2)}) collective-permute-start(f32[128,128]{1,0:T(8,128)S(1)} %add_add_fusion.1), channel_id=1, source_target_pairs={{0,8},{4,12},{8,0},{12,4},{16,24},{20,28},{24,16},{28,20},{1,9},{5... | collective-permute-start | bytes 196616 | tf_op jit(solution)/shard_map/ppermute | solution.py:414
  125.3 12.2 %collective-permute-start.14 = (f32[128,128]{1,0:T(8,128)S(1)}, f32[128,128]{1,0:T(8,128)S(1)}, u32[]{:S(2)}, u32[]{:S(2)}) collective-permute-start(f32[128,128]{1,0:T(8,128)S(1)} %add_add_fusion.1), channel_id=1, source_target_pairs={{0,16},{4,20},{8,24},{12,28},{16,0},{20,4},{24,8},{28,12},{1,17},{... | collective-permute-start | bytes 196616 | tf_op jit(solution)/shard_map/ppermute | solution.py:414
  127.7 9.8 %collective-permute-start.15 = (f32[128,128]{1,0:T(8,128)S(1)}, f32[128,128]{1,0:T(8,128)S(1)}, u32[]{:S(2)}, u32[]{:S(2)}) collective-permute-start(f32[128,128]{1,0:T(8,128)S(1)} %add_add_fusion.1), channel_id=1, source_target_pairs={{0,24},{4,28},{8,16},{12,20},{16,8},{20,12},{24,0},{28,4},{1,25},{... | collective-permute-start | bytes 196616 | tf_op jit(solution)/shard_map/ppermute | solution.py:414
  138.9 15.7 %all-to-all-start.5 = ((f32[32,16,128]{2,1,0:T(8,128)}), f32[32,16,128]{2,1,0:T(8,128)S(1)}, u32[]{:S(2)}, u32[]{:S(2)}) async-start(f32[32,16,128]{2,1,0:T(8,128)} %broadcast_in_dim.8), calls=%async_computation.5 | async-start | bytes 524288 | tf_op jit(solution)/shard_map/all_to_all | solution.py:418

commit v14 on v13

--- a/solution.py
+++ b/solution.py
@@ -135,13 +135,20 @@
     def _():
         sum_ref[...] = before_refs[0][...] if before_refs else jnp.zeros_like(sum_ref)
 
-    sum_ref[...] += mxu(high, jnp.concatenate([high, low], axis=1), TN)
+    half = width // 2
+    pair = jnp.concatenate([high, low], axis=1)
+    upper = mxu(high[:, :half], pair, TN)
+    lower = mxu(high[:, half:], pair[:, half:], TN)
+    sum_ref[:half, :] += upper
+    sum_ref[half:, half:] += lower
 
     @pl.when(step == pl.num_programs(0) - 1)
     def _():
         if last:
             cross = sum_ref[:, width:]
-            out_ref[...] = both_parts(sum_ref[:, :width] + cross + cross.T, 1)
+            left = jnp.concatenate([sum_ref[:half, :half], sum_ref[:half, half:width].T], axis=0)
+            same = jnp.concatenate([left, sum_ref[:, half:width]], axis=1)
+            out_ref[...] = both_parts(same + cross + cross.T, 1)
         else:
             out_ref[...] = sum_ref[...]
 

time: 158 us -> 158 us (level)
  no operation moved by 1% of the time
where the time goes in v14:
time: 158 us; the launch traced here: 156 us
  Pallas kernels  70.1 us (44%)
  starting transfers between devices  40.2 us (25%)
  waiting for transfers between devices  18.6 us (12%)
  blocking collectives  14.7 us (9%)
  local copies, waits for them, and re-layouts  8.5 us (5%)
  matrix products  1.92 us (1%)
  other arithmetic  1.59 us (1%)
    ppermute x16, starting transfers between devices, swap(): lax.ppermute(value, axis, [(i, i ^ offset) for i in range(lax.axis_size(a...  20.6 us
    all_to_all x5, starting transfers between devices, exchange(): return lax.all_to_all(value, axes, 0, 0, tiled=True)  19.6 us
    pallas_call x2, Pallas kernels, square_of(): call(functools.partial(square_kernel, last), 4 * count * block * width *...  15 us
    all_to_all x1, blocking collectives, exchange(): return lax.all_to_all(value, axes, 0, 0, tiled=True)  14.7 us
    all_to_all x5, waiting for transfers between devices, exchange(): return lax.all_to_all(value, axes, 0, 0, tiled=True)  11.8 us
    pallas_call x1, Pallas kernels, carry_rows(): call(functools.partial(carry_kernel, halves, share), 8 * flat_two.size *...  10.3 us
    pallas_call x1, Pallas kernels, sketch(): call(sketch_kernel, 2 * core_two.size * columns * 4, 4 * (core_two.size +...  9.8 us
    pallas_call x1, Pallas kernels, first_factor(): call(functools.partial(first_kernel, scale, band), 8 * raw.size * columns...  9.19 us
  transfers between devices with their start and end apart: 21, of which 8 were waited for; matrix products, arithmetic and copies ran while one was open for 3% of the time, Pallas kernels for 30%

profile of v14, /device:TPU:0, one launch (start us, length us, event | category | flops | bytes accessed | tf_op | source)
XLA Modules:
  0.0 156.5 jit_solution(12133297943041042615)
XLA Ops:
  0.6 9.8 %shard_map.67 = (f32[40,128,128]{2,1,0:T(8,128)}, f32[128,128]{1,0:T(8,128)}) custom-call(f32[128,40,512]{2,1,0:T(8,128)} %refs_0_.1, f32[512,128]{1,0:T(8,128)} %refs_1_.1, f32[128,40,128]{2,1,0:T(8,128)} %refs_2_.1), custom_call_target="tpu_custom_call" | custom-call | flops 2684354560 | bytes 15728640 | tf_op jit(solution)/shard_map/pallas_call | solution.py:102
  10.4 2.5 %constant_dynamic-slice_fusion.2 = (f32[10,128,128]{2,1,0:T(8,128)}, f32[10,128,128]{2,1,0:T(8,128)}) fusion(f32[40,128,128]{2,1,0:T(8,128)} %get-tuple-element.55, s32[]{:T(128)S(6)} %select_n.13, s32[]{:T(128)S(6)} %select_n.12), kind=kLoop, calls=%fused_computation.4 | loop fusion | bytes 2621448 | tf_op jit(solution)/shard_map/dynamic_slice | solution.py:470
  12.9 2.9 %collective-permute-start = (f32[10,128,128]{2,1,0:T(8,128)}, f32[10,128,128]{2,1,0:T(8,128)}, u32[]{:S(2)}, u32[]{:S(2)}) collective-permute-start(f32[10,128,128]{2,1,0:T(8,128)} %get-tuple-element.86), channel_id=1, source_target_pairs={{0,1},{1,0},{2,3},{3,2},{4,5},{5,4},{6,7},{7,6},{8,9},{9,8},{10,11... | collective-permute-start | bytes 1966088 | tf_op jit(solution)/shard_map/ppermute | solution.py:421
  15.8 1.5 collective-permute-start.1
  17.4 4.9 %all-to-all-start = ((f32[8,16,128]{2,1,0:T(8,128)}), f32[8,16,128]{2,1,0:T(8,128)S(1)}, u32[]{:S(2)}, u32[]{:S(2)}) async-start(f32[8,16,128]{2,1,0:T(8,128)} %bitcast.2), calls=%async_computation | async-start | bytes 131072 | tf_op jit(solution)/shard_map/all_to_all | solution.py:425
  22.2 6.5 %shard_map.68.refs_0_ = f32[512,1024]{1,0:T(8,128)} custom-call(f32[5120,512]{1,0:T(8,128)} %bitcast.13), custom_call_target="tpu_custom_call" | custom-call | flops 2147483648 | bytes 4194304 | tf_op jit(solution)/shard_map/pallas_call | solution.py:160
  28.8 0.0 all-to-all-done
  28.8 0.7 broadcast_in_dim.6
  29.5 4.2 %all-to-all-start.1 = ((f32[32,16,128]{2,1,0:T(8,128)}), f32[32,16,128]{2,1,0:T(8,128)S(1)}, u32[]{:S(2)}, u32[]{:S(2)}) async-start(f32[32,16,128]{2,1,0:T(8,128)} %broadcast_in_dim.6), calls=%async_computation.1 | async-start | bytes 524288 | tf_op jit(solution)/shard_map/all_to_all | solution.py:425
  33.7 0.0 collective-permute-done.refs_1_
  33.7 0.0 collective-permute-done.1.refs_2_
  33.7 0.9 constant_dynamic-slice_fusion.1
  34.6 2.7 %collective-permute-start.2 = (f32[10,128,128]{2,1,0:T(8,128)}, f32[10,128,128]{2,1,0:T(8,128)}, u32[]{:S(2)}, u32[]{:S(2)}) collective-permute-start(f32[10,128,128]{2,1,0:T(8,128)} %constant_dynamic-slice_fusion.1), channel_id=1, source_target_pairs={{0,3},{1,2},{2,1},{3,0},{4,7},{5,6},{6,5},{7,4},{8,11},{9,10},{10,... | collective-permute-start | bytes 1966088 | tf_op jit(solution)/shard_map/ppermute | solution.py:421
  37.3 8.5 %shard_map.69.square_ref = bf16[512,1024]{1,0:T(8,128)(2,1)} custom-call(f32[5120,512]{1,0:T(8,128)} %bitcast.14, f32[512,1024]{1,0:T(8,128)} %shard_map.68.refs_0_), custom_call_target="tpu_custom_call" | custom-call | flops 3221225472 | bytes 6291456 | tf_op jit(solution)/shard_map/pallas_call | solution.py:160
  45.8 0.0 all-to-all-done.1
  45.8 0.7 copy-done.2
  46.5 2.4 %shard_map.70 = f32[512,128]{1,0:T(8,128)} custom-call(bf16[512,1024]{1,0:T(8,128)(2,1)} %shard_map.69.square_ref, f32[512,128]{1,0:T(8,128)} %bitcast.20), custom_call_target="tpu_custom_call" | custom-call | flops 268435456 | bytes 1572864 | tf_op jit(solution)/shard_map/pallas_call | solution.py:178
  48.9 14.7 %all_to_all.30 = f32[32,16,128]{2,1,0:T(8,128)S(1)} all-to-all(f32[32,16,128]{2,1,0:T(8,128)} %bitcast.23), channel_id=1, replica_groups=mesh['cuts'=8,'rank'=4] {'cuts','rank'}, dimensions={0} | all-to-all | bytes 524288 | tf_op jit(solution)/shard_map/all_to_all | solution.py:425
  63.6 0.0 collective-permute-done.2.refs_3_
  63.6 0.7 broadcast_in_dim.7
  64.3 2.8 %all-to-all-start.3 = ((f32[32,16,128]{2,1,0:T(8,128)}), f32[32,16,128]{2,1,0:T(8,128)S(1)}, u32[]{:S(2)}, u32[]{:S(2)}) async-start(f32[32,16,128]{2,1,0:T(8,128)} %broadcast_in_dim.7), calls=%async_computation.3 | async-start | bytes 524288 | tf_op jit(solution)/shard_map/all_to_all | solution.py:425
  67.1 0.9 constant_dynamic-slice_fusion.refs_0_
  68.0 9.9 %all-to-all-done.3 = f32[32,16,128]{2,1,0:T(8,128)S(1)} async-done(((f32[32,16,128]{2,1,0:T(8,128)}), f32[32,16,128]{2,1,0:T(8,128)S(1)}, u32[]{:S(2)}, u32[]{:S(2)}) %all-to-all-start.3) | async-done | bytes 262176 | tf_op jit(solution)/shard_map/all_to_all | solution.py:425
  77.9 0.7 copy-done.1
  78.6 3.5 %shard_map.71 = (f32[5,128,128]{2,1,0:T(8,128)}, f32[5,128,128]{2,1,0:T(8,128)}) custom-call(s32[1]{0:T(128)} %bitcast.1.rank_ref, f32[512,128]{1,0:T(8,128)} %bitcast.18, f32[10,128,128]{2,1,0:T(8,128)} %constant_dynamic-slice_fusion.refs_0_, f32[10,128,128]{2,1,0:T(8,128)} %collective-permute-done.refs_1_, f32[10,128,128]{2,1,0:T(8,128)} %collective-permute-done.1.refs_2_, ...), custom_call_target="tpu_custom_call" | custom-call | flops 671088640 | bytes 2883584 | tf_op jit(solution)/shard_map/pallas_call | solution.py:208
  82.1 0.0 collective-permute-start.4
  82.1 1.4 collective-permute-start.3
  83.5 0.6 collective-permute-start.5
  84.1 2.0 %collective-permute-start.6 = (f32[5,128,128]{2,1,0:T(8,128)}, f32[5,128,128]{2,1,0:T(8,128)S(1)}, u32[]{:S(2)}, u32[]{:S(2)}) collective-permute-start(f32[5,128,128]{2,1,0:T(8,128)} %get-tuple-element.61.refs_1_.refs_5_), channel_id=1, source_target_pairs={{0,1},{1,0},{2,3},{3,2},{4,5},{5,4},{6,7},{7,6},{8,9},{9,8},{10,11... | collective-permute-start | bytes 983048 | tf_op jit(solution)/shard_map/ppermute | solution.py:421
  86.2 9.2 %shard_map.72 = (f32[160,128]{1,0:T(8,128)}, f32[512,128]{1,0:T(8,128)}, f32[128,128]{1,0:T(8,128)}) custom-call(s32[1]{0:T(128)} %bitcast.1.rank_ref, f32[512,128]{1,0:T(8,128)} %bitcast.21, f32[512,128]{1,0:T(8,128)} %bitcast.19), custom_call_target="tpu_custom_call" | custom-call | flops 67108864 | bytes 1048576 | tf_op jit(solution)/shard_map/pallas_call | solution.py:392
  95.3 0.0 collective-permute-done.4.refs_2_
  95.4 0.0 collective-permute-done.3.refs_7_
  95.4 0.1 collective-permute-start.9
  95.4 1.4 collective-permute-start.8
  96.8 3.1 %collective-permute-done.5.refs_3_ = f32[5,128,128]{2,1,0:T(8,128)S(1)} collective-permute-done((f32[5,128,128]{2,1,0:T(8,128)}, f32[5,128,128]{2,1,0:T(8,128)S(1)}, u32[]{:S(2)}, u32[]{:S(2)}) %collective-permute-start.5) | collective-permute-done | bytes 327712 | tf_op jit(solution)/shard_map/ppermute | solution.py:421
  99.9 0.1 collective-permute-done.6.refs_6_
  100.0 2.6 %shard_map.73 = f32[128,128]{1,0:T(8,128)} custom-call(f32[128,128]{1,0:T(8,128)} %get-tuple-element.69.inverse_ref, f32[5,128,128]{2,1,0:T(8,128)} %get-tuple-element.62.refs_0_.refs_1_, f32[5,128,128]{2,1,0:T(8,128)} %get-tuple-element.61.refs_1_.refs_5_), custom_call_target="tpu_custom_call" | custom-call | flops 335544320 | bytes 655360 | tf_op jit(solution)/shard_map/pallas_call | solution.py:232
  102.6 0.0 collective-permute-start.7
  102.6 1.5 collective-permute-done.7
  104.1 0.8 add.37
  104.9 0.2 collective-permute-done.9.refs_8_
  105.2 0.8 collective-permute-done.8.refs_4_
  106.0 0.7 copy-done.8
  106.7 10.3 %shard_map.74 = (f32[512,128]{1,0:T(8,128)}, f32[1280,128]{1,0:T(8,128)}) custom-call(s32[1]{0:T(128)} %bitcast.1.rank_ref, f32[160,128]{1,0:T(8,128)} %get-tuple-element.71.weight_ref, f32[5120,512]{1,0:T(8,128)} %bitcast.16, f32[5,128,128]{2,1,0:T(8,128)} %get-tuple-element.62.refs_0_.refs_1_, f32[5,128,128]{2,1,0:T(8,128)} %copy-done.3, ...), custom_call_target="tpu_custom_call" | custom-call | flops 2684354560 | bytes 13107200 | tf_op jit(solution)/shard_map/pallas_call | solution.py:281
  117.0 1.0 collective-permute-start.10
  118.0 1.2 collective-permute-start.11
  119.3 1.3 collective-permute-start.12
  120.5 2.8 %all-to-all-start.4 = ((f32[32,16,128]{2,1,0:T(8,128)}), f32[32,16,128]{2,1,0:T(8,128)S(1)}, u32[]{:S(2)}, u32[]{:S(2)}) async-start(f32[32,16,128]{2,1,0:T(8,128)} %bitcast.24), calls=%async_computation.4 | async-start | bytes 524288 | tf_op jit(solution)/shard_map/all_to_all | solution.py:425
  123.3 0.0 collective-permute-done.10
  123.3 0.0 collective-permute-done.11
  123.3 1.1 collective-permute-done.12
  124.4 0.8 collective-permute-start.13
  125.2 2.4 %collective-permute-start.14 = (f32[128,128]{1,0:T(8,128)S(1)}, f32[128,128]{1,0:T(8,128)S(1)}, u32[]{:S(2)}, u32[]{:S(2)}) collective-permute-start(f32[128,128]{1,0:T(8,128)S(1)} %add_add_fusion.1), channel_id=1, source_target_pairs={{0,16},{4,20},{8,24},{12,28},{16,0},{20,4},{24,8},{28,12},{1,17},{... | collective-permute-start | bytes 196616 | tf_op jit(solution)/shard_map/ppermute | solution.py:421
  127.6 1.3 collective-permute-start.15
  128.9 8.5 %shard_map.75 = f32[5120,128]{1,0:T(8,128)} custom-call(f32[5120,512]{1,0:T(8,128)} %bitcast.15, f32[512,128]{1,0:T(8,128)} %get-tuple-element.78.weight_ref), custom_call_target="tpu_custom_call" | custom-call | flops 2684354560 | bytes 13107200 | tf_op jit(solution)/shard_map/pallas_call | solution.py:310
  137.4 0.0 collective-permute-done.13
  137.4 0.0 collective-permute-done.14
  137.4 0.0 collective-permute-done.15
  137.4 0.6 add_add_fusion.gram_ref
  138.1 0.7 broadcast_in_dim.8
  138.8 5.0 %all-to-all-start.5 = ((f32[32,16,128]{2,1,0:T(8,128)}), f32[32,16,128]{2,1,0:T(8,128)S(1)}, u32[]{:S(2)}, u32[]{:S(2)}) async-start(f32[32,16,128]{2,1,0:T(8,128)} %broadcast_in_dim.8), calls=%async_computation.5 | async-start | bytes 524288 | tf_op jit(solution)/shard_map/all_to_all | solution.py:425
  143.8 8.8 %shard_map.76 = (f32[128,128]{1,0:T(8,128)}, f32[1280,128]{1,0:T(8,128)}) custom-call(f32[128,128]{1,0:T(8,128)} %add_add_fusion.gram_ref, f32[1280,128]{1,0:T(8,128)} %get-tuple-element.81.middle_ref), custom_call_target="tpu_custom_call" | custom-call | flops 167772160 | bytes 1310720 | tf_op jit(solution)/shard_map/pallas_call | solution.py:410
  152.6 1.9 %all-to-all-done.5 = f32[32,16,128]{2,1,0:T(8,128)S(1)} async-done(((f32[32,16,128]{2,1,0:T(8,128)}), f32[32,16,128]{2,1,0:T(8,128)S(1)}, u32[]{:S(2)}, u32[]{:S(2)}) %all-to-all-start.5) | async-done | bytes 262176 | tf_op jit(solution)/shard_map/all_to_all | solution.py:425
  154.6 1.9 %fusion = f32[128,512]{1,0:T(8,128)} fusion(f32[128,128]{1,0:T(8,128)} %get-tuple-element.83, f32[512,128]{1,0:T(8,128)S(1)} %bitcast.22), kind=kOutput, calls=%fused_computation.6 | convolution fusion | flops 100663296 | bytes 589824 | tf_op jit(solution)/shard_map/dot_general | solution.py:53
  (20 shorter events, 0.1 us)
Async XLA Ops:
  12.9 20.8 %collective-permute-start = (f32[10,128,128]{2,1,0:T(8,128)}, f32[10,128,128]{2,1,0:T(8,128)}, u32[]{:S(2)}, u32[]{:S(2)}) collective-permute-start(f32[10,128,128]{2,1,0:T(8,128)} %get-tuple-element.86), channel_id=1, source_target_pairs={{0,1},{1,0},{2,3},{3,2},{4,5},{5,4},{6,7},{7,6},{8,9},{9,8},{10,11... | collective-permute-start | bytes 1966088 | tf_op jit(solution)/shard_map/ppermute | solution.py:421
  15.8 17.9 %collective-permute-start.1 = (f32[10,128,128]{2,1,0:T(8,128)}, f32[10,128,128]{2,1,0:T(8,128)}, u32[]{:S(2)}, u32[]{:S(2)}) collective-permute-start(f32[10,128,128]{2,1,0:T(8,128)} %get-tuple-element.85), channel_id=1, source_target_pairs={{0,2},{1,3},{2,0},{3,1},{4,6},{5,7},{6,4},{7,5},{8,10},{9,11},{10,... | collective-permute-start | bytes 1966088 | tf_op jit(solution)/shard_map/ppermute | solution.py:421
  17.4 11.4 %all-to-all-start = ((f32[8,16,128]{2,1,0:T(8,128)}), f32[8,16,128]{2,1,0:T(8,128)S(1)}, u32[]{:S(2)}, u32[]{:S(2)}) async-start(f32[8,16,128]{2,1,0:T(8,128)} %bitcast.2), calls=%async_computation | async-start | bytes 131072 | tf_op jit(solution)/shard_map/all_to_all | solution.py:425
  22.2 11.5 %copy-start = (f32[40,128,128]{2,1,0:T(8,128)S(1)}, f32[40,128,128]{2,1,0:T(8,128)}, u32[]{:S(2)}) copy-start(f32[40,128,128]{2,1,0:T(8,128)} %get-tuple-element.55) | copy-start | bytes 7864324
  29.5 16.3 %all-to-all-start.1 = ((f32[32,16,128]{2,1,0:T(8,128)}), f32[32,16,128]{2,1,0:T(8,128)S(1)}, u32[]{:S(2)}, u32[]{:S(2)}) async-start(f32[32,16,128]{2,1,0:T(8,128)} %broadcast_in_dim.6), calls=%async_computation.1 | async-start | bytes 524288 | tf_op jit(solution)/shard_map/all_to_all | solution.py:425
  34.6 29.0 %collective-permute-start.2 = (f32[10,128,128]{2,1,0:T(8,128)}, f32[10,128,128]{2,1,0:T(8,128)}, u32[]{:S(2)}, u32[]{:S(2)}) collective-permute-start(f32[10,128,128]{2,1,0:T(8,128)} %constant_dynamic-slice_fusion.1), channel_id=1, source_target_pairs={{0,3},{1,2},{2,1},{3,0},{4,7},{5,6},{6,5},{7,4},{8,11},{9,10},{10,... | collective-permute-start | bytes 1966088 | tf_op jit(solution)/shard_map/ppermute | solution.py:421
  45.8 0.7 copy-start.2
  64.3 13.5 %all-to-all-start.3 = ((f32[32,16,128]{2,1,0:T(8,128)}), f32[32,16,128]{2,1,0:T(8,128)S(1)}, u32[]{:S(2)}, u32[]{:S(2)}) async-start(f32[32,16,128]{2,1,0:T(8,128)} %broadcast_in_dim.7), calls=%async_computation.3 | async-start | bytes 524288 | tf_op jit(solution)/shard_map/all_to_all | solution.py:425
  77.9 0.7 copy-start.1
  82.1 13.2 %collective-permute-start.4 = (f32[5,128,128]{2,1,0:T(8,128)}, f32[5,128,128]{2,1,0:T(8,128)S(1)}, u32[]{:S(2)}, u32[]{:S(2)}) collective-permute-start(f32[5,128,128]{2,1,0:T(8,128)} %get-tuple-element.62.refs_0_.refs_1_), channel_id=1, source_target_pairs={{0,1},{1,0},{2,3},{3,2},{4,5},{5,4},{6,7},{7,6},{8,9},{9,8},{10,11... | collective-permute-start | bytes 983048 | tf_op jit(solution)/shard_map/ppermute | solution.py:421
  82.1 13.2 %collective-permute-start.3 = (f32[5,128,128]{2,1,0:T(8,128)}, f32[5,128,128]{2,1,0:T(8,128)S(1)}, u32[]{:S(2)}, u32[]{:S(2)}) collective-permute-start(f32[5,128,128]{2,1,0:T(8,128)} %get-tuple-element.61.refs_1_.refs_5_), channel_id=1, source_target_pairs={{0,2},{1,3},{2,0},{3,1},{4,6},{5,7},{6,4},{7,5},{8,10},{9,11},{10,... | collective-permute-start | bytes 983048 | tf_op jit(solution)/shard_map/ppermute | solution.py:421
  83.5 16.4 %collective-permute-start.5 = (f32[5,128,128]{2,1,0:T(8,128)}, f32[5,128,128]{2,1,0:T(8,128)S(1)}, u32[]{:S(2)}, u32[]{:S(2)}) collective-permute-start(f32[5,128,128]{2,1,0:T(8,128)} %get-tuple-element.62.refs_0_.refs_1_), channel_id=1, source_target_pairs={{0,2},{1,3},{2,0},{3,1},{4,6},{5,7},{6,4},{7,5},{8,10},{9,11},{10,... | collective-permute-start | bytes 983048 | tf_op jit(solution)/shard_map/ppermute | solution.py:421
  84.1 15.9 %collective-permute-start.6 = (f32[5,128,128]{2,1,0:T(8,128)}, f32[5,128,128]{2,1,0:T(8,128)S(1)}, u32[]{:S(2)}, u32[]{:S(2)}) collective-permute-start(f32[5,128,128]{2,1,0:T(8,128)} %get-tuple-element.61.refs_1_.refs_5_), channel_id=1, source_target_pairs={{0,1},{1,0},{2,3},{3,2},{4,5},{5,4},{6,7},{7,6},{8,9},{9,8},{10,11... | collective-permute-start | bytes 983048 | tf_op jit(solution)/shard_map/ppermute | solution.py:421
  95.4 10.7 %copy-start.3 = (f32[5,128,128]{2,1,0:T(8,128)}, f32[5,128,128]{2,1,0:T(8,128)S(1)}, u32[]{:S(2)}) copy-start(f32[5,128,128]{2,1,0:T(8,128)S(1)} %collective-permute-done.4.refs_2_) | copy-start | bytes 983044
  95.4 10.7 %copy-start.4 = (f32[5,128,128]{2,1,0:T(8,128)}, f32[5,128,128]{2,1,0:T(8,128)S(1)}, u32[]{:S(2)}) copy-start(f32[5,128,128]{2,1,0:T(8,128)S(1)} %collective-permute-done.3.refs_7_) | copy-start | bytes 983044
  95.4 9.8 %collective-permute-start.9 = (f32[5,128,128]{2,1,0:T(8,128)S(1)}, f32[5,128,128]{2,1,0:T(8,128)S(1)}, u32[]{:S(2)}, u32[]{:S(2)}) collective-permute-start(f32[5,128,128]{2,1,0:T(8,128)S(1)} %collective-permute-done.3.refs_7_), channel_id=1, source_target_pairs={{0,1},{1,0},{2,3},{3,2},{4,5},{5,4},{6,7},{7,6},{8,9},{9,8},{10,11... | collective-permute-start | bytes 983048 | tf_op jit(solution)/shard_map/ppermute | solution.py:421
  95.4 10.6 %collective-permute-start.8 = (f32[5,128,128]{2,1,0:T(8,128)S(1)}, f32[5,128,128]{2,1,0:T(8,128)S(1)}, u32[]{:S(2)}, u32[]{:S(2)}) collective-permute-start(f32[5,128,128]{2,1,0:T(8,128)S(1)} %collective-permute-done.4.refs_2_), channel_id=1, source_target_pairs={{0,2},{1,3},{2,0},{3,1},{4,6},{5,7},{6,4},{7,5},{8,10},{9,11},{10,... | collective-permute-start | bytes 983048 | tf_op jit(solution)/shard_map/ppermute | solution.py:421
  99.9 6.1 %copy-start.5 = (f32[5,128,128]{2,1,0:T(8,128)}, f32[5,128,128]{2,1,0:T(8,128)S(1)}, u32[]{:S(2)}) copy-start(f32[5,128,128]{2,1,0:T(8,128)S(1)} %collective-permute-done.5.refs_3_) | copy-start | bytes 983044
  100.0 6.0 %copy-start.6 = (f32[5,128,128]{2,1,0:T(8,128)}, f32[5,128,128]{2,1,0:T(8,128)S(1)}, u32[]{:S(2)}) copy-start(f32[5,128,128]{2,1,0:T(8,128)S(1)} %collective-permute-done.6.refs_6_) | copy-start | bytes 983044
  102.6 1.5 collective-permute-start.7
  105.2 0.9 copy-start.7
  106.0 0.7 copy-start.8
  117.0 6.3 %collective-permute-start.10 = (f32[128,128]{1,0:T(8,128)S(1)}, f32[128,128]{1,0:T(8,128)S(1)}, u32[]{:S(2)}, u32[]{:S(2)}) collective-permute-start(f32[128,128]{1,0:T(8,128)S(1)} %add.37), channel_id=1, source_target_pairs={{0,1},{1,0},{2,3},{3,2},{4,5},{5,4},{6,7},{7,6},{8,9},{9,8},{10,11... | collective-permute-start | bytes 196616 | tf_op jit(solution)/shard_map/ppermute | solution.py:421
  118.0 5.3 %collective-permute-start.11 = (f32[128,128]{1,0:T(8,128)S(1)}, f32[128,128]{1,0:T(8,128)S(1)}, u32[]{:S(2)}, u32[]{:S(2)}) collective-permute-start(f32[128,128]{1,0:T(8,128)S(1)} %add.37), channel_id=1, source_target_pairs={{0,2},{1,3},{2,0},{3,1},{4,6},{5,7},{6,4},{7,5},{8,10},{9,11},{10,... | collective-permute-start | bytes 196616 | tf_op jit(solution)/shard_map/ppermute | solution.py:421
  119.3 5.2 %collective-permute-start.12 = (f32[128,128]{1,0:T(8,128)S(1)}, f32[128,128]{1,0:T(8,128)S(1)}, u32[]{:S(2)}, u32[]{:S(2)}) collective-permute-start(f32[128,128]{1,0:T(8,128)S(1)} %add.37), channel_id=1, source_target_pairs={{0,3},{1,2},{2,1},{3,0},{4,7},{5,6},{6,5},{7,4},{8,11},{9,10},{10,... | collective-permute-start | bytes 196616 | tf_op jit(solution)/shard_map/ppermute | solution.py:421
  120.5 17.5 %all-to-all-start.4 = ((f32[32,16,128]{2,1,0:T(8,128)}), f32[32,16,128]{2,1,0:T(8,128)S(1)}, u32[]{:S(2)}, u32[]{:S(2)}) async-start(f32[32,16,128]{2,1,0:T(8,128)} %bitcast.24), calls=%async_computation.4 | async-start | bytes 524288 | tf_op jit(solution)/shard_map/all_to_all | solution.py:425
  124.4 12.9 %collective-permute-start.13 = (f32[128,128]{1,0:T(8,128)S(1)}, f32[128,128]{1,0:T(8,128)S(1)}, u32[]{:S(2)}, u32[]{:S(2)}) collective-permute-start(f32[128,128]{1,0:T(8,128)S(1)} %add_add_fusion.1), channel_id=1, source_target_pairs={{0,8},{4,12},{8,0},{12,4},{16,24},{20,28},{24,16},{28,20},{1,9},{5... | collective-permute-start | bytes 196616 | tf_op jit(solution)/shard_map/ppermute | solution.py:421
  125.2 12.2 %collective-permute-start.14 = (f32[128,128]{1,0:T(8,128)S(1)}, f32[128,128]{1,0:T(8,128)S(1)}, u32[]{:S(2)}, u32[]{:S(2)}) collective-permute-start(f32[128,128]{1,0:T(8,128)S(1)} %add_add_fusion.1), channel_id=1, source_target_pairs={{0,16},{4,20},{8,24},{12,28},{16,0},{20,4},{24,8},{28,12},{1,17},{... | collective-permute-start | bytes 196616 | tf_op jit(solution)/shard_map/ppermute | solution.py:421
  127.6 9.8 %collective-permute-start.15 = (f32[128,128]{1,0:T(8,128)S(1)}, f32[128,128]{1,0:T(8,128)S(1)}, u32[]{:S(2)}, u32[]{:S(2)}) collective-permute-start(f32[128,128]{1,0:T(8,128)S(1)} %add_add_fusion.1), channel_id=1, source_target_pairs={{0,24},{4,28},{8,16},{12,20},{16,8},{20,12},{24,0},{28,4},{1,25},{... | collective-permute-start | bytes 196616 | tf_op jit(solution)/shard_map/ppermute | solution.py:421
  138.8 15.7 %all-to-all-start.5 = ((f32[32,16,128]{2,1,0:T(8,128)}), f32[32,16,128]{2,1,0:T(8,128)S(1)}, u32[]{:S(2)}, u32[]{:S(2)}) async-start(f32[32,16,128]{2,1,0:T(8,128)} %broadcast_in_dim.8), calls=%async_computation.5 | async-start | bytes 524288 | tf_op jit(solution)/shard_map/all_to_all | solution.py:425
